TPU v7x, 32 devices: a whole 2x2x4 slice. The times are simulated.
32 devices in a mesh: dp: 4 (over z), mp: 4 (over y, x), teach: 2 (over core).
Axes of the slice: x: 2, y: 2, z: 4, core: 2. Of those that a mesh axis runs over, the one named last changes fastest.
Arguments:
- patches: bfloat16 [64, 280, 768], P(('dp', 'teach')), may hold values from -6 to 6
- grid_sizes: int32 [64, 2], P(('dp', 'teach')), may hold values from 1 to 24, as said below
- label_ids: int32 [64, 2], P(('dp', 'teach')), may hold values from 0 to 999
- label_mix: float32 [64], P(('dp', 'teach')), may hold values from 0.3 to 0.7
- image_weight: float32 [64], P(('dp', 'teach')), may hold values from 0.5 to 13.5
- teacher_stem: bfloat16 [768, 224], replicated, may hold values from -0.21875 to 0.21875
- teacher_head: bfloat16 [224, 1000], P(None, 'mp'), may hold values from -2.390625 to 2.390625
- patch_weight: float32 [768, 768], P(('dp', 'teach')), may hold values from -0.21875 to 0.21875
- attn_weight: float32 [2, 4, 768, 768], P(None, None, ('dp', 'teach'), 'mp'), may hold values from -0.21875 to 0.21875
- mlp_weight: float32 [2, 2, 768, 3072], P(None, None, ('dp', 'teach'), 'mp'), may hold values from -0.15309311 to 0.15309311
- head_weight: float32 [2, 768, 1000], P(None, ('dp', 'teach'), 'mp'), may hold values from -0.4330127 to 0.4330127
- vector_params: float32 [65, 768], replicated, may hold values from -1.7 to 1.7
- split_biases: float32 [11216], P('mp'), may hold values from -1.8 to 1.8
- patch_first: float32 [768, 768], P(('dp', 'teach')), may hold values from -0.02734375 to 0.02734375
- attn_first: float32 [2, 4, 768, 768], P(None, None, ('dp', 'teach'), 'mp'), may hold values from -0.02734375 to 0.02734375
- mlp_first: float32 [2, 2, 768, 3072], P(None, None, ('dp', 'teach'), 'mp'), may hold values from -0.02734375 to 0.02734375
- head_first: float32 [2, 768, 1000], P(None, ('dp', 'teach'), 'mp'), may hold values from -0.02734375 to 0.02734375
- vector_first: float32 [65, 768], replicated, may hold values from -0.02734375 to 0.02734375
- bias_first: float32 [11216], P('mp'), may hold values from -0.02734375 to 0.02734375
- patch_second: float32 [768, 768], P(('dp', 'teach')), may hold values from 2.0345053e-05 to 8.138021e-05
- attn_second: float32 [2, 4, 768, 768], P(None, None, ('dp', 'teach'), 'mp'), may hold values from 2.0345053e-05 to 8.138021e-05
- mlp_second: float32 [2, 2, 768, 3072], P(None, None, ('dp', 'teach'), 'mp'), may hold values from 2.0345053e-05 to 8.138021e-05
- head_second: float32 [2, 768, 1000], P(None, ('dp', 'teach'), 'mp'), may hold values from 2.0345053e-05 to 8.138021e-05
- vector_second: float32 [65, 768], replicated, may hold values from 2.0345053e-05 to 8.138021e-05
- bias_second: float32 [11216], P('mp'), may hold values from 2.0345053e-05 to 8.138021e-05
- decay_mask: int32 [17], replicated, may hold values from 0 to 1
- layer_ids: int32 [17], replicated, may hold values from 0 to 2
- step_count: int32 [1], replicated, may hold values from 2 to 20
Outputs:
- patch_updated: float32 [768, 768], P(('dp', 'teach'))
- attn_updated: float32 [2, 4, 768, 768], P(None, None, ('dp', 'teach'), 'mp')
- mlp_updated: float32 [2, 2, 768, 3072], P(None, None, ('dp', 'teach'), 'mp')
- head_updated: float32 [2, 768, 1000], P(None, ('dp', 'teach'), 'mp')
- vector_updated: float32 [65, 768], replicated
- bias_updated: float32 [11216], P('mp')
- patch_moment: float32 [768, 768], P(('dp', 'teach'))
- attn_moment: float32 [2, 4, 768, 768], P(None, None, ('dp', 'teach'), 'mp')
- mlp_moment: float32 [2, 2, 768, 3072], P(None, None, ('dp', 'teach'), 'mp')
- head_moment: float32 [2, 768, 1000], P(None, ('dp', 'teach'), 'mp')
- vector_moment: float32 [65, 768], replicated
- bias_moment: float32 [11216], P('mp')
- patch_square: float32 [768, 768], P(('dp', 'teach'))
- attn_square: float32 [2, 4, 768, 768], P(None, None, ('dp', 'teach'), 'mp')
- mlp_square: float32 [2, 2, 768, 3072], P(None, None, ('dp', 'teach'), 'mp')
- head_square: float32 [2, 768, 1000], P(None, ('dp', 'teach'), 'mp')
- vector_square: float32 [65, 768], replicated
- bias_square: float32 [11216], P('mp')
- lamb_norms: float32 [2, 17], replicated
- trust_ratios: float32 [17], replicated
- loss_value: float32 [], replicated
Inputs may be any that keep to these rules, and one draw needn't show every extreme that they name: `grid_sizes`: each image's grid has gh * gw <= 280.
All inputs are finite; a program needn't handle non-finite values.
Results may differ from a plain program's by a relative error of at most 0.014.
The roundings to bfloat16 on the way count: a program that leaves them out, or rounds other values in their place, can miss the bound.
Values may be sent and summed in bfloat16 or wider, within the bound.
No kernel may reach another device: no remote copies, remote signals or barrier semaphores. Data moves between devices by JAX's collectives and lax.ppermute only.
A program may use at most 256 MiB of HBM per device.

v0:
```python
import jax
import jax.numpy as jnp
from jax import lax
from jax.sharding import PartitionSpec as P

D = 768
HD = 64
G = 24
PMAX = 280
L = 2
R = 282


EPS_NORM = 1e-06
EPS_LAMB = 1e-06
BETA = 0.5
DECAY = 0.05
BASE_RATE = 0.4
LAYER_DECAY = 0.8
SCALE = 0.125
MASKED = -1e30
HIGH = lax.Precision.HIGHEST


def matmul(left, right):
    return jnp.dot(left, right, preferred_element_type=jnp.float32)


def matmul_nt(left, right):
    return lax.dot_general(
        left, right, (((1,), (1,)), ((), ())), preferred_element_type=jnp.float32
    )


def matmul_tn(left, right):
    return lax.dot_general(
        left, right, (((0,), (0,)), ((), ())), preferred_element_type=jnp.float32
    )


def gelu_exact(values):
    return jax.nn.gelu(values, approximate=False)


def reduce_rows(partial_value):
    return lax.psum(partial_value, "mp")


def norm_forward(values, gain_row, bias_row):
    centre = values - jnp.mean(values, axis=-1, keepdims=True)
    scaled = lax.rsqrt(jnp.mean(centre * centre, axis=-1, keepdims=True) + EPS_NORM)
    normed = centre * scaled
    return (normed * gain_row + bias_row, normed, scaled)


def norm_backward(grad_out, normed, scaled, gain_row):
    grad_normed = grad_out * gain_row
    inner_sum = jnp.mean(grad_normed, axis=-1, keepdims=True)
    cross_term = jnp.mean(grad_normed * normed, axis=-1, keepdims=True)
    grad_in = scaled * (grad_normed - inner_sum - normed * cross_term)
    return (grad_in, jnp.sum(grad_out * normed, axis=0), jnp.sum(grad_out, axis=0))


def masked_scores(queries, key_rows, allowed):
    scores = (
        jnp.einsum("qhd,khd->hqk", queries, key_rows, preferred_element_type=jnp.float32) * SCALE
    )
    return jnp.where(allowed[None], scores, MASKED)


def attend_block(operands):
    queries, key_rows, value_rows, allowed = operands
    scores = masked_scores(queries, key_rows, allowed)
    row_peak = jnp.max(scores, axis=-1, keepdims=True)
    exponent = jnp.exp(scores - row_peak)
    row_total = jnp.sum(exponent, axis=-1, keepdims=True)
    soft_rows = (exponent / row_total).astype(jnp.bfloat16)
    attended = jnp.einsum("hqk,khd->qhd", soft_rows, value_rows, preferred_element_type=jnp.float32)
    return (attended.astype(jnp.bfloat16), (row_peak + jnp.log(row_total))[..., 0])


def attend_back(operands):
    queries, key_rows, value_rows, allowed, grad_rows, log_total = operands
    scores = masked_scores(queries, key_rows, allowed)
    soft_rows = jnp.exp(scores - log_total[..., None])
    grad_soft = jnp.einsum(
        "qhd,khd->hqk", grad_rows, value_rows, preferred_element_type=jnp.float32
    )
    inner_sum = jnp.sum(soft_rows * grad_soft, axis=-1, keepdims=True)
    grad_scores = (soft_rows * (grad_soft - inner_sum)).astype(jnp.bfloat16)
    grad_queries = (
        jnp.einsum("hqk,khd->qhd", grad_scores, key_rows, preferred_element_type=jnp.float32)
        * SCALE
    )
    grad_keys = (
        jnp.einsum("hqk,qhd->khd", grad_scores, queries, preferred_element_type=jnp.float32) * SCALE
    )
    grad_values = jnp.einsum(
        "hqk,qhd->khd",
        soft_rows.astype(jnp.bfloat16),
        grad_rows,
        preferred_element_type=jnp.float32,
    )
    return (
        grad_queries.astype(jnp.bfloat16),
        grad_keys.astype(jnp.bfloat16),
        grad_values.astype(jnp.bfloat16),
    )


def to_groups(values, group_rows):
    return values.reshape(values.shape[0] // group_rows, group_rows, -1, HD)


def layer_forward(residual, attn_mats, mlp_mats, gain_rows, biases, allowed, group_rows):
    query_bias, value_bias, up_bias = biases
    first_own, normed_a, scaled_a = norm_forward(residual, gain_rows[0], gain_rows[1])
    first_in = first_own.astype(jnp.bfloat16)
    queries = (matmul(first_in, attn_mats[0]) + query_bias).astype(jnp.bfloat16)
    key_rows = matmul(first_in, attn_mats[1]).astype(jnp.bfloat16)
    value_rows = (matmul(first_in, attn_mats[2]) + value_bias).astype(jnp.bfloat16)
    attended, log_total = lax.map(
        attend_block,
        (
            to_groups(queries, group_rows),
            to_groups(key_rows, group_rows),
            to_groups(value_rows, group_rows),
            allowed,
        ),
    )
    attended = attended.reshape(queries.shape[0], -1)
    middle = residual + reduce_rows(matmul_nt(attended, attn_mats[3])) + gain_rows[4]
    second_own, normed_b, scaled_b = norm_forward(middle, gain_rows[2], gain_rows[3])
    second_in = second_own.astype(jnp.bfloat16)
    upward = matmul(second_in, mlp_mats[0]) + up_bias
    hidden = gelu_exact(upward).astype(jnp.bfloat16)
    output = middle + reduce_rows(matmul_nt(hidden, mlp_mats[1])) + gain_rows[5]
    saved_acts = (
        normed_a,
        scaled_a,
        first_in,
        queries,
        key_rows,
        value_rows,
        attended,
        log_total,
        normed_b,
        scaled_b,
        second_in,
        upward,
        hidden,
    )
    return (output, saved_acts)


def layer_backward(grad_resid, attn_mats, mlp_mats, gain_rows, saved_acts, allowed, group_rows):
    (
        normed_a,
        scaled_a,
        first_in,
        queries,
        key_rows,
        value_rows,
        attended,
        log_total,
        normed_b,
        scaled_b,
        second_in,
        upward,
        hidden,
    ) = saved_acts
    row_count = queries.shape[0]
    grad_branch = grad_resid.astype(jnp.bfloat16)
    grad_down = matmul_tn(grad_branch, hidden)
    grad_hidden = matmul(grad_branch, mlp_mats[1])
    grad_upward = jax.vjp(gelu_exact, upward)[1](grad_hidden)[0].astype(jnp.bfloat16)
    grad_up = matmul_tn(second_in, grad_upward)
    grad_second = reduce_rows(matmul_nt(grad_upward, mlp_mats[0]))
    grad_middle, grad_gain_b, grad_shift_b = norm_backward(
        grad_second, normed_b, scaled_b, gain_rows[2]
    )
    grad_middle = grad_middle + grad_resid
    grad_mixed = grad_middle.astype(jnp.bfloat16)
    grad_outproj = matmul_tn(grad_mixed, attended)
    grad_attended = matmul(grad_mixed, attn_mats[3]).astype(jnp.bfloat16)
    grad_q, grad_k, grad_v = lax.map(
        attend_back,
        (
            to_groups(queries, group_rows),
            to_groups(key_rows, group_rows),
            to_groups(value_rows, group_rows),
            allowed,
            to_groups(grad_attended, group_rows),
            log_total,
        ),
    )
    grad_q = grad_q.reshape(row_count, -1)
    grad_k = grad_k.reshape(row_count, -1)
    grad_v = grad_v.reshape(row_count, -1)
    partial_first = (
        matmul_nt(grad_q, attn_mats[0])
        + matmul_nt(grad_k, attn_mats[1])
        + matmul_nt(grad_v, attn_mats[2])
    )
    grad_first = reduce_rows(partial_first)
    grad_in, grad_gain_a, grad_shift_a = norm_backward(grad_first, normed_a, scaled_a, gain_rows[0])
    grad_in = grad_in + grad_middle
    attn_grads = jnp.stack(
        [
            matmul_tn(first_in, grad_q),
            matmul_tn(first_in, grad_k),
            matmul_tn(first_in, grad_v),
            grad_outproj,
        ]
    )
    mlp_grads = jnp.stack([grad_up, grad_down])
    gain_grads = jnp.stack(
        [
            grad_gain_a,
            grad_shift_a,
            grad_gain_b,
            grad_shift_b,
            jnp.sum(grad_middle, axis=0),
            jnp.sum(grad_resid, axis=0),
        ]
    )
    bias_grads = jnp.concatenate(
        [
            jnp.sum(grad_q, axis=0, dtype=jnp.float32),
            jnp.sum(grad_v, axis=0, dtype=jnp.float32),
            jnp.sum(grad_upward, axis=0, dtype=jnp.float32),
        ]
    )
    return (grad_in, attn_grads, mlp_grads, gain_grads, bias_grads)


def adam_direction(gradient, first_moment, second_moment, correct_first, correct_second):
    new_first = BETA * first_moment + (1.0 - BETA) * gradient
    new_second = BETA * second_moment + (1.0 - BETA) * gradient * gradient
    return (
        new_first,
        new_second,
        new_first / correct_first / (jnp.sqrt(new_second / correct_second) + EPS_LAMB),
    )


def split_params(values):
    layered = values[1 : 1 + 6 * L].reshape(L, 6)
    return (
        values[0],
        layered[:, :4],
        layered[:, 4:],
        values[1 + 6 * L : 3 + 6 * L],
        values[3 + 6 * L],
        values[4 + 6 * L],
    )


def expand_params(pieces):
    return (
        pieces[0],
        pieces[1][:, :, None, None],
        pieces[2][:, :, None, None],
        pieces[3][:, None, None],
        pieces[4],
        pieces[5],
    )


def order_params(pieces):
    layered = jnp.concatenate([pieces[1], pieces[2]], axis=1).reshape(-1)
    return jnp.concatenate([pieces[0][None], layered, pieces[3], pieces[4][None], pieces[5][None]])


def squares_of(pieces, mp_first, data_first):
    return order_params(
        (
            jnp.sum(pieces[0] * pieces[0]) * mp_first,
            jnp.sum(pieces[1] * pieces[1], axis=(2, 3)),
            jnp.sum(pieces[2] * pieces[2], axis=(2, 3)),
            jnp.sum(pieces[3] * pieces[3], axis=(1, 2)),
            jnp.sum(pieces[4] * pieces[4]) * mp_first * data_first,
            jnp.sum(pieces[5] * pieces[5]) * data_first,
        )
    )


def per_device(
    patches,
    grid_sizes,
    label_ids,
    label_mix,
    image_weight,
    teacher_stem,
    teacher_head,
    patch_weight,
    attn_weight,
    mlp_weight,
    head_weight,
    vector_params,
    split_biases,
    patch_first,
    attn_first,
    mlp_first,
    head_first,
    vector_first,
    bias_first,
    patch_second,
    attn_second,
    mlp_second,
    head_second,
    vector_second,
    bias_second,
    decay_mask,
    layer_ids,
    step_count,
):
    weight_sum = lax.psum(jnp.sum(image_weight), ("dp", "teach"))
    patch_full, attn_full, mlp_full, head_full = (
        lax.all_gather(patch_weight.astype(jnp.bfloat16), ("dp", "teach"), axis=0, tiled=True),
        lax.all_gather(attn_weight.astype(jnp.bfloat16), ("dp", "teach"), axis=2, tiled=True),
        lax.all_gather(mlp_weight.astype(jnp.bfloat16), ("dp", "teach"), axis=2, tiled=True),
        lax.all_gather(head_weight.astype(jnp.bfloat16), ("dp", "teach"), axis=1, tiled=True),
    )
    images = patches.shape[0]
    rows_total = images * R
    width_local = attn_full.shape[3]
    ff_local = mlp_full.shape[3]
    class_local = head_full.shape[2]
    head_row = 6 * L
    mp_first = (lax.axis_index("mp") == 0).astype(jnp.float32)
    data_first = (lax.axis_index(("dp", "teach")) == 0).astype(jnp.float32)
    layer_biases = []
    for layer_num in range(L):
        offset = layer_num * (2 * width_local + ff_local)
        layer_biases.append(
            (
                split_biases[offset : offset + width_local],
                split_biases[offset + width_local : offset + 2 * width_local],
                split_biases[offset + 2 * width_local : offset + 2 * width_local + ff_local],
            )
        )
    head_start = L * (2 * width_local + ff_local)
    cls_bias = split_biases[head_start : head_start + class_local]
    dist_bias = split_biases[head_start + class_local : head_start + 2 * class_local]
    grid_rows = grid_sizes[:, 0:1]
    grid_cols = grid_sizes[:, 1:2]
    slot_ids = jnp.arange(PMAX, dtype=jnp.int32)[None, :]
    patch_live = slot_ids < grid_rows * grid_cols
    table_slots = jnp.arange(G, dtype=jnp.int32)
    row_onehot = (
        ((slot_ids // grid_cols)[..., None] == table_slots)
        .astype(jnp.float32)
        .reshape(images * PMAX, G)
    )
    col_onehot = (
        ((slot_ids % grid_cols)[..., None] == table_slots)
        .astype(jnp.float32)
        .reshape(images * PMAX, G)
    )
    patch_source = jnp.concatenate(
        [
            jnp.ones((images * PMAX, 1), jnp.float32),
            jnp.zeros((images * PMAX, 2), jnp.float32),
            row_onehot,
            col_onehot,
        ],
        axis=1,
    ).reshape(images, PMAX, 3 + 2 * G)
    token_source = jnp.broadcast_to(
        jnp.eye(2, 3 + 2 * G, 1, dtype=jnp.float32), (images, 2, 3 + 2 * G)
    )
    sources = jnp.concatenate([token_source, patch_source], axis=1).reshape(rows_total, 3 + 2 * G)
    flat_patches = patches.reshape(images * PMAX, -1)
    embedded = matmul(flat_patches, patch_full).reshape(images, PMAX, D)
    embedded_rows = jnp.concatenate(
        [jnp.zeros((images, 2, D), jnp.float32), embedded], axis=1
    ).reshape(rows_total, D)
    residual = embedded_rows + jnp.dot(sources, vector_params[head_row + 2 :], precision=HIGH)
    key_live = jnp.concatenate([jnp.ones((images, 2), dtype=bool), patch_live], axis=1)
    group_size = 2
    group_rows = group_size * R
    row_image = jnp.arange(group_rows, dtype=jnp.int32) // R
    allowed = (row_image[:, None] == row_image[None, :])[None] & key_live.reshape(
        images // group_size, 1, group_rows
    )
    saved_all = []
    for layer_num in range(L):
        residual, saved_acts = layer_forward(
            residual,
            attn_full[layer_num],
            mlp_full[layer_num],
            vector_params[6 * layer_num : 6 * layer_num + 6],
            layer_biases[layer_num],
            allowed,
            group_rows,
        )
        saved_all.append(saved_acts)
    final_own, normed_f, scaled_f = norm_forward(
        residual, vector_params[head_row], vector_params[head_row + 1]
    )
    final_rows = final_own.astype(jnp.bfloat16).reshape(images, R, D)[:, :2]
    logits_cls = matmul(final_rows[:, 0], head_full[0]) + cls_bias
    logits_dist = matmul(final_rows[:, 1], head_full[1]) + dist_bias
    stem_rows = gelu_exact(matmul(flat_patches, teacher_stem)).reshape(images, PMAX, -1)
    live_float = patch_live.astype(jnp.float32)
    pooled = (
        jnp.sum(stem_rows * live_float[..., None], axis=1)
        / jnp.sum(live_float, axis=1, keepdims=True)
    ).astype(jnp.bfloat16)
    logits_teacher = matmul(pooled, teacher_head)
    peak_cls, peak_dist, peak_teacher = lax.pmax(
        (
            jnp.max(logits_cls, axis=1),
            jnp.max(logits_dist, axis=1),
            jnp.max(logits_teacher, axis=1),
        ),
        "mp",
    )
    exp_cls = jnp.exp(logits_cls - peak_cls[:, None])
    exp_dist = jnp.exp(logits_dist - peak_dist[:, None])
    exp_teacher = jnp.exp(logits_teacher - peak_teacher[:, None])
    class_ids = lax.axis_index("mp") * class_local + jnp.arange(class_local, dtype=jnp.int32)
    target = label_mix[:, None] * (label_ids[:, 0:1] == class_ids).astype(jnp.float32) + (
        1.0 - label_mix[:, None]
    ) * (label_ids[:, 1:2] == class_ids).astype(jnp.float32)
    sum_cls, sum_dist, sum_teacher, target_dot, teacher_dot = lax.psum(
        (
            jnp.sum(exp_cls, axis=1),
            jnp.sum(exp_dist, axis=1),
            jnp.sum(exp_teacher, axis=1),
            jnp.sum(target * logits_cls, axis=1),
            jnp.sum(exp_teacher * logits_dist, axis=1),
        ),
        "mp",
    )
    log_cls = peak_cls + jnp.log(sum_cls)
    log_dist = peak_dist + jnp.log(sum_dist)
    log_teacher = peak_teacher + jnp.log(sum_teacher)
    loss_rows = 0.5 * (log_cls - target_dot) + 0.5 * (log_dist - teacher_dot / sum_teacher)
    loss_part = jnp.sum(image_weight * loss_rows) / weight_sum
    row_scale = (0.5 * image_weight / weight_sum)[:, None]
    grad_cls = row_scale * (jnp.exp(logits_cls - log_cls[:, None]) - target)
    teacher_soft = jnp.exp(logits_teacher - log_teacher[:, None])
    grad_dist = row_scale * (jnp.exp(logits_dist - log_dist[:, None]) - teacher_soft)
    grad_cls_low = grad_cls.astype(jnp.bfloat16)
    grad_dist_low = grad_dist.astype(jnp.bfloat16)
    head_grads = jnp.stack(
        [matmul_tn(final_rows[:, 0], grad_cls_low), matmul_tn(final_rows[:, 1], grad_dist_low)]
    )
    head_bias_grads = jnp.concatenate([jnp.sum(grad_cls, axis=0), jnp.sum(grad_dist, axis=0)])
    grad_final = lax.psum(
        jnp.stack(
            [matmul_nt(grad_cls_low, head_full[0]), matmul_nt(grad_dist_low, head_full[1])], axis=1
        ),
        "mp",
    )
    grad_final_rows = jnp.concatenate(
        [grad_final, jnp.zeros((images, PMAX, D), jnp.float32)], axis=1
    ).reshape(rows_total, D)
    grad_resid, grad_gain_f, grad_shift_f = norm_backward(
        grad_final_rows, normed_f, scaled_f, vector_params[head_row]
    )
    attn_list = [None] * L
    mlp_list = [None] * L
    gain_list = [None] * L
    bias_list = [None] * L
    for layer_num in reversed(range(L)):
        grad_resid, attn_step, mlp_step, gain_step, bias_step = layer_backward(
            grad_resid,
            attn_full[layer_num],
            mlp_full[layer_num],
            vector_params[6 * layer_num : 6 * layer_num + 6],
            saved_all[layer_num],
            allowed,
            group_rows,
        )
        attn_list[layer_num] = attn_step
        mlp_list[layer_num] = mlp_step
        gain_list[layer_num] = gain_step
        bias_list[layer_num] = bias_step
    grad_low = grad_resid.astype(jnp.bfloat16)
    grad_embedded_low = grad_low.reshape(images, R, D)[:, 2:].reshape(images * PMAX, D)
    patch_grad = matmul_tn(flat_patches, grad_embedded_low)
    source_grads = jnp.dot(sources.T, grad_resid, precision=HIGH)
    vector_grads = jnp.concatenate(
        [jnp.concatenate(gain_list, axis=0), jnp.stack([grad_gain_f, grad_shift_f]), source_grads],
        axis=0,
    )
    vector_grads = vector_grads * mp_first
    bias_grads = jnp.concatenate(bias_list + [head_bias_grads])
    bias_block = (jnp.arange(lax.axis_size("mp"), dtype=jnp.int32) == lax.axis_index("mp")).astype(
        jnp.float32
    )[:, None] * bias_grads[None, :]
    patch_grad, attn_grads, mlp_grads, head_grads = (
        lax.psum_scatter(patch_grad, ("dp", "teach"), scatter_dimension=0, tiled=True),
        lax.psum_scatter(jnp.stack(attn_list), ("dp", "teach"), scatter_dimension=2, tiled=True),
        lax.psum_scatter(jnp.stack(mlp_list), ("dp", "teach"), scatter_dimension=2, tiled=True),
        lax.psum_scatter(head_grads, ("dp", "teach"), scatter_dimension=1, tiled=True),
    )
    vector_grads, bias_block = lax.psum((vector_grads, bias_block), ("dp", "mp", "teach"))
    bias_grads = bias_block[lax.axis_index("mp")]
    step_power = step_count[0].astype(jnp.float32)
    correct_first = 1.0 - jnp.power(BETA, step_power)
    correct_second = 1.0 - jnp.power(BETA, step_power)
    weights = (patch_weight, attn_weight, mlp_weight, head_weight, vector_params, split_biases)
    gradients = (patch_grad, attn_grads, mlp_grads, head_grads, vector_grads, bias_grads)
    firsts = (patch_first, attn_first, mlp_first, head_first, vector_first, bias_first)
    seconds = (patch_second, attn_second, mlp_second, head_second, vector_second, bias_second)
    decay_pieces = expand_params(split_params(decay_mask.astype(jnp.float32)))
    results = [
        adam_direction(gradients[slot], firsts[slot], seconds[slot], correct_first, correct_second)
        for slot in range(6)
    ]
    directions = [
        results[slot][2] + DECAY * decay_pieces[slot] * weights[slot] for slot in range(6)
    ]
    weights_sq, direction_sq, loss_value = lax.psum(
        (
            squares_of(weights, mp_first, data_first),
            squares_of(directions, mp_first, data_first),
            loss_part * mp_first,
        ),
        ("dp", "mp", "teach"),
    )
    weight_norm = jnp.sqrt(weights_sq)
    update_norm = jnp.sqrt(direction_sq)
    trust_ratio = weight_norm / update_norm
    rates = BASE_RATE * jnp.power(LAYER_DECAY, 2.0 - layer_ids.astype(jnp.float32)) * trust_ratio
    rate_pieces = expand_params(split_params(rates))
    updated = [weights[slot] - rate_pieces[slot] * directions[slot] for slot in range(6)]
    norm_table = jnp.stack([weight_norm, update_norm])
    return (
        updated[0],
        updated[1],
        updated[2],
        updated[3],
        updated[4],
        updated[5],
        results[0][0],
        results[1][0],
        results[2][0],
        results[3][0],
        results[4][0],
        results[5][0],
        results[0][1],
        results[1][1],
        results[2][1],
        results[3][1],
        results[4][1],
        results[5][1],
        norm_table,
        trust_ratio,
        loss_value,
    )


def solution(mesh):
    placed = (
        P(("dp", "teach"), None, None),
        P(("dp", "teach"), None),
        P(("dp", "teach"), None),
        P(("dp", "teach")),
        P(("dp", "teach")),
        P(),
        P(None, "mp"),
        P(("dp", "teach"), None),
        P(None, None, ("dp", "teach"), "mp"),
        P(None, None, ("dp", "teach"), "mp"),
        P(None, ("dp", "teach"), "mp"),
        P(),
        P("mp"),
        P(("dp", "teach"), None),
        P(None, None, ("dp", "teach"), "mp"),
        P(None, None, ("dp", "teach"), "mp"),
        P(None, ("dp", "teach"), "mp"),
        P(),
        P("mp"),
        P(("dp", "teach"), None),
        P(None, None, ("dp", "teach"), "mp"),
        P(None, None, ("dp", "teach"), "mp"),
        P(None, ("dp", "teach"), "mp"),
        P(),
        P("mp"),
        P(),
        P(),
        P(),
    )
    return jax.shard_map(
        per_device,
        mesh=mesh,
        in_specs=placed,
        out_specs=(
            P(("dp", "teach"), None),
            P(None, None, ("dp", "teach"), "mp"),
            P(None, None, ("dp", "teach"), "mp"),
            P(None, ("dp", "teach"), "mp"),
            P(),
            P("mp"),
            P(("dp", "teach"), None),
            P(None, None, ("dp", "teach"), "mp"),
            P(None, None, ("dp", "teach"), "mp"),
            P(None, ("dp", "teach"), "mp"),
            P(),
            P("mp"),
            P(("dp", "teach"), None),
            P(None, None, ("dp", "teach"), "mp"),
            P(None, None, ("dp", "teach"), "mp"),
            P(None, ("dp", "teach"), "mp"),
            P(),
            P("mp"),
            P(),
            P(),
            P(),
        ),
        check_vma=False,
    )
```

profile of v0, /device:TPU:0, one launch (start us, length us, event | category | flops | bytes accessed | tf_op | source)
XLA Modules:
  0.0 2349.1 jit_solution(1432227691912756192)
XLA Ops:
  23.3 12.3 all-gather.4.cloned.1.call-done
  49.2 8.9 fusion.252
  63.7 12.2 all-gather.6.cloned.1.call-done
  106.4 29.6 %while.52 = (s32[]{:T(128)}, bf16[4,564,3,64]{1,3,2,0:T(8,128)(2,1)}, f32[4,3,564]{2,1,0:T(4,128)S(1)}, bf16[4,564,3,64]{1,3,2,0:T(8,128)(2,1)}, pred[4,564,564]...) while((s32[]{:T(128)}, ...), condition=%wide.region_12.13_spmd, body=%wide.region_9.12_spmd.sunk | while | flops 255855776 | bytes 14091677 | solution.py:122
  150.5 144.3 %all-reduce.16.cloned.1.call-done = f32[2256,768]{1,0:T(8,128)} async-done(((f32[2256,768]{1,0:T(8,128)}), f32[2256,768]{1,0:T(8,128)}) %all-reduce.16.cloned.1.call-update) | async-done | bytes 6930448 | tf_op jit(solution)/shard_map/psum | solution.py:46
  306.1 42.6 %all-gather.8.cloned.1.call-done = bf16[2,2,768,768]{3,2,1,0:T(8,128)(2,1)} async-done(((bf16[2,2,96,768]{3,2,1,0:T(8,128)(2,1)}), bf16[2,2,768,768]{3,2,1,0:T(8,128)(2,1)}) %all-gather.8.cloned.1.call-update) | async-done | bytes 4718608 | tf_op jit(solution)/shard_map/all_gather | solution.py:322
  348.7 20.4 multiply_convert_fusion.3
  370.8 6.1 fusion.183
  377.0 147.9 %all-reduce.18.cloned.1.call-done = f32[2256,768]{1,0:T(8,128)} async-done(((f32[2256,768]{1,0:T(8,128)}), f32[2256,768]{1,0:T(8,128)}) %all-reduce.18.cloned.1.call-update) | async-done | bytes 6930448 | tf_op jit(solution)/shard_map/psum | solution.py:46
  564.7 29.8 %while.53 = (s32[]{:T(128)}, bf16[4,564,3,64]{1,3,2,0:T(8,128)(2,1)}, f32[4,3,564]{2,1,0:T(4,128)S(1)}, bf16[4,564,3,64]{1,3,2,0:T(8,128)(2,1)}, pred[4,564,564]...) while((s32[]{:T(128)}, ...), condition=%wide.region_22.23_spmd, body=%wide.region_19.22_spmd.sunk | while | flops 255855776 | bytes 14091677 | solution.py:122
  605.5 149.2 %all-reduce.20.cloned.1.call-done = f32[2256,768]{1,0:T(8,128)} async-done(((f32[2256,768]{1,0:T(8,128)}), f32[2256,768]{1,0:T(8,128)}) %all-reduce.20.cloned.1.call-update) | async-done | bytes 6930448 | tf_op jit(solution)/shard_map/psum | solution.py:46
  766.7 20.0 multiply_convert_fusion.2
  793.7 7.7 fusion.137
  811.0 16.6 all_gather.15
  827.6 115.3 %all-reduce.22.cloned.1.call-done = f32[2256,768]{1,0:T(8,128)} async-done(((f32[2256,768]{1,0:T(8,128)}), f32[2256,768]{1,0:T(8,128)}) %all-reduce.22.cloned.1.call-update) | async-done | bytes 6930448 | tf_op jit(solution)/shard_map/psum | solution.py:46
  962.5 9.7 all-reduce.5
  974.4 9.1 all-reduce.4
  985.3 14.3 psum.145
  1005.4 16.6 psum.149
  1032.0 6.8 multiply_reduce_fusion.2
  1039.9 6.9 fusion.231
  1046.8 11.4 convert_reduce_fusion
  1060.1 6.1 fusion.184
  1066.3 145.5 %all-reduce.24.cloned.1.call-done = f32[2256,768]{1,0:T(8,128)} async-done(((f32[2256,768]{1,0:T(8,128)}), f32[2256,768]{1,0:T(8,128)}) %all-reduce.24.cloned.1.call-update) | async-done | bytes 6930448 | tf_op jit(solution)/shard_map/psum | solution.py:46
  1211.8 7.6 multiply_reduce_fusion.3
  1219.4 7.2 fusion.232
  1241.4 57.5 %while.54 = (s32[]{:T(128)}, bf16[4,564,3,64]{1,3,2,0:T(8,128)(2,1)}, bf16[4,564,3,64]{1,3,2,0:T(8,128)(2,1)}, bf16[4,564,3,64]{1,3,2,0:T(8,128)(2,1)}, bf16[4,5...) while((s32[]{:T(128)}, ...), condition=%wide.region_53.54_spmd, body=%wide.region_51.53_spmd.sunk | while | flops 625598400 | bytes 37382544 | solution.py:186
  1326.0 149.2 %all-reduce.26.cloned.1.call-done = f32[2256,768]{1,0:T(8,128)} async-done(((f32[2256,768]{1,0:T(8,128)}), f32[2256,768]{1,0:T(8,128)}) %all-reduce.26.cloned.1.call-update) | async-done | bytes 6930448 | tf_op jit(solution)/shard_map/psum | solution.py:46
  1475.3 6.8 multiply_reduce_fusion.4
  1482.2 6.8 fusion.233
  1489.1 11.1 convert_reduce_fusion.1
  1506.9 149.2 %all-reduce.28.cloned.1.call-done = f32[2256,768]{1,0:T(8,128)} async-done(((f32[2256,768]{1,0:T(8,128)}), f32[2256,768]{1,0:T(8,128)}) %all-reduce.28.cloned.1.call-update) | async-done | bytes 6930448 | tf_op jit(solution)/shard_map/psum | solution.py:46
  1656.2 7.0 multiply_reduce_fusion.5
  1663.2 6.6 fusion.234
  1684.5 57.5 %while.55 = (s32[]{:T(128)}, bf16[4,564,3,64]{1,3,2,0:T(8,128)(2,1)}, bf16[4,564,3,64]{1,3,2,0:T(8,128)(2,1)}, bf16[4,564,3,64]{1,3,2,0:T(8,128)(2,1)}, bf16[4,5...) while((s32[]{:T(128)}, ...), condition=%wide.region_62.63_spmd, body=%wide.region_60.62_spmd.sunk | while | flops 625598400 | bytes 37382544 | solution.py:186
  1788.5 129.8 %all-reduce.30.cloned.1.call-done = f32[2256,768]{1,0:T(8,128)} async-done(((f32[2256,768]{1,0:T(8,128)}), f32[2256,768]{1,0:T(8,128)}) %all-reduce.30.cloned.1.call-update) | async-done | bytes 6930448 | tf_op jit(solution)/shard_map/psum | solution.py:46
  1918.3 7.0 multiply_reduce_fusion.6
  1925.4 8.6 fusion.239
  1948.4 7.3 copy.282
  1955.7 8.3 reshape.651
  1967.8 6.4 fusion.169
  1977.6 6.3 convolution_bitcast_fusion
  2032.5 40.1 %psum.155 = f32[4,2804]{1,0:T(4,128)S(1)} all-reduce(f32[4,2804]{1,0:T(4,128)S(1)} %broadcast_multiply_fusion.1), channel_id=1, replica_groups=mesh['dp'=4,'mp'=4,'teach'=2] {'dp','mp','teach'}, use_global_device_ids=true, to_apply=%region_98.99 | all-reduce | flops 11216 | bytes 89728 | tf_op jit(solution)/shard_map/psum | solution.py:501
  2075.9 6.2 all-reduce.32.cloned.1.call-done
  2086.9 53.3 %reduce-scatter.15.cloned.1.call-done = f32[96,1536]{1,0:T(8,128)} async-done(((f32[768,1536]{1,0:T(8,128)}), f32[96,1536]{1,0:T(8,128)}) %reduce-scatter.15.cloned.1.call-update) | async-done | bytes 589840
  2153.9 23.1 reduce-scatter.13.cloned.1.call-done
  2184.6 93.3 %reduce-scatter.9.cloned.1.call-done = f32[2,2,96,768]{3,2,1,0:T(8,128)} async-done(((f32[2,2,768,768]{3,2,1,0:T(8,128)}), f32[2,2,96,768]{3,2,1,0:T(8,128)}) %reduce-scatter.9.cloned.1.call-update) | async-done | bytes 1179664 | tf_op jit(solution)/shard_map/reduce_scatter | solution.py:498
  2285.0 37.8 %all-reduce.3 = (f32[17]{0:T(128)S(1)}, f32[17]{0:T(128)S(1)}, f32[]{:T(128)}) all-reduce(f32[17]{0:T(128)S(1)} %concatenate.44, f32[17]{0:T(128)S(1)} %concatenate.35, f32[]{:T(128)S(6)} %mul.882), channel_id=1, replica_groups=mesh['dp'=4,'mp'=4,'teach'=2] {'dp','mp','teach'}, use_global_device_ids=true, to_apply=%region_100.101 | all-reduce | flops 35 | bytes 280 | tf_op jit(solution)/shard_map/psum | solution.py:518
  (629 shorter events, 615.6 us)
Async XLA Ops:
  7.2 28.5 %copy-start = (bf16[8,280,768]{2,1,0:T(8,128)(2,1)S(1)}, bf16[8,280,768]{2,1,0:T(8,128)(2,1)}, u32[]{:S(2)}) copy-start(bf16[8,280,768]{2,1,0:T(8,128)(2,1)} %param.36) | copy-start | bytes 10321924
  7.2 13.4 copy-start.51
  7.2 28.4 %all-gather.4.cloned.1.call-start = ((), (), s32[]{:S(2)}) async-start(), calls=%async_computation.4 | async-start | bytes 1327104 | tf_op jit(solution)/shard_map/all_gather | solution.py:320
  9.8 66.1 %all-gather.6.cloned.1.call-start = ((), (), s32[]{:S(2)}) async-start(), calls=%async_computation.5 | async-start | bytes 3538944 | tf_op jit(solution)/shard_map/all_gather | solution.py:321
  12.7 282.1 %all-reduce.16.cloned.1.call-start = ((), (), s32[]{:S(2)}) async-start(), calls=%async_computation.6 | async-start | bytes 13860864 | tf_op jit(solution)/shard_map/psum | solution.py:46
  20.7 38.5 %copy-start.63 = (f32[768]{0:T(1024)}, f32[768]{0:T(1024)S(1)}, u32[]{:S(2)}) copy-start(f32[768]{0:T(1024)S(1)} %get-tuple-element.521) | copy-start | bytes 9220
  20.7 280.8 %copy-start.58 = (f32[768]{0:T(1024)}, f32[768]{0:T(1024)S(1)}, u32[]{:S(2)}) copy-start(f32[768]{0:T(1024)S(1)} %get-tuple-element.518) | copy-start | bytes 9220
  146.8 201.9 %all-gather.8.cloned.1.call-start = ((), (), s32[]{:S(2)}) async-start(), calls=%async_computation.7 | async-start | bytes 5308416 | tf_op jit(solution)/shard_map/all_gather | solution.py:322
  150.0 374.9 %all-reduce.18.cloned.1.call-start = ((), (), s32[]{:S(2)}) async-start(), calls=%async_computation.8 | async-start | bytes 13860864 | tf_op jit(solution)/shard_map/psum | solution.py:46
  150.5 198.2 %copy-start.85 = (f32[768]{0:T(1024)}, f32[768]{0:T(1024)S(1)}, u32[]{:S(2)}) copy-start(f32[768]{0:T(1024)S(1)} %get-tuple-element.687) | copy-start | bytes 9220
  376.9 377.9 %all-reduce.20.cloned.1.call-start = ((), (), s32[]{:S(2)}) async-start(), calls=%async_computation.9 | async-start | bytes 13860864 | tf_op jit(solution)/shard_map/psum | solution.py:46
  605.5 149.3 %copy-start.73 = (f32[768]{0:T(1024)S(1)}, f32[768]{0:T(1024)}, u32[]{:S(2)}) copy-start(f32[768]{0:T(1024)} %get-tuple-element.513) | copy-start | bytes 9220
  605.5 337.4 %all-reduce.22.cloned.1.call-start = ((), (), s32[]{:S(2)}) async-start(), calls=%async_computation.10 | async-start | bytes 13860864 | tf_op jit(solution)/shard_map/psum | solution.py:46
  763.9 22.9 copy-start.34
  793.6 418.2 %all-reduce.24.cloned.1.call-start = ((), (), s32[]{:S(2)}) async-start(), calls=%async_computation.11 | async-start | bytes 13860864 | tf_op jit(solution)/shard_map/psum | solution.py:46
  801.4 141.5 %copy-start.71 = (f32[768]{0:T(1024)S(1)}, f32[768]{0:T(1024)}, u32[]{:S(2)}) copy-start(f32[768]{0:T(1024)} %get-tuple-element.510) | copy-start | bytes 9220
  806.7 166.3 %copy-start.92 = (f32[8]{0:T(128)}, f32[8]{0:T(128)S(1)}, u32[]{:S(2)}) copy-start(f32[8]{0:T(128)S(1)} %broadcast_subtract_fusion) | copy-start | bytes 100
  972.2 11.2 copy-start.94
  972.2 11.2 copy-start.95
  1046.8 11.4 copy-start.11
  1066.2 409.0 %all-reduce.26.cloned.1.call-start = ((), (), s32[]{:S(2)}) async-start(), calls=%async_computation.12 | async-start | bytes 13860864 | tf_op jit(solution)/shard_map/psum | solution.py:46
  1325.9 149.3 %copy-start.42 = (f32[2256]{0:T(1024)S(1)}, f32[2256]{0:T(1024)}, u32[]{:S(2)}) copy-start(f32[2256]{0:T(1024)} %copy-done.41) | copy-start | bytes 27076
  1325.9 149.3 %copy-start.50 = (f32[2256]{0:T(1024)S(1)}, f32[2256]{0:T(1024)}, u32[]{:S(2)}) copy-start(f32[2256]{0:T(1024)} %copy-done.49) | copy-start | bytes 27076
  1325.9 149.3 %copy-start.61 = (f32[768]{0:T(1024)S(1)}, f32[768]{0:T(1024)}, u32[]{:S(2)}) copy-start(f32[768]{0:T(1024)} %get-tuple-element.515) | copy-start | bytes 9220
  1326.0 330.2 %all-reduce.28.cloned.1.call-start = ((), (), s32[]{:S(2)}) async-start(), calls=%async_computation.13 | async-start | bytes 13860864 | tf_op jit(solution)/shard_map/psum | solution.py:46
  1475.3 13.8 slice-start.6
  1489.1 11.2 copy-start.12
  1506.8 149.3 %copy-start.40 = (f32[2256]{0:T(1024)S(1)}, f32[2256]{0:T(1024)}, u32[]{:S(2)}) copy-start(f32[2256]{0:T(1024)} %copy-done.39) | copy-start | bytes 27076
  1506.8 149.3 %copy-start.48 = (f32[2256]{0:T(1024)S(1)}, f32[2256]{0:T(1024)}, u32[]{:S(2)}) copy-start(f32[2256]{0:T(1024)} %copy-done.47) | copy-start | bytes 27076
  1506.8 149.3 %copy-start.59 = (f32[768]{0:T(1024)S(1)}, f32[768]{0:T(1024)}, u32[]{:S(2)}) copy-start(f32[768]{0:T(1024)} %copy-done.58) | copy-start | bytes 9220
  1506.9 411.4 %all-reduce.30.cloned.1.call-start = ((), (), s32[]{:S(2)}) async-start(), calls=%async_computation.14 | async-start | bytes 13860864 | tf_op jit(solution)/shard_map/psum | solution.py:46
  1769.0 253.9 %reduce-scatter.11.cloned.1.call-start = ((), (), s32[]{:S(2)}) async-start(), calls=%async_computation.16 | async-start | bytes 1769472 | tf_op jit(solution)/shard_map/reduce_scatter | solution.py:499
  1771.6 310.5 %all-reduce.32.cloned.1.call-start = ((), (), s32[]{:S(2)}) async-start(), calls=%async_computation.17 | async-start | bytes 442368 | tf_op jit(solution)/shard_map/psum | solution.py:501
  1786.0 132.3 %copy-start.38 = (f32[2256]{0:T(1024)S(1)}, f32[2256]{0:T(1024)}, u32[]{:S(2)}) copy-start(f32[2256]{0:T(1024)} %copy-done.37) | copy-start | bytes 27076
  1786.0 132.3 %copy-start.46 = (f32[2256]{0:T(1024)S(1)}, f32[2256]{0:T(1024)}, u32[]{:S(2)}) copy-start(f32[2256]{0:T(1024)} %copy-done.45) | copy-start | bytes 27076
  1786.0 132.3 %copy-start.64 = (f32[768]{0:T(1024)S(1)}, f32[768]{0:T(1024)}, u32[]{:S(2)}) copy-start(f32[768]{0:T(1024)} %copy-done.63) | copy-start | bytes 9220
  1943.6 196.7 %reduce-scatter.15.cloned.1.call-start = ((), (), s32[]{:S(2)}) async-start(), calls=%async_computation.19 | async-start | bytes 5308416
  1964.0 213.0 %reduce-scatter.13.cloned.1.call-start = ((), (), s32[]{:S(2)}) async-start(), calls=%async_computation.18 | async-start | bytes 2654208
  1977.4 300.6 %reduce-scatter.9.cloned.1.call-start = ((), (), s32[]{:S(2)}) async-start(), calls=%async_computation.15 | async-start | bytes 10616832 | tf_op jit(solution)/shard_map/reduce_scatter | solution.py:498
  2010.0 21.7 copy-start.84
  2010.0 21.7 copy-start.87
  2010.0 21.7 copy-start.88
  2010.0 21.7 copy-start.89
  2010.0 62.7 %copy-start.52 = (f32[2804]{0:T(1024)S(1)}, f32[2804]{0:T(1024)}, u32[]{:S(2)}) copy-start(f32[2804]{0:T(1024)} %param.48) | copy-start | bytes 33652
  2010.0 62.7 %copy-start.81 = (f32[2804]{0:T(1024)S(1)}, f32[2804]{0:T(1024)}, u32[]{:S(2)}) copy-start(f32[2804]{0:T(1024)} %param.60) | copy-start | bytes 33652
  2149.2 128.8 %copy-start.83 = (f32[2,2]{1,0:T(2,128)S(1)}, f32[2,2]{1,0:T(2,128)}, u32[]{:S(2)}) copy-start(f32[2,2]{1,0:T(2,128)} %slice_multiply_fusion) | copy-start | bytes 52
  2182.0 101.0 %copy-start.93 = (f32[2]{0:T(128)S(1)}, f32[2]{0:T(128)}, u32[]{:S(2)}) copy-start(f32[2]{0:T(128)} %get-tuple-element.632) | copy-start | bytes 28
  2182.0 140.7 %copy-start.101 = (s32[17]{0:T(128)S(1)}, s32[17]{0:T(128)}, u32[]{:S(2)}) copy-start(s32[17]{0:T(128)} %param.62) | copy-start | bytes 208
  (88 other events, 324.9 us)
Sparse Core Ops, SparseCore 0:
  10.3 25.3 all-gather.3
  37.8 38.0 all-gather.5
  146.9 147.8 all-reduce.15
  296.8 51.8 all-gather.7
  377.0 147.8 all-reduce.17
  605.6 149.1 all-reduce.19
  793.7 149.1 all-reduce.21
  1066.3 145.4 all-reduce.23
  1326.1 149.1 all-reduce.25
  1507.0 149.1 all-reduce.27
  1769.1 149.1 all-reduce.29
  1920.5 34.4 reduce-scatter.10
  1961.0 121.0 all-reduce.31
  2084.3 55.9 reduce-scatter.14
  2142.4 34.5 reduce-scatter.12
  2179.2 98.7 reduce-scatter.8
where the time goes:
time: 2370 us; the launch traced here: 2350 us
  waiting for transfers between devices  1370 us (58%)
  matrix products  347 us (15%)
  local copies, waits for them, and re-layouts  245 us (10%)
  other arithmetic  213 us (9%)
  blocking collectives  144 us (6%)
  between operations  23.8 us (1%)
    psum x8, waiting for transfers between devices, reduce_rows(): return lax.psum(partial_value, 'mp')  1130 us
    dot_general x17, matrix products, matmul(): return jnp.dot(left, right, preferred_element_type=jnp.float32)  110 us
    reduce_scatter x1, waiting for transfers between devices, per_device(): lax.psum_scatter(jnp.stack(mlp_list), ('dp', 'teach'), scatter_dimension=...  93.3 us
    unnamed x243, local copies, waits for them, and re-layouts  80.8 us
    unnamed x18, waiting for transfers between devices  76.7 us
    dot_general x14, matrix products, matmul_nt(): lax.dot_general(left, right, (((1,), (1,)), ((), ())), preferred_element_...  54.5 us
  transfers between devices with their start and end apart: 16, of which 15 were waited for; matrix products, arithmetic and copies ran while one was open for 9% of the time, Pallas kernels for 0%

commit v1 on v0

v1 whole, which is shorter than its diff:
```python
import functools

import jax
import jax.numpy as jnp
from jax import lax
from jax.experimental import pallas as pl
from jax.experimental.pallas import tpu as pltpu
from jax.sharding import PartitionSpec as P

D = 768
HD = 64
G = 24
PMAX = 280
L = 2
RP = 288
TOK = 280
HR = 16

EPS_NORM = 1e-06
EPS_LAMB = 1e-06
BETA = 0.5
DECAY = 0.05
BASE_RATE = 0.4
LAYER_DECAY = 0.8
SCALE = 0.125
MASKED = -1e30
HIGH = lax.Precision.HIGHEST
ROOT_HALF = 0.7071067811865476
DENSITY = 0.3989422804014327
BF = jnp.bfloat16
F32 = jnp.float32
ALL = ("dp", "mp", "teach")
VMEM_LIMIT = 56 * 1024 * 1024
FLOP_PER_US = 1_150_000_000


def dot_nn(left, right):
    return lax.dot_general(
        left, right, (((1,), (0,)), ((), ())), preferred_element_type=F32
    )


def dot_nt(left, right):
    return lax.dot_general(
        left, right, (((1,), (1,)), ((), ())), preferred_element_type=F32
    )


def dot_tn(left, right):
    return lax.dot_general(
        left, right, (((0,), (0,)), ((), ())), preferred_element_type=F32
    )


def gelu_erf(values):
    return 0.5 * values * (1.0 + lax.erf(values * ROOT_HALF))


def norm_stats(values):
    centre = values - jnp.mean(values, axis=-1, keepdims=True)
    scaled = lax.rsqrt(jnp.mean(centre * centre, axis=-1, keepdims=True) + EPS_NORM)
    return centre * scaled, scaled


def norm_back(grad_out, normed, scaled, gain_row):
    grad_normed = grad_out * gain_row
    inner_sum = jnp.mean(grad_normed, axis=-1, keepdims=True)
    cross_term = jnp.mean(grad_normed * normed, axis=-1, keepdims=True)
    return scaled * (grad_normed - inner_sum - normed * cross_term)


def row_sum(values):
    return jnp.sum(values, axis=0, keepdims=True)


def start_weights(full, buf, sems):
    steps, _, teach, rows, _ = full.shape
    copies = []
    for core in range(teach):
        for step in range(steps):
            at = (core * steps + step) * rows
            copies.append(
                pltpu.make_async_copy(
                    full.at[step, :, core], buf.at[:, pl.ds(at, rows)], sems.at[core * steps + step]
                )
            )
    for copy in copies:
        copy.start()
    return copies


def split_out(half, place, grad_buf, mine_ref, other_ref, block):
    mine = pl.multiple_of(place * half, 128)
    theirs = pl.multiple_of((1 - place) * half, 128)
    mine_ref[block] = grad_buf[pl.ds(mine, half), :]
    other_ref[block] = grad_buf[pl.ds(theirs, half), :]


def attn_forward_kernel(
    mp,
    ni,
    wl,
    resid_ref,
    vec_ref,
    bias_ref,
    live_ref,
    full,
    first_ref,
    qkv_ref,
    att_ref,
    lse_ref,
    mid_ref,
    buf,
    sems,
):
    copies = start_weights(full, buf, sems)
    resid = resid_ref[...]
    normed, _ = norm_stats(resid)
    first_ref[...] = (normed * vec_ref[0:1] + vec_ref[1:2]).astype(BF)
    mid_ref[...] = resid + vec_ref[4:5]
    for copy in copies:
        copy.wait()

    def body(block, carry):
        qkv = dot_nn(first_ref[...], buf[block, :, : 3 * wl]) + bias_ref[block]
        qkv_ref[block] = qkv.astype(BF)
        for image in range(ni):
            rows = slice(image * RP, (image + 1) * RP)
            live = live_ref[image] > 0.0
            for head in range(wl // HD):
                at = head * HD
                queries = qkv_ref[block, rows, at : at + HD]
                keys = qkv_ref[block, rows, wl + at : wl + at + HD]
                vals = qkv_ref[block, rows, 2 * wl + at : 2 * wl + at + HD]
                scores = jnp.where(live, dot_nt(queries, keys) * SCALE, MASKED)
                peak = jnp.max(scores, axis=-1, keepdims=True)
                expo = jnp.exp(scores - peak)
                total = jnp.sum(expo, axis=-1, keepdims=True)
                soft = (expo * (1.0 / total)).astype(BF)
                att_ref[block, rows, at : at + HD] = dot_nn(soft, vals).astype(BF)
                lse_ref[block, rows, head : head + 1] = peak + jnp.log(total)
        mid_ref[...] += dot_nt(att_ref[block], buf[block, :, 3 * wl :])
        return carry

    lax.fori_loop(0, mp, body, 0)


def mlp_forward_kernel(
    mp,
    chunk,
    mid_ref,
    vec_ref,
    bias_ref,
    full,
    second_ref,
    hidden_ref,
    slope_ref,
    out_ref,
    buf,
    sems,
):
    fl = hidden_ref.shape[2]
    copies = start_weights(full, buf, sems)
    middle = mid_ref[...]
    normed, _ = norm_stats(middle)
    second_ref[...] = (normed * vec_ref[2:3] + vec_ref[3:4]).astype(BF)
    out_ref[...] = middle + vec_ref[5:6]
    for copy in copies:
        copy.wait()
    row_count = mid_ref.shape[0]

    def body(block, carry):
        for start in range(0, row_count, chunk):
            rows = slice(start, start + chunk)
            upward = dot_nn(second_ref[rows, :], buf[block, :, :fl]) + bias_ref[block]
            share = 0.5 + 0.5 * lax.erf(upward * ROOT_HALF)
            hidden = (upward * share).astype(BF)
            hidden_ref[block, rows, :] = hidden
            slope_ref[block, rows, :] = share + upward * (
                DENSITY * jnp.exp(-0.5 * upward * upward)
            )
            out_ref[rows, :] += dot_nt(hidden, buf[block, :, fl:])
        return carry

    lax.fori_loop(0, mp, body, 0)


def head_kernel(
    mp,
    ni,
    wc,
    place_ref,
    resid_ref,
    vec_ref,
    bias_ref,
    ids_ref,
    labels_ref,
    mix_ref,
    scale_ref,
    weight_ref,
    pooled_ref,
    teacher_ref,
    full,
    mine_ref,
    other_ref,
    hbias_ref,
    grad_ref,
    vgrad_ref,
    loss_ref,
    buf,
    cls_buf,
    dist_buf,
    gw_buf,
    sems,
):
    half = mine_ref.shape[1]
    copies = start_weights(full, buf, sems)
    cls_buf[...] = jnp.zeros_like(cls_buf)
    dist_buf[...] = jnp.zeros_like(dist_buf)
    for image in range(ni):
        at = image * RP + TOK
        cls_buf[image : image + 1, :] = resid_ref[at : at + 1, :]
        dist_buf[image : image + 1, :] = resid_ref[at + 1 : at + 2, :]
    grad_ref[...] = jnp.zeros_like(grad_ref)
    normed_c, scaled_c = norm_stats(cls_buf[...])
    normed_d, scaled_d = norm_stats(dist_buf[...])
    gain, shift = vec_ref[0:1], vec_ref[1:2]
    final_c = (normed_c * gain + shift).astype(BF)
    final_d = (normed_d * gain + shift).astype(BF)
    for copy in copies:
        copy.wait()
    cls, dist, teach, goal = [], [], [], []
    mix = mix_ref[:, 0:1]
    for block in range(mp):
        ids = ids_ref[block]
        valid = ids >= 0
        both = bias_ref[block]
        cls.append(
            jnp.where(valid, dot_nn(final_c, buf[block, :, :wc]) + both[:, :wc], MASKED)
        )
        dist.append(
            jnp.where(valid, dot_nn(final_d, buf[block, :, wc:]) + both[:, wc:], MASKED)
        )
        teach.append(jnp.where(valid, dot_nn(pooled_ref[...], teacher_ref[block]), MASKED))
        first = (labels_ref[:, 0:1] == ids).astype(F32)
        second = (labels_ref[:, 1:2] == ids).astype(F32)
        goal.append(mix * first + (1.0 - mix) * second)

    def log_total(parts):
        peak = functools.reduce(
            jnp.maximum, [jnp.max(part, axis=-1, keepdims=True) for part in parts]
        )
        total = sum(jnp.sum(jnp.exp(part - peak), axis=-1, keepdims=True) for part in parts)
        return peak + jnp.log(total)

    log_c, log_d, log_t = log_total(cls), log_total(dist), log_total(teach)
    prob = [jnp.exp(part - log_t) for part in teach]
    dot_c = sum(jnp.sum(g * c, axis=-1, keepdims=True) for g, c in zip(goal, cls))
    dot_d = sum(jnp.sum(p * d, axis=-1, keepdims=True) for p, d in zip(prob, dist))
    loss_rows = 0.5 * (log_c - dot_c) + 0.5 * (log_d - dot_d)
    loss_ref[...] = jnp.broadcast_to(row_sum(weight_ref[:, 0:1] * loss_rows), loss_ref.shape)
    scale = scale_ref[:, 0:1]
    gfin_c = jnp.zeros(cls_buf.shape, F32)
    gfin_d = jnp.zeros(dist_buf.shape, F32)
    for block in range(mp):
        grad_c = scale * (jnp.exp(cls[block] - log_c) - goal[block])
        grad_d = scale * (jnp.exp(dist[block] - log_d) - prob[block])
        hbias_ref[block, :, :wc] = row_sum(grad_c)
        hbias_ref[block, :, wc:] = row_sum(grad_d)
        low_c, low_d = grad_c.astype(BF), grad_d.astype(BF)
        gw_buf[:, :wc] = dot_tn(final_c, low_c).astype(BF)
        gw_buf[:, wc:] = dot_tn(final_d, low_d).astype(BF)
        split_out(half, place_ref[0], gw_buf, mine_ref, other_ref, block)
        gfin_c += dot_nt(low_c, buf[block, :, :wc])
        gfin_d += dot_nt(low_d, buf[block, :, wc:])
    vgrad_ref[...] = jnp.zeros_like(vgrad_ref)
    vgrad_ref[0:1, :] = row_sum(gfin_c * normed_c) + row_sum(gfin_d * normed_d)
    vgrad_ref[1:2, :] = row_sum(gfin_c) + row_sum(gfin_d)
    cls_buf[...] = norm_back(gfin_c, normed_c, scaled_c, gain)
    dist_buf[...] = norm_back(gfin_d, normed_d, scaled_d, gain)
    for image in range(ni):
        at = image * RP + TOK
        grad_ref[at : at + 1, :] = cls_buf[image : image + 1, :]
        grad_ref[at + 1 : at + 2, :] = dist_buf[image : image + 1, :]


def mlp_backward_kernel(
    mp,
    place_ref,
    grad_ref,
    mid_ref,
    vec_ref,
    second_ref,
    hidden_ref,
    slope_ref,
    full,
    gmid_ref,
    mine_ref,
    other_ref,
    gbias_ref,
    vgrad_ref,
    buf,
    branch_buf,
    branch_t,
    second_t,
    gw_buf,
    sems,
):
    fl = hidden_ref.shape[2]
    half = mine_ref.shape[1]
    place = place_ref[0]
    copies = start_weights(full, buf, sems)
    branch_buf[...] = grad_ref[...].astype(BF)
    branch_t[...] = branch_buf[...].T
    second_t[...] = second_ref[...].T
    gmid_ref[...] = jnp.zeros_like(gmid_ref)
    for copy in copies:
        copy.wait()

    def body(block, carry):
        gup = (dot_nn(branch_buf[...], buf[block, :, fl:]) * slope_ref[block]).astype(BF)
        gbias_ref[block] = row_sum(gup.astype(F32))
        gmid_ref[...] += dot_nt(gup, buf[block, :, :fl])
        gw_buf[:, :fl] = dot_nn(second_t[...], gup).astype(BF)
        gw_buf[:, fl:] = dot_nn(branch_t[...], hidden_ref[block]).astype(BF)
        split_out(half, place, gw_buf, mine_ref, other_ref, block)
        return carry

    lax.fori_loop(0, mp, body, 0)
    normed, scaled = norm_stats(mid_ref[...])
    gsec = gmid_ref[...]
    grad = grad_ref[...]
    vgrad_ref[...] = jnp.zeros_like(vgrad_ref)
    vgrad_ref[2:3, :] = row_sum(gsec * normed)
    vgrad_ref[3:4, :] = row_sum(gsec)
    vgrad_ref[5:6, :] = row_sum(grad)
    gmid = norm_back(gsec, normed, scaled, vec_ref[2:3]) + grad
    vgrad_ref[4:5, :] = row_sum(gmid)
    gmid_ref[...] = gmid


def attn_backward_kernel(
    mp,
    ni,
    wl,
    place_ref,
    gmid_ref,
    resid_ref,
    vec_ref,
    live_ref,
    first_ref,
    qkv_ref,
    att_ref,
    lse_ref,
    full,
    gres_ref,
    mine_ref,
    other_ref,
    gbias_ref,
    vgrad_ref,
    buf,
    mixed_buf,
    mixed_t,
    first_t,
    gatt_buf,
    gqkv_buf,
    gw_buf,
    sems,
):
    half = mine_ref.shape[1]
    place = place_ref[0]
    copies = start_weights(full, buf, sems)
    mixed_buf[...] = gmid_ref[...].astype(BF)
    mixed_t[...] = mixed_buf[...].T
    first_t[...] = first_ref[...].T
    gres_ref[...] = jnp.zeros_like(gres_ref)
    for copy in copies:
        copy.wait()

    def body(block, carry):
        gatt_buf[...] = dot_nn(mixed_buf[...], buf[block, :, 3 * wl :]).astype(BF)
        for image in range(ni):
            rows = slice(image * RP, (image + 1) * RP)
            live = live_ref[image] > 0.0
            for head in range(wl // HD):
                at = head * HD
                queries = qkv_ref[block, rows, at : at + HD]
                keys = qkv_ref[block, rows, wl + at : wl + at + HD]
                vals = qkv_ref[block, rows, 2 * wl + at : 2 * wl + at + HD]
                gatt = gatt_buf[rows, at : at + HD]
                scores = jnp.where(live, dot_nt(queries, keys) * SCALE, MASKED)
                soft = jnp.exp(scores - lse_ref[block, rows, head : head + 1])
                gsoft = dot_nt(gatt, vals)
                inner = jnp.sum(soft * gsoft, axis=-1, keepdims=True)
                gscore = (soft * (gsoft - inner)).astype(BF)
                gqkv_buf[rows, at : at + HD] = (dot_nn(gscore, keys) * SCALE).astype(BF)
                gqkv_buf[rows, wl + at : wl + at + HD] = (dot_tn(gscore, queries) * SCALE).astype(BF)
                gqkv_buf[rows, 2 * wl + at : 2 * wl + at + HD] = dot_tn(soft.astype(BF), gatt).astype(BF)
        gqkv = gqkv_buf[...]
        gbias_ref[block] = row_sum(gqkv.astype(F32))
        gres_ref[...] += dot_nt(gqkv, buf[block, :, : 3 * wl])
        gw_buf[:, : 3 * wl] = dot_nn(first_t[...], gqkv).astype(BF)
        gw_buf[:, 3 * wl :] = dot_nn(mixed_t[...], att_ref[block]).astype(BF)
        split_out(half, place, gw_buf, mine_ref, other_ref, block)
        return carry

    lax.fori_loop(0, mp, body, 0)
    normed, scaled = norm_stats(resid_ref[...])
    gfirst = gres_ref[...]
    vgrad_ref[...] = jnp.zeros_like(vgrad_ref)
    vgrad_ref[0:1, :] = row_sum(gfirst * normed)
    vgrad_ref[1:2, :] = row_sum(gfirst)
    gres_ref[...] = norm_back(gfirst, normed, scaled, vec_ref[0:1]) + gmid_ref[...]


def call(kernel, outs, scratch, ins, micros, after=()):
    specs, arrays = [], []

    def ordered(*refs):
        return kernel(*refs[: len(ins)], *refs[len(ins) + len(after) :])

    for item in [*ins, *[("hbm", array) for array in after]]:
        if isinstance(item, tuple):
            specs.append(pl.BlockSpec(memory_space=pl.ANY if item[0] == "hbm" else pltpu.SMEM))
            arrays.append(item[1])
        else:
            specs.append(pl.BlockSpec(memory_space=pltpu.VMEM))
            arrays.append(item)
    out_shape = [jax.ShapeDtypeStruct(shape, dtype) for shape, dtype in outs]
    moved = sum(a.size * a.dtype.itemsize for a in arrays)
    moved += sum(s.size * s.dtype.itemsize for s in out_shape)
    return pl.pallas_call(
        ordered if after else kernel,
        out_shape=out_shape,
        in_specs=specs,
        out_specs=[pl.BlockSpec(memory_space=pltpu.VMEM)] * len(out_shape),
        scratch_shapes=scratch,
        compiler_params=pltpu.CompilerParams(vmem_limit_bytes=VMEM_LIMIT),
        cost_estimate=pl.CostEstimate(
            flops=micros * FLOP_PER_US, bytes_accessed=moved, transcendentals=0
        ),
    )(*arrays)


def gather_unit(local):
    dp, mp, teach = lax.axis_size("dp"), lax.axis_size("mp"), lax.axis_size("teach")
    rows, width = local.shape
    full = lax.all_gather(local, ALL, axis=0, tiled=True).reshape(dp, mp, teach, rows, width)
    if rows % 16:
        full = full.transpose(1, 2, 0, 3, 4).reshape(1, mp, teach, dp * rows, width)
    return ("hbm", full)


def swap(values, axis, distance):
    size = lax.axis_size(axis)
    return lax.ppermute(values, axis, [(rank, rank ^ distance) for rank in range(size)])


def add_low(left, right):
    return (left.astype(F32) + right.astype(F32)).astype(BF)


def sum_all(values):
    for axis in ("teach", "mp", "dp"):
        distance = 1
        while distance < lax.axis_size(axis):
            values = values + swap(values, axis, distance)
            distance *= 2
    return values


def gather_mp(values):
    size = lax.axis_size("mp")
    parts = jnp.stack([values] + [swap(values, "mp", step) for step in range(1, size)])
    return parts[lax.axis_index("mp") ^ jnp.arange(size, dtype=jnp.int32)]


class Scatter:
    def __init__(self, mine, other):
        self.mine = mine
        self.got = swap(other, "teach", 1)
        self.stage = 0
        self.total = None

    def step(self):
        self.stage += 1
        if self.stage == 1:
            here = lax.axis_index("mp")
            self.cut = cut = self.mine.shape[1] // 2
            self.blocks = [
                add_low(
                    lax.dynamic_index_in_dim(self.mine, here ^ far, 0, False),
                    lax.dynamic_index_in_dim(self.got, here ^ far, 0, False),
                )
                for far in range(4)
            ]
            sent = [self.blocks[3][:cut], self.blocks[3][cut:]]
        elif self.stage == 2:
            cut, blocks = self.cut, self.blocks
            sent = [
                jnp.concatenate([blocks[1][:cut], add_low(blocks[1][cut:], self.by_two)]),
                jnp.concatenate([add_low(blocks[2][:cut], self.by_one), blocks[2][cut:]]),
            ]
        elif self.stage == 3:
            near = self.by_one.astype(F32) + self.by_two.astype(F32)
            total = (self.blocks[0].astype(F32) + near).astype(BF)
            self.total = lax.psum_scatter(total, "dp", scatter_dimension=0, tiled=True)
            return [total]
        else:
            return []
        self.by_one = swap(sent[0], "mp", 1)
        self.by_two = swap(sent[1], "mp", 2)
        return sent

    def result(self):
        while self.total is None:
            self.step()
        return self.total.astype(F32)


def adam_direction(gradient, first_moment, second_moment, correct_first, correct_second):
    new_first = BETA * first_moment + (1.0 - BETA) * gradient
    new_second = BETA * second_moment + (1.0 - BETA) * gradient * gradient
    return (
        new_first,
        new_second,
        new_first / correct_first / (jnp.sqrt(new_second / correct_second) + EPS_LAMB),
    )


def split_params(values):
    layered = values[1 : 1 + 6 * L].reshape(L, 6)
    return (
        values[0],
        layered[:, :4],
        layered[:, 4:],
        values[1 + 6 * L : 3 + 6 * L],
        values[3 + 6 * L],
        values[4 + 6 * L],
    )


def expand_params(pieces):
    return (
        pieces[0],
        pieces[1][:, :, None, None],
        pieces[2][:, :, None, None],
        pieces[3][:, None, None],
        pieces[4],
        pieces[5],
    )


def order_params(pieces):
    layered = jnp.concatenate([pieces[1], pieces[2]], axis=1).reshape(-1)
    return jnp.concatenate([pieces[0][None], layered, pieces[3], pieces[4][None], pieces[5][None]])


def squares_of(pieces, mp_first, data_first):
    return order_params(
        (
            jnp.sum(pieces[0] * pieces[0]) * mp_first,
            jnp.sum(pieces[1] * pieces[1], axis=(2, 3)),
            jnp.sum(pieces[2] * pieces[2], axis=(2, 3)),
            jnp.sum(pieces[3] * pieces[3], axis=(1, 2)),
            jnp.sum(pieces[4] * pieces[4]) * mp_first * data_first,
            jnp.sum(pieces[5] * pieces[5]) * data_first,
        )
    )


def per_device(
    patches,
    grid_sizes,
    label_ids,
    label_mix,
    image_weight,
    teacher_stem,
    teacher_head,
    patch_weight,
    attn_weight,
    mlp_weight,
    head_weight,
    vector_params,
    split_biases,
    patch_first,
    attn_first,
    mlp_first,
    head_first,
    vector_first,
    bias_first,
    patch_second,
    attn_second,
    mlp_second,
    head_second,
    vector_second,
    bias_second,
    decay_mask,
    layer_ids,
    step_count,
):
    dp, mp, teach = lax.axis_size("dp"), lax.axis_size("mp"), lax.axis_size("teach")
    here_mp = lax.axis_index("mp")
    here_teach = lax.axis_index("teach")
    place = here_teach.astype(jnp.int32).reshape(1)
    mp_first = (here_mp == 0).astype(F32)
    data_first = (lax.axis_index(("dp", "teach")) == 0).astype(F32)
    rows_own = patch_weight.shape[0]
    half = dp * rows_own
    wl = attn_weight.shape[3]
    fl = mlp_weight.shape[3]
    cl = head_weight.shape[2]
    wc = -(-cl // 128) * 128
    head_row = 6 * L

    def inward(values):
        lead = values.shape[:-1]
        cut = values.reshape(*lead, dp, teach, rows_own)
        return jnp.swapaxes(cut, -3, -2).reshape(*lead, D)

    def outward(values):
        lead = values.shape[:-1]
        cut = values.reshape(*lead, teach, dp, rows_own)
        return jnp.swapaxes(cut, -3, -2).reshape(*lead, D)

    ni = patches.shape[0] // mp

    def take(array):
        return lax.dynamic_slice_in_dim(array, here_mp * ni, ni, 0)

    patches, grid_sizes, label_ids = take(patches), take(grid_sizes), take(label_ids)
    label_mix, image_weight = take(label_mix), take(image_weight)
    weight_sum = sum_all(jnp.sum(image_weight).reshape(1))[0]

    quarter = rows_own // mp
    patch_low = inward(patch_weight).astype(BF)
    patch_all = lax.all_gather(
        lax.dynamic_slice_in_dim(patch_low, here_mp * quarter, quarter, 0), ALL, axis=0, tiled=True
    ).reshape(dp, mp, teach, quarter, D)
    attn_units, mlp_units = [], []
    for layer in range(L):
        attn_low = jnp.concatenate([attn_weight[layer, part] for part in range(4)], axis=1)
        attn_units.append(gather_unit(attn_low.astype(BF)))
        mlp_low = jnp.concatenate([mlp_weight[layer, 0], mlp_weight[layer, 1]], axis=1)
        mlp_units.append(gather_unit(mlp_low.astype(BF)))
    head_pad = jnp.pad(head_weight, ((0, 0), (0, 0), (0, wc - cl)))
    head_unit = gather_unit(jnp.concatenate([head_pad[0], head_pad[1]], axis=1).astype(BF))
    teacher_all = gather_mp(jnp.pad(teacher_head, ((0, 0), (0, wc - cl))))
    bias_all = gather_mp(split_biases)

    vec_in = inward(vector_params)
    layer_vecs = [
        jnp.pad(vec_in[6 * layer : 6 * layer + 6], ((0, 2), (0, 0))) for layer in range(L)
    ]
    final_vec = jnp.pad(vec_in[head_row : head_row + 2], ((0, 6), (0, 0)))
    attn_bias, up_bias = [], []
    span = 2 * wl + fl
    for layer in range(L):
        part = bias_all[:, layer * span : (layer + 1) * span]
        zero = jnp.zeros((mp, wl), F32)
        attn_bias.append(
            jnp.concatenate([part[:, :wl], zero, part[:, wl : 2 * wl]], axis=1)[:, None]
        )
        up_bias.append(part[:, None, 2 * wl :])
    pad_class = ((0, 0), (0, wc - cl))
    head_bias = jnp.concatenate(
        [
            jnp.pad(bias_all[:, L * span : L * span + cl], pad_class),
            jnp.pad(bias_all[:, L * span + cl : L * span + 2 * cl], pad_class),
        ],
        axis=1,
    )[:, None]

    grid_rows, grid_cols = grid_sizes[:, 0:1], grid_sizes[:, 1:2]
    slot_ids = jnp.arange(PMAX, dtype=jnp.int32)[None, :]
    patch_live = slot_ids < grid_rows * grid_cols
    live_float = patch_live.astype(F32)
    live_rows = jnp.concatenate(
        [live_float, jnp.ones((ni, 2), F32), jnp.zeros((ni, RP - PMAX - 2), F32)], axis=1
    )[:, None, :]
    table = jnp.arange(G, dtype=jnp.int32)
    source_patch = jnp.concatenate(
        [
            jnp.ones((ni, PMAX, 1), F32),
            jnp.zeros((ni, PMAX, 2), F32),
            ((slot_ids // grid_cols)[..., None] == table).astype(F32),
            ((slot_ids % grid_cols)[..., None] == table).astype(F32),
        ],
        axis=2,
    )
    source_token = jnp.broadcast_to(jnp.eye(2, 3 + 2 * G, 1, dtype=F32), (ni, 2, 3 + 2 * G))
    sources = jnp.concatenate(
        [source_patch, source_token, jnp.zeros((ni, RP - PMAX - 2, 3 + 2 * G), F32)], axis=1
    ).reshape(ni * RP, 3 + 2 * G)

    stem_rows = gelu_erf(dot_nn(patches.reshape(ni * PMAX, -1), teacher_stem)).reshape(ni, PMAX, -1)
    pooled = (
        jnp.sum(stem_rows * live_float[..., None], axis=1)
        / jnp.sum(live_float, axis=1, keepdims=True)
    ).astype(BF)

    patch_full = patch_all.transpose(0, 2, 1, 3, 4).reshape(D, D)
    patch_rows = jnp.pad(patches, ((0, 0), (0, RP - PMAX), (0, 0))).reshape(ni * RP, -1)
    residual = dot_nn(patch_rows, patch_full) + jnp.dot(
        sources, vec_in[head_row + 2 :], precision=HIGH
    )

    n = ni * RP
    parts = head_unit[1].shape[0] * teach
    saved = []
    for layer in range(L):
        first, qkv, attended, lse, middle = call(
            functools.partial(attn_forward_kernel, mp, ni, wl),
            [
                ((n, D), BF),
                ((mp, n, 3 * wl), BF),
                ((mp, n, wl), BF),
                ((mp, n, wl // HD), F32),
                ((n, D), F32),
            ],
            [pltpu.VMEM((mp, D, 4 * wl), BF), pltpu.SemaphoreType.DMA((parts,))],
            [residual, layer_vecs[layer], attn_bias[layer], live_rows, attn_units[layer]],
            20,
        )
        second, hidden, slope, output = call(
            functools.partial(mlp_forward_kernel, mp, n // 4),
            [((n, D), BF), ((mp, n, fl), BF), ((mp, n, fl), F32), ((n, D), F32)],
            [pltpu.VMEM((mp, D, 2 * fl), BF), pltpu.SemaphoreType.DMA((parts,))],
            [middle, layer_vecs[layer], up_bias[layer], mlp_units[layer]],
            20,
        )
        saved.append((residual, first, qkv, attended, lse, middle, second, hidden, slope))
        residual = output

    def wide(values):
        return jnp.pad(values.reshape(ni, -1), ((0, HR - ni), (0, 0)))

    lanes = jnp.arange(wc, dtype=jnp.int32)
    class_ids = jnp.where(lanes[None] < cl, jnp.arange(mp, dtype=jnp.int32)[:, None] * cl + lanes[None], -1)[:, None]
    head_mine, head_other, head_bgrad, grad, final_vgrad, loss_part = call(
        functools.partial(head_kernel, mp, ni, wc),
        [
            ((mp, half, 2 * wc), BF),
            ((mp, half, 2 * wc), BF),
            ((mp, 1, 2 * wc), F32),
            ((n, D), F32),
            ((8, D), F32),
            ((8, 128), F32),
        ],
        [
            pltpu.VMEM((mp, D, 2 * wc), BF),
            pltpu.VMEM((HR, D), F32),
            pltpu.VMEM((HR, D), F32),
            pltpu.VMEM((D, 2 * wc), BF),
            pltpu.SemaphoreType.DMA((parts,)),
        ],
        [
            ("smem", place),
            residual,
            final_vec,
            head_bias,
            class_ids,
            wide(label_ids),
            wide(label_mix),
            wide(0.5 * image_weight / weight_sum),
            wide(image_weight / weight_sum),
            wide(pooled),
            teacher_all,
            head_unit,
        ],
        8,
    )
    head_scatter = Scatter(head_mine, head_other)
    flying = [head_scatter]
    sending = [head_other]

    def proceed(fresh):
        moved = [array for unit in flying for array in unit.step()]
        flying.append(fresh)
        return moved

    attn_list, mlp_list = [None] * L, [None] * L
    gain_list, bias_list = [None] * L, [None] * L
    for layer in reversed(range(L)):
        resid_in, first, qkv, attended, lse, middle, second, hidden, slope = saved[layer]
        gmid, mlp_mine, mlp_other, up_bgrad, mlp_vgrad = call(
            functools.partial(mlp_backward_kernel, mp),
            [
                ((n, D), F32),
                ((mp, half, 2 * fl), BF),
                ((mp, half, 2 * fl), BF),
                ((mp, 1, fl), F32),
                ((8, D), F32),
            ],
            [
                pltpu.VMEM((mp, D, 2 * fl), BF),
                pltpu.VMEM((n, D), BF),
                pltpu.VMEM((D, n), BF),
                pltpu.VMEM((D, n), BF),
                pltpu.VMEM((D, 2 * fl), BF),
                pltpu.SemaphoreType.DMA((parts,)),
            ],
            [
                ("smem", place),
                grad,
                middle,
                layer_vecs[layer],
                second,
                hidden,
                slope,
                mlp_units[layer],
            ],
            27,
            sending,
        )
        mlp_list[layer] = Scatter(mlp_mine, mlp_other)
        sending = proceed(mlp_list[layer])
        grad, attn_mine, attn_other, qkv_bgrad, attn_vgrad = call(
            functools.partial(attn_backward_kernel, mp, ni, wl),
            [
                ((n, D), F32),
                ((mp, half, 4 * wl), BF),
                ((mp, half, 4 * wl), BF),
                ((mp, 1, 3 * wl), F32),
                ((8, D), F32),
            ],
            [
                pltpu.VMEM((mp, D, 4 * wl), BF),
                pltpu.VMEM((n, D), BF),
                pltpu.VMEM((D, n), BF),
                pltpu.VMEM((D, n), BF),
                pltpu.VMEM((n, wl), BF),
                pltpu.VMEM((n, 3 * wl), BF),
                pltpu.VMEM((D, 4 * wl), BF),
                pltpu.SemaphoreType.DMA((parts,)),
            ],
            [
                ("smem", place),
                gmid,
                resid_in,
                layer_vecs[layer],
                live_rows,
                first,
                qkv,
                attended,
                lse,
                attn_units[layer],
            ],
            33,
            sending,
        )
        attn_list[layer] = Scatter(attn_mine, attn_other)
        sending = proceed(attn_list[layer])
        gain_list[layer] = (attn_vgrad + mlp_vgrad)[:6]
        bias_list[layer] = jnp.concatenate(
            [qkv_bgrad[:, 0, :wl], qkv_bgrad[:, 0, 2 * wl :], up_bgrad[:, 0]], axis=1
        )

    patch_grad = dot_tn(patch_rows, grad.astype(BF)).astype(BF)
    patch_grad = patch_grad.reshape(dp, 2, mp, quarter, D).transpose(1, 2, 0, 3, 4)
    patch_grad = patch_grad.reshape(2, mp, dp * quarter, D)
    patch_grad = Scatter(
        lax.dynamic_index_in_dim(patch_grad, here_teach, 0, False),
        lax.dynamic_index_in_dim(patch_grad, 1 - here_teach, 0, False),
    ).result()
    patch_grad = outward(gather_mp(patch_grad).reshape(rows_own, D))

    source_grads = lax.dot_general(
        sources, grad, (((0,), (0,)), ((), ())), precision=HIGH, preferred_element_type=F32
    )
    vector_grads = outward(
        jnp.concatenate(gain_list + [final_vgrad[:2], source_grads], axis=0)
    )
    bias_blocks = jnp.concatenate(
        bias_list + [head_bgrad[:, 0, :cl], head_bgrad[:, 0, wc : wc + cl]], axis=1
    )
    bias_size = bias_blocks.shape[1]
    flat = jnp.concatenate([vector_grads.reshape(-1), bias_blocks.reshape(-1)])
    flat = jnp.pad(flat, (0, -flat.size % 1024)).reshape(-1, 128)
    flat = sum_all(flat).reshape(-1)
    vector_grads = flat[: vector_params.size].reshape(vector_params.shape)
    bias_grads = lax.dynamic_slice_in_dim(
        flat, vector_params.size + here_mp * bias_size, bias_size, 0
    )

    attn_list = [unit.result() for unit in attn_list]
    mlp_list = [unit.result() for unit in mlp_list]
    head_grads = head_scatter.result()
    attn_grads = jnp.stack(
        [
            jnp.stack([attn_list[layer][:, part * wl : (part + 1) * wl] for part in range(4)])
            for layer in range(L)
        ]
    )
    mlp_grads = jnp.stack(
        [jnp.stack([mlp_list[layer][:, :fl], mlp_list[layer][:, fl:]]) for layer in range(L)]
    )
    head_grads = jnp.stack([head_grads[:, :cl], head_grads[:, wc : wc + cl]])

    step_power = step_count[0].astype(F32)
    correct_first = 1.0 - jnp.power(BETA, step_power)
    correct_second = 1.0 - jnp.power(BETA, step_power)
    weights = (patch_weight, attn_weight, mlp_weight, head_weight, vector_params, split_biases)
    gradients = (patch_grad, attn_grads, mlp_grads, head_grads, vector_grads, bias_grads)
    firsts = (patch_first, attn_first, mlp_first, head_first, vector_first, bias_first)
    seconds = (patch_second, attn_second, mlp_second, head_second, vector_second, bias_second)
    decay_pieces = expand_params(split_params(decay_mask.astype(F32)))
    results = [
        adam_direction(gradients[slot], firsts[slot], seconds[slot], correct_first, correct_second)
        for slot in range(6)
    ]
    directions = [
        results[slot][2] + DECAY * decay_pieces[slot] * weights[slot] for slot in range(6)
    ]
    totals = sum_all(
        jnp.concatenate(
            [
                squares_of(weights, mp_first, data_first),
                squares_of(directions, mp_first, data_first),
                loss_part[0, :1],
            ]
        )
    )
    npar = (totals.size - 1) // 2
    weights_sq, direction_sq, loss_value = totals[:npar], totals[npar : 2 * npar], totals[2 * npar]
    weight_norm = jnp.sqrt(weights_sq)
    update_norm = jnp.sqrt(direction_sq)
    trust_ratio = weight_norm / update_norm
    rates = BASE_RATE * jnp.power(LAYER_DECAY, 2.0 - layer_ids.astype(F32)) * trust_ratio
    rate_pieces = expand_params(split_params(rates))
    updated = [weights[slot] - rate_pieces[slot] * directions[slot] for slot in range(6)]
    norm_table = jnp.stack([weight_norm, update_norm])
    return (
        *updated,
        *[results[slot][0] for slot in range(6)],
        *[results[slot][1] for slot in range(6)],
        norm_table,
        trust_ratio,
        loss_value,
    )


def solution(mesh):
    rows = ("dp", "teach")
    moments = (
        P(rows, None),
        P(None, None, rows, "mp"),
        P(None, None, rows, "mp"),
        P(None, rows, "mp"),
        P(),
        P("mp"),
    )
    placed = (
        P(rows, None, None),
        P(rows, None),
        P(rows, None),
        P(rows),
        P(rows),
        P(),
        P(None, "mp"),
        *moments,
        *moments,
        *moments,
        P(),
        P(),
        P(),
    )
    return jax.shard_map(
        per_device,
        mesh=mesh,
        in_specs=placed,
        out_specs=(*moments, *moments, *moments, P(), P(), P()),
        check_vma=False,
    )
```

time: 2370 us -> 854 us (0.36)
  waiting for transfers between devices: 1370 us -> 391 us
  matrix products: 347 us -> 7.9 us
  Pallas kernels: 0 us -> 213 us
  local copies, waits for them, and re-layouts: 245 us -> 56.2 us
  blocking collectives: 144 us -> 0 us
  other arithmetic: 213 us -> 92.6 us
  starting transfers between devices: 1.28 us -> 58 us
    psum x9 -> x0, waiting for transfers between devices: 1140 us -> none  [the longest x8 1130 us: reduce_rows(): return lax.psum(partial_value, 'mp')]
    dot_general x104 -> x5, matrix products: 347 us -> 7.9 us  [the longest x1 2.85 us: per_device(): jnp.dot(sources, vec_in[head_row + 2:], precision=HIGH)]
    pallas_call x0 -> x9, Pallas kernels: none -> 213 us  [call(): pl.pallas_call(ordered if after else kernel, out_shape=out_shape, in_spec...]
    all_gather x3 -> x6, waiting for transfers between devices: 67.1 us -> 250 us  [the longest x5 250 us: gather_unit(): lax.all_gather(local, ALL, axis=0, tiled=True)]
    ppermute x0 -> x54, waiting for transfers between devices: none -> 128 us  [swap(): lax.ppermute(values, axis, [(rank, rank ^ distance) for rank in range(siz...]
    psum x5 -> x0, blocking collectives: 118 us -> none  [the longest x1 40.1 us: per_device(): lax.psum((vector_grads, bias_block), ('dp', 'mp', 'teach'))]
    reduce_sum x35 -> x1, other arithmetic: 110 us -> 0.68 us  [per_device(): weight_sum = sum_all(jnp.sum(image_weight).reshape(1))[0]]
    reduce_scatter x2 -> x6, waiting for transfers between devices: 93.4 us -> 11.9 us  [step(): self.total = lax.psum_scatter(total, 'dp', scatter_dimension=0, tiled=True)]
  transfers between devices with their start and end apart: 16 -> 66, of which waited for: 15 -> 31; matrix products, arithmetic and copies ran while one was open for 9% -> 15% of each run, Pallas kernels for 0% -> 24%
where the time goes in v1:
time: 854 us; the launch traced here: 845 us
  waiting for transfers between devices  391 us (46%)
  Pallas kernels  213 us (25%)
  other arithmetic  92.6 us (11%)
  starting transfers between devices  58 us (7%)
  local copies, waits for them, and re-layouts  56.2 us (7%)
  between operations  26.6 us (3%)
    all_gather x5, waiting for transfers between devices, gather_unit(): lax.all_gather(local, ALL, axis=0, tiled=True)  250 us
    pallas_call x9, Pallas kernels, call(): pl.pallas_call(ordered if after else kernel, out_shape=out_shape, in_spec...  213 us
    ppermute x54, waiting for transfers between devices, swap(): lax.ppermute(values, axis, [(rank, rank ^ distance) for rank in range(siz...  128 us
    ppermute x54, starting transfers between devices, swap(): lax.ppermute(values, axis, [(rank, rank ^ distance) for rank in range(siz...  57.3 us
  transfers between devices with their start and end apart: 66, of which 31 were waited for; matrix products, arithmetic and copies ran while one was open for 15% of the time, Pallas kernels for 24%

profile of v1, /device:TPU:0, one launch (start us, length us, event | category | flops | bytes accessed | tf_op | source)
XLA Modules:
  0.0 845.0 jit_solution(17365163292374284329)
XLA Ops:
  7.3 2.6 multiply_reduce_fusion.6
  25.6 4.0 collective-permute-start.2
  32.5 2.8 collective-permute-start.10
  78.3 2.9 collective-permute-start.6
  82.6 3.9 collective-permute-start.7
  100.8 2.9 convolution_add_fusion.resid_ref.refs_2_
  103.7 35.9 %all-gather.9.cloned.1.call-done = bf16[3072,768]{1,0:T(8,128)(2,1)} async-done(((bf16[96,768]{1,0:T(8,128)(2,1)}), bf16[3072,768]{1,0:T(8,128)(2,1)}) %all-gather.9.cloned.1.call-update) | async-done | bytes 4718608 | tf_op jit(solution)/shard_map/all_gather | solution.py:448
  139.6 21.3 %shard_map.427 = (bf16[576,768]{1,0:T(8,128)(2,1)}, bf16[4,576,576]{2,1,0:T(8,128)(2,1)}, bf16[4,576,192]{2,1,0:T(8,128)(2,1)}, f32[4,576,3]{2,1,0:T(8,128)}, f32[576,768]{1,0:T(8,128)}) custom-call(f32[576,768]{1,0:T(8,128)} %convolution_add_fusion.resid_ref.refs_2_, f32[8,768]{1,0:T(8,128)} %pad.53.vec_ref.refs_3_, f32[4,1,576]{2,1,0:T(1,128)} %copy.76.bias_ref, ...), custom_call_target="tpu_custom_call" | custom-call | flops 23000000512 | bytes 12744960 | tf_op jit(solution)/shard_map/pallas_call | solution.py:432
  160.9 63.1 %all-gather.11.cloned.1.call-done = bf16[3072,1536]{1,0:T(8,128)(2,1)} async-done(((bf16[96,1536]{1,0:T(8,128)(2,1)}), bf16[3072,1536]{1,0:T(8,128)(2,1)}) %all-gather.11.cloned.1.call-update) | async-done | bytes 9437200 | tf_op jit(solution)/shard_map/all_gather | solution.py:448
  224.0 19.0 %shard_map.428 = (bf16[576,768]{1,0:T(8,128)(2,1)}, bf16[4,576,768]{2,1,0:T(8,128)(2,1)}, f32[4,576,768]{2,1,0:T(8,128)}, f32[576,768]{1,0:T(8,128)}) custom-call(f32[576,768]{1,0:T(8,128)} %get-tuple-element.65.mid_ref.refs_2_, f32[8,768]{1,0:T(8,128)} %pad.53.vec_ref.refs_3_, f32[4,1,768]{2,1,0:T(1,128)} %broadcast_in_dim.89.bias_ref, ...), custom_call_target="tpu_custom_call" | custom-call | flops 23000000512 | bytes 24514560 | tf_op jit(solution)/shard_map/pallas_call | solution.py:432
  243.0 46.6 %all-gather.13.cloned.1.call-done = bf16[3072,768]{1,0:T(8,128)(2,1)} async-done(((bf16[96,768]{1,0:T(8,128)(2,1)}), bf16[3072,768]{1,0:T(8,128)(2,1)}) %all-gather.13.cloned.1.call-update) | async-done | bytes 4718608 | tf_op jit(solution)/shard_map/all_gather | solution.py:448
  289.6 21.1 %shard_map.429 = (bf16[576,768]{1,0:T(8,128)(2,1)}, bf16[4,576,576]{2,1,0:T(8,128)(2,1)}, bf16[4,576,192]{2,1,0:T(8,128)(2,1)}, f32[4,576,3]{2,1,0:T(8,128)}, f32[576,768]{1,0:T(8,128)}) custom-call(f32[576,768]{1,0:T(8,128)} %get-tuple-element.66.resid_ref.refs_2_, f32[8,768]{1,0:T(8,128)} %pad.54.vec_ref.refs_3_, f32[4,1,576]{2,1,0:T(1,128)} %broadcast_in_dim.90.bias_ref, ...), custom_call_target="tpu_custom_call" | custom-call | flops 23000000512 | bytes 12744960 | tf_op jit(solution)/shard_map/pallas_call | solution.py:432
  310.7 63.1 %all-gather.15.cloned.1.call-done = bf16[3072,1536]{1,0:T(8,128)(2,1)} async-done(((bf16[96,1536]{1,0:T(8,128)(2,1)}), bf16[3072,1536]{1,0:T(8,128)(2,1)}) %all-gather.15.cloned.1.call-update) | async-done | bytes 9437200 | tf_op jit(solution)/shard_map/all_gather | solution.py:448
  373.8 19.1 %shard_map.430 = (bf16[576,768]{1,0:T(8,128)(2,1)}, bf16[4,576,768]{2,1,0:T(8,128)(2,1)}, f32[4,576,768]{2,1,0:T(8,128)}, f32[576,768]{1,0:T(8,128)}) custom-call(f32[576,768]{1,0:T(8,128)} %get-tuple-element.67.mid_ref.refs_2_, f32[8,768]{1,0:T(8,128)} %pad.54.vec_ref.refs_3_, f32[4,1,768]{2,1,0:T(1,128)} %broadcast_in_dim.91.bias_ref, ...), custom_call_target="tpu_custom_call" | custom-call | flops 23000000512 | bytes 24514560 | tf_op jit(solution)/shard_map/pallas_call | solution.py:432
  392.9 41.8 %all-gather.17.cloned.1.call-done = bf16[3072,512]{1,0:T(8,128)(2,1)} async-done(((bf16[96,512]{1,0:T(8,128)(2,1)}), bf16[3072,512]{1,0:T(8,128)(2,1)}) %all-gather.17.cloned.1.call-update) | async-done | bytes 3145744 | tf_op jit(solution)/shard_map/all_gather | solution.py:448
  434.6 8.3 shard_map.431
  443.2 28.2 %shard_map.432 = (f32[576,768]{1,0:T(8,128)}, bf16[4,384,1536]{2,1,0:T(8,128)(2,1)}, bf16[4,384,1536]{2,1,0:T(8,128)(2,1)}, f32[4,1,768]{2,1,0:T(1,128)}, f32[8,768]{1,0:T(8,128)}) custom-call(s32[1]{0:T(128)} %bitcast.4.place_ref.refs_0_, f32[576,768]{1,0:T(8,128)} %get-tuple-element.69.refs_1_, f32[576,768]{1,0:T(8,128)} %get-tuple-element.67.mid_ref.refs_2_, ...), custom_call_target="tpu_custom_call" | custom-call | flops 31050000384 | bytes 37318660 | tf_op jit(solution)/shard_map/pallas_call | solution.py:432
  474.2 33.9 %shard_map.433 = (f32[576,768]{1,0:T(8,128)}, bf16[4,384,768]{2,1,0:T(8,128)(2,1)}, bf16[4,384,768]{2,1,0:T(8,128)(2,1)}, f32[4,1,576]{2,1,0:T(1,128)}, f32[8,768]{1,0:T(8,128)}) custom-call(s32[1]{0:T(128)} %bitcast.4.place_ref.refs_0_, f32[576,768]{1,0:T(8,128)} %get-tuple-element.74.refs_1_, f32[576,768]{1,0:T(8,128)} %get-tuple-element.66.resid_ref.refs_2_, ...), custom_call_target="tpu_custom_call" | custom-call | flops 37950001152 | bytes 19650820 | tf_op jit(solution)/shard_map/pallas_call | solution.py:432
  511.9 8.1 collective-permute-done.16
  530.0 11.8 %reduce-scatter.17.cloned.1.call-done = bf16[96,512]{1,0:T(8,128)(2,1)} async-done(((bf16[384,512]{1,0:T(8,128)(2,1)}), bf16[96,512]{1,0:T(8,128)(2,1)}) %reduce-scatter.17.cloned.1.call-update) | async-done | bytes 98320 | tf_op jit(solution)/shard_map/reduce_scatter | solution.py:507
  544.2 2.4 add_convert_fusion.9
  549.8 4.5 collective-permute-done.35
  557.6 4.0 add_convert_fusion.5
  564.1 28.3 %shard_map.434 = (f32[576,768]{1,0:T(8,128)}, bf16[4,384,1536]{2,1,0:T(8,128)(2,1)}, bf16[4,384,1536]{2,1,0:T(8,128)(2,1)}, f32[4,1,768]{2,1,0:T(1,128)}, f32[8,768]{1,0:T(8,128)}) custom-call(s32[1]{0:T(128)} %bitcast.4.place_ref.refs_0_, f32[576,768]{1,0:T(8,128)} %get-tuple-element.80.refs_1_, f32[576,768]{1,0:T(8,128)} %get-tuple-element.65.mid_ref.refs_2_, ...), custom_call_target="tpu_custom_call" | custom-call | flops 31050000384 | bytes 37711876 | tf_op jit(solution)/shard_map/pallas_call | solution.py:432
  595.2 33.8 %shard_map.435 = (f32[576,768]{1,0:T(8,128)}, bf16[4,384,768]{2,1,0:T(8,128)(2,1)}, bf16[4,384,768]{2,1,0:T(8,128)(2,1)}, f32[4,1,576]{2,1,0:T(1,128)}, f32[8,768]{1,0:T(8,128)}) custom-call(s32[1]{0:T(128)} %bitcast.4.place_ref.refs_0_, f32[576,768]{1,0:T(8,128)} %get-tuple-element.86.refs_1_, f32[576,768]{1,0:T(8,128)} %convolution_add_fusion.resid_ref.refs_2_, ...), custom_call_target="tpu_custom_call" | custom-call | flops 37950001152 | bytes 22599940 | tf_op jit(solution)/shard_map/pallas_call | solution.py:432
  629.0 2.6 convolution_convert_fusion
  634.3 2.5 fusion.7
  642.6 24.2 %collective-permute-done.23 = bf16[48,768]{1,0:T(8,128)(2,1)S(1)} collective-permute-done((bf16[48,768]{1,0:T(8,128)(2,1)S(1)}, bf16[48,768]{1,0:T(8,128)(2,1)S(1)}, u32[]{:S(2)}, u32[]{:S(2)}) %collective-permute-start.23) | collective-permute-done | bytes 73760 | tf_op jit(solution)/shard_map/ppermute | solution.py:456
  668.4 2.8 collective-permute-done.21
  672.8 3.6 collective-permute-done.24
  678.1 3.4 collective-permute-done.22
  683.3 3.9 fusion
  687.3 2.4 add_convert_fusion.13
  691.7 4.8 collective-permute-done.31
  702.0 4.0 add_convert_fusion.3
  708.5 13.9 %collective-permute-done.40 = bf16[192,1536]{1,0:T(8,128)(2,1)S(1)} collective-permute-done((bf16[192,1536]{1,0:T(8,128)(2,1)S(1)}, bf16[192,1536]{1,0:T(8,128)(2,1)S(1)}, u32[]{:S(2)}, u32[]{:S(2)}) %collective-permute-start.40) | collective-permute-done | bytes 589856 | tf_op jit(solution)/shard_map/ppermute | solution.py:456
  729.4 2.7 fusion.8
  735.2 18.1 %collective-permute-done.45 = f32[480,128]{1,0:T(8,128)S(1)} collective-permute-done((f32[480,128]{1,0:T(8,128)S(1)}, f32[480,128]{1,0:T(8,128)S(1)}, u32[]{:S(2)}, u32[]{:S(2)}) %collective-permute-start.45) | collective-permute-done | bytes 245792 | tf_op jit(solution)/shard_map/ppermute | solution.py:456
  754.9 3.6 fusion.1
  764.5 14.8 %collective-permute-done.47 = f32[480,128]{1,0:T(8,128)S(1)} collective-permute-done((f32[480,128]{1,0:T(8,128)S(1)}, f32[480,128]{1,0:T(8,128)S(1)}, u32[]{:S(2)}, u32[]{:S(2)}) %collective-permute-start.47) | collective-permute-done | bytes 245792 | tf_op jit(solution)/shard_map/ppermute | solution.py:456
  783.7 6.2 collective-permute-done.48
  792.3 2.0 multiply_reduce_fusion.11
  799.6 2.9 multiply_reduce_fusion.2
  805.1 4.0 multiply_reduce_fusion
  812.7 2.2 collective-permute-done.50
  816.3 2.2 collective-permute-done.51
  818.5 3.5 collective-permute-done.52
  822.6 3.8 collective-permute-done.53
  (514 shorter events, 171.0 us)
Async XLA Ops:
  7.2 91.2 %all-gather.7.cloned.1.call-start = ((), (), s32[]{:S(2)}) async-start(), calls=%async_computation.6 | async-start | bytes 1216512 | tf_op jit(solution)/shard_map/all_gather | solution.py:637
  16.5 123.1 %all-gather.9.cloned.1.call-start = ((), (), s32[]{:S(2)}) async-start(), calls=%async_computation.7 | async-start | bytes 4866048 | tf_op jit(solution)/shard_map/all_gather | solution.py:448
  19.2 204.7 %all-gather.11.cloned.1.call-start = ((), (), s32[]{:S(2)}) async-start(), calls=%async_computation.8 | async-start | bytes 9732096 | tf_op jit(solution)/shard_map/all_gather | solution.py:448
  22.1 267.5 %all-gather.13.cloned.1.call-start = ((), (), s32[]{:S(2)}) async-start(), calls=%async_computation.9 | async-start | bytes 4866048 | tf_op jit(solution)/shard_map/all_gather | solution.py:448
  23.8 350.0 %all-gather.15.cloned.1.call-start = ((), (), s32[]{:S(2)}) async-start(), calls=%async_computation.10 | async-start | bytes 9732096 | tf_op jit(solution)/shard_map/all_gather | solution.py:448
  25.6 409.1 %all-gather.17.cloned.1.call-start = ((), (), s32[]{:S(2)}) async-start(), calls=%async_computation.11 | async-start | bytes 3244032 | tf_op jit(solution)/shard_map/all_gather | solution.py:448
  25.6 64.2 %collective-permute-start.2 = (f32[2804]{0:T(1024)}, f32[2804]{0:T(1024)}, u32[]{:S(2)}, u32[]{:S(2)}) collective-permute-start(f32[2804]{0:T(1024)} %param.40), channel_id=1, source_target_pairs={{0,6},{2,4},{4,2},{6,0},{1,7},{3,5},{5,3},{7,1},{8,14},{10,12},{12... | collective-permute-start | bytes 33656 | tf_op jit(solution)/shard_map/ppermute | solution.py:456
  29.6 61.2 %collective-permute-start.1 = (f32[2804]{0:T(1024)}, f32[2804]{0:T(1024)}, u32[]{:S(2)}, u32[]{:S(2)}) collective-permute-start(f32[2804]{0:T(1024)} %param.40), channel_id=1, source_target_pairs={{0,4},{2,6},{4,0},{6,2},{1,5},{3,7},{5,1},{7,3},{8,12},{10,14},{12... | collective-permute-start | bytes 33656 | tf_op jit(solution)/shard_map/ppermute | solution.py:456
  30.1 61.4 %collective-permute-start = (f32[2804]{0:T(1024)}, f32[2804]{0:T(1024)}, u32[]{:S(2)}, u32[]{:S(2)}) collective-permute-start(f32[2804]{0:T(1024)} %param.40), channel_id=1, source_target_pairs={{0,2},{2,0},{4,6},{6,4},{1,3},{3,1},{5,7},{7,5},{8,10},{10,8},{12,... | collective-permute-start | bytes 33656 | tf_op jit(solution)/shard_map/ppermute | solution.py:456
  30.9 37.5 %collective-permute-start.3 = (f32[1]{0:T(128)}, f32[1]{0:T(128)}, u32[]{:S(2)}, u32[]{:S(2)}) collective-permute-start(f32[1]{0:T(128)} %bitcast.35), channel_id=1, source_target_pairs={{0,1},{1,0},{2,3},{3,2},{4,5},{5,4},{6,7},{7,6},{8,9},{9,8},{10,11... | collective-permute-start | bytes 20 | tf_op jit(solution)/shard_map/ppermute | solution.py:456
  32.5 63.6 %collective-permute-start.10 = (bf16[224,256]{1,0:T(8,128)(2,1)}, bf16[224,256]{1,0:T(8,128)(2,1)}, u32[]{:S(2)}, u32[]{:S(2)}) collective-permute-start(bf16[224,256]{1,0:T(8,128)(2,1)} %get-tuple-element.200), channel_id=1, source_target_pairs={{0,6},{2,4},{4,2},{6,0},{1,7},{3,5},{5,3},{7,1},{8,14},{10,12},{12... | collective-permute-start | bytes 344072 | tf_op jit(solution)/shard_map/ppermute | solution.py:456
  36.9 504.9 %reduce-scatter.17.cloned.1.call-start = ((), (), s32[]{:S(2)}) async-start(), calls=%async_computation.17 | async-start | bytes 491520 | tf_op jit(solution)/shard_map/reduce_scatter | solution.py:507
  87.2 8.8 %collective-permute-start.9 = (bf16[224,256]{1,0:T(8,128)(2,1)}, bf16[224,256]{1,0:T(8,128)(2,1)S(1)}, u32[]{:S(2)}, u32[]{:S(2)}) collective-permute-start(bf16[224,256]{1,0:T(8,128)(2,1)} %get-tuple-element.200), channel_id=1, source_target_pairs={{0,4},{2,6},{4,0},{6,2},{1,5},{3,7},{5,1},{7,3},{8,12},{10,14},{12... | collective-permute-start | bytes 344072 | tf_op jit(solution)/shard_map/ppermute | solution.py:456
  442.9 28.8 %collective-permute-start.11 = (bf16[4,384,512]{2,1,0:T(8,128)(2,1)}, bf16[4,384,512]{2,1,0:T(8,128)(2,1)S(1)}, u32[]{:S(2)}, u32[]{:S(2)}) collective-permute-start(bf16[4,384,512]{2,1,0:T(8,128)(2,1)} %get-tuple-element.73.refs_8_), channel_id=1, source_target_pairs={{0,1},{1,0},{2,3},{3,2},{4,5},{5,4},{6,7},{7,6},{8,9},{9,8},{10,11... | collective-permute-start | bytes 4718600 | tf_op jit(solution)/shard_map/ppermute | solution.py:456
  471.4 86.1 %collective-permute-start.14 = (bf16[4,384,1536]{2,1,0:T(8,128)(2,1)}, bf16[4,384,1536]{2,1,0:T(8,128)(2,1)}, u32[]{:S(2)}, u32[]{:S(2)}) collective-permute-start(bf16[4,384,1536]{2,1,0:T(8,128)(2,1)} %get-tuple-element.85), channel_id=1, source_target_pairs={{0,1},{1,0},{2,3},{3,2},{4,5},{5,4},{6,7},{7,6},{8,9},{9,8},{10,11... | collective-permute-start | bytes 14155784 | tf_op jit(solution)/shard_map/ppermute | solution.py:456
  472.1 37.8 %collective-permute-start.12 = (bf16[192,512]{1,0:T(8,128)(2,1)S(1)}, bf16[192,512]{1,0:T(8,128)(2,1)S(1)}, u32[]{:S(2)}, u32[]{:S(2)}) collective-permute-start(bf16[192,512]{1,0:T(8,128)(2,1)S(1)} %get-tuple-element.171.refs_11_), channel_id=1, source_target_pairs={{0,4},{2,6},{4,0},{6,2},{1,5},{3,7},{5,1},{7,3},{8,12},{10,14},{12... | collective-permute-start | bytes 589832 | tf_op jit(solution)/shard_map/ppermute | solution.py:456
  473.7 34.6 %collective-permute-start.13 = (bf16[192,512]{1,0:T(8,128)(2,1)S(1)}, bf16[192,512]{1,0:T(8,128)(2,1)S(1)}, u32[]{:S(2)}, u32[]{:S(2)}) collective-permute-start(bf16[192,512]{1,0:T(8,128)(2,1)S(1)} %get-tuple-element.172.refs_10_), channel_id=1, source_target_pairs={{0,2},{2,0},{4,6},{6,4},{1,3},{3,1},{5,7},{7,5},{8,10},{10,8},{12,... | collective-permute-start | bytes 589832 | tf_op jit(solution)/shard_map/ppermute | solution.py:456
  508.1 34.6 %collective-permute-start.19 = (bf16[4,384,768]{2,1,0:T(8,128)(2,1)}, bf16[4,384,768]{2,1,0:T(8,128)(2,1)S(1)}, u32[]{:S(2)}, u32[]{:S(2)}) collective-permute-start(bf16[4,384,768]{2,1,0:T(8,128)(2,1)} %get-tuple-element.92), channel_id=1, source_target_pairs={{0,1},{1,0},{2,3},{3,2},{4,5},{5,4},{6,7},{7,6},{8,9},{9,8},{10,11... | collective-permute-start | bytes 7077896 | tf_op jit(solution)/shard_map/ppermute | solution.py:456
  508.4 11.6 %collective-permute-start.16 = (bf16[384,512]{1,0:T(8,128)(2,1)S(1)}, bf16[384,512]{1,0:T(8,128)(2,1)S(1)}, u32[]{:S(2)}, u32[]{:S(2)}) collective-permute-start(bf16[384,512]{1,0:T(8,128)(2,1)S(1)} %pad_maximum_fusion.12.refs_9_), channel_id=1, source_target_pairs={{0,4},{2,6},{4,0},{6,2},{1,5},{3,7},{5,1},{7,3},{8,12},{10,14},{12... | collective-permute-start | bytes 1179656 | tf_op jit(solution)/shard_map/ppermute | solution.py:456
  510.0 11.3 %collective-permute-start.15 = (bf16[384,512]{1,0:T(8,128)(2,1)S(1)}, bf16[384,512]{1,0:T(8,128)(2,1)S(1)}, u32[]{:S(2)}, u32[]{:S(2)}) collective-permute-start(bf16[384,512]{1,0:T(8,128)(2,1)S(1)} %pad_maximum_fusion.11.refs_8_), channel_id=1, source_target_pairs={{0,2},{2,0},{4,6},{6,4},{1,3},{3,1},{5,7},{7,5},{8,10},{10,8},{12,... | collective-permute-start | bytes 1179656 | tf_op jit(solution)/shard_map/ppermute | solution.py:456
  522.3 231.7 %reduce-scatter.11.cloned.1.call-start = ((), (), s32[]{:S(2)}) async-start(), calls=%async_computation.14 | async-start | bytes 737280 | tf_op jit(solution)/shard_map/reduce_scatter | solution.py:507
  548.2 8.0 collective-permute-start.33
  554.4 79.9 %collective-permute-start.36 = (bf16[384,768]{1,0:T(8,128)(2,1)S(1)}, bf16[384,768]{1,0:T(8,128)(2,1)S(1)}, u32[]{:S(2)}, u32[]{:S(2)}) collective-permute-start(bf16[384,768]{1,0:T(8,128)(2,1)S(1)} %pad_maximum_fusion.9), channel_id=1, source_target_pairs={{0,4},{2,6},{4,0},{6,2},{1,5},{3,7},{5,1},{7,3},{8,12},{10,14},{12... | collective-permute-start | bytes 1769480 | tf_op jit(solution)/shard_map/ppermute | solution.py:456
  556.3 78.0 %collective-permute-start.34 = (bf16[384,768]{1,0:T(8,128)(2,1)S(1)}, bf16[384,768]{1,0:T(8,128)(2,1)S(1)}, u32[]{:S(2)}, u32[]{:S(2)}) collective-permute-start(bf16[384,768]{1,0:T(8,128)(2,1)S(1)} %pad_maximum_fusion.8), channel_id=1, source_target_pairs={{0,2},{2,0},{4,6},{6,4},{1,3},{3,1},{5,7},{7,5},{8,10},{10,8},{12,... | collective-permute-start | bytes 1769480 | tf_op jit(solution)/shard_map/ppermute | solution.py:456
  561.7 31.0 %collective-permute-start.17 = (bf16[192,1536]{1,0:T(8,128)(2,1)S(1)}, bf16[192,1536]{1,0:T(8,128)(2,1)S(1)}, u32[]{:S(2)}, u32[]{:S(2)}) collective-permute-start(bf16[192,1536]{1,0:T(8,128)(2,1)S(1)} %get-tuple-element.156.refs_11_), channel_id=1, source_target_pairs={{0,4},{2,6},{4,0},{6,2},{1,5},{3,7},{5,1},{7,3},{8,12},{10,14},{12... | collective-permute-start | bytes 1769480 | tf_op jit(solution)/shard_map/ppermute | solution.py:456
  562.3 31.6 %collective-permute-start.18 = (bf16[192,1536]{1,0:T(8,128)(2,1)S(1)}, bf16[192,1536]{1,0:T(8,128)(2,1)S(1)}, u32[]{:S(2)}, u32[]{:S(2)}) collective-permute-start(bf16[192,1536]{1,0:T(8,128)(2,1)S(1)} %get-tuple-element.157.refs_10_), channel_id=1, source_target_pairs={{0,2},{2,0},{4,6},{6,4},{1,3},{3,1},{5,7},{7,5},{8,10},{10,8},{12,... | collective-permute-start | bytes 1769480 | tf_op jit(solution)/shard_map/ppermute | solution.py:456
  592.5 109.5 %collective-permute-start.37 = (bf16[4,384,1536]{2,1,0:T(8,128)(2,1)}, bf16[4,384,1536]{2,1,0:T(8,128)(2,1)}, u32[]{:S(2)}, u32[]{:S(2)}) collective-permute-start(bf16[4,384,1536]{2,1,0:T(8,128)(2,1)} %get-tuple-element.97), channel_id=1, source_target_pairs={{0,1},{1,0},{2,3},{3,2},{4,5},{5,4},{6,7},{7,6},{8,9},{9,8},{10,11... | collective-permute-start | bytes 14155784 | tf_op jit(solution)/shard_map/ppermute | solution.py:456
  636.8 123.3 %reduce-scatter.7.cloned.1.call-start = ((), (), s32[]{:S(2)}) async-start(), calls=%async_computation.12 | async-start | bytes 184320 | tf_op jit(solution)/shard_map/reduce_scatter | solution.py:507
  636.9 46.3 %collective-permute-start.43 = (bf16[384,1536]{1,0:T(8,128)(2,1)}, bf16[384,1536]{1,0:T(8,128)(2,1)}, u32[]{:S(2)}, u32[]{:S(2)}) collective-permute-start(bf16[384,1536]{1,0:T(8,128)(2,1)} %pad_maximum_fusion.1.refs_12_), channel_id=1, source_target_pairs={{0,4},{2,6},{4,0},{6,2},{1,5},{3,7},{5,1},{7,3},{8,12},{10,14},{12... | collective-permute-start | bytes 3538952 | tf_op jit(solution)/shard_map/ppermute | solution.py:456
  637.5 45.8 %collective-permute-start.42 = (bf16[384,1536]{1,0:T(8,128)(2,1)}, bf16[384,1536]{1,0:T(8,128)(2,1)}, u32[]{:S(2)}, u32[]{:S(2)}) collective-permute-start(bf16[384,1536]{1,0:T(8,128)(2,1)} %pad_maximum_fusion.refs_11_), channel_id=1, source_target_pairs={{0,2},{2,0},{4,6},{6,4},{1,3},{3,1},{5,7},{7,5},{8,10},{10,8},{12,... | collective-permute-start | bytes 3538952 | tf_op jit(solution)/shard_map/ppermute | solution.py:456
  638.6 48.6 %collective-permute-start.28 = (bf16[4,384,768]{2,1,0:T(8,128)(2,1)}, bf16[4,384,768]{2,1,0:T(8,128)(2,1)}, u32[]{:S(2)}, u32[]{:S(2)}) collective-permute-start(bf16[4,384,768]{2,1,0:T(8,128)(2,1)} %get-tuple-element.95), channel_id=1, source_target_pairs={{0,1},{1,0},{2,3},{3,2},{4,5},{5,4},{6,7},{7,6},{8,9},{9,8},{10,11... | collective-permute-start | bytes 7077896 | tf_op jit(solution)/shard_map/ppermute | solution.py:456
  641.1 25.8 %collective-permute-start.23 = (bf16[48,768]{1,0:T(8,128)(2,1)S(1)}, bf16[48,768]{1,0:T(8,128)(2,1)S(1)}, u32[]{:S(2)}, u32[]{:S(2)}) collective-permute-start(bf16[48,768]{1,0:T(8,128)(2,1)S(1)} %get-tuple-element.198), channel_id=1, source_target_pairs={{0,2},{2,0},{4,6},{6,4},{1,3},{3,1},{5,7},{7,5},{8,10},{10,8},{12,... | collective-permute-start | bytes 221192 | tf_op jit(solution)/shard_map/ppermute | solution.py:456
  683.2 113.0 %reduce-scatter.15.cloned.1.call-start = ((), (), s32[]{:S(2)}) async-start(), calls=%async_computation.16 | async-start | bytes 1474560 | tf_op jit(solution)/shard_map/reduce_scatter | solution.py:507
  687.2 110.9 %reduce-scatter.9.cloned.1.call-start = ((), (), s32[]{:S(2)}) async-start(), calls=%async_computation.13 | async-start | bytes 737280 | tf_op jit(solution)/shard_map/reduce_scatter | solution.py:507
  691.0 9.7 %collective-permute-start.29 = (bf16[192,768]{1,0:T(8,128)(2,1)S(1)}, bf16[192,768]{1,0:T(8,128)(2,1)S(1)}, u32[]{:S(2)}, u32[]{:S(2)}) collective-permute-start(bf16[192,768]{1,0:T(8,128)(2,1)S(1)} %get-tuple-element.159), channel_id=1, source_target_pairs={{0,4},{2,6},{4,0},{6,2},{1,5},{3,7},{5,1},{7,3},{8,12},{10,14},{12... | collective-permute-start | bytes 884744 | tf_op jit(solution)/shard_map/ppermute | solution.py:456
  697.4 32.0 %collective-permute-start.32 = (bf16[384,768]{1,0:T(8,128)(2,1)}, bf16[384,768]{1,0:T(8,128)(2,1)}, u32[]{:S(2)}, u32[]{:S(2)}) collective-permute-start(bf16[384,768]{1,0:T(8,128)(2,1)} %pad_maximum_fusion.7), channel_id=1, source_target_pairs={{0,4},{2,6},{4,0},{6,2},{1,5},{3,7},{5,1},{7,3},{8,12},{10,14},{12... | collective-permute-start | bytes 1769480 | tf_op jit(solution)/shard_map/ppermute | solution.py:456
  701.6 27.8 %collective-permute-start.30 = (bf16[384,768]{1,0:T(8,128)(2,1)}, bf16[384,768]{1,0:T(8,128)(2,1)}, u32[]{:S(2)}, u32[]{:S(2)}) collective-permute-start(bf16[384,768]{1,0:T(8,128)(2,1)} %pad_maximum_fusion.6), channel_id=1, source_target_pairs={{0,2},{2,0},{4,6},{6,4},{1,3},{3,1},{5,7},{7,5},{8,10},{10,8},{12,... | collective-permute-start | bytes 1769480 | tf_op jit(solution)/shard_map/ppermute | solution.py:456
  706.1 16.3 %collective-permute-start.40 = (bf16[192,1536]{1,0:T(8,128)(2,1)S(1)}, bf16[192,1536]{1,0:T(8,128)(2,1)S(1)}, u32[]{:S(2)}, u32[]{:S(2)}) collective-permute-start(bf16[192,1536]{1,0:T(8,128)(2,1)S(1)} %get-tuple-element.155), channel_id=1, source_target_pairs={{0,2},{2,0},{4,6},{6,4},{1,3},{3,1},{5,7},{7,5},{8,10},{10,8},{12,... | collective-permute-start | bytes 1769480 | tf_op jit(solution)/shard_map/ppermute | solution.py:456
  707.8 18.7 %collective-permute-start.38 = (bf16[192,1536]{1,0:T(8,128)(2,1)S(1)}, bf16[192,1536]{1,0:T(8,128)(2,1)S(1)}, u32[]{:S(2)}, u32[]{:S(2)}) collective-permute-start(bf16[192,1536]{1,0:T(8,128)(2,1)S(1)} %get-tuple-element.154), channel_id=1, source_target_pairs={{0,4},{2,6},{4,0},{6,2},{1,5},{3,7},{5,1},{7,3},{8,12},{10,14},{12... | collective-permute-start | bytes 1769480 | tf_op jit(solution)/shard_map/ppermute | solution.py:456
  723.7 31.2 %collective-permute-start.41 = (bf16[384,1536]{1,0:T(8,128)(2,1)}, bf16[384,1536]{1,0:T(8,128)(2,1)}, u32[]{:S(2)}, u32[]{:S(2)}) collective-permute-start(bf16[384,1536]{1,0:T(8,128)(2,1)} %pad_maximum_fusion.3), channel_id=1, source_target_pairs={{0,4},{2,6},{4,0},{6,2},{1,5},{3,7},{5,1},{7,3},{8,12},{10,14},{12... | collective-permute-start | bytes 3538952 | tf_op jit(solution)/shard_map/ppermute | solution.py:456
  726.9 28.0 %collective-permute-start.39 = (bf16[384,1536]{1,0:T(8,128)(2,1)S(1)}, bf16[384,1536]{1,0:T(8,128)(2,1)S(1)}, u32[]{:S(2)}, u32[]{:S(2)}) collective-permute-start(bf16[384,1536]{1,0:T(8,128)(2,1)S(1)} %pad_maximum_fusion.2), channel_id=1, source_target_pairs={{0,2},{2,0},{4,6},{6,4},{1,3},{3,1},{5,7},{7,5},{8,10},{10,8},{12,... | collective-permute-start | bytes 3538952 | tf_op jit(solution)/shard_map/ppermute | solution.py:456
  732.2 70.3 %reduce-scatter.13.cloned.1.call-start = ((), (), s32[]{:S(2)}) async-start(), calls=%async_computation.15 | async-start | bytes 1474560 | tf_op jit(solution)/shard_map/reduce_scatter | solution.py:507
  732.5 20.8 %collective-permute-start.45 = (f32[480,128]{1,0:T(8,128)S(1)}, f32[480,128]{1,0:T(8,128)S(1)}, u32[]{:S(2)}, u32[]{:S(2)}) collective-permute-start(f32[480,128]{1,0:T(8,128)S(1)} %fusion.40), channel_id=1, source_target_pairs={{0,2},{2,0},{4,6},{6,4},{1,3},{3,1},{5,7},{7,5},{8,10},{10,8},{12,... | collective-permute-start | bytes 737288 | tf_op jit(solution)/shard_map/ppermute | solution.py:456
  760.0 19.3 %collective-permute-start.47 = (f32[480,128]{1,0:T(8,128)S(1)}, f32[480,128]{1,0:T(8,128)S(1)}, u32[]{:S(2)}, u32[]{:S(2)}) collective-permute-start(f32[480,128]{1,0:T(8,128)S(1)} %add.610), channel_id=1, source_target_pairs={{0,8},{8,0},{16,24},{24,16},{1,9},{9,1},{17,25},{25,17},{2,10},{10... | collective-permute-start | bytes 737288 | tf_op jit(solution)/shard_map/ppermute | solution.py:456
  760.9 18.5 %collective-permute-start.27 = (f32[24,768]{1,0:T(8,128)S(1)}, f32[24,768]{1,0:T(8,128)S(1)}, u32[]{:S(2)}, u32[]{:S(2)}) collective-permute-start(f32[24,768]{1,0:T(8,128)S(1)} %get-tuple-element.212), channel_id=1, source_target_pairs={{0,6},{2,4},{4,2},{6,0},{1,7},{3,5},{5,3},{7,1},{8,14},{10,12},{12... | collective-permute-start | bytes 221192 | tf_op jit(solution)/shard_map/ppermute | solution.py:456
  762.2 17.3 %collective-permute-start.26 = (f32[24,768]{1,0:T(8,128)S(1)}, f32[24,768]{1,0:T(8,128)S(1)}, u32[]{:S(2)}, u32[]{:S(2)}) collective-permute-start(f32[24,768]{1,0:T(8,128)S(1)} %get-tuple-element.212), channel_id=1, source_target_pairs={{0,4},{2,6},{4,0},{6,2},{1,5},{3,7},{5,1},{7,3},{8,12},{10,14},{12... | collective-permute-start | bytes 221192 | tf_op jit(solution)/shard_map/ppermute | solution.py:456
  763.2 16.3 %collective-permute-start.25 = (f32[24,768]{1,0:T(8,128)S(1)}, f32[24,768]{1,0:T(8,128)S(1)}, u32[]{:S(2)}, u32[]{:S(2)}) collective-permute-start(f32[24,768]{1,0:T(8,128)S(1)} %get-tuple-element.212), channel_id=1, source_target_pairs={{0,2},{2,0},{4,6},{6,4},{1,3},{3,1},{5,7},{7,5},{8,10},{10,8},{12,... | collective-permute-start | bytes 221192 | tf_op jit(solution)/shard_map/ppermute | solution.py:456
  779.4 10.5 %collective-permute-start.48 = (f32[480,128]{1,0:T(8,128)S(1)}, f32[480,128]{1,0:T(8,128)S(1)}, u32[]{:S(2)}, u32[]{:S(2)}) collective-permute-start(f32[480,128]{1,0:T(8,128)S(1)} %add.611), channel_id=1, source_target_pairs={{0,16},{8,24},{16,0},{24,8},{1,17},{9,25},{17,1},{25,9},{2,18},{10... | collective-permute-start | bytes 737288 | tf_op jit(solution)/shard_map/ppermute | solution.py:456
  (103 other events, 716.1 us)
Sparse Core Ops, SparseCore 0:
  16.6 56.7 all-gather.6
  76.9 62.6 all-gather.8
  143.1 80.8 all-gather.10
  227.3 62.2 all-gather.12
  292.9 80.8 all-gather.14
  377.0 57.5 all-gather.16
  522.4 19.4 reduce-scatter.16
  637.0 19.1 reduce-scatter.10
  683.3 16.8 reduce-scatter.6
  702.9 27.3 reduce-scatter.14
  733.2 20.6 reduce-scatter.8
  758.7 30.7 reduce-scatter.12

commit v2 on v1

v2 whole, which is shorter than its diff:
```python
import functools

import jax
import jax.numpy as jnp
from jax import lax
from jax.experimental import pallas as pl
from jax.experimental.pallas import tpu as pltpu
from jax.sharding import PartitionSpec as P

D = 768
HD = 64
G = 24
PMAX = 280
L = 2
RP = 288
TOK = 280
HR = 16

EPS_NORM = 1e-06
EPS_LAMB = 1e-06
BETA = 0.5
DECAY = 0.05
BASE_RATE = 0.4
LAYER_DECAY = 0.8
SCALE = 0.125
MASKED = -1e30
HIGH = lax.Precision.HIGHEST
ROOT_HALF = 0.7071067811865476
DENSITY = 0.3989422804014327
BF = jnp.bfloat16
F32 = jnp.float32
ALL = ("dp", "mp", "teach")
VMEM_LIMIT = 56 * 1024 * 1024
FLOP_PER_US = 1_150_000_000
BRIEF = 2
FAR = 3
PARTS = ((3, 1), (2, 0))


def dot_nn(left, right):
    return lax.dot_general(
        left, right, (((1,), (0,)), ((), ())), preferred_element_type=F32
    )


def dot_nt(left, right):
    return lax.dot_general(
        left, right, (((1,), (1,)), ((), ())), preferred_element_type=F32
    )


def dot_tn(left, right):
    return lax.dot_general(
        left, right, (((0,), (0,)), ((), ())), preferred_element_type=F32
    )


def gelu_erf(values):
    return 0.5 * values * (1.0 + lax.erf(values * ROOT_HALF))


def norm_stats(values):
    centre = values - jnp.mean(values, axis=-1, keepdims=True)
    scaled = lax.rsqrt(jnp.mean(centre * centre, axis=-1, keepdims=True) + EPS_NORM)
    return centre * scaled, scaled


def norm_back(grad_out, normed, scaled, gain_row):
    grad_normed = grad_out * gain_row
    inner_sum = jnp.mean(grad_normed, axis=-1, keepdims=True)
    cross_term = jnp.mean(grad_normed * normed, axis=-1, keepdims=True)
    return scaled * (grad_normed - inner_sum - normed * cross_term)


def row_sum(values):
    return jnp.sum(values, axis=0, keepdims=True)


def weight_copies(place_ref, steps, own, other, buf, sems):
    half = own[0].shape[0]
    here = place_ref[0]
    slots, sem = [], 0
    for slot, step in enumerate(steps):
        pieces = (FAR, FAR + 1) if step == FAR else (step,)
        copies = []
        for piece in pieces:
            size = half // len(pieces)
            for source, core in ((own[piece], here), (other[piece], 1 - here)):
                at = pl.multiple_of(core * half + (piece - pieces[0]) * size, 64)
                copies.append(
                    pltpu.make_async_copy(source, buf.at[slot, pl.ds(at, size)], sems.at[sem])
                )
                sem += 1
        slots.append(copies)
    return slots


def start_all(slots):
    for copies in slots:
        for copy in copies:
            copy.start()


def wait_slot(slots, now):
    for slot, copies in enumerate(slots):

        @pl.when(now == slot)
        def _():
            for copy in copies:
                copy.wait()


def split_out(half, place_ref, grad_buf, mine_ref, other_ref, slot):
    mine = pl.multiple_of(place_ref[0] * half, 128)
    theirs = pl.multiple_of((1 - place_ref[0]) * half, 128)
    mine_ref[slot] = grad_buf[pl.ds(mine, half), :]
    other_ref[slot] = grad_buf[pl.ds(theirs, half), :]


def attn_forward_kernel(
    mp,
    ni,
    wl,
    place_ref,
    resid_ref,
    vec_ref,
    bias_ref,
    live_ref,
    own,
    other,
    first_ref,
    qkv_ref,
    att_ref,
    lse_ref,
    mid_ref,
    buf,
    sems,
):
    now = pl.program_id(0)
    slots = weight_copies(place_ref, range(mp), own, other, buf, sems)

    @pl.when(now == 0)
    def _():
        start_all(slots)
        resid = resid_ref[...]
        normed, _ = norm_stats(resid)
        first_ref[...] = (normed * vec_ref[0:1] + vec_ref[1:2]).astype(BF)
        mid_ref[...] = resid + vec_ref[4:5]

    wait_slot(slots, now)
    qkv = dot_nn(first_ref[...], buf[now, :, : 3 * wl]) + bias_ref[0]
    qkv_ref[0] = qkv.astype(BF)
    for image in range(ni):
        rows = slice(image * RP, (image + 1) * RP)
        live = live_ref[image] > 0.0
        for head in range(wl // HD):
            at = head * HD
            queries = qkv_ref[0, rows, at : at + HD]
            keys = qkv_ref[0, rows, wl + at : wl + at + HD]
            vals = qkv_ref[0, rows, 2 * wl + at : 2 * wl + at + HD]
            scores = jnp.where(live, dot_nt(queries, keys) * SCALE, MASKED)
            peak = jnp.max(scores, axis=-1, keepdims=True)
            expo = jnp.exp(scores - peak)
            total = jnp.sum(expo, axis=-1, keepdims=True)
            soft = (expo * (1.0 / total)).astype(BF)
            att_ref[0, rows, at : at + HD] = dot_nn(soft, vals).astype(BF)
            lse_ref[0, rows, head : head + 1] = peak + jnp.log(total)
    mid_ref[...] += dot_nt(att_ref[0], buf[now, :, 3 * wl :])


def mlp_forward_kernel(
    mp,
    chunk,
    place_ref,
    mid_ref,
    vec_ref,
    bias_ref,
    own,
    other,
    second_ref,
    hidden_ref,
    slope_ref,
    out_ref,
    buf,
    sems,
):
    now = pl.program_id(0)
    fl = hidden_ref.shape[2]
    slots = weight_copies(place_ref, range(mp), own, other, buf, sems)

    @pl.when(now == 0)
    def _():
        start_all(slots)
        middle = mid_ref[...]
        normed, _ = norm_stats(middle)
        second_ref[...] = (normed * vec_ref[2:3] + vec_ref[3:4]).astype(BF)
        out_ref[...] = middle + vec_ref[5:6]

    wait_slot(slots, now)
    for start in range(0, mid_ref.shape[0], chunk):
        rows = slice(start, start + chunk)
        upward = dot_nn(second_ref[rows, :], buf[now, :, :fl]) + bias_ref[0]
        share = 0.5 + 0.5 * lax.erf(upward * ROOT_HALF)
        hidden = (upward * share).astype(BF)
        hidden_ref[0, rows, :] = hidden
        slope_ref[0, rows, :] = share + upward * (DENSITY * jnp.exp(-0.5 * upward * upward))
        out_ref[rows, :] += dot_nt(hidden, buf[now, :, fl:])


def head_kernel(
    mp,
    ni,
    wc,
    place_ref,
    resid_ref,
    vec_ref,
    bias_ref,
    ids_ref,
    labels_ref,
    mix_ref,
    scale_ref,
    weight_ref,
    pooled_ref,
    teacher_ref,
    own,
    other,
    mine_ref,
    other_ref,
    hbias_ref,
    grad_ref,
    vgrad_ref,
    loss_ref,
    buf,
    cls_buf,
    dist_buf,
    gw_buf,
    sems,
):
    half = mine_ref.shape[1]
    slots = weight_copies(place_ref, range(mp), own, other, buf, sems)
    start_all(slots)
    cls_buf[...] = jnp.zeros_like(cls_buf)
    dist_buf[...] = jnp.zeros_like(dist_buf)
    for image in range(ni):
        at = image * RP + TOK
        cls_buf[image : image + 1, :] = resid_ref[at : at + 1, :]
        dist_buf[image : image + 1, :] = resid_ref[at + 1 : at + 2, :]
    grad_ref[...] = jnp.zeros_like(grad_ref)
    normed_c, scaled_c = norm_stats(cls_buf[...])
    normed_d, scaled_d = norm_stats(dist_buf[...])
    gain, shift = vec_ref[0:1], vec_ref[1:2]
    final_c = (normed_c * gain + shift).astype(BF)
    final_d = (normed_d * gain + shift).astype(BF)
    for copies in slots:
        for copy in copies:
            copy.wait()
    cls, dist, teach, goal = [], [], [], []
    mix = mix_ref[:, 0:1]
    for block in range(mp):
        ids = ids_ref[block]
        valid = ids >= 0
        both = bias_ref[block]
        cls.append(
            jnp.where(valid, dot_nn(final_c, buf[block, :, :wc]) + both[:, :wc], MASKED)
        )
        dist.append(
            jnp.where(valid, dot_nn(final_d, buf[block, :, wc:]) + both[:, wc:], MASKED)
        )
        teach.append(jnp.where(valid, dot_nn(pooled_ref[...], teacher_ref[block]), MASKED))
        first = (labels_ref[:, 0:1] == ids).astype(F32)
        second = (labels_ref[:, 1:2] == ids).astype(F32)
        goal.append(mix * first + (1.0 - mix) * second)

    def log_total(parts):
        peak = functools.reduce(
            jnp.maximum, [jnp.max(part, axis=-1, keepdims=True) for part in parts]
        )
        total = sum(jnp.sum(jnp.exp(part - peak), axis=-1, keepdims=True) for part in parts)
        return peak + jnp.log(total)

    log_c, log_d, log_t = log_total(cls), log_total(dist), log_total(teach)
    prob = [jnp.exp(part - log_t) for part in teach]
    dot_c = sum(jnp.sum(g * c, axis=-1, keepdims=True) for g, c in zip(goal, cls))
    dot_d = sum(jnp.sum(p * d, axis=-1, keepdims=True) for p, d in zip(prob, dist))
    loss_rows = 0.5 * (log_c - dot_c) + 0.5 * (log_d - dot_d)
    loss_ref[...] = jnp.broadcast_to(row_sum(weight_ref[:, 0:1] * loss_rows), loss_ref.shape)
    scale = scale_ref[:, 0:1]
    gfin_c = jnp.zeros(cls_buf.shape, F32)
    gfin_d = jnp.zeros(dist_buf.shape, F32)
    for block in range(mp):
        grad_c = scale * (jnp.exp(cls[block] - log_c) - goal[block])
        grad_d = scale * (jnp.exp(dist[block] - log_d) - prob[block])
        hbias_ref[block, :, :wc] = row_sum(grad_c)
        hbias_ref[block, :, wc:] = row_sum(grad_d)
        low_c, low_d = grad_c.astype(BF), grad_d.astype(BF)
        gw_buf[:, :wc] = dot_tn(final_c, low_c).astype(BF)
        gw_buf[:, wc:] = dot_tn(final_d, low_d).astype(BF)
        split_out(half, place_ref, gw_buf, mine_ref, other_ref, block)
        gfin_c += dot_nt(low_c, buf[block, :, :wc])
        gfin_d += dot_nt(low_d, buf[block, :, wc:])
    vgrad_ref[...] = jnp.zeros_like(vgrad_ref)
    vgrad_ref[0:1, :] = row_sum(gfin_c * normed_c) + row_sum(gfin_d * normed_d)
    vgrad_ref[1:2, :] = row_sum(gfin_c) + row_sum(gfin_d)
    cls_buf[...] = norm_back(gfin_c, normed_c, scaled_c, gain)
    dist_buf[...] = norm_back(gfin_d, normed_d, scaled_d, gain)
    for image in range(ni):
        at = image * RP + TOK
        grad_ref[at : at + 1, :] = cls_buf[image : image + 1, :]
        grad_ref[at + 1 : at + 2, :] = dist_buf[image : image + 1, :]


def mlp_backward_kernel(
    steps,
    last,
    place_ref,
    grad_ref,
    mid_ref,
    vec_ref,
    second_ref,
    hidden_ref,
    slope_ref,
    own,
    other,
    *rest,
):
    if steps[0] != FAR:
        part_ref, *rest = rest
    (
        gmid_ref,
        mine_ref,
        other_ref,
        gbias_ref,
        vgrad_ref,
        buf,
        branch_buf,
        branch_t,
        second_t,
        gw_buf,
        sems,
    ) = rest
    now = pl.program_id(0)
    fl = hidden_ref.shape[2]
    half = mine_ref.shape[1]
    slots = weight_copies(place_ref, steps, own, other, buf, sems)

    @pl.when(now == 0)
    def _():
        start_all(slots)
        branch_buf[...] = grad_ref[...].astype(BF)
        branch_t[...] = branch_buf[...].T
        second_t[...] = second_ref[...].T
        if steps[0] == FAR:
            gmid_ref[...] = jnp.zeros_like(gmid_ref)
        else:
            gmid_ref[...] = part_ref[...]
        vgrad_ref[...] = jnp.zeros_like(vgrad_ref)

    wait_slot(slots, now)
    gup = (dot_nn(branch_buf[...], buf[now, :, fl:]) * slope_ref[0]).astype(BF)
    gbias_ref[0] = row_sum(gup.astype(F32))
    gmid_ref[...] += dot_nt(gup, buf[now, :, :fl])
    gw_buf[:, :fl] = dot_nn(second_t[...], gup).astype(BF)
    gw_buf[:, fl:] = dot_nn(branch_t[...], hidden_ref[0]).astype(BF)
    split_out(half, place_ref, gw_buf, mine_ref, other_ref, 0)
    if last:

        @pl.when(now == len(steps) - 1)
        def _():
            normed, scaled = norm_stats(mid_ref[...])
            gsec = gmid_ref[...]
            grad = grad_ref[...]
            vgrad_ref[2:3, :] = row_sum(gsec * normed)
            vgrad_ref[3:4, :] = row_sum(gsec)
            vgrad_ref[5:6, :] = row_sum(grad)
            gmid = norm_back(gsec, normed, scaled, vec_ref[2:3]) + grad
            vgrad_ref[4:5, :] = row_sum(gmid)
            gmid_ref[...] = gmid


def attn_backward_kernel(
    ni,
    wl,
    steps,
    last,
    place_ref,
    gmid_ref,
    resid_ref,
    vec_ref,
    live_ref,
    first_ref,
    qkv_ref,
    att_ref,
    lse_ref,
    own,
    other,
    *rest,
):
    if steps[0] != FAR:
        part_ref, *rest = rest
    (
        gres_ref,
        mine_ref,
        other_ref,
        gbias_ref,
        vgrad_ref,
        buf,
        mixed_buf,
        mixed_t,
        first_t,
        gatt_buf,
        gqkv_buf,
        gw_buf,
        sems,
    ) = rest
    now = pl.program_id(0)
    half = mine_ref.shape[1]
    slots = weight_copies(place_ref, steps, own, other, buf, sems)

    @pl.when(now == 0)
    def _():
        start_all(slots)
        mixed_buf[...] = gmid_ref[...].astype(BF)
        mixed_t[...] = mixed_buf[...].T
        first_t[...] = first_ref[...].T
        if steps[0] == FAR:
            gres_ref[...] = jnp.zeros_like(gres_ref)
        else:
            gres_ref[...] = part_ref[...]
        vgrad_ref[...] = jnp.zeros_like(vgrad_ref)

    wait_slot(slots, now)
    gatt_buf[...] = dot_nn(mixed_buf[...], buf[now, :, 3 * wl :]).astype(BF)
    for image in range(ni):
        rows = slice(image * RP, (image + 1) * RP)
        live = live_ref[image] > 0.0
        for head in range(wl // HD):
            at = head * HD
            queries = qkv_ref[0, rows, at : at + HD]
            keys = qkv_ref[0, rows, wl + at : wl + at + HD]
            vals = qkv_ref[0, rows, 2 * wl + at : 2 * wl + at + HD]
            gatt = gatt_buf[rows, at : at + HD]
            scores = jnp.where(live, dot_nt(queries, keys) * SCALE, MASKED)
            soft = jnp.exp(scores - lse_ref[0, rows, head : head + 1])
            gsoft = dot_nt(gatt, vals)
            inner = jnp.sum(soft * gsoft, axis=-1, keepdims=True)
            gscore = (soft * (gsoft - inner)).astype(BF)
            gqkv_buf[rows, at : at + HD] = (dot_nn(gscore, keys) * SCALE).astype(BF)
            gqkv_buf[rows, wl + at : wl + at + HD] = (dot_tn(gscore, queries) * SCALE).astype(BF)
            gqkv_buf[rows, 2 * wl + at : 2 * wl + at + HD] = dot_tn(soft.astype(BF), gatt).astype(BF)
    gqkv = gqkv_buf[...]
    gbias_ref[0] = row_sum(gqkv.astype(F32))
    gres_ref[...] += dot_nt(gqkv, buf[now, :, : 3 * wl])
    gw_buf[:, : 3 * wl] = dot_nn(first_t[...], gqkv).astype(BF)
    gw_buf[:, 3 * wl :] = dot_nn(mixed_t[...], att_ref[0]).astype(BF)
    split_out(half, place_ref, gw_buf, mine_ref, other_ref, 0)
    if last:

        @pl.when(now == len(steps) - 1)
        def _():
            normed, scaled = norm_stats(resid_ref[...])
            gfirst = gres_ref[...]
            vgrad_ref[0:1, :] = row_sum(gfirst * normed)
            vgrad_ref[1:2, :] = row_sum(gfirst)
            gres_ref[...] = norm_back(gfirst, normed, scaled, vec_ref[0:1]) + gmid_ref[...]


def call(kernel, outs, scratch, ins, steps=None, after=()):
    def whole(array):
        return pl.BlockSpec(array.shape, lambda i: (0,) * array.ndim)

    def each(array, base=0, stride=1):
        return pl.BlockSpec(
            (1, *array.shape[1:]), lambda i: (base + stride * i, *(0,) * (array.ndim - 1))
        )

    specs, arrays, sizes = [], [], []
    for item in [*ins, ("group", list(after))]:
        kind, item = item if isinstance(item, tuple) else ("vmem", item)
        group = item if kind == "group" else [item]
        sizes.append(len(group) if kind == "group" else None)
        if kind in ("group", "smem"):
            space = pl.ANY if kind == "group" else pltpu.SMEM
            specs += [pl.BlockSpec(memory_space=space)] * len(group)
        elif kind == "each":
            specs.append(each(item, steps[0], steps[1] - steps[0]))
        elif steps:
            specs.append(whole(item))
        else:
            specs.append(pl.BlockSpec(memory_space=pltpu.VMEM))
        arrays += group

    def grouped(*refs):
        given, at = [], 0
        for size in sizes:
            given.append(refs[at] if size is None else refs[at : at + size])
            at += 1 if size is None else size
        return kernel(*given[:-1], *refs[at:])

    out_shape = [jax.ShapeDtypeStruct(*out[:2]) for out in outs]
    if steps:
        out_specs = [
            each(shape) if len(out) > 2 else whole(shape) for out, shape in zip(outs, out_shape)
        ]
        grid = {"grid": (len(steps),)}
    else:
        out_specs = [pl.BlockSpec(memory_space=pltpu.VMEM)] * len(out_shape)
        grid = {}
    moved = sum(a.size * a.dtype.itemsize for a in arrays)
    moved += sum(s.size * s.dtype.itemsize for s in out_shape)
    return pl.pallas_call(
        grouped,
        out_shape=out_shape,
        in_specs=specs,
        out_specs=out_specs,
        **grid,
        scratch_shapes=scratch,
        compiler_params=pltpu.CompilerParams(vmem_limit_bytes=VMEM_LIMIT),
        cost_estimate=pl.CostEstimate(
            flops=BRIEF * FLOP_PER_US, bytes_accessed=moved, transcendentals=0
        ),
    )(*arrays)


def tie(values, *behind):
    if not behind:
        return values
    return lax.optimization_barrier((values, behind))[0]


def swap(values, axis, distance):
    size = lax.axis_size(axis)
    return lax.ppermute(values, axis, [(rank, rank ^ distance) for rank in range(size)])


class Gather:
    def __init__(self, near):
        self.near = near

    def square(self, *behind):
        near = tie(self.near, *behind)
        self.own = [near, swap(near, "mp", 1), swap(near, "mp", 2)]
        self.other = [swap(near, "teach", 1)]

    def corner(self, *behind):
        near, by_one, by_two = self.own
        cut = near.shape[0] // 2
        by_one, by_two = tie((by_one, by_two), *behind)
        self.own = [near, by_one, by_two, swap(by_two[:cut], "mp", 1), swap(by_one[cut:], "mp", 2)]
        self.other += [swap(by_one, "teach", 1), swap(by_two, "teach", 1)]

    def cores(self, *behind):
        far = tie(tuple(self.own[3:]), *behind)
        self.own[3:] = far
        self.other += [swap(piece, "teach", 1) for piece in far]

    def refs(self):
        return [("group", self.own), ("group", self.other)]


def add_low(left, right):
    return (left.astype(F32) + right.astype(F32)).astype(BF)


def sum_over(values, axis):
    distance = 1
    while distance < lax.axis_size(axis):
        values = values + swap(values, axis, distance)
        distance *= 2
    return values


def sum_all(values):
    for axis in ("teach", "mp", "dp"):
        values = sum_over(values, axis)
    return values


def gather_mp(values):
    size = lax.axis_size("mp")
    return jnp.stack([values] + [swap(values, "mp", step) for step in range(1, size)])


class Scatter:
    def __init__(self):
        self.waiting = []
        self.block = {}
        self.total = None

    def cores(self, steps, mine, other):
        self.waiting.append((steps, mine, swap(other, "teach", 1)))

    def added(self, *behind):
        for steps, mine, got in self.waiting:
            got = tie(got, *behind)
            for slot, step in enumerate(steps):
                self.block[step] = add_low(mine[slot], got[slot])
        self.waiting = []

    def corner(self, *behind):
        self.added(*behind)
        cut = self.block[FAR].shape[0] // 2
        sent = [self.block[FAR][:cut], self.block[FAR][cut:]]
        self.by_one = swap(sent[0], "mp", 1)
        self.by_two = swap(sent[1], "mp", 2)
        return sent

    def square(self, *behind):
        self.added(*behind)
        one, two = self.block[1], self.block[2]
        cut = one.shape[0] // 2
        by_one, by_two = tie((self.by_one, self.by_two), *behind)
        sent = [
            jnp.concatenate([one[:cut], add_low(one[cut:], by_two)]),
            jnp.concatenate([add_low(two[:cut], by_one), two[cut:]]),
        ]
        self.by_one = swap(sent[0], "mp", 1)
        self.by_two = swap(sent[1], "mp", 2)
        return sent

    def rows(self, *behind):
        by_one, by_two = tie((self.by_one, self.by_two), *behind)
        total = self.block[0].astype(F32) + (by_one.astype(F32) + by_two.astype(F32))
        total = total.astype(BF)
        self.total = lax.psum_scatter(total, "dp", scatter_dimension=0, tiled=True)
        return [total]

    def result(self):
        return self.total.astype(F32)


def adam_direction(gradient, first_moment, second_moment, correct_first, correct_second):
    new_first = BETA * first_moment + (1.0 - BETA) * gradient
    new_second = BETA * second_moment + (1.0 - BETA) * gradient * gradient
    return (
        new_first,
        new_second,
        new_first / correct_first / (jnp.sqrt(new_second / correct_second) + EPS_LAMB),
    )


def split_params(values):
    layered = values[1 : 1 + 6 * L].reshape(L, 6)
    return (
        values[0],
        layered[:, :4],
        layered[:, 4:],
        values[1 + 6 * L : 3 + 6 * L],
        values[3 + 6 * L],
        values[4 + 6 * L],
    )


def expand_params(pieces):
    return (
        pieces[0],
        pieces[1][:, :, None, None],
        pieces[2][:, :, None, None],
        pieces[3][:, None, None],
        pieces[4],
        pieces[5],
    )


def order_params(pieces):
    layered = jnp.concatenate([pieces[1], pieces[2]], axis=1).reshape(-1)
    return jnp.concatenate([pieces[0][None], layered, pieces[3], pieces[4][None], pieces[5][None]])


def squares_of(pieces, mp_first, data_first):
    return order_params(
        (
            jnp.sum(pieces[0] * pieces[0]) * mp_first,
            jnp.sum(pieces[1] * pieces[1], axis=(2, 3)),
            jnp.sum(pieces[2] * pieces[2], axis=(2, 3)),
            jnp.sum(pieces[3] * pieces[3], axis=(1, 2)),
            jnp.sum(pieces[4] * pieces[4]) * mp_first * data_first,
            jnp.sum(pieces[5] * pieces[5]) * data_first,
        )
    )


def per_device(
    patches,
    grid_sizes,
    label_ids,
    label_mix,
    image_weight,
    teacher_stem,
    teacher_head,
    patch_weight,
    attn_weight,
    mlp_weight,
    head_weight,
    vector_params,
    split_biases,
    patch_first,
    attn_first,
    mlp_first,
    head_first,
    vector_first,
    bias_first,
    patch_second,
    attn_second,
    mlp_second,
    head_second,
    vector_second,
    bias_second,
    decay_mask,
    layer_ids,
    step_count,
):
    dp, mp, teach = lax.axis_size("dp"), lax.axis_size("mp"), lax.axis_size("teach")
    here_mp = lax.axis_index("mp")
    here_teach = lax.axis_index("teach")
    place = ("smem", here_teach.astype(jnp.int32).reshape(1))
    mp_first = (here_mp == 0).astype(F32)
    data_first = (lax.axis_index(("dp", "teach")) == 0).astype(F32)
    rows_own = patch_weight.shape[0]
    half = dp * rows_own
    wl = attn_weight.shape[3]
    fl = mlp_weight.shape[3]
    cl = head_weight.shape[2]
    wc = -(-cl // 128) * 128
    head_row = 6 * L

    def inward(values):
        lead = values.shape[:-1]
        cut = values.reshape(*lead, dp, teach, rows_own)
        return jnp.swapaxes(cut, -3, -2).reshape(*lead, D)

    def outward(values):
        lead = values.shape[:-1]
        cut = values.reshape(*lead, teach, dp, rows_own)
        return jnp.swapaxes(cut, -3, -2).reshape(*lead, D)

    ni = patches.shape[0] // mp

    def take(array):
        return lax.dynamic_slice_in_dim(array, here_mp * ni, ni, 0)

    patches, grid_sizes, label_ids = take(patches), take(grid_sizes), take(label_ids)
    label_mix, image_weight = take(label_mix), take(image_weight)
    weight_sum = sum_all(jnp.sum(image_weight).reshape(1))[0]

    patch_low = inward(patch_weight).astype(BF)
    attn_low = [
        jnp.concatenate([attn_weight[layer, part] for part in range(4)], axis=1).astype(BF)
        for layer in range(L)
    ]
    mlp_low = [
        jnp.concatenate([mlp_weight[layer, 0], mlp_weight[layer, 1]], axis=1).astype(BF)
        for layer in range(L)
    ]
    head_pad = jnp.pad(head_weight, ((0, 0), (0, 0), (0, wc - cl)))
    head_low = jnp.concatenate([head_pad[0], head_pad[1]], axis=1).astype(BF)

    def gather_dp(*pieces):
        wide_piece = lax.all_gather(jnp.concatenate(pieces, axis=1), "dp", axis=0, tiled=True)
        cuts, at = [], 0
        for piece in pieces:
            cuts.append(wide_piece[:, at : at + piece.shape[1]])
            at += piece.shape[1]
        return cuts

    near = gather_dp(patch_low, attn_low[0]) + gather_dp(mlp_low[0])
    rest = [piece for layer in range(1, L) for piece in (attn_low[layer], mlp_low[layer])]
    near += gather_dp(*rest, head_low)
    teacher_all = gather_mp(jnp.pad(teacher_head, ((0, 0), (0, wc - cl))))
    bias_all = gather_mp(split_biases)
    near[0], near[1] = tie((near[0], near[1]), weight_sum, teacher_all, bias_all)
    patch_own = near[0]
    patch_other = swap(patch_own, "teach", 1)
    units = [Gather(piece) for piece in near[1:]]
    attn_units, mlp_units, head_unit = units[0:-1:2], units[1:-1:2], units[-1]

    vec_in = inward(vector_params)
    layer_vecs = [
        jnp.pad(vec_in[6 * layer : 6 * layer + 6], ((0, 2), (0, 0))) for layer in range(L)
    ]
    final_vec = jnp.pad(vec_in[head_row : head_row + 2], ((0, 6), (0, 0)))
    attn_bias, up_bias = [], []
    span = 2 * wl + fl
    for layer in range(L):
        part = bias_all[:, layer * span : (layer + 1) * span]
        zero = jnp.zeros((mp, wl), F32)
        attn_bias.append(
            jnp.concatenate([part[:, :wl], zero, part[:, wl : 2 * wl]], axis=1)[:, None]
        )
        up_bias.append(part[:, None, 2 * wl :])
    pad_class = ((0, 0), (0, wc - cl))
    head_bias = jnp.concatenate(
        [
            jnp.pad(bias_all[:, L * span : L * span + cl], pad_class),
            jnp.pad(bias_all[:, L * span + cl : L * span + 2 * cl], pad_class),
        ],
        axis=1,
    )[:, None]

    grid_rows, grid_cols = grid_sizes[:, 0:1], grid_sizes[:, 1:2]
    slot_ids = jnp.arange(PMAX, dtype=jnp.int32)[None, :]
    patch_live = slot_ids < grid_rows * grid_cols
    live_float = patch_live.astype(F32)
    live_rows = jnp.concatenate(
        [live_float, jnp.ones((ni, 2), F32), jnp.zeros((ni, RP - PMAX - 2), F32)], axis=1
    )[:, None, :]
    table = jnp.arange(G, dtype=jnp.int32)
    source_patch = jnp.concatenate(
        [
            jnp.ones((ni, PMAX, 1), F32),
            jnp.zeros((ni, PMAX, 2), F32),
            ((slot_ids // grid_cols)[..., None] == table).astype(F32),
            ((slot_ids % grid_cols)[..., None] == table).astype(F32),
        ],
        axis=2,
    )
    source_token = jnp.broadcast_to(jnp.eye(2, 3 + 2 * G, 1, dtype=F32), (ni, 2, 3 + 2 * G))
    sources = jnp.concatenate(
        [source_patch, source_token, jnp.zeros((ni, RP - PMAX - 2, 3 + 2 * G), F32)], axis=1
    ).reshape(ni * RP, 3 + 2 * G)

    stem_rows = gelu_erf(dot_nn(patches.reshape(ni * PMAX, -1), teacher_stem)).reshape(ni, PMAX, -1)
    pooled = (
        jnp.sum(stem_rows * live_float[..., None], axis=1)
        / jnp.sum(live_float, axis=1, keepdims=True)
    ).astype(BF)

    first_core = here_teach == 0
    patch_full = jnp.stack(
        [
            jnp.where(first_core, patch_own, patch_other).reshape(dp, rows_own, D),
            jnp.where(first_core, patch_other, patch_own).reshape(dp, rows_own, D),
        ],
        axis=1,
    ).reshape(D, D)
    patch_rows = jnp.pad(patches, ((0, 0), (0, RP - PMAX), (0, 0))).reshape(ni * RP, -1)
    residual = dot_nn(patch_rows, patch_full) + jnp.dot(
        sources, vec_in[head_row + 2 :], precision=HIGH
    )

    n = ni * RP
    parts = 2 * mp + 2
    saved = []
    def wide(values):
        return jnp.pad(values.reshape(ni, -1), ((0, HR - ni), (0, 0)))

    ranks = here_mp ^ jnp.arange(mp, dtype=jnp.int32)
    lanes = jnp.arange(wc, dtype=jnp.int32)
    class_ids = jnp.where(lanes[None] < cl, ranks[:, None] * cl + lanes[None], -1)[:, None]
    head_small = [
        class_ids,
        wide(label_ids),
        wide(label_mix),
        wide(0.5 * image_weight / weight_sum),
        wide(image_weight / weight_sum),
        wide(pooled),
    ]

    first_unit = units[0]
    first_unit.square()
    first_unit.corner(residual)
    units[1].square(*first_unit.own[3:])

    def arrive(at, done):
        here = units[at]
        ahead = units[at + 1 : at + 2] if at < len(units) - 3 else units[at + 1 :]
        if at == 0:
            here.cores()
            return [units[1].own[0], near[-1], *head_small, head_bias, *attn_bias, *up_bias]
        if at < len(units) - 2:
            here.corner(done)
            for unit in ahead:
                unit.square(*here.own[3:], done)
            here.cores(*[unit.own[0] for unit in ahead])
            return [unit.own[0] for unit in ahead]
        if at == len(units) - 2:
            here.corner(done)
            units[-1].corner(done)
            here.cores()
            units[-1].cores()
        return []

    for layer in range(L):
        sending = arrive(2 * layer, residual)
        first, qkv, attended, lse, middle = call(
            functools.partial(attn_forward_kernel, mp, ni, wl),
            [
                ((n, D), BF),
                ((mp, n, 3 * wl), BF, "each"),
                ((mp, n, wl), BF, "each"),
                ((mp, n, wl // HD), F32, "each"),
                ((n, D), F32),
            ],
            [pltpu.VMEM((mp, D, 4 * wl), BF), pltpu.SemaphoreType.DMA((parts,))],
            [place, residual, layer_vecs[layer], ("each", attn_bias[layer]), live_rows]
            + attn_units[layer].refs(),
            range(mp),
            sending,
        )
        sending = arrive(2 * layer + 1, middle)
        second, hidden, slope, output = call(
            functools.partial(mlp_forward_kernel, mp, n // 4),
            [((n, D), BF), ((mp, n, fl), BF, "each"), ((mp, n, fl), F32, "each"), ((n, D), F32)],
            [pltpu.VMEM((mp, D, 2 * fl), BF), pltpu.SemaphoreType.DMA((parts,))],
            [place, middle, layer_vecs[layer], ("each", up_bias[layer])]
            + mlp_units[layer].refs(),
            range(mp),
            sending,
        )
        saved.append((residual, first, qkv, attended, lse, middle, second, hidden, slope))
        residual = output

    head_mine, head_other, head_bgrad, grad, final_vgrad, loss_part = call(
        functools.partial(head_kernel, mp, ni, wc),
        [
            ((mp, half, 2 * wc), BF),
            ((mp, half, 2 * wc), BF),
            ((mp, 1, 2 * wc), F32),
            ((n, D), F32),
            ((8, D), F32),
            ((8, 128), F32),
        ],
        [
            pltpu.VMEM((mp, D, 2 * wc), BF),
            pltpu.VMEM((HR, D), F32),
            pltpu.VMEM((HR, D), F32),
            pltpu.VMEM((D, 2 * wc), BF),
            pltpu.SemaphoreType.DMA((parts,)),
        ],
        [
            place,
            residual,
            final_vec,
            head_bias,
            *head_small,
            teacher_all,
            *head_unit.refs(),
        ],
    )
    head_out = Scatter()
    head_out.cores(range(mp), head_mine, head_other)
    mlp_out, attn_out = [Scatter() for _ in range(L)], [Scatter() for _ in range(L)]
    agenda = {0: [], 1: [(head_out, "corner")], 2: [(head_out, "square")], 3: [(head_out, "rows")]}
    slot = 0
    for layer in reversed(range(L)):
        for at, unit in ((slot + 1, mlp_out[layer]), (slot + 3, attn_out[layer])):
            wait = 2 if unit is mlp_out[layer] else 1
            for moment, what in ((at + 1, "corner"), (at + 2, "square"), (at + 2 + wait, "rows")):
                agenda.setdefault(moment, []).append((unit, what))
        slot += 4
    final = slot

    def proceed(moment, done):
        sent = []
        for unit, what in agenda.pop(moment, []):
            sent += getattr(unit, what)(done)
        return sent

    sending = [head_other]
    gain_list, bias_list = [None] * L, [None] * L
    slot = 0
    for layer in reversed(range(L)):
        resid_in, first, qkv, attended, lse, middle, second, hidden, slope = saved[layer]
        part = []
        up_bgrad, qkv_bgrad = {}, {}
        for steps in PARTS:
            count = len(steps)
            gmid, mine, other, bgrad, mlp_vgrad = call(
                functools.partial(mlp_backward_kernel, steps, steps is PARTS[-1]),
                [
                    ((n, D), F32),
                    ((count, half, 2 * fl), BF, "each"),
                    ((count, half, 2 * fl), BF, "each"),
                    ((count, 1, fl), F32, "each"),
                    ((8, D), F32),
                ],
                [
                    pltpu.VMEM((count, D, 2 * fl), BF),
                    pltpu.VMEM((n, D), BF),
                    pltpu.VMEM((D, n), BF),
                    pltpu.VMEM((D, n), BF),
                    pltpu.VMEM((D, 2 * fl), BF),
                    pltpu.SemaphoreType.DMA((2 * count + 2,)),
                ],
                [place, grad, middle, layer_vecs[layer], second, ("each", hidden), ("each", slope)]
                + mlp_units[layer].refs()
                + part,
                steps,
                sending,
            )
            part = [gmid]
            up_bgrad.update({step: bgrad[at, 0] for at, step in enumerate(steps)})
            slot += 1
            mlp_out[layer].cores(steps, mine, other)
            sending = [other] + proceed(slot, gmid)
        part = []
        for steps in PARTS:
            count = len(steps)
            grad, mine, other, bgrad, attn_vgrad = call(
                functools.partial(attn_backward_kernel, ni, wl, steps, steps is PARTS[-1]),
                [
                    ((n, D), F32),
                    ((count, half, 4 * wl), BF, "each"),
                    ((count, half, 4 * wl), BF, "each"),
                    ((count, 1, 3 * wl), F32, "each"),
                    ((8, D), F32),
                ],
                [
                    pltpu.VMEM((count, D, 4 * wl), BF),
                    pltpu.VMEM((n, D), BF),
                    pltpu.VMEM((D, n), BF),
                    pltpu.VMEM((D, n), BF),
                    pltpu.VMEM((n, wl), BF),
                    pltpu.VMEM((n, 3 * wl), BF),
                    pltpu.VMEM((D, 4 * wl), BF),
                    pltpu.SemaphoreType.DMA((2 * count + 2,)),
                ],
                [place, gmid, resid_in, layer_vecs[layer], live_rows, first]
                + [("each", qkv), ("each", attended), ("each", lse)]
                + attn_units[layer].refs()
                + part,
                steps,
                sending,
            )
            part = [grad]
            qkv_bgrad.update({step: bgrad[at, 0] for at, step in enumerate(steps)})
            slot += 1
            attn_out[layer].cores(steps, mine, other)
            sending = [other] + proceed(slot, grad)
        gain_list[layer] = (attn_vgrad + mlp_vgrad)[:6]
        bias_list[layer] = jnp.stack(
            [
                jnp.concatenate(
                    [qkv_bgrad[step][:wl], qkv_bgrad[step][2 * wl :], up_bgrad[step]]
                )
                for step in range(mp)
            ]
        )
    for moment in sorted(agenda):
        proceed(moment, grad)

    patch_grad = dot_tn(patch_rows, grad.astype(BF)).astype(BF)
    patch_grad = patch_grad.reshape(dp, teach, rows_own, D)
    patch_mine = lax.dynamic_index_in_dim(patch_grad, here_teach, 1, False)
    patch_sent = lax.dynamic_index_in_dim(patch_grad, 1 - here_teach, 1, False)
    patch_grad = add_low(patch_mine, swap(patch_sent, "teach", 1)).reshape(dp * rows_own, D)
    patch_grad = lax.psum_scatter(patch_grad, "dp", scatter_dimension=0, tiled=True)
    patch_grad = outward(sum_over(patch_grad.astype(F32), "mp"))

    source_grads = lax.dot_general(
        sources, grad, (((0,), (0,)), ((), ())), precision=HIGH, preferred_element_type=F32
    )
    vector_grads = outward(
        jnp.concatenate(gain_list + [final_vgrad[:2], source_grads], axis=0)
    )
    bias_blocks = jnp.concatenate(
        bias_list + [head_bgrad[:, 0, :cl], head_bgrad[:, 0, wc : wc + cl]], axis=1
    )[ranks]
    bias_size = bias_blocks.shape[1]
    flat = jnp.concatenate([vector_grads.reshape(-1), bias_blocks.reshape(-1)])
    flat = jnp.pad(flat, (0, -flat.size % 1024)).reshape(-1, 128)
    flat = sum_all(flat).reshape(-1)
    vector_grads = flat[: vector_params.size].reshape(vector_params.shape)
    bias_grads = lax.dynamic_slice_in_dim(
        flat, vector_params.size + here_mp * bias_size, bias_size, 0
    )

    attn_list = [unit.result() for unit in attn_out]
    mlp_list = [unit.result() for unit in mlp_out]
    head_grads = head_out.result()
    attn_grads = jnp.stack(
        [
            jnp.stack([attn_list[layer][:, part * wl : (part + 1) * wl] for part in range(4)])
            for layer in range(L)
        ]
    )
    mlp_grads = jnp.stack(
        [jnp.stack([mlp_list[layer][:, :fl], mlp_list[layer][:, fl:]]) for layer in range(L)]
    )
    head_grads = jnp.stack([head_grads[:, :cl], head_grads[:, wc : wc + cl]])

    step_power = step_count[0].astype(F32)
    correct_first = 1.0 - jnp.power(BETA, step_power)
    correct_second = 1.0 - jnp.power(BETA, step_power)
    weights = (patch_weight, attn_weight, mlp_weight, head_weight, vector_params, split_biases)
    gradients = (patch_grad, attn_grads, mlp_grads, head_grads, vector_grads, bias_grads)
    firsts = (patch_first, attn_first, mlp_first, head_first, vector_first, bias_first)
    seconds = (patch_second, attn_second, mlp_second, head_second, vector_second, bias_second)
    decay_pieces = expand_params(split_params(decay_mask.astype(F32)))
    results = [
        adam_direction(gradients[slot], firsts[slot], seconds[slot], correct_first, correct_second)
        for slot in range(6)
    ]
    directions = [
        results[slot][2] + DECAY * decay_pieces[slot] * weights[slot] for slot in range(6)
    ]
    totals = sum_all(
        jnp.concatenate(
            [
                squares_of(weights, mp_first, data_first),
                squares_of(directions, mp_first, data_first),
                loss_part[0, :1],
            ]
        )
    )
    npar = (totals.size - 1) // 2
    weights_sq, direction_sq, loss_value = totals[:npar], totals[npar : 2 * npar], totals[2 * npar]
    weight_norm = jnp.sqrt(weights_sq)
    update_norm = jnp.sqrt(direction_sq)
    trust_ratio = weight_norm / update_norm
    rates = BASE_RATE * jnp.power(LAYER_DECAY, 2.0 - layer_ids.astype(F32)) * trust_ratio
    rate_pieces = expand_params(split_params(rates))
    updated = [weights[slot] - rate_pieces[slot] * directions[slot] for slot in range(6)]
    norm_table = jnp.stack([weight_norm, update_norm])
    return (
        *updated,
        *[results[slot][0] for slot in range(6)],
        *[results[slot][1] for slot in range(6)],
        norm_table,
        trust_ratio,
        loss_value,
    )


def solution(mesh):
    rows = ("dp", "teach")
    moments = (
        P(rows, None),
        P(None, None, rows, "mp"),
        P(None, None, rows, "mp"),
        P(None, rows, "mp"),
        P(),
        P("mp"),
    )
    placed = (
        P(rows, None, None),
        P(rows, None),
        P(rows, None),
        P(rows),
        P(rows),
        P(),
        P(None, "mp"),
        *moments,
        *moments,
        *moments,
        P(),
        P(),
        P(),
    )
    return jax.shard_map(
        per_device,
        mesh=mesh,
        in_specs=placed,
        out_specs=(*moments, *moments, *moments, P(), P(), P()),
        check_vma=False,
    )
```

time: 854 us -> 662 us (0.78)
  waiting for transfers between devices: 391 us -> 151 us
  local copies, waits for them, and re-layouts: 56.2 us -> 80.9 us
  starting transfers between devices: 58 us -> 77.6 us
    all_gather x6 -> x3, waiting for transfers between devices: 250 us -> 13.3 us  [gather_dp(): lax.all_gather(jnp.concatenate(pieces, axis=1), 'dp', axis=0, tiled=True)]
    ppermute x54 -> x99, starting transfers between devices: 57.3 us -> 77 us  [swap(): lax.ppermute(values, axis, [(rank, rank ^ distance) for rank in range(siz...]
    unnamed x175 -> x287, local copies, waits for them, and re-layouts: 5.41 us -> 19.1 us
    slice x20 -> x38, local copies, waits for them, and re-layouts: 1.16 us -> 13.2 us  [the longest x4 4.4 us: gather_dp(): cuts.append(wide_piece[:, at:at + piece.shape[1]])]
    reduce_scatter x6, waiting for transfers between devices: 11.9 us -> 0.05 us  [the longest x5 0.05 us: rows(): self.total = lax.psum_scatter(total, 'dp', scatter_dimension=0, tiled=True)]
    ppermute x54 -> x99, waiting for transfers between devices: 128 us -> 137 us  [swap(): lax.ppermute(values, axis, [(rank, rank ^ distance) for rank in range(siz...]
    convert_element_type x18 -> x20, other arithmetic: 15.3 us -> 20.7 us  [add_low(): return (left.astype(F32) + right.astype(F32)).astype(BF)]
    pallas_call x9 -> x13, Pallas kernels: 213 us -> 215 us  [call(): pl.pallas_call(grouped, out_shape=out_shape, in_specs=specs, out_specs=ou...]
  transfers between devices with their start and end apart: 66 -> 108, of which waited for: 31 -> 35; matrix products, arithmetic and copies ran while one was open for 15% -> 21% of each run, Pallas kernels for 24% -> 32%
where the time goes in v2:
time: 662 us; the launch traced here: 652 us
  Pallas kernels  215 us (32%)
  waiting for transfers between devices  151 us (23%)
  other arithmetic  94.2 us (14%)
  local copies, waits for them, and re-layouts  80.9 us (12%)
  starting transfers between devices  77.6 us (12%)
  between operations  27.2 us (4%)
    pallas_call x13, Pallas kernels, call(): pl.pallas_call(grouped, out_shape=out_shape, in_specs=specs, out_specs=ou...  215 us
    ppermute x99, waiting for transfers between devices, swap(): lax.ppermute(values, axis, [(rank, rank ^ distance) for rank in range(siz...  137 us
    ppermute x99, starting transfers between devices, swap(): lax.ppermute(values, axis, [(rank, rank ^ distance) for rank in range(siz...  77 us
    convert_element_type x20, other arithmetic, add_low(): return (left.astype(F32) + right.astype(F32)).astype(BF)  20.7 us
    unnamed x287, local copies, waits for them, and re-layouts  19.1 us
    convert_element_type x5, other arithmetic, rows(): total = total.astype(BF)  15.2 us
    all_gather x3, waiting for transfers between devices, gather_dp(): lax.all_gather(jnp.concatenate(pieces, axis=1), 'dp', axis=0, tiled=True)  13.3 us
  transfers between devices with their start and end apart: 108, of which 35 were waited for; matrix products, arithmetic and copies ran while one was open for 21% of the time, Pallas kernels for 32%

profile of v2, /device:TPU:0, one launch (start us, length us, event | category | flops | bytes accessed | tf_op | source)
XLA Modules:
  0.0 652.2 jit_solution(1772998960093400151)
XLA Ops:
  7.3 2.5 multiply_reduce_fusion.6
  21.6 3.0 collective-permute-start.9
  49.6 2.8 collective-permute-start.1
  55.3 2.1 collective-permute-done.2
  58.1 2.9 collective-permute-start.3
  62.3 3.9 collective-permute-start.4
  72.6 2.4 collective-permute-done.7
  85.5 2.8 convolution_add_fusion.refs_1_.refs_2_
  88.4 10.1 %collective-permute-done.13.refs_7_.refs_11_ = bf16[384,768]{1,0:T(8,128)(2,1)S(1)} collective-permute-done((bf16[384,768]{1,0:T(8,128)(2,1)S(1)}, bf16[384,768]{1,0:T(8,128)(2,1)S(1)}, u32[]{:S(2)}, u32[]{:S(2)}) %collective-permute-start.13) | collective-permute-done | bytes 589856 | tf_op jit(solution)/shard_map/ppermute | solution.py:532
  104.1 4.0 collective-permute-done.14.refs_8_.refs_12_
  119.0 13.3 %all-gather.8.cloned.1.call-done = bf16[384,2816]{1,0:T(8,128)(2,1)} async-done(((bf16[96,2816]{1,0:T(8,128)(2,1)}), bf16[384,2816]{1,0:T(8,128)(2,1)}) %all-gather.8.cloned.1.call-update) | async-done | bytes 2162704 | tf_op jit(solution)/shard_map/all_gather | solution.py:758
  134.8 20.3 %shard_map.427 = (bf16[576,768]{1,0:T(8,128)(2,1)}, bf16[4,576,576]{2,1,0:T(8,128)(2,1)}, bf16[4,576,192]{2,1,0:T(8,128)(2,1)}, f32[4,576,3]{2,1,0:T(8,128)}, f32[576,768]{1,0:T(8,128)}) custom-call(s32[1]{0:T(128)} %bitcast.4.refs_0_, f32[576,768]{1,0:T(8,128)} %convolution_add_fusion.refs_1_.refs_2_, f32[8,768]{1,0:T(8,128)} %pad.54.refs_2_.refs_3_, ...), custom_call_target="tpu_custom_call" | custom-call | flops 2300000000 | bytes 14380612 | tf_op jit(solution)/shard_map/pallas_call | solution.py:510
  160.0 10.4 %collective-permute-done.23.refs_7_.refs_10_ = bf16[192,1536]{1,0:T(8,128)(2,1)S(1)} collective-permute-done((bf16[192,1536]{1,0:T(8,128)(2,1)S(1)}, bf16[192,1536]{1,0:T(8,128)(2,1)S(1)}, u32[]{:S(2)}, u32[]{:S(2)}) %collective-permute-start.23) | collective-permute-done | bytes 589856 | tf_op jit(solution)/shard_map/ppermute | solution.py:532
  177.4 15.0 %shard_map.428 = (bf16[576,768]{1,0:T(8,128)(2,1)}, bf16[4,576,768]{2,1,0:T(8,128)(2,1)}, f32[4,576,768]{2,1,0:T(8,128)}, f32[576,768]{1,0:T(8,128)}) custom-call(s32[1]{0:T(128)} %bitcast.4.refs_0_, f32[576,768]{1,0:T(8,128)} %get-tuple-element.135.refs_1_.refs_2_, f32[8,768]{1,0:T(8,128)} %pad.54.refs_2_.refs_3_, f32[4,1,768]{2,1,0:T(1,128)} %copy.91.refs_26_.refs_3_, ...), custom_call_target="tpu_custom_call" | custom-call | flops 2300000000 | bytes 25104388 | tf_op jit(solution)/shard_map/pallas_call | solution.py:510
  195.3 6.3 collective-permute-done.32.refs_8_.refs_12_
  212.3 20.6 %shard_map.429 = (bf16[576,768]{1,0:T(8,128)(2,1)}, bf16[4,576,576]{2,1,0:T(8,128)(2,1)}, bf16[4,576,192]{2,1,0:T(8,128)(2,1)}, f32[4,576,3]{2,1,0:T(8,128)}, f32[576,768]{1,0:T(8,128)}) custom-call(s32[1]{0:T(128)} %bitcast.4.refs_0_, f32[576,768]{1,0:T(8,128)} %get-tuple-element.141.refs_1_.refs_2_, f32[8,768]{1,0:T(8,128)} %pad.63.refs_2_.refs_3_, ...), custom_call_target="tpu_custom_call" | custom-call | flops 2300000000 | bytes 14317828 | tf_op jit(solution)/shard_map/pallas_call | solution.py:510
  232.9 4.5 collective-permute-done.49.refs_13_
  248.3 11.6 %collective-permute-done.41.refs_7_.refs_10_ = bf16[192,1536]{1,0:T(8,128)(2,1)} collective-permute-done((bf16[192,1536]{1,0:T(8,128)(2,1)S(1)}, bf16[192,1536]{1,0:T(8,128)(2,1)}, u32[]{:S(2)}, u32[]{:S(2)}) %collective-permute-start.41) | collective-permute-done | bytes 589856 | tf_op jit(solution)/shard_map/ppermute | solution.py:532
  264.5 14.8 %shard_map.430 = (bf16[576,768]{1,0:T(8,128)(2,1)}, bf16[4,576,768]{2,1,0:T(8,128)(2,1)}, f32[4,576,768]{2,1,0:T(8,128)}, f32[576,768]{1,0:T(8,128)}) custom-call(s32[1]{0:T(128)} %bitcast.4.refs_0_, f32[576,768]{1,0:T(8,128)} %get-tuple-element.148.refs_1_.refs_2_, f32[8,768]{1,0:T(8,128)} %pad.63.refs_2_.refs_3_, f32[4,1,768]{2,1,0:T(1,128)} %copy.92.refs_27_.refs_3_, ...), custom_call_target="tpu_custom_call" | custom-call | flops 2300000000 | bytes 24514564 | tf_op jit(solution)/shard_map/pallas_call | solution.py:510
  280.4 8.3 %shard_map.431 = (bf16[4,384,512]{2,1,0:T(8,128)(2,1)}, bf16[4,384,512]{2,1,0:T(8,128)(2,1)}, f32[4,1,512]{2,1,0:T(1,128)}, f32[576,768]{1,0:T(8,128)}, f32[8,768]{1,0:T(8,128)}, /*index=5*/f32[8,128]{1,0:T(8,128)}) custom-call(s32[1]{0:T(128)} %bitcast.4.refs_0_, f32[576,768]{1,0:T(8,128)} %get-tuple-element.151.refs_1_, f32[8,768]{1,0:T(8,128)} %pad.64.refs_2_, ...), custom_call_target="tpu_custom_call" | custom-call | flops 2300000000 | bytes 10370372 | tf_op jit(solution)/shard_map/pallas_call | solution.py:510
  290.6 14.0 %shard_map.432 = (f32[576,768]{1,0:T(8,128)}, bf16[2,384,1536]{2,1,0:T(8,128)(2,1)}, bf16[2,384,1536]{2,1,0:T(8,128)(2,1)}, f32[2,1,768]{2,1,0:T(1,128)}, f32[8,768]{1,0:T(8,128)}) custom-call(s32[1]{0:T(128)} %bitcast.4.refs_0_, f32[576,768]{1,0:T(8,128)} %get-tuple-element.154.refs_1_, f32[576,768]{1,0:T(8,128)} %get-tuple-element.148.refs_1_.refs_2_, ...), custom_call_target="tpu_custom_call" | custom-call | flops 2300000000 | bytes 32593924 | tf_op jit(solution)/shard_map/pallas_call | solution.py:510
  309.4 16.2 %shard_map.433 = (f32[576,768]{1,0:T(8,128)}, bf16[2,384,1536]{2,1,0:T(8,128)(2,1)}, bf16[2,384,1536]{2,1,0:T(8,128)(2,1)}, f32[2,1,768]{2,1,0:T(1,128)}, f32[8,768]{1,0:T(8,128)}) custom-call(s32[1]{0:T(128)} %bitcast.4.refs_0_, f32[576,768]{1,0:T(8,128)} %get-tuple-element.154.refs_1_, f32[576,768]{1,0:T(8,128)} %get-tuple-element.148.refs_1_.refs_2_, ...), custom_call_target="tpu_custom_call" | custom-call | flops 2300000000 | bytes 35543044 | tf_op jit(solution)/shard_map/pallas_call | solution.py:510
  330.9 17.7 %shard_map.434 = (f32[576,768]{1,0:T(8,128)}, bf16[2,384,768]{2,1,0:T(8,128)(2,1)}, bf16[2,384,768]{2,1,0:T(8,128)(2,1)}, f32[2,1,576]{2,1,0:T(1,128)}, f32[8,768]{1,0:T(8,128)}) custom-call(s32[1]{0:T(128)} %bitcast.4.refs_0_, f32[576,768]{1,0:T(8,128)} %get-tuple-element.163.refs_1_, f32[576,768]{1,0:T(8,128)} %get-tuple-element.141.refs_1_.refs_2_, ...), custom_call_target="tpu_custom_call" | custom-call | flops 2300000000 | bytes 21219076 | tf_op jit(solution)/shard_map/pallas_call | solution.py:510
  350.2 2.3 fusion.14.refs_21_
  359.9 20.3 %shard_map.435 = (f32[576,768]{1,0:T(8,128)}, bf16[2,384,768]{2,1,0:T(8,128)(2,1)}, bf16[2,384,768]{2,1,0:T(8,128)(2,1)}, f32[2,1,576]{2,1,0:T(1,128)}, f32[8,768]{1,0:T(8,128)}) custom-call(s32[1]{0:T(128)} %bitcast.4.refs_0_, f32[576,768]{1,0:T(8,128)} %get-tuple-element.163.refs_1_, f32[576,768]{1,0:T(8,128)} %get-tuple-element.141.refs_1_.refs_2_, ...), custom_call_target="tpu_custom_call" | custom-call | flops 2300000000 | bytes 22595332 | tf_op jit(solution)/shard_map/pallas_call | solution.py:510
  384.0 13.9 %shard_map.436 = (f32[576,768]{1,0:T(8,128)}, bf16[2,384,1536]{2,1,0:T(8,128)(2,1)}, bf16[2,384,1536]{2,1,0:T(8,128)(2,1)}, f32[2,1,768]{2,1,0:T(1,128)}, f32[8,768]{1,0:T(8,128)}) custom-call(s32[1]{0:T(128)} %bitcast.4.refs_0_, f32[576,768]{1,0:T(8,128)} %get-tuple-element.181.refs_1_, f32[576,768]{1,0:T(8,128)} %get-tuple-element.135.refs_1_.refs_2_, ...), custom_call_target="tpu_custom_call" | custom-call | flops 2300000000 | bytes 32790532 | tf_op jit(solution)/shard_map/pallas_call | solution.py:510
  402.2 3.6 fusion.1.refs_19_
  405.8 16.3 %shard_map.437 = (f32[576,768]{1,0:T(8,128)}, bf16[2,384,1536]{2,1,0:T(8,128)(2,1)}, bf16[2,384,1536]{2,1,0:T(8,128)(2,1)}, f32[2,1,768]{2,1,0:T(1,128)}, f32[8,768]{1,0:T(8,128)}) custom-call(s32[1]{0:T(128)} %bitcast.4.refs_0_, f32[576,768]{1,0:T(8,128)} %get-tuple-element.181.refs_1_, f32[576,768]{1,0:T(8,128)} %get-tuple-element.135.refs_1_.refs_2_, ...), custom_call_target="tpu_custom_call" | custom-call | flops 2300000000 | bytes 37509124 | tf_op jit(solution)/shard_map/pallas_call | solution.py:510
  423.8 2.7 fusion.9.refs_20_
  431.6 2.9 add_convert_fusion.2
  437.6 17.5 %shard_map.438 = (f32[576,768]{1,0:T(8,128)}, bf16[2,384,768]{2,1,0:T(8,128)(2,1)}, bf16[2,384,768]{2,1,0:T(8,128)(2,1)}, f32[2,1,576]{2,1,0:T(1,128)}, f32[8,768]{1,0:T(8,128)}) custom-call(s32[1]{0:T(128)} %bitcast.4.refs_0_, f32[576,768]{1,0:T(8,128)} %get-tuple-element.196.refs_1_, f32[576,768]{1,0:T(8,128)} %convolution_add_fusion.refs_1_.refs_2_, ...), custom_call_target="tpu_custom_call" | custom-call | flops 2300000000 | bytes 21022468 | tf_op jit(solution)/shard_map/pallas_call | solution.py:510
  466.4 20.2 %shard_map.439 = (f32[576,768]{1,0:T(8,128)}, bf16[2,384,768]{2,1,0:T(8,128)(2,1)}, bf16[2,384,768]{2,1,0:T(8,128)(2,1)}, f32[2,1,576]{2,1,0:T(1,128)}, f32[8,768]{1,0:T(8,128)}) custom-call(s32[1]{0:T(128)} %bitcast.4.refs_0_, f32[576,768]{1,0:T(8,128)} %get-tuple-element.196.refs_1_, f32[576,768]{1,0:T(8,128)} %convolution_add_fusion.refs_1_.refs_2_, ...), custom_call_target="tpu_custom_call" | custom-call | flops 2300000000 | bytes 22202116 | tf_op jit(solution)/shard_map/pallas_call | solution.py:510
  497.8 2.1 collective-permute-done.84
  519.5 5.0 collective-permute-done.86
  524.5 2.7 fusion.5
  527.3 22.0 %collective-permute-done.90 = f32[480,128]{1,0:T(8,128)} collective-permute-done((f32[480,128]{1,0:T(8,128)}, f32[480,128]{1,0:T(8,128)}, u32[]{:S(2)}, u32[]{:S(2)}) %collective-permute-start.90) | collective-permute-done | bytes 245792 | tf_op jit(solution)/shard_map/ppermute | solution.py:532
  553.5 4.6 collective-permute-done.91
  559.3 3.9 fusion
  570.2 23.2 %collective-permute-done.93 = f32[480,128]{1,0:T(8,128)S(1)} collective-permute-done((f32[480,128]{1,0:T(8,128)S(1)}, f32[480,128]{1,0:T(8,128)S(1)}, u32[]{:S(2)}, u32[]{:S(2)}) %collective-permute-start.93) | collective-permute-done | bytes 245792 | tf_op jit(solution)/shard_map/ppermute | solution.py:532
  594.3 2.0 multiply_reduce_fusion.11
  597.7 2.6 multiply_reduce_fusion.7
  606.3 3.1 multiply_reduce_fusion.2
  612.1 4.0 multiply_reduce_fusion
  619.5 2.4 collective-permute-done.95
  623.1 2.3 collective-permute-done.96
  625.4 3.5 collective-permute-done.97
  629.0 4.4 collective-permute-done.98
  640.0 2.5 multiply_subtract_fusion.5
  (739 shorter events, 225.4 us)
Async XLA Ops:
  7.2 69.6 %all-gather.4.cloned.1.call-start = ((), (), s32[]{:S(2)}) async-start(), calls=%async_computation.6 | async-start | bytes 1474560 | tf_op jit(solution)/shard_map/all_gather | solution.py:758
  18.7 85.4 %all-gather.6.cloned.1.call-start = ((), (), s32[]{:S(2)}) async-start(), calls=%async_computation.7 | async-start | bytes 1474560 | tf_op jit(solution)/shard_map/all_gather | solution.py:758
  21.6 110.7 %all-gather.8.cloned.1.call-start = ((), (), s32[]{:S(2)}) async-start(), calls=%async_computation.8 | async-start | bytes 2703360 | tf_op jit(solution)/shard_map/all_gather | solution.py:758
  21.6 47.3 %collective-permute-start.9 = (f32[2804]{0:T(1024)}, f32[2804]{0:T(1024)}, u32[]{:S(2)}, u32[]{:S(2)}) collective-permute-start(f32[2804]{0:T(1024)} %param.40), channel_id=1, source_target_pairs={{0,4},{2,6},{4,0},{6,2},{1,5},{3,7},{5,1},{7,3},{8,12},{10,14},{12... | collective-permute-start | bytes 33656 | tf_op jit(solution)/shard_map/ppermute | solution.py:532
  24.7 45.8 %collective-permute-start.8 = (f32[2804]{0:T(1024)}, f32[2804]{0:T(1024)}, u32[]{:S(2)}, u32[]{:S(2)}) collective-permute-start(f32[2804]{0:T(1024)} %param.40), channel_id=1, source_target_pairs={{0,2},{2,0},{4,6},{6,4},{1,3},{3,1},{5,7},{7,5},{8,10},{10,8},{12,... | collective-permute-start | bytes 33656 | tf_op jit(solution)/shard_map/ppermute | solution.py:532
  26.2 45.0 %collective-permute-start.10 = (f32[2804]{0:T(1024)}, f32[2804]{0:T(1024)}, u32[]{:S(2)}, u32[]{:S(2)}) collective-permute-start(f32[2804]{0:T(1024)} %param.40), channel_id=1, source_target_pairs={{0,6},{2,4},{4,2},{6,0},{1,7},{3,5},{5,3},{7,1},{8,14},{10,12},{12... | collective-permute-start | bytes 33656 | tf_op jit(solution)/shard_map/ppermute | solution.py:532
  26.9 21.3 %collective-permute-start = (f32[1]{0:T(128)}, f32[1]{0:T(128)}, u32[]{:S(2)}, u32[]{:S(2)}) collective-permute-start(f32[1]{0:T(128)} %bitcast.10), channel_id=1, source_target_pairs={{0,1},{1,0},{2,3},{3,2},{4,5},{5,4},{6,7},{7,6},{8,9},{9,8},{10,11... | collective-permute-start | bytes 20 | tf_op jit(solution)/shard_map/ppermute | solution.py:532
  28.5 44.1 %collective-permute-start.6 = (bf16[224,256]{1,0:T(8,128)(2,1)}, bf16[224,256]{1,0:T(8,128)(2,1)}, u32[]{:S(2)}, u32[]{:S(2)}) collective-permute-start(bf16[224,256]{1,0:T(8,128)(2,1)} %get-tuple-element.333), channel_id=1, source_target_pairs={{0,4},{2,6},{4,0},{6,2},{1,5},{3,7},{5,1},{7,3},{8,12},{10,14},{12... | collective-permute-start | bytes 344072 | tf_op jit(solution)/shard_map/ppermute | solution.py:532
  34.0 480.6 %reduce-scatter.17.cloned.1.call-start = ((), (), s32[]{:S(2)}) async-start(), calls=%async_computation.14 | async-start | bytes 491520 | tf_op jit(solution)/shard_map/reduce_scatter | solution.py:624
  82.6 29.8 %collective-permute-start.16 = (bf16[384,768]{1,0:T(8,128)(2,1)S(1)}, bf16[384,768]{1,0:T(8,128)(2,1)}, u32[]{:S(2)}, u32[]{:S(2)}) collective-permute-start(bf16[384,768]{1,0:T(8,128)(2,1)S(1)} %get-tuple-element.131.refs_5_.refs_9_), channel_id=1, source_target_pairs={{0,1},{1,0},{2,3},{3,2},{4,5},{5,4},{6,7},{7,6},{8,9},{9,8},{10,11... | collective-permute-start | bytes 1769480 | tf_op jit(solution)/shard_map/ppermute | solution.py:532
  108.8 46.4 %collective-permute-start.22 = (bf16[384,1536]{1,0:T(8,128)(2,1)}, bf16[384,1536]{1,0:T(8,128)(2,1)S(1)}, u32[]{:S(2)}, u32[]{:S(2)}) collective-permute-start(bf16[384,1536]{1,0:T(8,128)(2,1)} %all-gather.6.cloned.1.call-done.refs_15_.refs_4_.refs_7_), channel_id=1, source_target_pairs={{0,4},{2,6},{4,0},{6,2},{1,5},{3,7},{5,1},{7,3},{8,12},{10,14},{12... | collective-permute-start | bytes 3538952 | tf_op jit(solution)/shard_map/ppermute | solution.py:532
  110.0 45.2 %collective-permute-start.21 = (bf16[384,1536]{1,0:T(8,128)(2,1)}, bf16[384,1536]{1,0:T(8,128)(2,1)S(1)}, u32[]{:S(2)}, u32[]{:S(2)}) collective-permute-start(bf16[384,1536]{1,0:T(8,128)(2,1)} %all-gather.6.cloned.1.call-done.refs_15_.refs_4_.refs_7_), channel_id=1, source_target_pairs={{0,2},{2,0},{4,6},{6,4},{1,3},{3,1},{5,7},{7,5},{8,10},{10,8},{12,... | collective-permute-start | bytes 3538952 | tf_op jit(solution)/shard_map/ppermute | solution.py:532
  111.9 22.1 %collective-permute-start.17 = (bf16[384,768]{1,0:T(8,128)(2,1)}, bf16[384,768]{1,0:T(8,128)(2,1)}, u32[]{:S(2)}, u32[]{:S(2)}) collective-permute-start(bf16[384,768]{1,0:T(8,128)(2,1)} %collective-permute-done.12.refs_6_.refs_10_), channel_id=1, source_target_pairs={{0,1},{1,0},{2,3},{3,2},{4,5},{5,4},{6,7},{7,6},{8,9},{9,8},{10,11... | collective-permute-start | bytes 1769480 | tf_op jit(solution)/shard_map/ppermute | solution.py:532
  112.0 22.1 %collective-permute-start.18 = (bf16[384,768]{1,0:T(8,128)(2,1)S(1)}, bf16[384,768]{1,0:T(8,128)(2,1)}, u32[]{:S(2)}, u32[]{:S(2)}) collective-permute-start(bf16[384,768]{1,0:T(8,128)(2,1)S(1)} %collective-permute-done.13.refs_7_.refs_11_), channel_id=1, source_target_pairs={{0,1},{1,0},{2,3},{3,2},{4,5},{5,4},{6,7},{7,6},{8,9},{9,8},{10,11... | collective-permute-start | bytes 1769480 | tf_op jit(solution)/shard_map/ppermute | solution.py:532
  115.0 19.0 %collective-permute-start.20 = (bf16[192,768]{1,0:T(8,128)(2,1)}, bf16[192,768]{1,0:T(8,128)(2,1)S(1)}, u32[]{:S(2)}, u32[]{:S(2)}) collective-permute-start(bf16[192,768]{1,0:T(8,128)(2,1)} %collective-permute-done.15.refs_9_.refs_13_), channel_id=1, source_target_pairs={{0,1},{1,0},{2,3},{3,2},{4,5},{5,4},{6,7},{7,6},{8,9},{9,8},{10,11... | collective-permute-start | bytes 884744 | tf_op jit(solution)/shard_map/ppermute | solution.py:532
  172.1 20.3 %collective-permute-start.31 = (bf16[384,768]{1,0:T(8,128)(2,1)S(1)}, bf16[384,768]{1,0:T(8,128)(2,1)S(1)}, u32[]{:S(2)}, u32[]{:S(2)}) collective-permute-start(bf16[384,768]{1,0:T(8,128)(2,1)S(1)} %slice.949.refs_14_.refs_5_.refs_9_), channel_id=1, source_target_pairs={{0,4},{2,6},{4,0},{6,2},{1,5},{3,7},{5,1},{7,3},{8,12},{10,14},{12... | collective-permute-start | bytes 1769480 | tf_op jit(solution)/shard_map/ppermute | solution.py:532
  202.3 40.3 %collective-permute-start.40 = (bf16[384,1536]{1,0:T(8,128)(2,1)S(1)}, bf16[384,1536]{1,0:T(8,128)(2,1)S(1)}, u32[]{:S(2)}, u32[]{:S(2)}) collective-permute-start(bf16[384,1536]{1,0:T(8,128)(2,1)S(1)} %slice.951.refs_15_.refs_4_.refs_7_), channel_id=1, source_target_pairs={{0,4},{2,6},{4,0},{6,2},{1,5},{3,7},{5,1},{7,3},{8,12},{10,14},{12... | collective-permute-start | bytes 3538952 | tf_op jit(solution)/shard_map/ppermute | solution.py:532
  203.8 38.8 %collective-permute-start.39 = (bf16[384,1536]{1,0:T(8,128)(2,1)S(1)}, bf16[384,1536]{1,0:T(8,128)(2,1)S(1)}, u32[]{:S(2)}, u32[]{:S(2)}) collective-permute-start(bf16[384,1536]{1,0:T(8,128)(2,1)S(1)} %slice.951.refs_15_.refs_4_.refs_7_), channel_id=1, source_target_pairs={{0,2},{2,0},{4,6},{6,4},{1,3},{3,1},{5,7},{7,5},{8,10},{10,8},{12,... | collective-permute-start | bytes 3538952 | tf_op jit(solution)/shard_map/ppermute | solution.py:532
  207.8 29.6 %collective-permute-start.49 = (bf16[384,512]{1,0:T(8,128)(2,1)}, bf16[384,512]{1,0:T(8,128)(2,1)}, u32[]{:S(2)}, u32[]{:S(2)}) collective-permute-start(bf16[384,512]{1,0:T(8,128)(2,1)} %slice.942.refs_16_.refs_11_), channel_id=1, source_target_pairs={{0,4},{2,6},{4,0},{6,2},{1,5},{3,7},{5,1},{7,3},{8,12},{10,14},{12... | collective-permute-start | bytes 1179656 | tf_op jit(solution)/shard_map/ppermute | solution.py:532
  208.6 30.0 %collective-permute-start.48 = (bf16[384,512]{1,0:T(8,128)(2,1)}, bf16[384,512]{1,0:T(8,128)(2,1)}, u32[]{:S(2)}, u32[]{:S(2)}) collective-permute-start(bf16[384,512]{1,0:T(8,128)(2,1)} %slice.942.refs_16_.refs_11_), channel_id=1, source_target_pairs={{0,2},{2,0},{4,6},{6,4},{1,3},{3,1},{5,7},{7,5},{8,10},{10,8},{12,... | collective-permute-start | bytes 1179656 | tf_op jit(solution)/shard_map/ppermute | solution.py:532
  304.6 22.9 %collective-permute-start.60 = (bf16[2,384,1536]{2,1,0:T(8,128)(2,1)}, bf16[2,384,1536]{2,1,0:T(8,128)(2,1)S(1)}, u32[]{:S(2)}, u32[]{:S(2)}) collective-permute-start(bf16[2,384,1536]{2,1,0:T(8,128)(2,1)} %get-tuple-element.160.refs_18_), channel_id=1, source_target_pairs={{0,1},{1,0},{2,3},{3,2},{4,5},{5,4},{6,7},{7,6},{8,9},{9,8},{10,11... | collective-permute-start | bytes 7077896 | tf_op jit(solution)/shard_map/ppermute | solution.py:532
  306.7 19.0 %collective-permute-start.59 = (bf16[192,512]{1,0:T(8,128)(2,1)S(1)}, bf16[192,512]{1,0:T(8,128)(2,1)S(1)}, u32[]{:S(2)}, u32[]{:S(2)}) collective-permute-start(bf16[192,512]{1,0:T(8,128)(2,1)S(1)} %get-tuple-element.306.refs_20_), channel_id=1, source_target_pairs={{0,4},{2,6},{4,0},{6,2},{1,5},{3,7},{5,1},{7,3},{8,12},{10,14},{12... | collective-permute-start | bytes 589832 | tf_op jit(solution)/shard_map/ppermute | solution.py:532
  325.6 29.2 %collective-permute-start.65 = (bf16[2,384,1536]{2,1,0:T(8,128)(2,1)}, bf16[2,384,1536]{2,1,0:T(8,128)(2,1)}, u32[]{:S(2)}, u32[]{:S(2)}) collective-permute-start(bf16[2,384,1536]{2,1,0:T(8,128)(2,1)} %get-tuple-element.168.refs_19_), channel_id=1, source_target_pairs={{0,1},{1,0},{2,3},{3,2},{4,5},{5,4},{6,7},{7,6},{8,9},{9,8},{10,11... | collective-permute-start | bytes 7077896 | tf_op jit(solution)/shard_map/ppermute | solution.py:532
  325.8 22.8 %collective-permute-start.62 = (bf16[384,512]{1,0:T(8,128)(2,1)S(1)}, bf16[384,512]{1,0:T(8,128)(2,1)S(1)}, u32[]{:S(2)}, u32[]{:S(2)}) collective-permute-start(bf16[384,512]{1,0:T(8,128)(2,1)S(1)} %pad_maximum_fusion.13.refs_21_), channel_id=1, source_target_pairs={{0,4},{2,6},{4,0},{6,2},{1,5},{3,7},{5,1},{7,3},{8,12},{10,14},{12... | collective-permute-start | bytes 1179656 | tf_op jit(solution)/shard_map/ppermute | solution.py:532
  326.6 22.1 %collective-permute-start.61 = (bf16[384,512]{1,0:T(8,128)(2,1)S(1)}, bf16[384,512]{1,0:T(8,128)(2,1)S(1)}, u32[]{:S(2)}, u32[]{:S(2)}) collective-permute-start(bf16[384,512]{1,0:T(8,128)(2,1)S(1)} %pad_maximum_fusion.12.refs_20_), channel_id=1, source_target_pairs={{0,2},{2,0},{4,6},{6,4},{1,3},{3,1},{5,7},{7,5},{8,10},{10,8},{12,... | collective-permute-start | bytes 1179656 | tf_op jit(solution)/shard_map/ppermute | solution.py:532
  328.3 24.4 %collective-permute-start.64 = (bf16[192,1536]{1,0:T(8,128)(2,1)S(1)}, bf16[192,1536]{1,0:T(8,128)(2,1)}, u32[]{:S(2)}, u32[]{:S(2)}) collective-permute-start(bf16[192,1536]{1,0:T(8,128)(2,1)S(1)} %get-tuple-element.287.refs_23_), channel_id=1, source_target_pairs={{0,4},{2,6},{4,0},{6,2},{1,5},{3,7},{5,1},{7,3},{8,12},{10,14},{12... | collective-permute-start | bytes 1769480 | tf_op jit(solution)/shard_map/ppermute | solution.py:532
  329.6 23.0 %collective-permute-start.63 = (bf16[192,1536]{1,0:T(8,128)(2,1)S(1)}, bf16[192,1536]{1,0:T(8,128)(2,1)}, u32[]{:S(2)}, u32[]{:S(2)}) collective-permute-start(bf16[192,1536]{1,0:T(8,128)(2,1)S(1)} %get-tuple-element.288.refs_22_), channel_id=1, source_target_pairs={{0,2},{2,0},{4,6},{6,4},{1,3},{3,1},{5,7},{7,5},{8,10},{10,8},{12,... | collective-permute-start | bytes 1769480 | tf_op jit(solution)/shard_map/ppermute | solution.py:532
  352.5 200.1 %reduce-scatter.11.cloned.1.call-start = ((), (), s32[]{:S(2)}) async-start(), calls=%async_computation.11 | async-start | bytes 737280 | tf_op jit(solution)/shard_map/reduce_scatter | solution.py:624
  352.5 28.2 %collective-permute-start.66 = (bf16[2,384,768]{2,1,0:T(8,128)(2,1)S(1)}, bf16[2,384,768]{2,1,0:T(8,128)(2,1)}, u32[]{:S(2)}, u32[]{:S(2)}) collective-permute-start(bf16[2,384,768]{2,1,0:T(8,128)(2,1)S(1)} %copy-done.59), channel_id=1, source_target_pairs={{0,1},{1,0},{2,3},{3,2},{4,5},{5,4},{6,7},{7,6},{8,9},{9,8},{10,11... | collective-permute-start | bytes 3538952 | tf_op jit(solution)/shard_map/ppermute | solution.py:532
  354.0 46.9 %collective-permute-start.67 = (bf16[384,1536]{1,0:T(8,128)(2,1)S(1)}, bf16[384,1536]{1,0:T(8,128)(2,1)}, u32[]{:S(2)}, u32[]{:S(2)}) collective-permute-start(bf16[384,1536]{1,0:T(8,128)(2,1)S(1)} %pad_maximum_fusion.1.refs_22_), channel_id=1, source_target_pairs={{0,2},{2,0},{4,6},{6,4},{1,3},{3,1},{5,7},{7,5},{8,10},{10,8},{12,... | collective-permute-start | bytes 3538952 | tf_op jit(solution)/shard_map/ppermute | solution.py:532
  358.9 42.0 %collective-permute-start.68 = (bf16[384,1536]{1,0:T(8,128)(2,1)S(1)}, bf16[384,1536]{1,0:T(8,128)(2,1)}, u32[]{:S(2)}, u32[]{:S(2)}) collective-permute-start(bf16[384,1536]{1,0:T(8,128)(2,1)S(1)} %pad_maximum_fusion.2.refs_23_), channel_id=1, source_target_pairs={{0,4},{2,6},{4,0},{6,2},{1,5},{3,7},{5,1},{7,3},{8,12},{10,14},{12... | collective-permute-start | bytes 3538952 | tf_op jit(solution)/shard_map/ppermute | solution.py:532
  380.2 19.4 %collective-permute-start.71 = (bf16[2,384,768]{2,1,0:T(8,128)(2,1)}, bf16[2,384,768]{2,1,0:T(8,128)(2,1)}, u32[]{:S(2)}, u32[]{:S(2)}) collective-permute-start(bf16[2,384,768]{2,1,0:T(8,128)(2,1)} %get-tuple-element.185.refs_17_), channel_id=1, source_target_pairs={{0,1},{1,0},{2,3},{3,2},{4,5},{5,4},{6,7},{7,6},{8,9},{9,8},{10,11... | collective-permute-start | bytes 3538952 | tf_op jit(solution)/shard_map/ppermute | solution.py:532
  398.0 33.6 %collective-permute-start.74 = (bf16[2,384,1536]{2,1,0:T(8,128)(2,1)}, bf16[2,384,1536]{2,1,0:T(8,128)(2,1)}, u32[]{:S(2)}, u32[]{:S(2)}) collective-permute-start(bf16[2,384,1536]{2,1,0:T(8,128)(2,1)} %get-tuple-element.189.refs_18_), channel_id=1, source_target_pairs={{0,1},{1,0},{2,3},{3,2},{4,5},{5,4},{6,7},{7,6},{8,9},{9,8},{10,11... | collective-permute-start | bytes 7077896 | tf_op jit(solution)/shard_map/ppermute | solution.py:532
  398.2 23.9 %collective-permute-start.72 = (bf16[384,768]{1,0:T(8,128)(2,1)S(1)}, bf16[384,768]{1,0:T(8,128)(2,1)S(1)}, u32[]{:S(2)}, u32[]{:S(2)}) collective-permute-start(bf16[384,768]{1,0:T(8,128)(2,1)S(1)} %pad_maximum_fusion.7.refs_20_), channel_id=1, source_target_pairs={{0,2},{2,0},{4,6},{6,4},{1,3},{3,1},{5,7},{7,5},{8,10},{10,8},{12,... | collective-permute-start | bytes 1769480 | tf_op jit(solution)/shard_map/ppermute | solution.py:532
  400.9 21.2 %collective-permute-start.73 = (bf16[384,768]{1,0:T(8,128)(2,1)S(1)}, bf16[384,768]{1,0:T(8,128)(2,1)S(1)}, u32[]{:S(2)}, u32[]{:S(2)}) collective-permute-start(bf16[384,768]{1,0:T(8,128)(2,1)S(1)} %pad_maximum_fusion.8.refs_21_), channel_id=1, source_target_pairs={{0,4},{2,6},{4,0},{6,2},{1,5},{3,7},{5,1},{7,3},{8,12},{10,14},{12... | collective-permute-start | bytes 1769480 | tf_op jit(solution)/shard_map/ppermute | solution.py:532
  426.5 136.9 %reduce-scatter.15.cloned.1.call-start = ((), (), s32[]{:S(2)}) async-start(), calls=%async_computation.13 | async-start | bytes 1474560 | tf_op jit(solution)/shard_map/reduce_scatter | solution.py:624
  430.8 137.2 %reduce-scatter.7.cloned.1.call-start = ((), (), s32[]{:S(2)}) async-start(), calls=%async_computation.9 | async-start | bytes 737280 | tf_op jit(solution)/shard_map/reduce_scatter | solution.py:1046
  430.9 30.7 %collective-permute-start.77 = (bf16[2,384,1536]{2,1,0:T(8,128)(2,1)S(1)}, bf16[2,384,1536]{2,1,0:T(8,128)(2,1)}, u32[]{:S(2)}, u32[]{:S(2)}) collective-permute-start(bf16[2,384,1536]{2,1,0:T(8,128)(2,1)S(1)} %copy-done.38), channel_id=1, source_target_pairs={{0,1},{1,0},{2,3},{3,2},{4,5},{5,4},{6,7},{7,6},{8,9},{9,8},{10,11... | collective-permute-start | bytes 7077896 | tf_op jit(solution)/shard_map/ppermute | solution.py:532
  435.6 23.6 %collective-permute-start.76 = (bf16[192,1536]{1,0:T(8,128)(2,1)}, bf16[192,1536]{1,0:T(8,128)(2,1)}, u32[]{:S(2)}, u32[]{:S(2)}) collective-permute-start(bf16[192,1536]{1,0:T(8,128)(2,1)} %get-tuple-element.285.refs_22_), channel_id=1, source_target_pairs={{0,4},{2,6},{4,0},{6,2},{1,5},{3,7},{5,1},{7,3},{8,12},{10,14},{12... | collective-permute-start | bytes 1769480 | tf_op jit(solution)/shard_map/ppermute | solution.py:532
  436.5 22.8 %collective-permute-start.75 = (bf16[192,1536]{1,0:T(8,128)(2,1)}, bf16[192,1536]{1,0:T(8,128)(2,1)}, u32[]{:S(2)}, u32[]{:S(2)}) collective-permute-start(bf16[192,1536]{1,0:T(8,128)(2,1)} %get-tuple-element.286.refs_21_), channel_id=1, source_target_pairs={{0,2},{2,0},{4,6},{6,4},{1,3},{3,1},{5,7},{7,5},{8,10},{10,8},{12,... | collective-permute-start | bytes 1769480 | tf_op jit(solution)/shard_map/ppermute | solution.py:532
  459.2 28.9 %collective-permute-start.82 = (bf16[2,384,768]{2,1,0:T(8,128)(2,1)}, bf16[2,384,768]{2,1,0:T(8,128)(2,1)}, u32[]{:S(2)}, u32[]{:S(2)}) collective-permute-start(bf16[2,384,768]{2,1,0:T(8,128)(2,1)} %get-tuple-element.207.refs_20_), channel_id=1, source_target_pairs={{0,1},{1,0},{2,3},{3,2},{4,5},{5,4},{6,7},{7,6},{8,9},{9,8},{10,11... | collective-permute-start | bytes 3538952 | tf_op jit(solution)/shard_map/ppermute | solution.py:532
  504.5 100.7 %reduce-scatter.9.cloned.1.call-start = ((), (), s32[]{:S(2)}) async-start(), calls=%async_computation.10 | async-start | bytes 737280 | tf_op jit(solution)/shard_map/reduce_scatter | solution.py:624
  515.5 43.8 %collective-permute-start.87 = (bf16[384,1536]{1,0:T(8,128)(2,1)S(1)}, bf16[384,1536]{1,0:T(8,128)(2,1)}, u32[]{:S(2)}, u32[]{:S(2)}) collective-permute-start(bf16[384,1536]{1,0:T(8,128)(2,1)S(1)} %copy-done.24), channel_id=1, source_target_pairs={{0,2},{2,0},{4,6},{6,4},{1,3},{3,1},{5,7},{7,5},{8,10},{10,8},{12,... | collective-permute-start | bytes 3538952 | tf_op jit(solution)/shard_map/ppermute | solution.py:532
  516.8 42.5 %collective-permute-start.88 = (bf16[384,1536]{1,0:T(8,128)(2,1)S(1)}, bf16[384,1536]{1,0:T(8,128)(2,1)}, u32[]{:S(2)}, u32[]{:S(2)}) collective-permute-start(bf16[384,1536]{1,0:T(8,128)(2,1)S(1)} %copy-done.25), channel_id=1, source_target_pairs={{0,4},{2,6},{4,0},{6,2},{1,5},{3,7},{5,1},{7,3},{8,12},{10,14},{12... | collective-permute-start | bytes 3538952 | tf_op jit(solution)/shard_map/ppermute | solution.py:532
  518.7 30.7 %collective-permute-start.90 = (f32[480,128]{1,0:T(8,128)}, f32[480,128]{1,0:T(8,128)}, u32[]{:S(2)}, u32[]{:S(2)}) collective-permute-start(f32[480,128]{1,0:T(8,128)} %fusion.37), channel_id=1, source_target_pairs={{0,2},{2,0},{4,6},{6,4},{1,3},{3,1},{5,7},{7,5},{8,10},{10,8},{12,... | collective-permute-start | bytes 737288 | tf_op jit(solution)/shard_map/ppermute | solution.py:532
  527.2 82.2 %reduce-scatter.13.cloned.1.call-start = ((), (), s32[]{:S(2)}) async-start(), calls=%async_computation.12 | async-start | bytes 1474560 | tf_op jit(solution)/shard_map/reduce_scatter | solution.py:624
  567.0 26.3 %collective-permute-start.93 = (f32[480,128]{1,0:T(8,128)S(1)}, f32[480,128]{1,0:T(8,128)S(1)}, u32[]{:S(2)}, u32[]{:S(2)}) collective-permute-start(f32[480,128]{1,0:T(8,128)S(1)} %add.505), channel_id=1, source_target_pairs={{0,16},{8,24},{16,0},{24,8},{1,17},{9,25},{17,1},{25,9},{2,18},{10... | collective-permute-start | bytes 737288 | tf_op jit(solution)/shard_map/ppermute | solution.py:532
  569.0 24.4 %collective-permute-start.79 = (f32[96,768]{1,0:T(8,128)S(1)}, f32[96,768]{1,0:T(8,128)S(1)}, u32[]{:S(2)}, u32[]{:S(2)}) collective-permute-start(f32[96,768]{1,0:T(8,128)S(1)} %convert_element_type.649), channel_id=1, source_target_pairs={{0,2},{2,0},{4,6},{6,4},{1,3},{3,1},{5,7},{7,5},{8,10},{10,8},{12,... | collective-permute-start | bytes 884744 | tf_op jit(solution)/shard_map/ppermute | solution.py:532
  (202 other events, 1520.4 us)
Sparse Core Ops, SparseCore 0:
  18.8 33.1 all-gather.3
  54.1 29.5 all-gather.5
  85.9 46.3 all-gather.7
  352.6 18.0 reduce-scatter.16
  426.6 19.9 reduce-scatter.10
  448.9 27.5 reduce-scatter.14
  504.6 20.0 reduce-scatter.6
  527.6 20.3 reduce-scatter.8
  563.4 35.0 reduce-scatter.12

commit v3 on v2

--- a/solution.py
+++ b/solution.py
@@ -575,6 +575,31 @@
     return values
 
 
+def sum_and_gather(values, everywhere, cores, square):
+    for axis in ("dp", "teach", "mp"):
+        distance = 1
+        while distance < lax.axis_size(axis):
+            parts = [everywhere, square] if axis == "mp" else [everywhere, cores]
+            sent = jnp.concatenate([values] + [part.reshape(-1) for part in parts])
+            got = swap(sent, axis, distance)
+            first = (lax.axis_index(axis) // distance) % 2 == 0
+            at = values.size
+            values = values + got[:at]
+            doubled = []
+            for part in parts:
+                new = got[at : at + part.size].reshape(part.shape)
+                at += part.size
+                doubled.append(
+                    jnp.concatenate([jnp.where(first, part, new), jnp.where(first, new, part)])
+                )
+            if axis == "mp":
+                everywhere, square = doubled
+            else:
+                everywhere, cores = doubled
+            distance *= 2
+    return values, everywhere, cores, square
+
+
 def gather_mp(values):
     size = lax.axis_size("mp")
     return jnp.stack([values] + [swap(values, "mp", step) for step in range(1, size)])
@@ -584,21 +609,36 @@
     def __init__(self):
         self.waiting = []
         self.block = {}
-        self.total = None
+        self.extra = None
+        self.sections = []
+        self.pieces = None
 
     def cores(self, steps, mine, other):
         self.waiting.append((steps, mine, swap(other, "teach", 1)))
+
+    def attach(self, *sections):
+        self.sections = [mine.shape[1] for mine, _ in sections]
+        other = jnp.concatenate([other for _, other in sections], axis=1)
+        self.extra = (
+            jnp.concatenate([mine for mine, _ in sections], axis=1),
+            swap(other, "teach", 1),
+        )
 
     def added(self, *behind):
         for steps, mine, got in self.waiting:
             got = tie(got, *behind)
             for slot, step in enumerate(steps):
-                self.block[step] = add_low(mine[slot], got[slot])
+                block = add_low(mine[slot], got[slot])
+                self.cuts = [block.shape[0], *self.sections]
+                if self.extra:
+                    more = add_low(self.extra[0][step], self.extra[1][step])
+                    block = jnp.concatenate([block, more])
+                self.block[step] = block
         self.waiting = []
 
     def corner(self, *behind):
         self.added(*behind)
-        cut = self.block[FAR].shape[0] // 2
+        self.cut = cut = -(-self.block[FAR].shape[0] // 32) * 16
         sent = [self.block[FAR][:cut], self.block[FAR][cut:]]
         self.by_one = swap(sent[0], "mp", 1)
         self.by_two = swap(sent[1], "mp", 2)
@@ -607,7 +647,7 @@
     def square(self, *behind):
         self.added(*behind)
         one, two = self.block[1], self.block[2]
-        cut = one.shape[0] // 2
+        cut = self.cut
         by_one, by_two = tie((self.by_one, self.by_two), *behind)
         sent = [
             jnp.concatenate([one[:cut], add_low(one[cut:], by_two)]),
@@ -617,15 +657,24 @@
         self.by_two = swap(sent[1], "mp", 2)
         return sent
 
-    def rows(self, *behind):
+    def summed(self, *behind):
         by_one, by_two = tie((self.by_one, self.by_two), *behind)
         total = self.block[0].astype(F32) + (by_one.astype(F32) + by_two.astype(F32))
-        total = total.astype(BF)
-        self.total = lax.psum_scatter(total, "dp", scatter_dimension=0, tiled=True)
+        dp = lax.axis_size("dp")
+        width = total.shape[1]
+        parts, at = [], 0
+        for cut in self.cuts:
+            parts.append(total[at : at + cut].reshape(dp, -1, width))
+            at += cut
+        return jnp.concatenate(parts, axis=1).astype(BF).reshape(total.shape)
+
+    def rows(self, *behind):
+        total = self.summed(*behind)
+        self.pieces = lax.psum_scatter(total, "dp", scatter_dimension=0, tiled=True)
         return [total]
 
     def result(self):
-        return self.total.astype(F32)
+        return self.pieces.astype(F32)
 
 
 def adam_direction(gradient, first_moment, second_moment, correct_first, correct_second):
@@ -865,7 +914,7 @@
         ahead = units[at + 1 : at + 2] if at < len(units) - 3 else units[at + 1 :]
         if at == 0:
             here.cores()
-            return [units[1].own[0], near[-1], *head_small, head_bias, *attn_bias, *up_bias]
+            return [units[1].own[0], *head_small, head_bias, *attn_bias, *up_bias]
         if at < len(units) - 2:
             here.corner(done)
             for unit in ahead:
@@ -942,10 +991,16 @@
     agenda = {0: [], 1: [(head_out, "corner")], 2: [(head_out, "square")], 3: [(head_out, "rows")]}
     slot = 0
     for layer in reversed(range(L)):
-        for at, unit in ((slot + 1, mlp_out[layer]), (slot + 3, attn_out[layer])):
-            wait = 2 if unit is mlp_out[layer] else 1
-            for moment, what in ((at + 1, "corner"), (at + 2, "square"), (at + 2 + wait, "rows")):
-                agenda.setdefault(moment, []).append((unit, what))
+        plan = (
+            (mlp_out[layer], "corner", 2),
+            (mlp_out[layer], "square", 3),
+            (mlp_out[layer], "rows", 5 if layer else 4),
+            (attn_out[layer], "corner", 4),
+            (attn_out[layer], "square", 5),
+            (attn_out[layer], "rows", 6),
+        )
+        for unit, what, moment in plan:
+            agenda.setdefault(slot + moment, []).append((unit, what))
         slot += 4
     final = slot
 
@@ -1025,7 +1080,8 @@
             qkv_bgrad.update({step: bgrad[at, 0] for at, step in enumerate(steps)})
             slot += 1
             attn_out[layer].cores(steps, mine, other)
-            sending = [other] + proceed(slot, grad)
+            if slot < final:
+                sending = [other] + proceed(slot, grad)
         gain_list[layer] = (attn_vgrad + mlp_vgrad)[:6]
         bias_list[layer] = jnp.stack(
             [
@@ -1035,16 +1091,13 @@
                 for step in range(mp)
             ]
         )
-    for moment in sorted(agenda):
-        proceed(moment, grad)
-
+    quarter = rows_own // mp
     patch_grad = dot_tn(patch_rows, grad.astype(BF)).astype(BF)
-    patch_grad = patch_grad.reshape(dp, teach, rows_own, D)
-    patch_mine = lax.dynamic_index_in_dim(patch_grad, here_teach, 1, False)
-    patch_sent = lax.dynamic_index_in_dim(patch_grad, 1 - here_teach, 1, False)
-    patch_grad = add_low(patch_mine, swap(patch_sent, "teach", 1)).reshape(dp * rows_own, D)
-    patch_grad = lax.psum_scatter(patch_grad, "dp", scatter_dimension=0, tiled=True)
-    patch_grad = outward(sum_over(patch_grad.astype(F32), "mp"))
+    patch_grad = patch_grad.reshape(dp, teach, mp, quarter, D)
+
+    def patch_half(core):
+        kept = lax.dynamic_index_in_dim(patch_grad, core, 1, False)
+        return kept.transpose(1, 0, 2, 3)[ranks].reshape(mp, dp * quarter, D)
 
     source_grads = lax.dot_general(
         sources, grad, (((0,), (0,)), ((), ())), precision=HIGH, preferred_element_type=F32
@@ -1054,17 +1107,46 @@
     )
     bias_blocks = jnp.concatenate(
         bias_list + [head_bgrad[:, 0, :cl], head_bgrad[:, 0, wc : wc + cl]], axis=1
-    )[ranks]
-    bias_size = bias_blocks.shape[1]
-    flat = jnp.concatenate([vector_grads.reshape(-1), bias_blocks.reshape(-1)])
-    flat = jnp.pad(flat, (0, -flat.size % 1024)).reshape(-1, 128)
-    flat = sum_all(flat).reshape(-1)
-    vector_grads = flat[: vector_params.size].reshape(vector_params.shape)
-    bias_grads = lax.dynamic_slice_in_dim(
-        flat, vector_params.size + here_mp * bias_size, bias_size, 0
-    )
-
-    attn_list = [unit.result() for unit in attn_out]
+    )
+    devices = dp * teach
+    vector_piece = -(-vector_params.size // (mp * devices))
+    bias_piece = -(-split_biases.size // devices)
+
+    def padded(flat, size):
+        return jnp.pad(flat, ((0, 0), (0, size - flat.shape[1])))
+
+    more_rows = -(rows_own + quarter) % 16
+    while more_rows * D < vector_piece + bias_piece:
+        more_rows += 16
+    vector_cut = padded(vector_grads.reshape(1, -1), vector_piece * mp * devices)
+    small = jnp.concatenate(
+        [
+            vector_cut.reshape(mp, devices, vector_piece)[ranks],
+            padded(bias_blocks, bias_piece * devices).reshape(mp, devices, bias_piece),
+            jnp.zeros((mp, devices, more_rows * D - vector_piece - bias_piece), F32),
+        ],
+        axis=2,
+    )
+    small = small.astype(BF).reshape(mp, teach, dp * more_rows, D)
+
+    def small_half(core):
+        return lax.dynamic_index_in_dim(small, core, 1, False)
+
+    attn_out[0].attach(
+        (patch_half(here_teach), patch_half(1 - here_teach)),
+        (small_half(here_teach), small_half(1 - here_teach)),
+    )
+    ahead = [grad]
+    for moment in sorted(agenda):
+        for unit, what in agenda[moment]:
+            ahead += getattr(unit, what)(*ahead)
+    first_rows = attn_out[0].result()
+    patch_grad = outward(first_rows[rows_own : rows_own + quarter])
+    small = first_rows[rows_own + quarter :].reshape(-1)
+    vector_grads = small[:vector_piece]
+    bias_grads = small[vector_piece : vector_piece + bias_piece]
+
+    attn_list = [first_rows[:rows_own]] + [unit.result() for unit in attn_out[1:]]
     mlp_list = [unit.result() for unit in mlp_out]
     head_grads = head_out.result()
     attn_grads = jnp.stack(
@@ -1082,26 +1164,60 @@
     correct_first = 1.0 - jnp.power(BETA, step_power)
     correct_second = 1.0 - jnp.power(BETA, step_power)
     weights = (patch_weight, attn_weight, mlp_weight, head_weight, vector_params, split_biases)
-    gradients = (patch_grad, attn_grads, mlp_grads, head_grads, vector_grads, bias_grads)
     firsts = (patch_first, attn_first, mlp_first, head_first, vector_first, bias_first)
     seconds = (patch_second, attn_second, mlp_second, head_second, vector_second, bias_second)
     decay_pieces = expand_params(split_params(decay_mask.astype(F32)))
-    results = [
-        adam_direction(gradients[slot], firsts[slot], seconds[slot], correct_first, correct_second)
-        for slot in range(6)
-    ]
-    directions = [
-        results[slot][2] + DECAY * decay_pieces[slot] * weights[slot] for slot in range(6)
-    ]
-    totals = sum_all(
+
+    def direct(gradient, first, second, weight, decay):
+        new_first, new_second, direction = adam_direction(
+            gradient, first, second, correct_first, correct_second
+        )
+        return new_first, new_second, direction + DECAY * decay * weight
+
+    device = lax.axis_index(("teach", "dp"))
+
+    def patch_cut(array):
+        return lax.dynamic_slice_in_dim(array, here_mp * quarter, quarter, 0)
+
+    def vector_part(array):
+        flat = padded(array.reshape(1, -1), vector_piece * mp * devices)[0]
+        at = (here_mp * devices + device) * vector_piece
+        return lax.dynamic_slice_in_dim(flat, at, vector_piece, 0)
+
+    def bias_part(array):
+        flat = padded(array.reshape(1, -1), bias_piece * devices)[0]
+        return lax.dynamic_slice_in_dim(flat, device * bias_piece, bias_piece, 0)
+
+    pieces = (patch_grad, attn_grads, mlp_grads, head_grads, vector_grads, bias_grads)
+    own_part = (patch_cut, None, None, None, vector_part, bias_part)
+    results = []
+    for slot, part in enumerate(own_part):
+        others = (firsts[slot], seconds[slot], weights[slot])
+        if part is not None:
+            others = [part(array) for array in others]
+        results.append(direct(pieces[slot], *others, decay_pieces[slot]))
+    totals, vector_grads, bias_grads, patch_grad = sum_and_gather(
         jnp.concatenate(
             [
                 squares_of(weights, mp_first, data_first),
-                squares_of(directions, mp_first, data_first),
+                squares_of([result[2] for result in results], 1.0, 1.0),
                 loss_part[0, :1],
             ]
+        ),
+        vector_grads,
+        bias_grads,
+        patch_grad,
+    )
+    gathered = {
+        0: patch_grad,
+        4: vector_grads[: vector_params.size].reshape(vector_params.shape),
+        5: bias_grads[: split_biases.size],
+    }
+    for slot, gradient in gathered.items():
+        results[slot] = direct(
+            gradient, firsts[slot], seconds[slot], weights[slot], decay_pieces[slot]
         )
-    )
+    directions = [result[2] for result in results]
     npar = (totals.size - 1) // 2
     weights_sq, direction_sq, loss_value = totals[:npar], totals[npar : 2 * npar], totals[2 * npar]
     weight_norm = jnp.sqrt(weights_sq)

time: 662 us -> 640 us (0.967)
  waiting for transfers between devices: 151 us -> 114 us
  local copies, waits for them, and re-layouts: 80.9 us -> 99.7 us
    ppermute x99 -> x92, waiting for transfers between devices: 137 us -> 98.2 us  [swap(): lax.ppermute(values, axis, [(rank, rank ^ distance) for rank in range(siz...]
    reduce_scatter x6 -> x5, waiting for transfers between devices: 0.05 us -> 15.9 us  [rows(): self.pieces = lax.psum_scatter(total, 'dp', scatter_dimension=0, tiled=True)]
    all_gather x3, waiting for transfers between devices: 13.3 us -> 0.01 us  [gather_dp(): lax.all_gather(jnp.concatenate(pieces, axis=1), 'dp', axis=0, tiled=True)]
    ppermute x99 -> x92, starting transfers between devices: 77 us -> 71.7 us  [swap(): lax.ppermute(values, axis, [(rank, rank ^ distance) for rank in range(siz...]
    unnamed x287 -> x263, local copies, waits for them, and re-layouts: 19.1 us -> 14.1 us
    convert_element_type x11 -> x10, other arithmetic: 20.9 us -> 18.2 us  [the longest x4 11.9 us: summed(): return jnp.concatenate(parts, axis=1).astype(BF).reshape(total.shape)]
  transfers between devices with their start and end apart: 108 -> 100, of which waited for: 35 -> 32; matrix products, arithmetic and copies ran while one was open for 21% -> 23% of each run, Pallas kernels for 32% -> 33%
where the time goes in v3:
time: 640 us; the launch traced here: 630 us
  Pallas kernels  215 us (34%)
  waiting for transfers between devices  114 us (18%)
  local copies, waits for them, and re-layouts  99.7 us (16%)
  other arithmetic  93.3 us (15%)
  starting transfers between devices  72 us (11%)
  between operations  25.6 us (4%)
  matrix products  9.95 us (2%)
    pallas_call x13, Pallas kernels, call(): pl.pallas_call(grouped, out_shape=out_shape, in_specs=specs, out_specs=ou...  215 us
    ppermute x92, waiting for transfers between devices, swap(): lax.ppermute(values, axis, [(rank, rank ^ distance) for rank in range(siz...  98.2 us
    ppermute x92, starting transfers between devices, swap(): lax.ppermute(values, axis, [(rank, rank ^ distance) for rank in range(siz...  71.7 us
    convert_element_type x20, other arithmetic, add_low(): return (left.astype(F32) + right.astype(F32)).astype(BF)  23.2 us
    reduce_scatter x5, waiting for transfers between devices, rows(): self.pieces = lax.psum_scatter(total, 'dp', scatter_dimension=0, tiled=True)  15.9 us
    unnamed x263, local copies, waits for them, and re-layouts  14.1 us
  transfers between devices with their start and end apart: 100, of which 32 were waited for; matrix products, arithmetic and copies ran while one was open for 23% of the time, Pallas kernels for 33%

profile of v3, /device:TPU:0, one launch (start us, length us, event | category | flops | bytes accessed | tf_op | source)
XLA Modules:
  0.0 629.9 jit_solution(15073406375044217935)
XLA Ops:
  20.7 3.0 collective-permute-start.8
  46.5 2.1 collective-permute-done.1
  49.2 2.9 collective-permute-start.2
  53.4 2.9 collective-permute-start.3
  57.6 4.0 collective-permute-start.4
  67.3 2.9 collective-permute-done.7
  81.0 2.8 convolution_add_fusion.refs_1_.refs_2_
  83.8 9.9 %collective-permute-done.12.refs_6_.refs_10_ = bf16[384,768]{1,0:T(8,128)(2,1)S(1)} collective-permute-done((bf16[384,768]{1,0:T(8,128)(2,1)S(1)}, bf16[384,768]{1,0:T(8,128)(2,1)S(1)}, u32[]{:S(2)}, u32[]{:S(2)}) %collective-permute-start.12) | collective-permute-done | bytes 589856 | tf_op jit(solution)/shard_map/ppermute | solution.py:532
  99.4 4.1 collective-permute-done.14.refs_8_.refs_12_
  114.2 20.4 %shard_map.427 = (bf16[576,768]{1,0:T(8,128)(2,1)}, bf16[4,576,576]{2,1,0:T(8,128)(2,1)}, bf16[4,576,192]{2,1,0:T(8,128)(2,1)}, f32[4,576,3]{2,1,0:T(8,128)}, f32[576,768]{1,0:T(8,128)}) custom-call(s32[1]{0:T(128)} %bitcast.3.refs_0_, f32[576,768]{1,0:T(8,128)} %convolution_add_fusion.refs_1_.refs_2_, f32[8,768]{1,0:T(8,128)} %pad.65.refs_2_.refs_3_, ...), custom_call_target="tpu_custom_call" | custom-call | flops 2300000000 | bytes 13987396 | tf_op jit(solution)/shard_map/pallas_call | solution.py:510
  140.8 10.7 %collective-permute-done.23.refs_7_.refs_10_ = bf16[192,1536]{1,0:T(8,128)(2,1)} collective-permute-done((bf16[192,1536]{1,0:T(8,128)(2,1)}, bf16[192,1536]{1,0:T(8,128)(2,1)}, u32[]{:S(2)}, u32[]{:S(2)}) %collective-permute-start.23) | collective-permute-done | bytes 589856 | tf_op jit(solution)/shard_map/ppermute | solution.py:532
  157.8 15.0 %shard_map.428 = (bf16[576,768]{1,0:T(8,128)(2,1)}, bf16[4,576,768]{2,1,0:T(8,128)(2,1)}, f32[4,576,768]{2,1,0:T(8,128)}, f32[576,768]{1,0:T(8,128)}) custom-call(s32[1]{0:T(128)} %bitcast.3.refs_0_, f32[576,768]{1,0:T(8,128)} %get-tuple-element.135.refs_1_.refs_2_, f32[8,768]{1,0:T(8,128)} %pad.65.refs_2_.refs_3_, f32[4,1,768]{2,1,0:T(1,128)} %copy.75.refs_25_.refs_3_, ...), custom_call_target="tpu_custom_call" | custom-call | flops 2300000000 | bytes 25104388 | tf_op jit(solution)/shard_map/pallas_call | solution.py:510
  174.8 6.9 %collective-permute-done.32.refs_8_.refs_12_ = bf16[192,768]{1,0:T(8,128)(2,1)S(1)} collective-permute-done((bf16[192,768]{1,0:T(8,128)(2,1)S(1)}, bf16[192,768]{1,0:T(8,128)(2,1)S(1)}, u32[]{:S(2)}, u32[]{:S(2)}) %collective-permute-start.32) | collective-permute-done | bytes 294944 | tf_op jit(solution)/shard_map/ppermute | solution.py:532
  192.5 20.5 %shard_map.429 = (bf16[576,768]{1,0:T(8,128)(2,1)}, bf16[4,576,576]{2,1,0:T(8,128)(2,1)}, bf16[4,576,192]{2,1,0:T(8,128)(2,1)}, f32[4,576,3]{2,1,0:T(8,128)}, f32[576,768]{1,0:T(8,128)}) custom-call(s32[1]{0:T(128)} %bitcast.3.refs_0_, f32[576,768]{1,0:T(8,128)} %get-tuple-element.141.refs_1_.refs_2_, f32[8,768]{1,0:T(8,128)} %pad.74.refs_2_.refs_3_, ...), custom_call_target="tpu_custom_call" | custom-call | flops 2300000000 | bytes 14317828 | tf_op jit(solution)/shard_map/pallas_call | solution.py:510
  213.0 4.5 collective-permute-done.48.refs_12_
  228.4 11.6 %collective-permute-done.41.refs_7_.refs_10_ = bf16[192,1536]{1,0:T(8,128)(2,1)} collective-permute-done((bf16[192,1536]{1,0:T(8,128)(2,1)S(1)}, bf16[192,1536]{1,0:T(8,128)(2,1)}, u32[]{:S(2)}, u32[]{:S(2)}) %collective-permute-start.41) | collective-permute-done | bytes 589856 | tf_op jit(solution)/shard_map/ppermute | solution.py:532
  245.0 14.8 %shard_map.430 = (bf16[576,768]{1,0:T(8,128)(2,1)}, bf16[4,576,768]{2,1,0:T(8,128)(2,1)}, f32[4,576,768]{2,1,0:T(8,128)}, f32[576,768]{1,0:T(8,128)}) custom-call(s32[1]{0:T(128)} %bitcast.3.refs_0_, f32[576,768]{1,0:T(8,128)} %get-tuple-element.148.refs_1_.refs_2_, f32[8,768]{1,0:T(8,128)} %pad.74.refs_2_.refs_3_, f32[4,1,768]{2,1,0:T(1,128)} %copy.76.refs_26_.refs_3_, ...), custom_call_target="tpu_custom_call" | custom-call | flops 2300000000 | bytes 24514564 | tf_op jit(solution)/shard_map/pallas_call | solution.py:510
  260.9 8.2 %shard_map.431 = (bf16[4,384,512]{2,1,0:T(8,128)(2,1)}, bf16[4,384,512]{2,1,0:T(8,128)(2,1)}, f32[4,1,512]{2,1,0:T(1,128)}, f32[576,768]{1,0:T(8,128)}, f32[8,768]{1,0:T(8,128)}, /*index=5*/f32[8,128]{1,0:T(8,128)}) custom-call(s32[1]{0:T(128)} %bitcast.3.refs_0_, f32[576,768]{1,0:T(8,128)} %get-tuple-element.151.refs_1_, f32[8,768]{1,0:T(8,128)} %pad.75.refs_2_, ...), custom_call_target="tpu_custom_call" | custom-call | flops 2300000000 | bytes 10370372 | tf_op jit(solution)/shard_map/pallas_call | solution.py:510
  269.6 13.8 %shard_map.432 = (f32[576,768]{1,0:T(8,128)}, bf16[2,384,1536]{2,1,0:T(8,128)(2,1)}, bf16[2,384,1536]{2,1,0:T(8,128)(2,1)}, f32[2,1,768]{2,1,0:T(1,128)}, f32[8,768]{1,0:T(8,128)}) custom-call(s32[1]{0:T(128)} %bitcast.3.refs_0_, f32[576,768]{1,0:T(8,128)} %get-tuple-element.154.refs_1_, f32[576,768]{1,0:T(8,128)} %get-tuple-element.148.refs_1_.refs_2_, ...), custom_call_target="tpu_custom_call" | custom-call | flops 2300000000 | bytes 32593924 | tf_op jit(solution)/shard_map/pallas_call | solution.py:510
  288.4 16.2 %shard_map.433 = (f32[576,768]{1,0:T(8,128)}, bf16[2,384,1536]{2,1,0:T(8,128)(2,1)}, bf16[2,384,1536]{2,1,0:T(8,128)(2,1)}, f32[2,1,768]{2,1,0:T(1,128)}, f32[8,768]{1,0:T(8,128)}) custom-call(s32[1]{0:T(128)} %bitcast.3.refs_0_, f32[576,768]{1,0:T(8,128)} %get-tuple-element.154.refs_1_, f32[576,768]{1,0:T(8,128)} %get-tuple-element.148.refs_1_.refs_2_, ...), custom_call_target="tpu_custom_call" | custom-call | flops 2300000000 | bytes 35543044 | tf_op jit(solution)/shard_map/pallas_call | solution.py:510
  310.0 17.7 %shard_map.434 = (f32[576,768]{1,0:T(8,128)}, bf16[2,384,768]{2,1,0:T(8,128)(2,1)}, bf16[2,384,768]{2,1,0:T(8,128)(2,1)}, f32[2,1,576]{2,1,0:T(1,128)}, f32[8,768]{1,0:T(8,128)}) custom-call(s32[1]{0:T(128)} %bitcast.3.refs_0_, f32[576,768]{1,0:T(8,128)} %get-tuple-element.163.refs_1_, f32[576,768]{1,0:T(8,128)} %get-tuple-element.141.refs_1_.refs_2_, ...), custom_call_target="tpu_custom_call" | custom-call | flops 2300000000 | bytes 21219076 | tf_op jit(solution)/shard_map/pallas_call | solution.py:510
  337.7 20.2 %shard_map.435 = (f32[576,768]{1,0:T(8,128)}, bf16[2,384,768]{2,1,0:T(8,128)(2,1)}, bf16[2,384,768]{2,1,0:T(8,128)(2,1)}, f32[2,1,576]{2,1,0:T(1,128)}, f32[8,768]{1,0:T(8,128)}) custom-call(s32[1]{0:T(128)} %bitcast.3.refs_0_, f32[576,768]{1,0:T(8,128)} %get-tuple-element.163.refs_1_, f32[576,768]{1,0:T(8,128)} %get-tuple-element.141.refs_1_.refs_2_, ...), custom_call_target="tpu_custom_call" | custom-call | flops 2300000000 | bytes 22595332 | tf_op jit(solution)/shard_map/pallas_call | solution.py:510
  361.1 13.8 %shard_map.436 = (f32[576,768]{1,0:T(8,128)}, bf16[2,384,1536]{2,1,0:T(8,128)(2,1)}, bf16[2,384,1536]{2,1,0:T(8,128)(2,1)}, f32[2,1,768]{2,1,0:T(1,128)}, f32[8,768]{1,0:T(8,128)}) custom-call(s32[1]{0:T(128)} %bitcast.3.refs_0_, f32[576,768]{1,0:T(8,128)} %get-tuple-element.181.refs_1_, f32[576,768]{1,0:T(8,128)} %get-tuple-element.135.refs_1_.refs_2_, ...), custom_call_target="tpu_custom_call" | custom-call | flops 2300000000 | bytes 32790532 | tf_op jit(solution)/shard_map/pallas_call | solution.py:510
  378.7 3.6 fusion.1.refs_19_
  382.3 16.2 %shard_map.437 = (f32[576,768]{1,0:T(8,128)}, bf16[2,384,1536]{2,1,0:T(8,128)(2,1)}, bf16[2,384,1536]{2,1,0:T(8,128)(2,1)}, f32[2,1,768]{2,1,0:T(1,128)}, f32[8,768]{1,0:T(8,128)}) custom-call(s32[1]{0:T(128)} %bitcast.3.refs_0_, f32[576,768]{1,0:T(8,128)} %get-tuple-element.181.refs_1_, f32[576,768]{1,0:T(8,128)} %get-tuple-element.135.refs_1_.refs_2_, ...), custom_call_target="tpu_custom_call" | custom-call | flops 2300000000 | bytes 37509124 | tf_op jit(solution)/shard_map/pallas_call | solution.py:510
  400.3 2.7 fusion.8.refs_20_
  408.2 3.1 add_convert_fusion.2
  414.3 17.7 %shard_map.438 = (f32[576,768]{1,0:T(8,128)}, bf16[2,384,768]{2,1,0:T(8,128)(2,1)}, bf16[2,384,768]{2,1,0:T(8,128)(2,1)}, f32[2,1,576]{2,1,0:T(1,128)}, f32[8,768]{1,0:T(8,128)}) custom-call(s32[1]{0:T(128)} %bitcast.3.refs_0_, f32[576,768]{1,0:T(8,128)} %get-tuple-element.196.refs_1_, f32[576,768]{1,0:T(8,128)} %convolution_add_fusion.refs_1_.refs_2_, ...), custom_call_target="tpu_custom_call" | custom-call | flops 2300000000 | bytes 21022468 | tf_op jit(solution)/shard_map/pallas_call | solution.py:510
  433.3 2.1 concatenate.213
  435.9 2.1 concatenate.215
  446.0 20.5 %shard_map.439 = (f32[576,768]{1,0:T(8,128)}, bf16[2,384,768]{2,1,0:T(8,128)(2,1)}, bf16[2,384,768]{2,1,0:T(8,128)(2,1)}, f32[2,1,576]{2,1,0:T(1,128)}, f32[8,768]{1,0:T(8,128)}) custom-call(s32[1]{0:T(128)} %bitcast.3.refs_0_, f32[576,768]{1,0:T(8,128)} %get-tuple-element.196.refs_1_, f32[576,768]{1,0:T(8,128)} %convolution_add_fusion.refs_1_.refs_2_, ...), custom_call_target="tpu_custom_call" | custom-call | flops 2300000000 | bytes 22202116 | tf_op jit(solution)/shard_map/pallas_call | solution.py:510
  466.5 2.8 fusion.83
  469.4 2.1 convolution_convert_fusion
  473.9 2.3 dynamic-slice_bitcast_fusion
  491.5 2.4 fusion.29
  493.9 3.6 fusion
  504.9 7.1 %collective-permute-done.84 = bf16[256,768]{1,0:T(8,128)(2,1)} collective-permute-done((bf16[256,768]{1,0:T(8,128)(2,1)}, bf16[256,768]{1,0:T(8,128)(2,1)}, u32[]{:S(2)}, u32[]{:S(2)}) %collective-permute-start.84) | collective-permute-done | bytes 393248 | tf_op jit(solution)/shard_map/ppermute | solution.py:532
  526.1 8.7 %collective-permute-done.86 = bf16[512,768]{1,0:T(8,128)(2,1)} collective-permute-done((bf16[512,768]{1,0:T(8,128)(2,1)}, bf16[512,768]{1,0:T(8,128)(2,1)}, u32[]{:S(2)}, u32[]{:S(2)}) %collective-permute-start.86) | collective-permute-done | bytes 786464 | tf_op jit(solution)/shard_map/ppermute | solution.py:532
  543.9 3.5 multiply_reduce_fusion
  547.4 15.9 %reduce-scatter.6.cloned.1.call-done = bf16[128,768]{1,0:T(8,128)(2,1)} async-done(((bf16[512,768]{1,0:T(8,128)(2,1)}), bf16[128,768]{1,0:T(8,128)(2,1)}) %reduce-scatter.6.cloned.1.call-update) | async-done | bytes 196624 | tf_op jit(solution)/shard_map/reduce_scatter | solution.py:673
  564.6 3.2 multiply_reduce_fusion.2
  573.8 2.7 concatenate.233
  576.6 2.7 concatenate.232
  581.7 3.4 collective-permute-done.88
  588.4 4.0 collective-permute-done.90
  595.4 5.8 collective-permute-done.91
  612.3 2.5 multiply_subtract_fusion.3
  618.4 2.5 multiply_subtract_fusion.5
  (745 shorter events, 232.4 us)
Async XLA Ops:
  7.2 64.7 %all-gather.4.cloned.1.call-start = ((), (), s32[]{:S(2)}) async-start(), calls=%async_computation.5 | async-start | bytes 1474560 | tf_op jit(solution)/shard_map/all_gather | solution.py:807
  17.8 81.6 %all-gather.6.cloned.1.call-start = ((), (), s32[]{:S(2)}) async-start(), calls=%async_computation.6 | async-start | bytes 1474560 | tf_op jit(solution)/shard_map/all_gather | solution.py:807
  20.7 119.0 %all-gather.8.cloned.1.call-start = ((), (), s32[]{:S(2)}) async-start(), calls=%async_computation.7 | async-start | bytes 2703360 | tf_op jit(solution)/shard_map/all_gather | solution.py:807
  20.7 43.5 %collective-permute-start.8 = (f32[2804]{0:T(1024)}, f32[2804]{0:T(1024)}, u32[]{:S(2)}, u32[]{:S(2)}) collective-permute-start(f32[2804]{0:T(1024)} %param.40), channel_id=1, source_target_pairs={{0,2},{2,0},{4,6},{6,4},{1,3},{3,1},{5,7},{7,5},{8,10},{10,8},{12,... | collective-permute-start | bytes 33656 | tf_op jit(solution)/shard_map/ppermute | solution.py:532
  23.7 41.4 %collective-permute-start.9 = (f32[2804]{0:T(1024)}, f32[2804]{0:T(1024)}, u32[]{:S(2)}, u32[]{:S(2)}) collective-permute-start(f32[2804]{0:T(1024)} %param.40), channel_id=1, source_target_pairs={{0,4},{2,6},{4,0},{6,2},{1,5},{3,7},{5,1},{7,3},{8,12},{10,14},{12... | collective-permute-start | bytes 33656 | tf_op jit(solution)/shard_map/ppermute | solution.py:532
  25.2 40.6 %collective-permute-start.10 = (f32[2804]{0:T(1024)}, f32[2804]{0:T(1024)}, u32[]{:S(2)}, u32[]{:S(2)}) collective-permute-start(f32[2804]{0:T(1024)} %param.40), channel_id=1, source_target_pairs={{0,6},{2,4},{4,2},{6,0},{1,7},{3,5},{5,3},{7,1},{8,14},{10,12},{12... | collective-permute-start | bytes 33656 | tf_op jit(solution)/shard_map/ppermute | solution.py:532
  25.9 17.8 %collective-permute-start = (f32[1]{0:T(128)}, f32[1]{0:T(128)}, u32[]{:S(2)}, u32[]{:S(2)}) collective-permute-start(f32[1]{0:T(128)} %bitcast.10), channel_id=1, source_target_pairs={{0,1},{1,0},{2,3},{3,2},{4,5},{5,4},{6,7},{7,6},{8,9},{9,8},{10,11... | collective-permute-start | bytes 20 | tf_op jit(solution)/shard_map/ppermute | solution.py:532
  27.5 39.8 %collective-permute-start.5 = (bf16[224,256]{1,0:T(8,128)(2,1)}, bf16[224,256]{1,0:T(8,128)(2,1)}, u32[]{:S(2)}, u32[]{:S(2)}) collective-permute-start(bf16[224,256]{1,0:T(8,128)(2,1)} %get-tuple-element.361), channel_id=1, source_target_pairs={{0,2},{2,0},{4,6},{6,4},{1,3},{3,1},{5,7},{7,5},{8,10},{10,8},{12,... | collective-permute-start | bytes 344072 | tf_op jit(solution)/shard_map/ppermute | solution.py:532
  33.0 490.2 %reduce-scatter.14.cloned.1.call-start = ((), (), s32[]{:S(2)}) async-start(), calls=%async_computation.12 | async-start | bytes 491520 | tf_op jit(solution)/shard_map/reduce_scatter | solution.py:673
  78.8 28.6 %collective-permute-start.16 = (bf16[384,768]{1,0:T(8,128)(2,1)S(1)}, bf16[384,768]{1,0:T(8,128)(2,1)}, u32[]{:S(2)}, u32[]{:S(2)}) collective-permute-start(bf16[384,768]{1,0:T(8,128)(2,1)S(1)} %get-tuple-element.131.refs_5_.refs_9_), channel_id=1, source_target_pairs={{0,1},{1,0},{2,3},{3,2},{4,5},{5,4},{6,7},{7,6},{8,9},{9,8},{10,11... | collective-permute-start | bytes 1769480 | tf_op jit(solution)/shard_map/ppermute | solution.py:532
  104.6 30.0 %collective-permute-start.21 = (bf16[384,1536]{1,0:T(8,128)(2,1)}, bf16[384,1536]{1,0:T(8,128)(2,1)S(1)}, u32[]{:S(2)}, u32[]{:S(2)}) collective-permute-start(bf16[384,1536]{1,0:T(8,128)(2,1)} %all-gather.6.cloned.1.call-done.refs_15_.refs_4_.refs_7_), channel_id=1, source_target_pairs={{0,2},{2,0},{4,6},{6,4},{1,3},{3,1},{5,7},{7,5},{8,10},{10,8},{12,... | collective-permute-start | bytes 3538952 | tf_op jit(solution)/shard_map/ppermute | solution.py:532
  105.4 29.2 %collective-permute-start.22 = (bf16[384,1536]{1,0:T(8,128)(2,1)}, bf16[384,1536]{1,0:T(8,128)(2,1)S(1)}, u32[]{:S(2)}, u32[]{:S(2)}) collective-permute-start(bf16[384,1536]{1,0:T(8,128)(2,1)} %all-gather.6.cloned.1.call-done.refs_15_.refs_4_.refs_7_), channel_id=1, source_target_pairs={{0,4},{2,6},{4,0},{6,2},{1,5},{3,7},{5,1},{7,3},{8,12},{10,14},{12... | collective-permute-start | bytes 3538952 | tf_op jit(solution)/shard_map/ppermute | solution.py:532
  139.1 17.8 %collective-permute-start.26 = (bf16[384,1536]{1,0:T(8,128)(2,1)S(1)}, bf16[384,1536]{1,0:T(8,128)(2,1)}, u32[]{:S(2)}, u32[]{:S(2)}) collective-permute-start(bf16[384,1536]{1,0:T(8,128)(2,1)S(1)} %collective-permute-done.21.refs_5_.refs_8_), channel_id=1, source_target_pairs={{0,1},{1,0},{2,3},{3,2},{4,5},{5,4},{6,7},{7,6},{8,9},{9,8},{10,11... | collective-permute-start | bytes 3538952 | tf_op jit(solution)/shard_map/ppermute | solution.py:532
  153.8 19.0 %collective-permute-start.30 = (bf16[384,768]{1,0:T(8,128)(2,1)S(1)}, bf16[384,768]{1,0:T(8,128)(2,1)S(1)}, u32[]{:S(2)}, u32[]{:S(2)}) collective-permute-start(bf16[384,768]{1,0:T(8,128)(2,1)S(1)} %slice.1100.refs_14_.refs_5_.refs_9_), channel_id=1, source_target_pairs={{0,2},{2,0},{4,6},{6,4},{1,3},{3,1},{5,7},{7,5},{8,10},{10,8},{12,... | collective-permute-start | bytes 1769480 | tf_op jit(solution)/shard_map/ppermute | solution.py:532
  182.5 40.3 %collective-permute-start.39 = (bf16[384,1536]{1,0:T(8,128)(2,1)S(1)}, bf16[384,1536]{1,0:T(8,128)(2,1)S(1)}, u32[]{:S(2)}, u32[]{:S(2)}) collective-permute-start(bf16[384,1536]{1,0:T(8,128)(2,1)S(1)} %slice.1102.refs_15_.refs_4_.refs_7_), channel_id=1, source_target_pairs={{0,2},{2,0},{4,6},{6,4},{1,3},{3,1},{5,7},{7,5},{8,10},{10,8},{12,... | collective-permute-start | bytes 3538952 | tf_op jit(solution)/shard_map/ppermute | solution.py:532
  183.6 39.1 %collective-permute-start.40 = (bf16[384,1536]{1,0:T(8,128)(2,1)S(1)}, bf16[384,1536]{1,0:T(8,128)(2,1)S(1)}, u32[]{:S(2)}, u32[]{:S(2)}) collective-permute-start(bf16[384,1536]{1,0:T(8,128)(2,1)S(1)} %slice.1102.refs_15_.refs_4_.refs_7_), channel_id=1, source_target_pairs={{0,4},{2,6},{4,0},{6,2},{1,5},{3,7},{5,1},{7,3},{8,12},{10,14},{12... | collective-permute-start | bytes 3538952 | tf_op jit(solution)/shard_map/ppermute | solution.py:532
  187.9 29.6 %collective-permute-start.48 = (bf16[384,512]{1,0:T(8,128)(2,1)}, bf16[384,512]{1,0:T(8,128)(2,1)}, u32[]{:S(2)}, u32[]{:S(2)}) collective-permute-start(bf16[384,512]{1,0:T(8,128)(2,1)} %slice.1103.refs_16_.refs_11_), channel_id=1, source_target_pairs={{0,2},{2,0},{4,6},{6,4},{1,3},{3,1},{5,7},{7,5},{8,10},{10,8},{12,... | collective-permute-start | bytes 1179656 | tf_op jit(solution)/shard_map/ppermute | solution.py:532
  188.7 29.7 %collective-permute-start.49 = (bf16[384,512]{1,0:T(8,128)(2,1)}, bf16[384,512]{1,0:T(8,128)(2,1)}, u32[]{:S(2)}, u32[]{:S(2)}) collective-permute-start(bf16[384,512]{1,0:T(8,128)(2,1)} %slice.1103.refs_16_.refs_11_), channel_id=1, source_target_pairs={{0,4},{2,6},{4,0},{6,2},{1,5},{3,7},{5,1},{7,3},{8,12},{10,14},{12... | collective-permute-start | bytes 1179656 | tf_op jit(solution)/shard_map/ppermute | solution.py:532
  222.7 18.2 %collective-permute-start.43 = (bf16[384,1536]{1,0:T(8,128)(2,1)}, bf16[384,1536]{1,0:T(8,128)(2,1)S(1)}, u32[]{:S(2)}, u32[]{:S(2)}) collective-permute-start(bf16[384,1536]{1,0:T(8,128)(2,1)} %copy-done.2), channel_id=1, source_target_pairs={{0,1},{1,0},{2,3},{3,2},{4,5},{5,4},{6,7},{7,6},{8,9},{9,8},{10,11... | collective-permute-start | bytes 3538952 | tf_op jit(solution)/shard_map/ppermute | solution.py:532
  222.7 18.7 %collective-permute-start.44 = (bf16[384,1536]{1,0:T(8,128)(2,1)S(1)}, bf16[384,1536]{1,0:T(8,128)(2,1)S(1)}, u32[]{:S(2)}, u32[]{:S(2)}) collective-permute-start(bf16[384,1536]{1,0:T(8,128)(2,1)S(1)} %collective-permute-done.39.refs_5_.refs_8_), channel_id=1, source_target_pairs={{0,1},{1,0},{2,3},{3,2},{4,5},{5,4},{6,7},{7,6},{8,9},{9,8},{10,11... | collective-permute-start | bytes 3538952 | tf_op jit(solution)/shard_map/ppermute | solution.py:532
  223.3 18.2 %collective-permute-start.45 = (bf16[384,1536]{1,0:T(8,128)(2,1)S(1)}, bf16[384,1536]{1,0:T(8,128)(2,1)S(1)}, u32[]{:S(2)}, u32[]{:S(2)}) collective-permute-start(bf16[384,1536]{1,0:T(8,128)(2,1)S(1)} %collective-permute-done.40.refs_6_.refs_9_), channel_id=1, source_target_pairs={{0,1},{1,0},{2,3},{3,2},{4,5},{5,4},{6,7},{7,6},{8,9},{9,8},{10,11... | collective-permute-start | bytes 3538952 | tf_op jit(solution)/shard_map/ppermute | solution.py:532
  240.9 18.9 %collective-permute-start.52 = (bf16[384,512]{1,0:T(8,128)(2,1)}, bf16[384,512]{1,0:T(8,128)(2,1)}, u32[]{:S(2)}, u32[]{:S(2)}) collective-permute-start(bf16[384,512]{1,0:T(8,128)(2,1)} %slice.1103.refs_16_.refs_11_), channel_id=1, source_target_pairs={{0,1},{1,0},{2,3},{3,2},{4,5},{5,4},{6,7},{7,6},{8,9},{9,8},{10,11... | collective-permute-start | bytes 1179656 | tf_op jit(solution)/shard_map/ppermute | solution.py:532
  241.5 18.4 %collective-permute-start.53 = (bf16[384,512]{1,0:T(8,128)(2,1)}, bf16[384,512]{1,0:T(8,128)(2,1)S(1)}, u32[]{:S(2)}, u32[]{:S(2)}) collective-permute-start(bf16[384,512]{1,0:T(8,128)(2,1)} %collective-permute-done.48.refs_12_), channel_id=1, source_target_pairs={{0,1},{1,0},{2,3},{3,2},{4,5},{5,4},{6,7},{7,6},{8,9},{9,8},{10,11... | collective-permute-start | bytes 1179656 | tf_op jit(solution)/shard_map/ppermute | solution.py:532
  242.0 18.0 %collective-permute-start.54 = (bf16[384,512]{1,0:T(8,128)(2,1)}, bf16[384,512]{1,0:T(8,128)(2,1)S(1)}, u32[]{:S(2)}, u32[]{:S(2)}) collective-permute-start(bf16[384,512]{1,0:T(8,128)(2,1)} %collective-permute-done.49.refs_13_), channel_id=1, source_target_pairs={{0,1},{1,0},{2,3},{3,2},{4,5},{5,4},{6,7},{7,6},{8,9},{9,8},{10,11... | collective-permute-start | bytes 1179656 | tf_op jit(solution)/shard_map/ppermute | solution.py:532
  283.5 24.3 %collective-permute-start.60 = (bf16[2,384,1536]{2,1,0:T(8,128)(2,1)}, bf16[2,384,1536]{2,1,0:T(8,128)(2,1)S(1)}, u32[]{:S(2)}, u32[]{:S(2)}) collective-permute-start(bf16[2,384,1536]{2,1,0:T(8,128)(2,1)} %get-tuple-element.160.refs_18_), channel_id=1, source_target_pairs={{0,1},{1,0},{2,3},{3,2},{4,5},{5,4},{6,7},{7,6},{8,9},{9,8},{10,11... | collective-permute-start | bytes 7077896 | tf_op jit(solution)/shard_map/ppermute | solution.py:532
  304.6 28.5 %collective-permute-start.65 = (bf16[2,384,1536]{2,1,0:T(8,128)(2,1)}, bf16[2,384,1536]{2,1,0:T(8,128)(2,1)}, u32[]{:S(2)}, u32[]{:S(2)}) collective-permute-start(bf16[2,384,1536]{2,1,0:T(8,128)(2,1)} %get-tuple-element.168.refs_19_), channel_id=1, source_target_pairs={{0,1},{1,0},{2,3},{3,2},{4,5},{5,4},{6,7},{7,6},{8,9},{9,8},{10,11... | collective-permute-start | bytes 7077896 | tf_op jit(solution)/shard_map/ppermute | solution.py:532
  304.9 22.8 %collective-permute-start.62 = (bf16[384,512]{1,0:T(8,128)(2,1)S(1)}, bf16[384,512]{1,0:T(8,128)(2,1)S(1)}, u32[]{:S(2)}, u32[]{:S(2)}) collective-permute-start(bf16[384,512]{1,0:T(8,128)(2,1)S(1)} %pad_maximum_fusion.16.refs_21_), channel_id=1, source_target_pairs={{0,4},{2,6},{4,0},{6,2},{1,5},{3,7},{5,1},{7,3},{8,12},{10,14},{12... | collective-permute-start | bytes 1179656 | tf_op jit(solution)/shard_map/ppermute | solution.py:532
  306.5 21.3 %collective-permute-start.61 = (bf16[384,512]{1,0:T(8,128)(2,1)S(1)}, bf16[384,512]{1,0:T(8,128)(2,1)S(1)}, u32[]{:S(2)}, u32[]{:S(2)}) collective-permute-start(bf16[384,512]{1,0:T(8,128)(2,1)S(1)} %pad_maximum_fusion.15.refs_20_), channel_id=1, source_target_pairs={{0,2},{2,0},{4,6},{6,4},{1,3},{3,1},{5,7},{7,5},{8,10},{10,8},{12,... | collective-permute-start | bytes 1179656 | tf_op jit(solution)/shard_map/ppermute | solution.py:532
  308.5 22.0 %collective-permute-start.63 = (bf16[192,1536]{1,0:T(8,128)(2,1)S(1)}, bf16[192,1536]{1,0:T(8,128)(2,1)}, u32[]{:S(2)}, u32[]{:S(2)}) collective-permute-start(bf16[192,1536]{1,0:T(8,128)(2,1)S(1)} %get-tuple-element.309.refs_22_), channel_id=1, source_target_pairs={{0,2},{2,0},{4,6},{6,4},{1,3},{3,1},{5,7},{7,5},{8,10},{10,8},{12,... | collective-permute-start | bytes 1769480 | tf_op jit(solution)/shard_map/ppermute | solution.py:532
  309.4 21.1 %collective-permute-start.64 = (bf16[192,1536]{1,0:T(8,128)(2,1)S(1)}, bf16[192,1536]{1,0:T(8,128)(2,1)}, u32[]{:S(2)}, u32[]{:S(2)}) collective-permute-start(bf16[192,1536]{1,0:T(8,128)(2,1)S(1)} %get-tuple-element.308.refs_23_), channel_id=1, source_target_pairs={{0,4},{2,6},{4,0},{6,2},{1,5},{3,7},{5,1},{7,3},{8,12},{10,14},{12... | collective-permute-start | bytes 1769480 | tf_op jit(solution)/shard_map/ppermute | solution.py:532
  327.7 30.5 %collective-permute-start.66 = (bf16[2,384,768]{2,1,0:T(8,128)(2,1)}, bf16[2,384,768]{2,1,0:T(8,128)(2,1)S(1)}, u32[]{:S(2)}, u32[]{:S(2)}) collective-permute-start(bf16[2,384,768]{2,1,0:T(8,128)(2,1)} %get-tuple-element.174.refs_20_), channel_id=1, source_target_pairs={{0,1},{1,0},{2,3},{3,2},{4,5},{5,4},{6,7},{7,6},{8,9},{9,8},{10,11... | collective-permute-start | bytes 3538952 | tf_op jit(solution)/shard_map/ppermute | solution.py:532
  329.9 195.2 %reduce-scatter.8.cloned.1.call-start = ((), (), s32[]{:S(2)}) async-start(), calls=%async_computation.9 | async-start | bytes 737280 | tf_op jit(solution)/shard_map/reduce_scatter | solution.py:673
  331.8 46.0 %collective-permute-start.67 = (bf16[384,1536]{1,0:T(8,128)(2,1)S(1)}, bf16[384,1536]{1,0:T(8,128)(2,1)}, u32[]{:S(2)}, u32[]{:S(2)}) collective-permute-start(bf16[384,1536]{1,0:T(8,128)(2,1)S(1)} %pad_maximum_fusion.1.refs_22_), channel_id=1, source_target_pairs={{0,2},{2,0},{4,6},{6,4},{1,3},{3,1},{5,7},{7,5},{8,10},{10,8},{12,... | collective-permute-start | bytes 3538952 | tf_op jit(solution)/shard_map/ppermute | solution.py:532
  336.7 41.1 %collective-permute-start.68 = (bf16[384,1536]{1,0:T(8,128)(2,1)S(1)}, bf16[384,1536]{1,0:T(8,128)(2,1)}, u32[]{:S(2)}, u32[]{:S(2)}) collective-permute-start(bf16[384,1536]{1,0:T(8,128)(2,1)S(1)} %pad_maximum_fusion.2.refs_23_), channel_id=1, source_target_pairs={{0,4},{2,6},{4,0},{6,2},{1,5},{3,7},{5,1},{7,3},{8,12},{10,14},{12... | collective-permute-start | bytes 3538952 | tf_op jit(solution)/shard_map/ppermute | solution.py:532
  358.0 18.1 %collective-permute-start.71 = (bf16[2,384,768]{2,1,0:T(8,128)(2,1)}, bf16[2,384,768]{2,1,0:T(8,128)(2,1)}, u32[]{:S(2)}, u32[]{:S(2)}) collective-permute-start(bf16[2,384,768]{2,1,0:T(8,128)(2,1)} %get-tuple-element.185.refs_17_), channel_id=1, source_target_pairs={{0,1},{1,0},{2,3},{3,2},{4,5},{5,4},{6,7},{7,6},{8,9},{9,8},{10,11... | collective-permute-start | bytes 3538952 | tf_op jit(solution)/shard_map/ppermute | solution.py:532
  375.0 33.2 %collective-permute-start.74 = (bf16[2,384,1536]{2,1,0:T(8,128)(2,1)}, bf16[2,384,1536]{2,1,0:T(8,128)(2,1)}, u32[]{:S(2)}, u32[]{:S(2)}) collective-permute-start(bf16[2,384,1536]{2,1,0:T(8,128)(2,1)} %get-tuple-element.189.refs_18_), channel_id=1, source_target_pairs={{0,1},{1,0},{2,3},{3,2},{4,5},{5,4},{6,7},{7,6},{8,9},{9,8},{10,11... | collective-permute-start | bytes 7077896 | tf_op jit(solution)/shard_map/ppermute | solution.py:532
  375.2 23.4 %collective-permute-start.72 = (bf16[384,768]{1,0:T(8,128)(2,1)S(1)}, bf16[384,768]{1,0:T(8,128)(2,1)S(1)}, u32[]{:S(2)}, u32[]{:S(2)}) collective-permute-start(bf16[384,768]{1,0:T(8,128)(2,1)S(1)} %pad_maximum_fusion.10.refs_20_), channel_id=1, source_target_pairs={{0,2},{2,0},{4,6},{6,4},{1,3},{3,1},{5,7},{7,5},{8,10},{10,8},{12,... | collective-permute-start | bytes 1769480 | tf_op jit(solution)/shard_map/ppermute | solution.py:532
  377.8 20.8 %collective-permute-start.73 = (bf16[384,768]{1,0:T(8,128)(2,1)S(1)}, bf16[384,768]{1,0:T(8,128)(2,1)S(1)}, u32[]{:S(2)}, u32[]{:S(2)}) collective-permute-start(bf16[384,768]{1,0:T(8,128)(2,1)S(1)} %pad_maximum_fusion.11.refs_21_), channel_id=1, source_target_pairs={{0,4},{2,6},{4,0},{6,2},{1,5},{3,7},{5,1},{7,3},{8,12},{10,14},{12... | collective-permute-start | bytes 1769480 | tf_op jit(solution)/shard_map/ppermute | solution.py:532
  403.0 137.1 %reduce-scatter.12.cloned.1.call-start = ((), (), s32[]{:S(2)}) async-start(), calls=%async_computation.11 | async-start | bytes 1474560 | tf_op jit(solution)/shard_map/reduce_scatter | solution.py:673
  407.4 34.0 %collective-permute-start.77 = (bf16[2,384,1536]{2,1,0:T(8,128)(2,1)S(1)}, bf16[2,384,1536]{2,1,0:T(8,128)(2,1)}, u32[]{:S(2)}, u32[]{:S(2)}) collective-permute-start(bf16[2,384,1536]{2,1,0:T(8,128)(2,1)S(1)} %copy-done.31), channel_id=1, source_target_pairs={{0,1},{1,0},{2,3},{3,2},{4,5},{5,4},{6,7},{7,6},{8,9},{9,8},{10,11... | collective-permute-start | bytes 7077896 | tf_op jit(solution)/shard_map/ppermute | solution.py:532
  407.5 133.7 %reduce-scatter.10.cloned.1.call-start = ((), (), s32[]{:S(2)}) async-start(), calls=%async_computation.10 | async-start | bytes 1474560 | tf_op jit(solution)/shard_map/reduce_scatter | solution.py:673
  412.4 26.3 %collective-permute-start.75 = (bf16[192,1536]{1,0:T(8,128)(2,1)}, bf16[192,1536]{1,0:T(8,128)(2,1)}, u32[]{:S(2)}, u32[]{:S(2)}) collective-permute-start(bf16[192,1536]{1,0:T(8,128)(2,1)} %get-tuple-element.307.refs_21_), channel_id=1, source_target_pairs={{0,2},{2,0},{4,6},{6,4},{1,3},{3,1},{5,7},{7,5},{8,10},{10,8},{12,... | collective-permute-start | bytes 1769480 | tf_op jit(solution)/shard_map/ppermute | solution.py:532
  413.2 25.5 %collective-permute-start.76 = (bf16[192,1536]{1,0:T(8,128)(2,1)}, bf16[192,1536]{1,0:T(8,128)(2,1)}, u32[]{:S(2)}, u32[]{:S(2)}) collective-permute-start(bf16[192,1536]{1,0:T(8,128)(2,1)} %get-tuple-element.306.refs_22_), channel_id=1, source_target_pairs={{0,4},{2,6},{4,0},{6,2},{1,5},{3,7},{5,1},{7,3},{8,12},{10,14},{12... | collective-permute-start | bytes 1769480 | tf_op jit(solution)/shard_map/ppermute | solution.py:532
  440.0 53.9 %collective-permute-start.79 = (bf16[384,1536]{1,0:T(8,128)(2,1)S(1)}, bf16[384,1536]{1,0:T(8,128)(2,1)}, u32[]{:S(2)}, u32[]{:S(2)}) collective-permute-start(bf16[384,1536]{1,0:T(8,128)(2,1)S(1)} %pad_maximum_fusion.3.refs_21_), channel_id=1, source_target_pairs={{0,2},{2,0},{4,6},{6,4},{1,3},{3,1},{5,7},{7,5},{8,10},{10,8},{12,... | collective-permute-start | bytes 3538952 | tf_op jit(solution)/shard_map/ppermute | solution.py:532
  444.9 49.0 %collective-permute-start.80 = (bf16[384,1536]{1,0:T(8,128)(2,1)S(1)}, bf16[384,1536]{1,0:T(8,128)(2,1)}, u32[]{:S(2)}, u32[]{:S(2)}) collective-permute-start(bf16[384,1536]{1,0:T(8,128)(2,1)S(1)} %pad_maximum_fusion.4.refs_22_), channel_id=1, source_target_pairs={{0,4},{2,6},{4,0},{6,2},{1,5},{3,7},{5,1},{7,3},{8,12},{10,14},{12... | collective-permute-start | bytes 3538952 | tf_op jit(solution)/shard_map/ppermute | solution.py:532
  503.3 60.0 %reduce-scatter.6.cloned.1.call-start = ((), (), s32[]{:S(2)}) async-start(), calls=%async_computation.8 | async-start | bytes 983040 | tf_op jit(solution)/shard_map/reduce_scatter | solution.py:673
  515.6 19.2 %collective-permute-start.86 = (bf16[512,768]{1,0:T(8,128)(2,1)}, bf16[512,768]{1,0:T(8,128)(2,1)}, u32[]{:S(2)}, u32[]{:S(2)}) collective-permute-start(bf16[512,768]{1,0:T(8,128)(2,1)} %fusion.14), channel_id=1, source_target_pairs={{0,4},{2,6},{4,0},{6,2},{1,5},{3,7},{5,1},{7,3},{8,12},{10,14},{12... | collective-permute-start | bytes 2359304 | tf_op jit(solution)/shard_map/ppermute | solution.py:532
  517.8 18.7 %collective-permute-start.85 = (bf16[512,768]{1,0:T(8,128)(2,1)S(1)}, bf16[512,768]{1,0:T(8,128)(2,1)}, u32[]{:S(2)}, u32[]{:S(2)}) collective-permute-start(bf16[512,768]{1,0:T(8,128)(2,1)S(1)} %pad_maximum_fusion.7), channel_id=1, source_target_pairs={{0,2},{2,0},{4,6},{6,4},{1,3},{3,1},{5,7},{7,5},{8,10},{10,8},{12,... | collective-permute-start | bytes 2359304 | tf_op jit(solution)/shard_map/ppermute | solution.py:532
  (182 other events, 1200.0 us)
Sparse Core Ops, SparseCore 0:
  17.9 33.1 all-gather.3
  53.2 29.5 all-gather.5
  84.4 46.3 all-gather.7
  330.1 21.5 reduce-scatter.13
  403.1 22.3 reduce-scatter.7
  427.8 27.5 reduce-scatter.11
  503.4 29.1 reduce-scatter.9
  539.3 23.9 reduce-scatter.5

commit v4 on v3

--- a/solution.py
+++ b/solution.py
@@ -76,23 +76,40 @@
     return jnp.sum(values, axis=0, keepdims=True)
 
 
-def weight_copies(place_ref, steps, own, other, buf, sems):
+def tiled(half, rows):
+    return rows if rows % 16 == 0 else half
+
+
+def weight_copies(place_ref, run, steps, own, other, buf, sems, columns=(0, None)):
     half = own[0].shape[0]
     here = place_ref[0]
+    low = columns[0]
+    width = buf.shape[2]
     slots, sem = [], 0
     for slot, step in enumerate(steps):
         pieces = (FAR, FAR + 1) if step == FAR else (step,)
         copies = []
         for piece in pieces:
             size = half // len(pieces)
-            for source, core in ((own[piece], here), (other[piece], 1 - here)):
-                at = pl.multiple_of(core * half + (piece - pieces[0]) * size, 64)
-                copies.append(
-                    pltpu.make_async_copy(source, buf.at[slot, pl.ds(at, size)], sems.at[sem])
-                )
-                sem += 1
+            unit = min(run, size)
+            for at in range(0, size, unit):
+                row = (piece - pieces[0]) * size + at
+                for source, core in ((own[piece], here), (other[piece], 1 - here)):
+                    target = (row // run) * 2 * run + core * run + row % run
+                    copies.append(
+                        pltpu.make_async_copy(
+                            source.at[pl.ds(at, unit), pl.ds(low, width)],
+                            buf.at[slot, pl.ds(pl.multiple_of(target, 16), unit)],
+                            sems.at[sem],
+                        )
+                    )
+                    sem += 1
         slots.append(copies)
     return slots
+
+
+def copy_count(half, run, count):
+    return 2 * count * max(half // run, 2)
 
 
 def start_all(slots):
@@ -110,14 +127,17 @@
                 copy.wait()
 
 
-def split_out(half, place_ref, grad_buf, mine_ref, other_ref, slot):
-    mine = pl.multiple_of(place_ref[0] * half, 128)
-    theirs = pl.multiple_of((1 - place_ref[0]) * half, 128)
-    mine_ref[slot] = grad_buf[pl.ds(mine, half), :]
-    other_ref[slot] = grad_buf[pl.ds(theirs, half), :]
+def split_out(half, run, place_ref, grad_buf, mine_ref, other_ref, slot):
+    here = place_ref[0]
+    for at in range(0, half, run):
+        mine = pl.multiple_of(2 * at + here * run, 16)
+        theirs = pl.multiple_of(2 * at + (1 - here) * run, 16)
+        mine_ref[slot, at : at + run] = grad_buf[pl.ds(mine, run), :]
+        other_ref[slot, at : at + run] = grad_buf[pl.ds(theirs, run), :]
 
 
 def attn_forward_kernel(
+    run,
     mp,
     ni,
     wl,
@@ -137,7 +157,7 @@
     sems,
 ):
     now = pl.program_id(0)
-    slots = weight_copies(place_ref, range(mp), own, other, buf, sems)
+    slots = weight_copies(place_ref, run, range(mp), own, other, buf, sems)
 
     @pl.when(now == 0)
     def _():
@@ -169,6 +189,7 @@
 
 
 def mlp_forward_kernel(
+    run,
     mp,
     chunk,
     place_ref,
@@ -186,7 +207,7 @@
 ):
     now = pl.program_id(0)
     fl = hidden_ref.shape[2]
-    slots = weight_copies(place_ref, range(mp), own, other, buf, sems)
+    slots = weight_copies(place_ref, run, range(mp), own, other, buf, sems)
 
     @pl.when(now == 0)
     def _():
@@ -208,6 +229,8 @@
 
 
 def head_kernel(
+    run,
+    columns,
     mp,
     ni,
     wc,
@@ -237,7 +260,7 @@
     sems,
 ):
     half = mine_ref.shape[1]
-    slots = weight_copies(place_ref, range(mp), own, other, buf, sems)
+    slots = weight_copies(place_ref, run, range(mp), own, other, buf, sems, columns)
     start_all(slots)
     cls_buf[...] = jnp.zeros_like(cls_buf)
     dist_buf[...] = jnp.zeros_like(dist_buf)
@@ -295,7 +318,7 @@
         low_c, low_d = grad_c.astype(BF), grad_d.astype(BF)
         gw_buf[:, :wc] = dot_tn(final_c, low_c).astype(BF)
         gw_buf[:, wc:] = dot_tn(final_d, low_d).astype(BF)
-        split_out(half, place_ref, gw_buf, mine_ref, other_ref, block)
+        split_out(half, run, place_ref, gw_buf, mine_ref, other_ref, block)
         gfin_c += dot_nt(low_c, buf[block, :, :wc])
         gfin_d += dot_nt(low_d, buf[block, :, wc:])
     vgrad_ref[...] = jnp.zeros_like(vgrad_ref)
@@ -310,6 +333,7 @@
 
 
 def mlp_backward_kernel(
+    run,
     steps,
     last,
     place_ref,
@@ -341,7 +365,7 @@
     now = pl.program_id(0)
     fl = hidden_ref.shape[2]
     half = mine_ref.shape[1]
-    slots = weight_copies(place_ref, steps, own, other, buf, sems)
+    slots = weight_copies(place_ref, run, steps, own, other, buf, sems)
 
     @pl.when(now == 0)
     def _():
@@ -361,7 +385,7 @@
     gmid_ref[...] += dot_nt(gup, buf[now, :, :fl])
     gw_buf[:, :fl] = dot_nn(second_t[...], gup).astype(BF)
     gw_buf[:, fl:] = dot_nn(branch_t[...], hidden_ref[0]).astype(BF)
-    split_out(half, place_ref, gw_buf, mine_ref, other_ref, 0)
+    split_out(half, run, place_ref, gw_buf, mine_ref, other_ref, 0)
     if last:
 
         @pl.when(now == len(steps) - 1)
@@ -378,6 +402,7 @@
 
 
 def attn_backward_kernel(
+    run,
     ni,
     wl,
     steps,
@@ -414,7 +439,7 @@
     ) = rest
     now = pl.program_id(0)
     half = mine_ref.shape[1]
-    slots = weight_copies(place_ref, steps, own, other, buf, sems)
+    slots = weight_copies(place_ref, run, steps, own, other, buf, sems)
 
     @pl.when(now == 0)
     def _():
@@ -452,7 +477,7 @@
     gres_ref[...] += dot_nt(gqkv, buf[now, :, : 3 * wl])
     gw_buf[:, : 3 * wl] = dot_nn(first_t[...], gqkv).astype(BF)
     gw_buf[:, 3 * wl :] = dot_nn(mixed_t[...], att_ref[0]).astype(BF)
-    split_out(half, place_ref, gw_buf, mine_ref, other_ref, 0)
+    split_out(half, run, place_ref, gw_buf, mine_ref, other_ref, 0)
     if last:
 
         @pl.when(now == len(steps) - 1)
@@ -540,13 +565,16 @@
         near = tie(self.near, *behind)
         self.own = [near, swap(near, "mp", 1), swap(near, "mp", 2)]
         self.other = [swap(near, "teach", 1)]
+        return [near]
 
     def corner(self, *behind):
         near, by_one, by_two = self.own
         cut = near.shape[0] // 2
         by_one, by_two = tie((by_one, by_two), *behind)
-        self.own = [near, by_one, by_two, swap(by_two[:cut], "mp", 1), swap(by_one[cut:], "mp", 2)]
+        lower, upper = by_two[:cut], by_one[cut:]
+        self.own = [near, by_one, by_two, swap(lower, "mp", 1), swap(upper, "mp", 2)]
         self.other += [swap(by_one, "teach", 1), swap(by_two, "teach", 1)]
+        return [lower, upper]
 
     def cores(self, *behind):
         far = tie(tuple(self.own[3:]), *behind)
@@ -575,29 +603,43 @@
     return values
 
 
+def join_kernel(sizes, bit_ref, own_ref, got_ref, out_ref):
+    first = bit_ref[0] == 0
+    size = sizes[0]
+    out_ref[:size] = own_ref[:size] + got_ref[:size]
+    at, to = size, size
+    for size in sizes[1:]:
+        own, got = own_ref[at : at + size], got_ref[at : at + size]
+        out_ref[to : to + size] = jnp.where(first, own, got)
+        out_ref[to + size : to + 2 * size] = jnp.where(first, got, own)
+        at, to = at + size, to + 2 * size
+
+
 def sum_and_gather(values, everywhere, cores, square):
+    parts = jnp.concatenate([values, everywhere, cores])
+    sizes = [values.shape[0], everywhere.shape[0], cores.shape[0]]
     for axis in ("dp", "teach", "mp"):
         distance = 1
+        if axis == "mp":
+            cores = parts[sizes[0] + sizes[1] :]
+            parts, sizes = parts[: sizes[0] + sizes[1]], sizes[:2]
         while distance < lax.axis_size(axis):
-            parts = [everywhere, square] if axis == "mp" else [everywhere, cores]
-            sent = jnp.concatenate([values] + [part.reshape(-1) for part in parts])
-            got = swap(sent, axis, distance)
-            first = (lax.axis_index(axis) // distance) % 2 == 0
-            at = values.size
-            values = values + got[:at]
-            doubled = []
-            for part in parts:
-                new = got[at : at + part.size].reshape(part.shape)
-                at += part.size
-                doubled.append(
-                    jnp.concatenate([jnp.where(first, part, new), jnp.where(first, new, part)])
-                )
+            got = swap(parts, axis, distance)
+            bit = (lax.axis_index(axis) // distance) % 2
+            new_sizes = [sizes[0], *[2 * size for size in sizes[1:]]]
+            parts = call(
+                functools.partial(join_kernel, sizes),
+                [((sum(new_sizes), 128), F32)],
+                [],
+                [("smem", bit.astype(jnp.int32).reshape(1)), parts, got],
+            )[0]
+            sizes = new_sizes
             if axis == "mp":
-                everywhere, square = doubled
-            else:
-                everywhere, cores = doubled
+                other = swap(square, axis, distance)
+                pair = [jnp.where(bit == 0, square, other), jnp.where(bit == 0, other, square)]
+                square = jnp.concatenate(pair)
             distance *= 2
-    return values, everywhere, cores, square
+    return parts[: sizes[0]], parts[sizes[0] :], cores, square
 
 
 def gather_mp(values):
@@ -772,12 +814,18 @@
     wc = -(-cl // 128) * 128
     head_row = 6 * L
 
+    run = tiled(half, rows_own)
+
     def inward(values):
+        if run == rows_own:
+            return values
         lead = values.shape[:-1]
         cut = values.reshape(*lead, dp, teach, rows_own)
         return jnp.swapaxes(cut, -3, -2).reshape(*lead, D)
 
     def outward(values):
+        if run == rows_own:
+            return values
         lead = values.shape[:-1]
         cut = values.reshape(*lead, teach, dp, rows_own)
         return jnp.swapaxes(cut, -3, -2).reshape(*lead, D)
@@ -787,9 +835,9 @@
     def take(array):
         return lax.dynamic_slice_in_dim(array, here_mp * ni, ni, 0)
 
+    weight_part = jnp.sum(image_weight).reshape(1)
     patches, grid_sizes, label_ids = take(patches), take(grid_sizes), take(label_ids)
     label_mix, image_weight = take(label_mix), take(image_weight)
-    weight_sum = sum_all(jnp.sum(image_weight).reshape(1))[0]
 
     patch_low = inward(patch_weight).astype(BF)
     attn_low = [
@@ -812,15 +860,12 @@
         return cuts
 
     near = gather_dp(patch_low, attn_low[0]) + gather_dp(mlp_low[0])
+    mlp_low[-1] = jnp.concatenate([mlp_low[-1], head_low], axis=1)
+    head_columns = (2 * fl, 2 * wc)
     rest = [piece for layer in range(1, L) for piece in (attn_low[layer], mlp_low[layer])]
-    near += gather_dp(*rest, head_low)
+    near += gather_dp(*rest)
+    bias_all = gather_mp(split_biases)
     teacher_all = gather_mp(jnp.pad(teacher_head, ((0, 0), (0, wc - cl))))
-    bias_all = gather_mp(split_biases)
-    near[0], near[1] = tie((near[0], near[1]), weight_sum, teacher_all, bias_all)
-    patch_own = near[0]
-    patch_other = swap(patch_own, "teach", 1)
-    units = [Gather(piece) for piece in near[1:]]
-    attn_units, mlp_units, head_unit = units[0:-1:2], units[1:-1:2], units[-1]
 
     vec_in = inward(vector_params)
     layer_vecs = [
@@ -873,6 +918,38 @@
         / jnp.sum(live_float, axis=1, keepdims=True)
     ).astype(BF)
 
+    ranks = here_mp ^ jnp.arange(mp, dtype=jnp.int32)
+    quarter = rows_own // mp
+    patch_rows = jnp.pad(patches, ((0, 0), (0, RP - PMAX), (0, 0))).reshape(ni * RP, -1)
+    sides = here_teach ^ jnp.arange(teach, dtype=jnp.int32)
+    patches_t = patch_rows.T.reshape(dp, teach, mp, quarter, ni * RP).transpose(1, 2, 0, 3, 4)
+    patches_t = patches_t[sides][:, ranks].reshape(-1, ni * RP)
+
+    def wide(values):
+        return jnp.pad(values.reshape(ni, -1), ((0, HR - ni), (0, 0)))
+
+    lanes = jnp.arange(wc, dtype=jnp.int32)
+    class_ids = jnp.where(lanes[None] < cl, ranks[:, None] * cl + lanes[None], -1)[:, None]
+    head_small = [class_ids, wide(label_ids), wide(label_mix), wide(pooled)]
+
+    near[0], near[1] = tie(
+        (near[0], near[1]),
+        *attn_bias,
+        *up_bias,
+        head_bias,
+        *layer_vecs,
+        final_vec,
+        live_rows,
+        sources,
+        patches_t,
+        *head_small,
+        teacher_all,
+    )
+    patch_own = near[0]
+    patch_other = swap(patch_own, "teach", 1)
+    units = [Gather(piece) for piece in near[1:]]
+    attn_units, mlp_units, head_unit = units[0::2], units[1::2], units[-1]
+
     first_core = here_teach == 0
     patch_full = jnp.stack(
         [
@@ -881,57 +958,31 @@
         ],
         axis=1,
     ).reshape(D, D)
-    patch_rows = jnp.pad(patches, ((0, 0), (0, RP - PMAX), (0, 0))).reshape(ni * RP, -1)
     residual = dot_nn(patch_rows, patch_full) + jnp.dot(
         sources, vec_in[head_row + 2 :], precision=HIGH
     )
 
     n = ni * RP
-    parts = 2 * mp + 2
+    parts = copy_count(half, run, mp)
     saved = []
-    def wide(values):
-        return jnp.pad(values.reshape(ni, -1), ((0, HR - ni), (0, 0)))
-
-    ranks = here_mp ^ jnp.arange(mp, dtype=jnp.int32)
-    lanes = jnp.arange(wc, dtype=jnp.int32)
-    class_ids = jnp.where(lanes[None] < cl, ranks[:, None] * cl + lanes[None], -1)[:, None]
-    head_small = [
-        class_ids,
-        wide(label_ids),
-        wide(label_mix),
-        wide(0.5 * image_weight / weight_sum),
-        wide(image_weight / weight_sum),
-        wide(pooled),
-    ]
-
-    first_unit = units[0]
-    first_unit.square()
-    first_unit.corner(residual)
-    units[1].square(*first_unit.own[3:])
+    units[0].square()
+    units[0].corner(residual)
+    units[1].square(*units[0].own[3:])
 
     def arrive(at, done):
         here = units[at]
-        ahead = units[at + 1 : at + 2] if at < len(units) - 3 else units[at + 1 :]
-        if at == 0:
-            here.cores()
-            return [units[1].own[0], *head_small, head_bias, *attn_bias, *up_bias]
-        if at < len(units) - 2:
+        ahead = units[at + 1 : at + 2]
+        if at > 0:
             here.corner(done)
             for unit in ahead:
                 unit.square(*here.own[3:], done)
-            here.cores(*[unit.own[0] for unit in ahead])
-            return [unit.own[0] for unit in ahead]
-        if at == len(units) - 2:
-            here.corner(done)
-            units[-1].corner(done)
-            here.cores()
-            units[-1].cores()
-        return []
+        here.cores(*[unit.own[0] for unit in ahead])
+        return [unit.own[0] for unit in ahead]
 
     for layer in range(L):
         sending = arrive(2 * layer, residual)
         first, qkv, attended, lse, middle = call(
-            functools.partial(attn_forward_kernel, mp, ni, wl),
+            functools.partial(attn_forward_kernel, run, mp, ni, wl),
             [
                 ((n, D), BF),
                 ((mp, n, 3 * wl), BF, "each"),
@@ -945,9 +996,17 @@
             range(mp),
             sending,
         )
+        if layer == 0:
+            weight_sum = sum_over(sum_over(tie(weight_part, middle), "teach"), "dp")[0]
+            shares = [
+                wide(0.5 * image_weight / weight_sum),
+                wide(image_weight / weight_sum),
+            ]
+            for unit in units[2:]:
+                unit.near = tie(unit.near, *shares)
         sending = arrive(2 * layer + 1, middle)
         second, hidden, slope, output = call(
-            functools.partial(mlp_forward_kernel, mp, n // 4),
+            functools.partial(mlp_forward_kernel, run, mp, n // 4),
             [((n, D), BF), ((mp, n, fl), BF, "each"), ((mp, n, fl), F32, "each"), ((n, D), F32)],
             [pltpu.VMEM((mp, D, 2 * fl), BF), pltpu.SemaphoreType.DMA((parts,))],
             [place, middle, layer_vecs[layer], ("each", up_bias[layer])]
@@ -959,7 +1018,7 @@
         residual = output
 
     head_mine, head_other, head_bgrad, grad, final_vgrad, loss_part = call(
-        functools.partial(head_kernel, mp, ni, wc),
+        functools.partial(head_kernel, run, head_columns, mp, ni, wc),
         [
             ((mp, half, 2 * wc), BF),
             ((mp, half, 2 * wc), BF),
@@ -980,7 +1039,9 @@
             residual,
             final_vec,
             head_bias,
-            *head_small,
+            *head_small[:3],
+            *shares,
+            head_small[3],
             teacher_all,
             *head_unit.refs(),
         ],
@@ -1020,7 +1081,7 @@
         for steps in PARTS:
             count = len(steps)
             gmid, mine, other, bgrad, mlp_vgrad = call(
-                functools.partial(mlp_backward_kernel, steps, steps is PARTS[-1]),
+                functools.partial(mlp_backward_kernel, run, steps, steps is PARTS[-1]),
                 [
                     ((n, D), F32),
                     ((count, half, 2 * fl), BF, "each"),
@@ -1034,7 +1095,7 @@
                     pltpu.VMEM((D, n), BF),
                     pltpu.VMEM((D, n), BF),
                     pltpu.VMEM((D, 2 * fl), BF),
-                    pltpu.SemaphoreType.DMA((2 * count + 2,)),
+                    pltpu.SemaphoreType.DMA((copy_count(half, run, count),)),
                 ],
                 [place, grad, middle, layer_vecs[layer], second, ("each", hidden), ("each", slope)]
                 + mlp_units[layer].refs()
@@ -1043,7 +1104,7 @@
                 sending,
             )
             part = [gmid]
-            up_bgrad.update({step: bgrad[at, 0] for at, step in enumerate(steps)})
+            up_bgrad.update({step: bgrad[at] for at, step in enumerate(steps)})
             slot += 1
             mlp_out[layer].cores(steps, mine, other)
             sending = [other] + proceed(slot, gmid)
@@ -1051,7 +1112,7 @@
         for steps in PARTS:
             count = len(steps)
             grad, mine, other, bgrad, attn_vgrad = call(
-                functools.partial(attn_backward_kernel, ni, wl, steps, steps is PARTS[-1]),
+                functools.partial(attn_backward_kernel, run, ni, wl, steps, steps is PARTS[-1]),
                 [
                     ((n, D), F32),
                     ((count, half, 4 * wl), BF, "each"),
@@ -1067,7 +1128,7 @@
                     pltpu.VMEM((n, wl), BF),
                     pltpu.VMEM((n, 3 * wl), BF),
                     pltpu.VMEM((D, 4 * wl), BF),
-                    pltpu.SemaphoreType.DMA((2 * count + 2,)),
+                    pltpu.SemaphoreType.DMA((copy_count(half, run, count),)),
                 ],
                 [place, gmid, resid_in, layer_vecs[layer], live_rows, first]
                 + [("each", qkv), ("each", attended), ("each", lse)]
@@ -1077,40 +1138,36 @@
                 sending,
             )
             part = [grad]
-            qkv_bgrad.update({step: bgrad[at, 0] for at, step in enumerate(steps)})
+            qkv_bgrad.update({step: bgrad[at] for at, step in enumerate(steps)})
             slot += 1
             attn_out[layer].cores(steps, mine, other)
             if slot < final:
                 sending = [other] + proceed(slot, grad)
         gain_list[layer] = (attn_vgrad + mlp_vgrad)[:6]
-        bias_list[layer] = jnp.stack(
+        bias_list[layer] = jnp.concatenate(
             [
-                jnp.concatenate(
-                    [qkv_bgrad[step][:wl], qkv_bgrad[step][2 * wl :], up_bgrad[step]]
-                )
-                for step in range(mp)
-            ]
+                jnp.concatenate([qkv_bgrad[step][:, :wl] for step in range(mp)]),
+                jnp.concatenate([qkv_bgrad[step][:, 2 * wl :] for step in range(mp)]),
+                jnp.concatenate([up_bgrad[step] for step in range(mp)]),
+            ],
+            axis=1,
         )
-    quarter = rows_own // mp
-    patch_grad = dot_tn(patch_rows, grad.astype(BF)).astype(BF)
-    patch_grad = patch_grad.reshape(dp, teach, mp, quarter, D)
-
-    def patch_half(core):
-        kept = lax.dynamic_index_in_dim(patch_grad, core, 1, False)
-        return kept.transpose(1, 0, 2, 3)[ranks].reshape(mp, dp * quarter, D)
+    ahead = mlp_out[0].rows(grad)
+    agenda[final].remove((mlp_out[0], "rows"))
+    grad = tie(grad, *ahead)
+    patch_grad = dot_nn(patches_t, grad.astype(BF)).astype(BF)
+    patch_grad = patch_grad.reshape(teach, mp, dp * quarter, D)
 
     source_grads = lax.dot_general(
         sources, grad, (((0,), (0,)), ((), ())), precision=HIGH, preferred_element_type=F32
     )
-    vector_grads = outward(
-        jnp.concatenate(gain_list + [final_vgrad[:2], source_grads], axis=0)
-    )
+    vector_grads = jnp.concatenate(gain_list + [final_vgrad[:2], source_grads], axis=0)
     bias_blocks = jnp.concatenate(
         bias_list + [head_bgrad[:, 0, :cl], head_bgrad[:, 0, wc : wc + cl]], axis=1
     )
     devices = dp * teach
-    vector_piece = -(-vector_params.size // (mp * devices))
-    bias_piece = -(-split_biases.size // devices)
+    vector_piece = -(-vector_params.size // (mp * devices * 1024)) * 1024
+    bias_piece = -(-split_biases.size // (devices * 1024)) * 1024
 
     def padded(flat, size):
         return jnp.pad(flat, ((0, 0), (0, size - flat.shape[1])))
@@ -1133,18 +1190,17 @@
         return lax.dynamic_index_in_dim(small, core, 1, False)
 
     attn_out[0].attach(
-        (patch_half(here_teach), patch_half(1 - here_teach)),
+        (patch_grad[0], patch_grad[1]),
         (small_half(here_teach), small_half(1 - here_teach)),
     )
-    ahead = [grad]
     for moment in sorted(agenda):
         for unit, what in agenda[moment]:
             ahead += getattr(unit, what)(*ahead)
     first_rows = attn_out[0].result()
     patch_grad = outward(first_rows[rows_own : rows_own + quarter])
-    small = first_rows[rows_own + quarter :].reshape(-1)
-    vector_grads = small[:vector_piece]
-    bias_grads = small[vector_piece : vector_piece + bias_piece]
+    small = first_rows[rows_own + quarter :].reshape(-1, 128)
+    vector_grads = small[: vector_piece // 128]
+    bias_grads = small[vector_piece // 128 : (vector_piece + bias_piece) // 128]
 
     attn_list = [first_rows[:rows_own]] + [unit.result() for unit in attn_out[1:]]
     mlp_list = [unit.result() for unit in mlp_out]
@@ -1180,13 +1236,14 @@
         return lax.dynamic_slice_in_dim(array, here_mp * quarter, quarter, 0)
 
     def vector_part(array):
-        flat = padded(array.reshape(1, -1), vector_piece * mp * devices)[0]
+        flat = padded(inward(array).reshape(1, -1), vector_piece * mp * devices)[0]
         at = (here_mp * devices + device) * vector_piece
-        return lax.dynamic_slice_in_dim(flat, at, vector_piece, 0)
+        return lax.dynamic_slice_in_dim(flat, at, vector_piece, 0).reshape(-1, 128)
 
     def bias_part(array):
         flat = padded(array.reshape(1, -1), bias_piece * devices)[0]
-        return lax.dynamic_slice_in_dim(flat, device * bias_piece, bias_piece, 0)
+        part = lax.dynamic_slice_in_dim(flat, device * bias_piece, bias_piece, 0)
+        return part.reshape(-1, 128)
 
     pieces = (patch_grad, attn_grads, mlp_grads, head_grads, vector_grads, bias_grads)
     own_part = (patch_cut, None, None, None, vector_part, bias_part)
@@ -1196,29 +1253,31 @@
         if part is not None:
             others = [part(array) for array in others]
         results.append(direct(pieces[slot], *others, decay_pieces[slot]))
+    totals = jnp.concatenate(
+        [
+            squares_of(weights, mp_first, data_first),
+            squares_of([result[2] for result in results], 1.0, 1.0),
+            loss_part[0, :1],
+        ]
+    )
+    npar = (totals.size - 1) // 2
     totals, vector_grads, bias_grads, patch_grad = sum_and_gather(
-        jnp.concatenate(
-            [
-                squares_of(weights, mp_first, data_first),
-                squares_of([result[2] for result in results], 1.0, 1.0),
-                loss_part[0, :1],
-            ]
-        ),
+        jnp.pad(totals, (0, -totals.size % 1024)).reshape(-1, 128),
         vector_grads,
         bias_grads,
         patch_grad,
     )
     gathered = {
         0: patch_grad,
-        4: vector_grads[: vector_params.size].reshape(vector_params.shape),
-        5: bias_grads[: split_biases.size],
+        4: outward(vector_grads.reshape(-1)[: vector_params.size].reshape(vector_params.shape)),
+        5: bias_grads.reshape(-1)[: split_biases.size],
     }
     for slot, gradient in gathered.items():
         results[slot] = direct(
             gradient, firsts[slot], seconds[slot], weights[slot], decay_pieces[slot]
         )
     directions = [result[2] for result in results]
-    npar = (totals.size - 1) // 2
+    totals = totals.reshape(-1)
     weights_sq, direction_sq, loss_value = totals[:npar], totals[npar : 2 * npar], totals[2 * npar]
     weight_norm = jnp.sqrt(weights_sq)
     update_norm = jnp.sqrt(direction_sq)

time: 640 us -> 610 us (0.953)
  local copies, waits for them, and re-layouts: 99.7 us -> 70.1 us
  Pallas kernels: 215 us -> 224 us
  starting transfers between devices: 72 us -> 65.2 us
    pallas_call x13 -> x18, Pallas kernels: 215 us -> 224 us  [call(): pl.pallas_call(grouped, out_shape=out_shape, in_specs=specs, out_specs=ou...]
    concatenate x14 -> x0, local copies, waits for them, and re-layouts: 8.82 us -> none  [the longest x8 4.69 us: per_device(): jnp.concatenate([qkv_bgrad[step][:wl], qkv_bgrad[step][2 * wl:], up_bgrad...]
    ppermute x92 -> x83, starting transfers between devices: 71.7 us -> 64.5 us  [swap(): lax.ppermute(values, axis, [(rank, rank ^ distance) for rank in range(siz...]
    unnamed x263 -> x270, local copies, waits for them, and re-layouts: 14.1 us -> 17.6 us
    ppermute x92 -> x83, waiting for transfers between devices: 98.2 us -> 101 us  [swap(): lax.ppermute(values, axis, [(rank, rank ^ distance) for rank in range(siz...]
  transfers between devices with their start and end apart: 100 -> 91, of which waited for: 32 -> 34; matrix products, arithmetic and copies ran while one was open for 23% -> 21% of each run, Pallas kernels for 33% -> 33%
where the time goes in v4:
time: 610 us; the launch traced here: 601 us
  Pallas kernels  224 us (37%)
  waiting for transfers between devices  117 us (19%)
  other arithmetic  91.4 us (15%)
  local copies, waits for them, and re-layouts  70.1 us (11%)
  starting transfers between devices  65.2 us (11%)
  between operations  24.2 us (4%)
  matrix products  8.93 us (1%)
    pallas_call x18, Pallas kernels, call(): pl.pallas_call(grouped, out_shape=out_shape, in_specs=specs, out_specs=ou...  224 us
    ppermute x83, waiting for transfers between devices, swap(): lax.ppermute(values, axis, [(rank, rank ^ distance) for rank in range(siz...  101 us
    ppermute x83, starting transfers between devices, swap(): lax.ppermute(values, axis, [(rank, rank ^ distance) for rank in range(siz...  64.5 us
    convert_element_type x20, other arithmetic, add_low(): return (left.astype(F32) + right.astype(F32)).astype(BF)  18.6 us
    unnamed x270, local copies, waits for them, and re-layouts  17.6 us
    reduce_scatter x5, waiting for transfers between devices, rows(): self.pieces = lax.psum_scatter(total, 'dp', scatter_dimension=0, tiled=True)  15.5 us
  transfers between devices with their start and end apart: 91, of which 34 were waited for; matrix products, arithmetic and copies ran while one was open for 21% of the time, Pallas kernels for 33%

profile of v4, /device:TPU:0, one launch (start us, length us, event | category | flops | bytes accessed | tf_op | source)
XLA Modules:
  0.0 601.0 jit_solution(14388746962179784617)
XLA Ops:
  10.6 1.8 concatenate.144
  12.4 3.0 collective-permute-start
  18.6 1.9 collective-permute-start.3
  37.6 1.8 add_multiply_fusion
  56.2 1.8 pad_maximum_fusion.12.refs_10_
  66.0 2.8 convolution_add_fusion.refs_1_.refs_2_
  68.8 7.7 %collective-permute-done.7.refs_6_.refs_10_ = bf16[384,768]{1,0:T(8,128)(2,1)S(1)} collective-permute-done((bf16[384,768]{1,0:T(8,128)(2,1)S(1)}, bf16[384,768]{1,0:T(8,128)(2,1)S(1)}, u32[]{:S(2)}, u32[]{:S(2)}) %collective-permute-start.7) | collective-permute-done | bytes 589856 | tf_op jit(solution)/shard_map/ppermute | solution.py:557
  79.1 6.2 %collective-permute-done.10.refs_9_.refs_13_ = bf16[192,768]{1,0:T(8,128)(2,1)S(1)} collective-permute-done((bf16[192,768]{1,0:T(8,128)(2,1)S(1)}, bf16[192,768]{1,0:T(8,128)(2,1)S(1)}, u32[]{:S(2)}, u32[]{:S(2)}) %collective-permute-start.10) | collective-permute-done | bytes 294944 | tf_op jit(solution)/shard_map/ppermute | solution.py:557
  93.8 20.5 %shard_map.427 = (bf16[576,768]{1,0:T(8,128)(2,1)}, bf16[4,576,576]{2,1,0:T(8,128)(2,1)}, bf16[4,576,192]{2,1,0:T(8,128)(2,1)}, f32[4,576,3]{2,1,0:T(8,128)}, f32[576,768]{1,0:T(8,128)}) custom-call(s32[1]{0:T(128)} %bitcast.8.refs_0_, f32[576,768]{1,0:T(8,128)} %convolution_add_fusion.refs_1_.refs_2_, f32[8,768]{1,0:T(8,128)} %slice_select_fusion.refs_2_.refs_3_, ...), custom_call_target="tpu_custom_call" | custom-call | flops 2300000000 | bytes 13924612 | tf_op jit(solution)/shard_map/pallas_call | solution.py:535
  119.1 2.0 collective-permute-done.20
  122.3 3.0 collective-permute-start.21
  126.6 3.9 collective-permute-start.22
  141.0 15.1 %shard_map.428 = (bf16[576,768]{1,0:T(8,128)(2,1)}, bf16[4,576,768]{2,1,0:T(8,128)(2,1)}, f32[4,576,768]{2,1,0:T(8,128)}, f32[576,768]{1,0:T(8,128)}) custom-call(s32[1]{0:T(128)} %bitcast.8.refs_0_, f32[576,768]{1,0:T(8,128)} %get-tuple-element.140.refs_1_.refs_2_, f32[8,768]{1,0:T(8,128)} %slice_select_fusion.refs_2_.refs_3_, f32[4,1,768]{2,1,0:T(1,128)} %copy.80.refs_3_, ...), custom_call_target="tpu_custom_call" | custom-call | flops 2300000000 | bytes 25104388 | tf_op jit(solution)/shard_map/pallas_call | solution.py:535
  160.1 5.1 collective-permute-done.30.refs_8_.refs_12_
  173.8 20.6 %shard_map.429 = (bf16[576,768]{1,0:T(8,128)(2,1)}, bf16[4,576,576]{2,1,0:T(8,128)(2,1)}, bf16[4,576,192]{2,1,0:T(8,128)(2,1)}, f32[4,576,3]{2,1,0:T(8,128)}, f32[576,768]{1,0:T(8,128)}) custom-call(s32[1]{0:T(128)} %bitcast.8.refs_0_, f32[576,768]{1,0:T(8,128)} %get-tuple-element.148.refs_1_.refs_2_, f32[8,768]{1,0:T(8,128)} %pad.84.refs_2_.refs_3_, ...), custom_call_target="tpu_custom_call" | custom-call | flops 2300000000 | bytes 14317828 | tf_op jit(solution)/shard_map/pallas_call | solution.py:535
  194.4 7.1 %collective-permute-done.37.refs_5_.refs_12_.refs_8_ = bf16[384,2048]{1,0:T(8,128)(2,1)S(1)} collective-permute-done((bf16[384,2048]{1,0:T(8,128)(2,1)S(1)}, bf16[384,2048]{1,0:T(8,128)(2,1)S(1)}, u32[]{:S(2)}, u32[]{:S(2)}) %collective-permute-start.37) | collective-permute-done | bytes 1572896 | tf_op jit(solution)/shard_map/ppermute | solution.py:557
  206.0 17.6 %collective-permute-done.39.refs_7_.refs_14_.refs_10_ = bf16[192,2048]{1,0:T(8,128)(2,1)} collective-permute-done((bf16[192,2048]{1,0:T(8,128)(2,1)S(1)}, bf16[192,2048]{1,0:T(8,128)(2,1)}, u32[]{:S(2)}, u32[]{:S(2)}) %collective-permute-start.39) | collective-permute-done | bytes 786464 | tf_op jit(solution)/shard_map/ppermute | solution.py:557
  227.6 14.8 %shard_map.430 = (bf16[576,768]{1,0:T(8,128)(2,1)}, bf16[4,576,768]{2,1,0:T(8,128)(2,1)}, f32[4,576,768]{2,1,0:T(8,128)}, f32[576,768]{1,0:T(8,128)}) custom-call(s32[1]{0:T(128)} %bitcast.8.refs_0_, f32[576,768]{1,0:T(8,128)} %get-tuple-element.155.refs_1_.refs_2_, f32[8,768]{1,0:T(8,128)} %pad.84.refs_2_.refs_3_, f32[4,1,768]{2,1,0:T(1,128)} %copy.82.refs_3_, ...), custom_call_target="tpu_custom_call" | custom-call | flops 2300000000 | bytes 27660292 | tf_op jit(solution)/shard_map/pallas_call | solution.py:535
  242.4 8.6 %shard_map.431 = (bf16[4,384,512]{2,1,0:T(8,128)(2,1)}, bf16[4,384,512]{2,1,0:T(8,128)(2,1)}, f32[4,1,512]{2,1,0:T(1,128)}, f32[576,768]{1,0:T(8,128)}, f32[8,768]{1,0:T(8,128)}, /*index=5*/f32[8,128]{1,0:T(8,128)}) custom-call(s32[1]{0:T(128)} %bitcast.8.refs_0_, f32[576,768]{1,0:T(8,128)} %get-tuple-element.158.refs_1_, f32[8,768]{1,0:T(8,128)} %pad.85.refs_2_, ...), custom_call_target="tpu_custom_call" | custom-call | flops 2300000000 | bytes 19807556 | tf_op jit(solution)/shard_map/pallas_call | solution.py:535
  253.8 14.1 %shard_map.432 = (f32[576,768]{1,0:T(8,128)}, bf16[2,384,1536]{2,1,0:T(8,128)(2,1)}, bf16[2,384,1536]{2,1,0:T(8,128)(2,1)}, f32[2,1,768]{2,1,0:T(1,128)}, f32[8,768]{1,0:T(8,128)}) custom-call(s32[1]{0:T(128)} %bitcast.8.refs_0_, f32[576,768]{1,0:T(8,128)} %get-tuple-element.159.refs_1_, f32[576,768]{1,0:T(8,128)} %get-tuple-element.155.refs_1_.refs_2_, ...), custom_call_target="tpu_custom_call" | custom-call | flops 2300000000 | bytes 35739652 | tf_op jit(solution)/shard_map/pallas_call | solution.py:535
  273.2 16.2 %shard_map.433 = (f32[576,768]{1,0:T(8,128)}, bf16[2,384,1536]{2,1,0:T(8,128)(2,1)}, bf16[2,384,1536]{2,1,0:T(8,128)(2,1)}, f32[2,1,768]{2,1,0:T(1,128)}, f32[8,768]{1,0:T(8,128)}) custom-call(s32[1]{0:T(128)} %bitcast.8.refs_0_, f32[576,768]{1,0:T(8,128)} %get-tuple-element.159.refs_1_, f32[576,768]{1,0:T(8,128)} %get-tuple-element.155.refs_1_.refs_2_, ...), custom_call_target="tpu_custom_call" | custom-call | flops 2300000000 | bytes 38688772 | tf_op jit(solution)/shard_map/pallas_call | solution.py:535
  295.5 17.8 %shard_map.434 = (f32[576,768]{1,0:T(8,128)}, bf16[2,384,768]{2,1,0:T(8,128)(2,1)}, bf16[2,384,768]{2,1,0:T(8,128)(2,1)}, f32[2,1,576]{2,1,0:T(1,128)}, f32[8,768]{1,0:T(8,128)}) custom-call(s32[1]{0:T(128)} %bitcast.8.refs_0_, f32[576,768]{1,0:T(8,128)} %get-tuple-element.168.refs_1_, f32[576,768]{1,0:T(8,128)} %get-tuple-element.148.refs_1_.refs_2_, ...), custom_call_target="tpu_custom_call" | custom-call | flops 2300000000 | bytes 21219076 | tf_op jit(solution)/shard_map/pallas_call | solution.py:535
  314.1 2.0 fusion.16.refs_21_
  323.7 20.3 %shard_map.435 = (f32[576,768]{1,0:T(8,128)}, bf16[2,384,768]{2,1,0:T(8,128)(2,1)}, bf16[2,384,768]{2,1,0:T(8,128)(2,1)}, f32[2,1,576]{2,1,0:T(1,128)}, f32[8,768]{1,0:T(8,128)}) custom-call(s32[1]{0:T(128)} %bitcast.8.refs_0_, f32[576,768]{1,0:T(8,128)} %get-tuple-element.168.refs_1_, f32[576,768]{1,0:T(8,128)} %get-tuple-element.148.refs_1_.refs_2_, ...), custom_call_target="tpu_custom_call" | custom-call | flops 2300000000 | bytes 22595332 | tf_op jit(solution)/shard_map/pallas_call | solution.py:535
  348.1 14.0 %shard_map.436 = (f32[576,768]{1,0:T(8,128)}, bf16[2,384,1536]{2,1,0:T(8,128)(2,1)}, bf16[2,384,1536]{2,1,0:T(8,128)(2,1)}, f32[2,1,768]{2,1,0:T(1,128)}, f32[8,768]{1,0:T(8,128)}) custom-call(s32[1]{0:T(128)} %bitcast.8.refs_0_, f32[576,768]{1,0:T(8,128)} %get-tuple-element.186.refs_1_, f32[576,768]{1,0:T(8,128)} %get-tuple-element.140.refs_1_.refs_2_, ...), custom_call_target="tpu_custom_call" | custom-call | flops 2300000000 | bytes 32790532 | tf_op jit(solution)/shard_map/pallas_call | solution.py:535
  367.5 3.6 fusion.1.refs_19_
  371.1 16.3 %shard_map.437 = (f32[576,768]{1,0:T(8,128)}, bf16[2,384,1536]{2,1,0:T(8,128)(2,1)}, bf16[2,384,1536]{2,1,0:T(8,128)(2,1)}, f32[2,1,768]{2,1,0:T(1,128)}, f32[8,768]{1,0:T(8,128)}) custom-call(s32[1]{0:T(128)} %bitcast.8.refs_0_, f32[576,768]{1,0:T(8,128)} %get-tuple-element.186.refs_1_, f32[576,768]{1,0:T(8,128)} %get-tuple-element.140.refs_1_.refs_2_, ...), custom_call_target="tpu_custom_call" | custom-call | flops 2300000000 | bytes 37509124 | tf_op jit(solution)/shard_map/pallas_call | solution.py:535
  387.5 2.5 fusion.8.refs_20_
  390.8 2.2 add_convert_fusion.2
  395.2 17.8 %shard_map.438 = (f32[576,768]{1,0:T(8,128)}, bf16[2,384,768]{2,1,0:T(8,128)(2,1)}, bf16[2,384,768]{2,1,0:T(8,128)(2,1)}, f32[2,1,576]{2,1,0:T(1,128)}, f32[8,768]{1,0:T(8,128)}) custom-call(s32[1]{0:T(128)} %bitcast.8.refs_0_, f32[576,768]{1,0:T(8,128)} %get-tuple-element.201.refs_1_, f32[576,768]{1,0:T(8,128)} %convolution_add_fusion.refs_1_.refs_2_, ...), custom_call_target="tpu_custom_call" | custom-call | flops 2300000000 | bytes 21022468 | tf_op jit(solution)/shard_map/pallas_call | solution.py:535
  419.1 20.5 %shard_map.439 = (f32[576,768]{1,0:T(8,128)}, bf16[2,384,768]{2,1,0:T(8,128)(2,1)}, bf16[2,384,768]{2,1,0:T(8,128)(2,1)}, f32[2,1,576]{2,1,0:T(1,128)}, f32[8,768]{1,0:T(8,128)}) custom-call(s32[1]{0:T(128)} %bitcast.8.refs_0_, f32[576,768]{1,0:T(8,128)} %get-tuple-element.201.refs_1_, f32[576,768]{1,0:T(8,128)} %convolution_add_fusion.refs_1_.refs_2_, ...), custom_call_target="tpu_custom_call" | custom-call | flops 2300000000 | bytes 22202116 | tf_op jit(solution)/shard_map/pallas_call | solution.py:535
  442.7 3.9 collective-permute-done.69
  446.6 4.1 fusion
  453.7 2.3 convolution_convert_fusion
  472.4 6.1 %collective-permute-done.72 = bf16[256,768]{1,0:T(8,128)(2,1)} collective-permute-done((bf16[256,768]{1,0:T(8,128)(2,1)}, bf16[256,768]{1,0:T(8,128)(2,1)}, u32[]{:S(2)}, u32[]{:S(2)}) %collective-permute-start.72) | collective-permute-done | bytes 393248 | tf_op jit(solution)/shard_map/ppermute | solution.py:557
  478.5 2.5 collective-permute-done.73
  489.3 13.0 %collective-permute-done.75 = bf16[512,768]{1,0:T(8,128)(2,1)} collective-permute-done((bf16[512,768]{1,0:T(8,128)(2,1)}, bf16[512,768]{1,0:T(8,128)(2,1)}, u32[]{:S(2)}, u32[]{:S(2)}) %collective-permute-start.75) | collective-permute-done | bytes 786464 | tf_op jit(solution)/shard_map/ppermute | solution.py:557
  510.3 3.5 multiply_reduce_fusion
  513.8 15.5 %reduce-scatter.6.cloned.1.call-done = bf16[128,768]{1,0:T(8,128)(2,1)} async-done(((bf16[512,768]{1,0:T(8,128)(2,1)}), bf16[128,768]{1,0:T(8,128)(2,1)}) %reduce-scatter.6.cloned.1.call-update) | async-done | bytes 196624 | tf_op jit(solution)/shard_map/reduce_scatter | solution.py:715
  531.3 3.2 multiply_reduce_fusion.2
  541.6 2.7 concatenate.180
  544.4 3.7 collective-permute-done.76.refs_2_
  550.8 4.2 collective-permute-done.77.refs_2_
  563.8 2.1 collective-permute-done.79.refs_2_
  570.1 3.1 collective-permute-done.80.refs_2_
  573.9 1.7 shard_map.444
  582.3 2.0 multiply_subtract_fusion.5
  584.3 2.5 multiply_subtract_fusion.3
  (699 shorter events, 207.8 us)
Async XLA Ops:
  7.2 50.8 %all-gather.4.cloned.1.call-start = ((), (), s32[]{:S(2)}) async-start(), calls=%async_computation.5 | async-start | bytes 1474560 | tf_op jit(solution)/shard_map/all_gather | solution.py:855
  12.4 66.7 %all-gather.6.cloned.1.call-start = ((), (), s32[]{:S(2)}) async-start(), calls=%async_computation.6 | async-start | bytes 1474560 | tf_op jit(solution)/shard_map/all_gather | solution.py:855
  12.4 37.8 %collective-permute-start = (f32[2804]{0:T(1024)}, f32[2804]{0:T(1024)}, u32[]{:S(2)}, u32[]{:S(2)}) collective-permute-start(f32[2804]{0:T(1024)} %param.40), channel_id=1, source_target_pairs={{0,2},{2,0},{4,6},{6,4},{1,3},{3,1},{5,7},{7,5},{8,10},{10,8},{12,... | collective-permute-start | bytes 33656 | tf_op jit(solution)/shard_map/ppermute | solution.py:557
  15.4 35.6 %collective-permute-start.1 = (f32[2804]{0:T(1024)}, f32[2804]{0:T(1024)}, u32[]{:S(2)}, u32[]{:S(2)}) collective-permute-start(f32[2804]{0:T(1024)} %param.40), channel_id=1, source_target_pairs={{0,4},{2,6},{4,0},{6,2},{1,5},{3,7},{5,1},{7,3},{8,12},{10,14},{12... | collective-permute-start | bytes 33656 | tf_op jit(solution)/shard_map/ppermute | solution.py:557
  17.0 34.8 %collective-permute-start.2 = (f32[2804]{0:T(1024)}, f32[2804]{0:T(1024)}, u32[]{:S(2)}, u32[]{:S(2)}) collective-permute-start(f32[2804]{0:T(1024)} %param.40), channel_id=1, source_target_pairs={{0,6},{2,4},{4,2},{6,0},{1,7},{3,5},{5,3},{7,1},{8,14},{10,12},{12... | collective-permute-start | bytes 33656 | tf_op jit(solution)/shard_map/ppermute | solution.py:557
  18.6 36.0 %collective-permute-start.3 = (bf16[224,256]{1,0:T(8,128)(2,1)}, bf16[224,256]{1,0:T(8,128)(2,1)}, u32[]{:S(2)}, u32[]{:S(2)}) collective-permute-start(bf16[224,256]{1,0:T(8,128)(2,1)} %get-tuple-element.338), channel_id=1, source_target_pairs={{0,2},{2,0},{4,6},{6,4},{1,3},{3,1},{5,7},{7,5},{8,10},{10,8},{12,... | collective-permute-start | bytes 344072 | tf_op jit(solution)/shard_map/ppermute | solution.py:557
  20.5 34.0 %collective-permute-start.4 = (bf16[224,256]{1,0:T(8,128)(2,1)}, bf16[224,256]{1,0:T(8,128)(2,1)}, u32[]{:S(2)}, u32[]{:S(2)}) collective-permute-start(bf16[224,256]{1,0:T(8,128)(2,1)} %get-tuple-element.338), channel_id=1, source_target_pairs={{0,4},{2,6},{4,0},{6,2},{1,5},{3,7},{5,1},{7,3},{8,12},{10,14},{12... | collective-permute-start | bytes 344072 | tf_op jit(solution)/shard_map/ppermute | solution.py:557
  24.9 110.2 %all-gather.8.cloned.1.call-start = ((), (), s32[]{:S(2)}) async-start(), calls=%async_computation.7 | async-start | bytes 2703360 | tf_op jit(solution)/shard_map/all_gather | solution.py:855
  60.7 425.7 %reduce-scatter.14.cloned.1.call-start = ((), (), s32[]{:S(2)}) async-start(), calls=%async_computation.12 | async-start | bytes 491520 | tf_op jit(solution)/shard_map/reduce_scatter | solution.py:715
  86.5 27.8 %collective-permute-start.16 = (bf16[384,1536]{1,0:T(8,128)(2,1)}, bf16[384,1536]{1,0:T(8,128)(2,1)S(1)}, u32[]{:S(2)}, u32[]{:S(2)}) collective-permute-start(bf16[384,1536]{1,0:T(8,128)(2,1)} %all-gather.6.cloned.1.call-done.refs_15_.refs_4_.refs_7_), channel_id=1, source_target_pairs={{0,2},{2,0},{4,6},{6,4},{1,3},{3,1},{5,7},{7,5},{8,10},{10,8},{12,... | collective-permute-start | bytes 3538952 | tf_op jit(solution)/shard_map/ppermute | solution.py:557
  87.6 26.8 %collective-permute-start.17 = (bf16[384,1536]{1,0:T(8,128)(2,1)}, bf16[384,1536]{1,0:T(8,128)(2,1)S(1)}, u32[]{:S(2)}, u32[]{:S(2)}) collective-permute-start(bf16[384,1536]{1,0:T(8,128)(2,1)} %all-gather.6.cloned.1.call-done.refs_15_.refs_4_.refs_7_), channel_id=1, source_target_pairs={{0,4},{2,6},{4,0},{6,2},{1,5},{3,7},{5,1},{7,3},{8,12},{10,14},{12... | collective-permute-start | bytes 3538952 | tf_op jit(solution)/shard_map/ppermute | solution.py:557
  115.3 20.9 %collective-permute-start.18 = (bf16[192,1536]{1,0:T(8,128)(2,1)}, bf16[192,1536]{1,0:T(8,128)(2,1)}, u32[]{:S(2)}, u32[]{:S(2)}) collective-permute-start(bf16[192,1536]{1,0:T(8,128)(2,1)} %slice.762), channel_id=1, source_target_pairs={{0,2},{2,0},{4,6},{6,4},{1,3},{3,1},{5,7},{7,5},{8,10},{10,8},{12,... | collective-permute-start | bytes 1769480 | tf_op jit(solution)/shard_map/ppermute | solution.py:557
  116.9 19.3 %collective-permute-start.19 = (bf16[192,1536]{1,0:T(8,128)(2,1)}, bf16[192,1536]{1,0:T(8,128)(2,1)}, u32[]{:S(2)}, u32[]{:S(2)}) collective-permute-start(bf16[192,1536]{1,0:T(8,128)(2,1)} %slice.763), channel_id=1, source_target_pairs={{0,4},{2,6},{4,0},{6,2},{1,5},{3,7},{5,1},{7,3},{8,12},{10,14},{12... | collective-permute-start | bytes 1769480 | tf_op jit(solution)/shard_map/ppermute | solution.py:557
  118.0 18.9 %collective-permute-start.23 = (bf16[384,1536]{1,0:T(8,128)(2,1)S(1)}, bf16[384,1536]{1,0:T(8,128)(2,1)}, u32[]{:S(2)}, u32[]{:S(2)}) collective-permute-start(bf16[384,1536]{1,0:T(8,128)(2,1)S(1)} %copy-done.6), channel_id=1, source_target_pairs={{0,1},{1,0},{2,3},{3,2},{4,5},{5,4},{6,7},{7,6},{8,9},{9,8},{10,11... | collective-permute-start | bytes 3538952 | tf_op jit(solution)/shard_map/ppermute | solution.py:557
  136.8 19.3 %collective-permute-start.28 = (bf16[384,768]{1,0:T(8,128)(2,1)S(1)}, bf16[384,768]{1,0:T(8,128)(2,1)S(1)}, u32[]{:S(2)}, u32[]{:S(2)}) collective-permute-start(bf16[384,768]{1,0:T(8,128)(2,1)S(1)} %slice.983.refs_14_.refs_5_.refs_9_), channel_id=1, source_target_pairs={{0,2},{2,0},{4,6},{6,4},{1,3},{3,1},{5,7},{7,5},{8,10},{10,8},{12,... | collective-permute-start | bytes 1769480 | tf_op jit(solution)/shard_map/ppermute | solution.py:557
  166.4 35.2 %collective-permute-start.37 = (bf16[384,2048]{1,0:T(8,128)(2,1)S(1)}, bf16[384,2048]{1,0:T(8,128)(2,1)S(1)}, u32[]{:S(2)}, u32[]{:S(2)}) collective-permute-start(bf16[384,2048]{1,0:T(8,128)(2,1)S(1)} %slice.984.refs_15_.refs_4_.refs_11_.refs_7_), channel_id=1, source_target_pairs={{0,2},{2,0},{4,6},{6,4},{1,3},{3,1},{5,7},{7,5},{8,10},{10,8},{12,... | collective-permute-start | bytes 4718600 | tf_op jit(solution)/shard_map/ppermute | solution.py:557
  167.1 35.0 %collective-permute-start.38 = (bf16[384,2048]{1,0:T(8,128)(2,1)S(1)}, bf16[384,2048]{1,0:T(8,128)(2,1)}, u32[]{:S(2)}, u32[]{:S(2)}) collective-permute-start(bf16[384,2048]{1,0:T(8,128)(2,1)S(1)} %slice.984.refs_15_.refs_4_.refs_11_.refs_7_), channel_id=1, source_target_pairs={{0,4},{2,6},{4,0},{6,2},{1,5},{3,7},{5,1},{7,3},{8,12},{10,14},{12... | collective-permute-start | bytes 4718600 | tf_op jit(solution)/shard_map/ppermute | solution.py:557
  171.9 53.7 %collective-permute-start.41 = (bf16[384,2048]{1,0:T(8,128)(2,1)S(1)}, bf16[384,2048]{1,0:T(8,128)(2,1)}, u32[]{:S(2)}, u32[]{:S(2)}) collective-permute-start(bf16[384,2048]{1,0:T(8,128)(2,1)S(1)} %slice.984.refs_15_.refs_4_.refs_11_.refs_7_), channel_id=1, source_target_pairs={{0,1},{1,0},{2,3},{3,2},{4,5},{5,4},{6,7},{7,6},{8,9},{9,8},{10,11... | collective-permute-start | bytes 4718600 | tf_op jit(solution)/shard_map/ppermute | solution.py:557
  202.2 23.4 %collective-permute-start.42 = (bf16[384,2048]{1,0:T(8,128)(2,1)S(1)}, bf16[384,2048]{1,0:T(8,128)(2,1)}, u32[]{:S(2)}, u32[]{:S(2)}) collective-permute-start(bf16[384,2048]{1,0:T(8,128)(2,1)S(1)} %collective-permute-done.37.refs_5_.refs_12_.refs_8_), channel_id=1, source_target_pairs={{0,1},{1,0},{2,3},{3,2},{4,5},{5,4},{6,7},{7,6},{8,9},{9,8},{10,11... | collective-permute-start | bytes 4718600 | tf_op jit(solution)/shard_map/ppermute | solution.py:557
  203.5 20.1 %collective-permute-start.39 = (bf16[192,2048]{1,0:T(8,128)(2,1)S(1)}, bf16[192,2048]{1,0:T(8,128)(2,1)}, u32[]{:S(2)}, u32[]{:S(2)}) collective-permute-start(bf16[192,2048]{1,0:T(8,128)(2,1)S(1)} %slice.776), channel_id=1, source_target_pairs={{0,2},{2,0},{4,6},{6,4},{1,3},{3,1},{5,7},{7,5},{8,10},{10,8},{12,... | collective-permute-start | bytes 2359304 | tf_op jit(solution)/shard_map/ppermute | solution.py:557
  204.9 20.7 %collective-permute-start.43 = (bf16[384,2048]{1,0:T(8,128)(2,1)}, bf16[384,2048]{1,0:T(8,128)(2,1)}, u32[]{:S(2)}, u32[]{:S(2)}) collective-permute-start(bf16[384,2048]{1,0:T(8,128)(2,1)} %collective-permute-done.38.refs_6_.refs_13_.refs_9_), channel_id=1, source_target_pairs={{0,1},{1,0},{2,3},{3,2},{4,5},{5,4},{6,7},{7,6},{8,9},{9,8},{10,11... | collective-permute-start | bytes 4718600 | tf_op jit(solution)/shard_map/ppermute | solution.py:557
  205.1 19.8 %collective-permute-start.40 = (bf16[192,2048]{1,0:T(8,128)(2,1)S(1)}, bf16[192,2048]{1,0:T(8,128)(2,1)}, u32[]{:S(2)}, u32[]{:S(2)}) collective-permute-start(bf16[192,2048]{1,0:T(8,128)(2,1)S(1)} %slice.777), channel_id=1, source_target_pairs={{0,4},{2,6},{4,0},{6,2},{1,5},{3,7},{5,1},{7,3},{8,12},{10,14},{12... | collective-permute-start | bytes 2359304 | tf_op jit(solution)/shard_map/ppermute | solution.py:557
  267.9 24.8 %collective-permute-start.49 = (bf16[2,384,1536]{2,1,0:T(8,128)(2,1)}, bf16[2,384,1536]{2,1,0:T(8,128)(2,1)S(1)}, u32[]{:S(2)}, u32[]{:S(2)}) collective-permute-start(bf16[2,384,1536]{2,1,0:T(8,128)(2,1)} %get-tuple-element.165.refs_18_), channel_id=1, source_target_pairs={{0,1},{1,0},{2,3},{3,2},{4,5},{5,4},{6,7},{7,6},{8,9},{9,8},{10,11... | collective-permute-start | bytes 7077896 | tf_op jit(solution)/shard_map/ppermute | solution.py:557
  271.1 19.2 %collective-permute-start.47 = (bf16[192,512]{1,0:T(8,128)(2,1)S(1)}, bf16[192,512]{1,0:T(8,128)(2,1)S(1)}, u32[]{:S(2)}, u32[]{:S(2)}) collective-permute-start(bf16[192,512]{1,0:T(8,128)(2,1)S(1)} %get-tuple-element.317.refs_19_), channel_id=1, source_target_pairs={{0,2},{2,0},{4,6},{6,4},{1,3},{3,1},{5,7},{7,5},{8,10},{10,8},{12,... | collective-permute-start | bytes 589832 | tf_op jit(solution)/shard_map/ppermute | solution.py:557
  289.4 29.2 %collective-permute-start.54 = (bf16[2,384,1536]{2,1,0:T(8,128)(2,1)}, bf16[2,384,1536]{2,1,0:T(8,128)(2,1)}, u32[]{:S(2)}, u32[]{:S(2)}) collective-permute-start(bf16[2,384,1536]{2,1,0:T(8,128)(2,1)} %get-tuple-element.173.refs_19_), channel_id=1, source_target_pairs={{0,1},{1,0},{2,3},{3,2},{4,5},{5,4},{6,7},{7,6},{8,9},{9,8},{10,11... | collective-permute-start | bytes 7077896 | tf_op jit(solution)/shard_map/ppermute | solution.py:557
  290.4 22.9 %collective-permute-start.51 = (bf16[384,512]{1,0:T(8,128)(2,1)S(1)}, bf16[384,512]{1,0:T(8,128)(2,1)S(1)}, u32[]{:S(2)}, u32[]{:S(2)}) collective-permute-start(bf16[384,512]{1,0:T(8,128)(2,1)S(1)} %pad_maximum_fusion.16.refs_21_), channel_id=1, source_target_pairs={{0,4},{2,6},{4,0},{6,2},{1,5},{3,7},{5,1},{7,3},{8,12},{10,14},{12... | collective-permute-start | bytes 1179656 | tf_op jit(solution)/shard_map/ppermute | solution.py:557
  291.7 21.6 %collective-permute-start.50 = (bf16[384,512]{1,0:T(8,128)(2,1)S(1)}, bf16[384,512]{1,0:T(8,128)(2,1)S(1)}, u32[]{:S(2)}, u32[]{:S(2)}) collective-permute-start(bf16[384,512]{1,0:T(8,128)(2,1)S(1)} %pad_maximum_fusion.15.refs_20_), channel_id=1, source_target_pairs={{0,2},{2,0},{4,6},{6,4},{1,3},{3,1},{5,7},{7,5},{8,10},{10,8},{12,... | collective-permute-start | bytes 1179656 | tf_op jit(solution)/shard_map/ppermute | solution.py:557
  293.4 22.8 %collective-permute-start.52 = (bf16[192,1536]{1,0:T(8,128)(2,1)S(1)}, bf16[192,1536]{1,0:T(8,128)(2,1)}, u32[]{:S(2)}, u32[]{:S(2)}) collective-permute-start(bf16[192,1536]{1,0:T(8,128)(2,1)S(1)} %get-tuple-element.291.refs_22_), channel_id=1, source_target_pairs={{0,2},{2,0},{4,6},{6,4},{1,3},{3,1},{5,7},{7,5},{8,10},{10,8},{12,... | collective-permute-start | bytes 1769480 | tf_op jit(solution)/shard_map/ppermute | solution.py:557
  294.6 21.7 %collective-permute-start.53 = (bf16[192,1536]{1,0:T(8,128)(2,1)S(1)}, bf16[192,1536]{1,0:T(8,128)(2,1)}, u32[]{:S(2)}, u32[]{:S(2)}) collective-permute-start(bf16[192,1536]{1,0:T(8,128)(2,1)S(1)} %get-tuple-element.290.refs_23_), channel_id=1, source_target_pairs={{0,4},{2,6},{4,0},{6,2},{1,5},{3,7},{5,1},{7,3},{8,12},{10,14},{12... | collective-permute-start | bytes 1769480 | tf_op jit(solution)/shard_map/ppermute | solution.py:557
  313.3 31.0 %collective-permute-start.55 = (bf16[2,384,768]{2,1,0:T(8,128)(2,1)}, bf16[2,384,768]{2,1,0:T(8,128)(2,1)}, u32[]{:S(2)}, u32[]{:S(2)}) collective-permute-start(bf16[2,384,768]{2,1,0:T(8,128)(2,1)} %get-tuple-element.179.refs_20_), channel_id=1, source_target_pairs={{0,1},{1,0},{2,3},{3,2},{4,5},{5,4},{6,7},{7,6},{8,9},{9,8},{10,11... | collective-permute-start | bytes 3538952 | tf_op jit(solution)/shard_map/ppermute | solution.py:557
  316.1 172.2 %reduce-scatter.8.cloned.1.call-start = ((), (), s32[]{:S(2)}) async-start(), calls=%async_computation.9 | async-start | bytes 737280 | tf_op jit(solution)/shard_map/reduce_scatter | solution.py:715
  317.6 48.9 %collective-permute-start.56 = (bf16[384,1536]{1,0:T(8,128)(2,1)S(1)}, bf16[384,1536]{1,0:T(8,128)(2,1)}, u32[]{:S(2)}, u32[]{:S(2)}) collective-permute-start(bf16[384,1536]{1,0:T(8,128)(2,1)S(1)} %pad_maximum_fusion.1.refs_22_), channel_id=1, source_target_pairs={{0,2},{2,0},{4,6},{6,4},{1,3},{3,1},{5,7},{7,5},{8,10},{10,8},{12,... | collective-permute-start | bytes 3538952 | tf_op jit(solution)/shard_map/ppermute | solution.py:557
  322.5 44.0 %collective-permute-start.57 = (bf16[384,1536]{1,0:T(8,128)(2,1)S(1)}, bf16[384,1536]{1,0:T(8,128)(2,1)}, u32[]{:S(2)}, u32[]{:S(2)}) collective-permute-start(bf16[384,1536]{1,0:T(8,128)(2,1)S(1)} %pad_maximum_fusion.2.refs_23_), channel_id=1, source_target_pairs={{0,4},{2,6},{4,0},{6,2},{1,5},{3,7},{5,1},{7,3},{8,12},{10,14},{12... | collective-permute-start | bytes 3538952 | tf_op jit(solution)/shard_map/ppermute | solution.py:557
  344.0 21.1 %collective-permute-start.60 = (bf16[2,384,768]{2,1,0:T(8,128)(2,1)}, bf16[2,384,768]{2,1,0:T(8,128)(2,1)}, u32[]{:S(2)}, u32[]{:S(2)}) collective-permute-start(bf16[2,384,768]{2,1,0:T(8,128)(2,1)} %get-tuple-element.190.refs_17_), channel_id=1, source_target_pairs={{0,1},{1,0},{2,3},{3,2},{4,5},{5,4},{6,7},{7,6},{8,9},{9,8},{10,11... | collective-permute-start | bytes 3538952 | tf_op jit(solution)/shard_map/ppermute | solution.py:557
  362.1 28.6 %collective-permute-start.63 = (bf16[2,384,1536]{2,1,0:T(8,128)(2,1)}, bf16[2,384,1536]{2,1,0:T(8,128)(2,1)}, u32[]{:S(2)}, u32[]{:S(2)}) collective-permute-start(bf16[2,384,1536]{2,1,0:T(8,128)(2,1)} %get-tuple-element.194.refs_18_), channel_id=1, source_target_pairs={{0,1},{1,0},{2,3},{3,2},{4,5},{5,4},{6,7},{7,6},{8,9},{9,8},{10,11... | collective-permute-start | bytes 7077896 | tf_op jit(solution)/shard_map/ppermute | solution.py:557
  363.9 23.5 %collective-permute-start.61 = (bf16[384,768]{1,0:T(8,128)(2,1)S(1)}, bf16[384,768]{1,0:T(8,128)(2,1)}, u32[]{:S(2)}, u32[]{:S(2)}) collective-permute-start(bf16[384,768]{1,0:T(8,128)(2,1)S(1)} %pad_maximum_fusion.10.refs_20_), channel_id=1, source_target_pairs={{0,2},{2,0},{4,6},{6,4},{1,3},{3,1},{5,7},{7,5},{8,10},{10,8},{12,... | collective-permute-start | bytes 1769480 | tf_op jit(solution)/shard_map/ppermute | solution.py:557
  366.5 20.9 %collective-permute-start.62 = (bf16[384,768]{1,0:T(8,128)(2,1)S(1)}, bf16[384,768]{1,0:T(8,128)(2,1)S(1)}, u32[]{:S(2)}, u32[]{:S(2)}) collective-permute-start(bf16[384,768]{1,0:T(8,128)(2,1)S(1)} %pad_maximum_fusion.11.refs_21_), channel_id=1, source_target_pairs={{0,4},{2,6},{4,0},{6,2},{1,5},{3,7},{5,1},{7,3},{8,12},{10,14},{12... | collective-permute-start | bytes 1769480 | tf_op jit(solution)/shard_map/ppermute | solution.py:557
  390.1 116.4 %reduce-scatter.12.cloned.1.call-start = ((), (), s32[]{:S(2)}) async-start(), calls=%async_computation.11 | async-start | bytes 1474560 | tf_op jit(solution)/shard_map/reduce_scatter | solution.py:715
  390.3 25.1 %collective-permute-start.66 = (bf16[2,384,1536]{2,1,0:T(8,128)(2,1)}, bf16[2,384,1536]{2,1,0:T(8,128)(2,1)}, u32[]{:S(2)}, u32[]{:S(2)}) collective-permute-start(bf16[2,384,1536]{2,1,0:T(8,128)(2,1)} %get-tuple-element.206.refs_19_), channel_id=1, source_target_pairs={{0,1},{1,0},{2,3},{3,2},{4,5},{5,4},{6,7},{7,6},{8,9},{9,8},{10,11... | collective-permute-start | bytes 7077896 | tf_op jit(solution)/shard_map/ppermute | solution.py:557
  390.6 117.0 %reduce-scatter.10.cloned.1.call-start = ((), (), s32[]{:S(2)}) async-start(), calls=%async_computation.10 | async-start | bytes 1474560 | tf_op jit(solution)/shard_map/reduce_scatter | solution.py:715
  393.1 20.8 %collective-permute-start.64 = (bf16[192,1536]{1,0:T(8,128)(2,1)S(1)}, bf16[192,1536]{1,0:T(8,128)(2,1)S(1)}, u32[]{:S(2)}, u32[]{:S(2)}) collective-permute-start(bf16[192,1536]{1,0:T(8,128)(2,1)S(1)} %get-tuple-element.289.refs_21_), channel_id=1, source_target_pairs={{0,2},{2,0},{4,6},{6,4},{1,3},{3,1},{5,7},{7,5},{8,10},{10,8},{12,... | collective-permute-start | bytes 1769480 | tf_op jit(solution)/shard_map/ppermute | solution.py:557
  394.1 19.8 %collective-permute-start.65 = (bf16[192,1536]{1,0:T(8,128)(2,1)S(1)}, bf16[192,1536]{1,0:T(8,128)(2,1)S(1)}, u32[]{:S(2)}, u32[]{:S(2)}) collective-permute-start(bf16[192,1536]{1,0:T(8,128)(2,1)S(1)} %get-tuple-element.288.refs_22_), channel_id=1, source_target_pairs={{0,4},{2,6},{4,0},{6,2},{1,5},{3,7},{5,1},{7,3},{8,12},{10,14},{12... | collective-permute-start | bytes 1769480 | tf_op jit(solution)/shard_map/ppermute | solution.py:557
  413.8 50.5 %collective-permute-start.71 = (bf16[2,384,768]{2,1,0:T(8,128)(2,1)}, bf16[2,384,768]{2,1,0:T(8,128)(2,1)}, u32[]{:S(2)}, u32[]{:S(2)}) collective-permute-start(bf16[2,384,768]{2,1,0:T(8,128)(2,1)} %get-tuple-element.212.refs_20_), channel_id=1, source_target_pairs={{0,1},{1,0},{2,3},{3,2},{4,5},{5,4},{6,7},{7,6},{8,9},{9,8},{10,11... | collective-permute-start | bytes 3538952 | tf_op jit(solution)/shard_map/ppermute | solution.py:557
  414.2 28.5 %collective-permute-start.68 = (bf16[384,1536]{1,0:T(8,128)(2,1)S(1)}, bf16[384,1536]{1,0:T(8,128)(2,1)}, u32[]{:S(2)}, u32[]{:S(2)}) collective-permute-start(bf16[384,1536]{1,0:T(8,128)(2,1)S(1)} %pad_maximum_fusion.3.refs_21_), channel_id=1, source_target_pairs={{0,2},{2,0},{4,6},{6,4},{1,3},{3,1},{5,7},{7,5},{8,10},{10,8},{12,... | collective-permute-start | bytes 3538952 | tf_op jit(solution)/shard_map/ppermute | solution.py:557
  418.0 28.5 %collective-permute-start.69 = (bf16[384,1536]{1,0:T(8,128)(2,1)S(1)}, bf16[384,1536]{1,0:T(8,128)(2,1)}, u32[]{:S(2)}, u32[]{:S(2)}) collective-permute-start(bf16[384,1536]{1,0:T(8,128)(2,1)S(1)} %pad_maximum_fusion.4.refs_22_), channel_id=1, source_target_pairs={{0,4},{2,6},{4,0},{6,2},{1,5},{3,7},{5,1},{7,3},{8,12},{10,14},{12... | collective-permute-start | bytes 3538952 | tf_op jit(solution)/shard_map/ppermute | solution.py:557
  439.6 24.7 %collective-permute-start.67 = (bf16[2,384,768]{2,1,0:T(8,128)(2,1)}, bf16[2,384,768]{2,1,0:T(8,128)(2,1)}, u32[]{:S(2)}, u32[]{:S(2)}) collective-permute-start(bf16[2,384,768]{2,1,0:T(8,128)(2,1)} %get-tuple-element.218), channel_id=1, source_target_pairs={{0,1},{1,0},{2,3},{3,2},{4,5},{5,4},{6,7},{7,6},{8,9},{9,8},{10,11... | collective-permute-start | bytes 3538952 | tf_op jit(solution)/shard_map/ppermute | solution.py:557
  467.8 61.6 %reduce-scatter.6.cloned.1.call-start = ((), (), s32[]{:S(2)}) async-start(), calls=%async_computation.8 | async-start | bytes 983040 | tf_op jit(solution)/shard_map/reduce_scatter | solution.py:715
  483.0 19.3 %collective-permute-start.75 = (bf16[512,768]{1,0:T(8,128)(2,1)}, bf16[512,768]{1,0:T(8,128)(2,1)}, u32[]{:S(2)}, u32[]{:S(2)}) collective-permute-start(bf16[512,768]{1,0:T(8,128)(2,1)} %fusion.14), channel_id=1, source_target_pairs={{0,4},{2,6},{4,0},{6,2},{1,5},{3,7},{5,1},{7,3},{8,12},{10,14},{12... | collective-permute-start | bytes 2359304 | tf_op jit(solution)/shard_map/ppermute | solution.py:557
  (174 other events, 1010.2 us)
Sparse Core Ops, SparseCore 0:
  12.5 33.1 all-gather.3
  47.8 29.5 all-gather.5
  79.0 46.3 all-gather.7
  316.3 20.9 reduce-scatter.13
  390.2 22.3 reduce-scatter.7
  414.8 27.4 reduce-scatter.11
  467.9 29.2 reduce-scatter.9
  505.7 23.5 reduce-scatter.5

commit v5 on v4

--- a/solution.py
+++ b/solution.py
@@ -241,7 +241,7 @@
     ids_ref,
     labels_ref,
     mix_ref,
-    scale_ref,
+    total_ref,
     weight_ref,
     pooled_ref,
     teacher_ref,
@@ -306,8 +306,9 @@
     dot_c = sum(jnp.sum(g * c, axis=-1, keepdims=True) for g, c in zip(goal, cls))
     dot_d = sum(jnp.sum(p * d, axis=-1, keepdims=True) for p, d in zip(prob, dist))
     loss_rows = 0.5 * (log_c - dot_c) + 0.5 * (log_d - dot_d)
-    loss_ref[...] = jnp.broadcast_to(row_sum(weight_ref[:, 0:1] * loss_rows), loss_ref.shape)
-    scale = scale_ref[:, 0:1]
+    share = weight_ref[:, 0:1] / total_ref[0]
+    loss_ref[...] = jnp.broadcast_to(row_sum(share * loss_rows), loss_ref.shape)
+    scale = 0.5 * weight_ref[:, 0:1] / total_ref[0]
     gfin_c = jnp.zeros(cls_buf.shape, F32)
     gfin_d = jnp.zeros(dist_buf.shape, F32)
     for block in range(mp):
@@ -930,7 +931,7 @@
 
     lanes = jnp.arange(wc, dtype=jnp.int32)
     class_ids = jnp.where(lanes[None] < cl, ranks[:, None] * cl + lanes[None], -1)[:, None]
-    head_small = [class_ids, wide(label_ids), wide(label_mix), wide(pooled)]
+    head_small = [class_ids, wide(label_ids), wide(label_mix), wide(image_weight), wide(pooled)]
 
     near[0], near[1] = tie(
         (near[0], near[1]),
@@ -997,13 +998,9 @@
             sending,
         )
         if layer == 0:
-            weight_sum = sum_over(sum_over(tie(weight_part, middle), "teach"), "dp")[0]
-            shares = [
-                wide(0.5 * image_weight / weight_sum),
-                wide(image_weight / weight_sum),
-            ]
+            weight_sum = sum_over(sum_over(tie(weight_part, middle), "teach"), "dp")
             for unit in units[2:]:
-                unit.near = tie(unit.near, *shares)
+                unit.near = tie(unit.near, weight_sum)
         sending = arrive(2 * layer + 1, middle)
         second, hidden, slope, output = call(
             functools.partial(mlp_forward_kernel, run, mp, n // 4),
@@ -1040,8 +1037,8 @@
             final_vec,
             head_bias,
             *head_small[:3],
-            *shares,
-            head_small[3],
+            ("smem", weight_sum),
+            *head_small[3:],
             teacher_all,
             *head_unit.refs(),
         ],

time: 610 us -> 608 us (level)
    unnamed x270 -> x272, local copies, waits for them, and re-layouts: 17.6 us -> 17.5 us
  transfers between devices with their start and end apart: 91 -> 91, of which waited for: 34 -> 34; matrix products, arithmetic and copies ran while one was open for 21% -> 20% of each run, Pallas kernels for 33% -> 33%
where the time goes in v5:
time: 608 us; the launch traced here: 599 us
  Pallas kernels  224 us (37%)
  waiting for transfers between devices  117 us (19%)
  other arithmetic  90.9 us (15%)
  local copies, waits for them, and re-layouts  68.2 us (11%)
  starting transfers between devices  65.1 us (11%)
  between operations  24.2 us (4%)
  matrix products  8.92 us (1%)
    pallas_call x18, Pallas kernels, call(): pl.pallas_call(grouped, out_shape=out_shape, in_specs=specs, out_specs=ou...  224 us
    ppermute x83, waiting for transfers between devices, swap(): lax.ppermute(values, axis, [(rank, rank ^ distance) for rank in range(siz...  101 us
    ppermute x83, starting transfers between devices, swap(): lax.ppermute(values, axis, [(rank, rank ^ distance) for rank in range(siz...  64.4 us
    convert_element_type x20, other arithmetic, add_low(): return (left.astype(F32) + right.astype(F32)).astype(BF)  18.6 us
    unnamed x272, local copies, waits for them, and re-layouts  17.5 us
    reduce_scatter x5, waiting for transfers between devices, rows(): self.pieces = lax.psum_scatter(total, 'dp', scatter_dimension=0, tiled=True)  15.3 us
    convert_element_type x4, other arithmetic, summed(): return jnp.concatenate(parts, axis=1).astype(BF).reshape(total.shape)  12.2 us
  transfers between devices with their start and end apart: 91, of which 34 were waited for; matrix products, arithmetic and copies ran while one was open for 20% of the time, Pallas kernels for 33%

profile of v5, /device:TPU:0, one launch (start us, length us, event | category | flops | bytes accessed | tf_op | source)
XLA Modules:
  0.0 598.6 jit_solution(12857599137893137643)
XLA Ops:
  10.7 1.8 concatenate.144
  12.5 3.0 collective-permute-start
  18.6 1.9 collective-permute-start.3
  37.7 1.8 add_multiply_fusion
  57.0 1.8 pad_maximum_fusion.12.refs_10_
  66.7 2.8 convolution_add_fusion.refs_1_.refs_2_
  69.6 7.8 %collective-permute-done.7.refs_6_.refs_10_ = bf16[384,768]{1,0:T(8,128)(2,1)S(1)} collective-permute-done((bf16[384,768]{1,0:T(8,128)(2,1)S(1)}, bf16[384,768]{1,0:T(8,128)(2,1)S(1)}, u32[]{:S(2)}, u32[]{:S(2)}) %collective-permute-start.7) | collective-permute-done | bytes 589856 | tf_op jit(solution)/shard_map/ppermute | solution.py:558
  79.9 6.2 %collective-permute-done.10.refs_9_.refs_13_ = bf16[192,768]{1,0:T(8,128)(2,1)S(1)} collective-permute-done((bf16[192,768]{1,0:T(8,128)(2,1)S(1)}, bf16[192,768]{1,0:T(8,128)(2,1)S(1)}, u32[]{:S(2)}, u32[]{:S(2)}) %collective-permute-start.10) | collective-permute-done | bytes 294944 | tf_op jit(solution)/shard_map/ppermute | solution.py:558
  94.6 20.5 %shard_map.427 = (bf16[576,768]{1,0:T(8,128)(2,1)}, bf16[4,576,576]{2,1,0:T(8,128)(2,1)}, bf16[4,576,192]{2,1,0:T(8,128)(2,1)}, f32[4,576,3]{2,1,0:T(8,128)}, f32[576,768]{1,0:T(8,128)}) custom-call(s32[1]{0:T(128)} %bitcast.8.refs_0_, f32[576,768]{1,0:T(8,128)} %convolution_add_fusion.refs_1_.refs_2_, f32[8,768]{1,0:T(8,128)} %slice_select_fusion.refs_2_.refs_3_, ...), custom_call_target="tpu_custom_call" | custom-call | flops 2300000000 | bytes 13924612 | tf_op jit(solution)/shard_map/pallas_call | solution.py:536
  119.9 2.0 collective-permute-done.20
  123.1 2.8 collective-permute-start.21
  127.3 3.9 collective-permute-start.22
  139.2 15.1 %shard_map.428 = (bf16[576,768]{1,0:T(8,128)(2,1)}, bf16[4,576,768]{2,1,0:T(8,128)(2,1)}, f32[4,576,768]{2,1,0:T(8,128)}, f32[576,768]{1,0:T(8,128)}) custom-call(s32[1]{0:T(128)} %bitcast.8.refs_0_, f32[576,768]{1,0:T(8,128)} %get-tuple-element.140.refs_1_.refs_2_, f32[8,768]{1,0:T(8,128)} %slice_select_fusion.refs_2_.refs_3_, f32[4,1,768]{2,1,0:T(1,128)} %copy.77.refs_3_, ...), custom_call_target="tpu_custom_call" | custom-call | flops 2300000000 | bytes 25104388 | tf_op jit(solution)/shard_map/pallas_call | solution.py:536
  158.3 4.9 collective-permute-done.30.refs_8_.refs_12_
  171.8 20.7 %shard_map.429 = (bf16[576,768]{1,0:T(8,128)(2,1)}, bf16[4,576,576]{2,1,0:T(8,128)(2,1)}, bf16[4,576,192]{2,1,0:T(8,128)(2,1)}, f32[4,576,3]{2,1,0:T(8,128)}, f32[576,768]{1,0:T(8,128)}) custom-call(s32[1]{0:T(128)} %bitcast.8.refs_0_, f32[576,768]{1,0:T(8,128)} %get-tuple-element.148.refs_1_.refs_2_, f32[8,768]{1,0:T(8,128)} %pad.81.refs_2_.refs_3_, ...), custom_call_target="tpu_custom_call" | custom-call | flops 2300000000 | bytes 14317828 | tf_op jit(solution)/shard_map/pallas_call | solution.py:536
  192.4 6.9 %collective-permute-done.37.refs_5_.refs_12_.refs_8_ = bf16[384,2048]{1,0:T(8,128)(2,1)S(1)} collective-permute-done((bf16[384,2048]{1,0:T(8,128)(2,1)S(1)}, bf16[384,2048]{1,0:T(8,128)(2,1)S(1)}, u32[]{:S(2)}, u32[]{:S(2)}) %collective-permute-start.37) | collective-permute-done | bytes 1572896 | tf_op jit(solution)/shard_map/ppermute | solution.py:558
  203.7 17.6 %collective-permute-done.39.refs_7_.refs_14_.refs_10_ = bf16[192,2048]{1,0:T(8,128)(2,1)} collective-permute-done((bf16[192,2048]{1,0:T(8,128)(2,1)S(1)}, bf16[192,2048]{1,0:T(8,128)(2,1)}, u32[]{:S(2)}, u32[]{:S(2)}) %collective-permute-start.39) | collective-permute-done | bytes 786464 | tf_op jit(solution)/shard_map/ppermute | solution.py:558
  225.3 14.9 %shard_map.430 = (bf16[576,768]{1,0:T(8,128)(2,1)}, bf16[4,576,768]{2,1,0:T(8,128)(2,1)}, f32[4,576,768]{2,1,0:T(8,128)}, f32[576,768]{1,0:T(8,128)}) custom-call(s32[1]{0:T(128)} %bitcast.8.refs_0_, f32[576,768]{1,0:T(8,128)} %get-tuple-element.155.refs_1_.refs_2_, f32[8,768]{1,0:T(8,128)} %pad.81.refs_2_.refs_3_, f32[4,1,768]{2,1,0:T(1,128)} %copy.79.refs_3_, ...), custom_call_target="tpu_custom_call" | custom-call | flops 2300000000 | bytes 27660292 | tf_op jit(solution)/shard_map/pallas_call | solution.py:536
  240.2 8.7 %shard_map.431 = (bf16[4,384,512]{2,1,0:T(8,128)(2,1)}, bf16[4,384,512]{2,1,0:T(8,128)(2,1)}, f32[4,1,512]{2,1,0:T(1,128)}, f32[576,768]{1,0:T(8,128)}, f32[8,768]{1,0:T(8,128)}, /*index=5*/f32[8,128]{1,0:T(8,128)}) custom-call(s32[1]{0:T(128)} %bitcast.8.refs_0_, f32[576,768]{1,0:T(8,128)} %get-tuple-element.158.refs_1_, f32[8,768]{1,0:T(8,128)} %pad.82.refs_2_, ...), custom_call_target="tpu_custom_call" | custom-call | flops 2300000000 | bytes 19807496 | tf_op jit(solution)/shard_map/pallas_call | solution.py:536
  251.5 14.1 %shard_map.432 = (f32[576,768]{1,0:T(8,128)}, bf16[2,384,1536]{2,1,0:T(8,128)(2,1)}, bf16[2,384,1536]{2,1,0:T(8,128)(2,1)}, f32[2,1,768]{2,1,0:T(1,128)}, f32[8,768]{1,0:T(8,128)}) custom-call(s32[1]{0:T(128)} %bitcast.8.refs_0_, f32[576,768]{1,0:T(8,128)} %get-tuple-element.159.refs_1_, f32[576,768]{1,0:T(8,128)} %get-tuple-element.155.refs_1_.refs_2_, ...), custom_call_target="tpu_custom_call" | custom-call | flops 2300000000 | bytes 35739652 | tf_op jit(solution)/shard_map/pallas_call | solution.py:536
  270.8 16.2 %shard_map.433 = (f32[576,768]{1,0:T(8,128)}, bf16[2,384,1536]{2,1,0:T(8,128)(2,1)}, bf16[2,384,1536]{2,1,0:T(8,128)(2,1)}, f32[2,1,768]{2,1,0:T(1,128)}, f32[8,768]{1,0:T(8,128)}) custom-call(s32[1]{0:T(128)} %bitcast.8.refs_0_, f32[576,768]{1,0:T(8,128)} %get-tuple-element.159.refs_1_, f32[576,768]{1,0:T(8,128)} %get-tuple-element.155.refs_1_.refs_2_, ...), custom_call_target="tpu_custom_call" | custom-call | flops 2300000000 | bytes 38688772 | tf_op jit(solution)/shard_map/pallas_call | solution.py:536
  293.1 17.8 %shard_map.434 = (f32[576,768]{1,0:T(8,128)}, bf16[2,384,768]{2,1,0:T(8,128)(2,1)}, bf16[2,384,768]{2,1,0:T(8,128)(2,1)}, f32[2,1,576]{2,1,0:T(1,128)}, f32[8,768]{1,0:T(8,128)}) custom-call(s32[1]{0:T(128)} %bitcast.8.refs_0_, f32[576,768]{1,0:T(8,128)} %get-tuple-element.168.refs_1_, f32[576,768]{1,0:T(8,128)} %get-tuple-element.148.refs_1_.refs_2_, ...), custom_call_target="tpu_custom_call" | custom-call | flops 2300000000 | bytes 21219076 | tf_op jit(solution)/shard_map/pallas_call | solution.py:536
  311.8 2.0 fusion.16.refs_21_
  321.3 20.3 %shard_map.435 = (f32[576,768]{1,0:T(8,128)}, bf16[2,384,768]{2,1,0:T(8,128)(2,1)}, bf16[2,384,768]{2,1,0:T(8,128)(2,1)}, f32[2,1,576]{2,1,0:T(1,128)}, f32[8,768]{1,0:T(8,128)}) custom-call(s32[1]{0:T(128)} %bitcast.8.refs_0_, f32[576,768]{1,0:T(8,128)} %get-tuple-element.168.refs_1_, f32[576,768]{1,0:T(8,128)} %get-tuple-element.148.refs_1_.refs_2_, ...), custom_call_target="tpu_custom_call" | custom-call | flops 2300000000 | bytes 22595332 | tf_op jit(solution)/shard_map/pallas_call | solution.py:536
  345.7 14.0 %shard_map.436 = (f32[576,768]{1,0:T(8,128)}, bf16[2,384,1536]{2,1,0:T(8,128)(2,1)}, bf16[2,384,1536]{2,1,0:T(8,128)(2,1)}, f32[2,1,768]{2,1,0:T(1,128)}, f32[8,768]{1,0:T(8,128)}) custom-call(s32[1]{0:T(128)} %bitcast.8.refs_0_, f32[576,768]{1,0:T(8,128)} %get-tuple-element.186.refs_1_, f32[576,768]{1,0:T(8,128)} %get-tuple-element.140.refs_1_.refs_2_, ...), custom_call_target="tpu_custom_call" | custom-call | flops 2300000000 | bytes 32790532 | tf_op jit(solution)/shard_map/pallas_call | solution.py:536
  365.2 3.6 fusion.1.refs_19_
  368.8 16.3 %shard_map.437 = (f32[576,768]{1,0:T(8,128)}, bf16[2,384,1536]{2,1,0:T(8,128)(2,1)}, bf16[2,384,1536]{2,1,0:T(8,128)(2,1)}, f32[2,1,768]{2,1,0:T(1,128)}, f32[8,768]{1,0:T(8,128)}) custom-call(s32[1]{0:T(128)} %bitcast.8.refs_0_, f32[576,768]{1,0:T(8,128)} %get-tuple-element.186.refs_1_, f32[576,768]{1,0:T(8,128)} %get-tuple-element.140.refs_1_.refs_2_, ...), custom_call_target="tpu_custom_call" | custom-call | flops 2300000000 | bytes 37509124 | tf_op jit(solution)/shard_map/pallas_call | solution.py:536
  385.2 2.5 fusion.8.refs_20_
  388.4 2.2 add_convert_fusion.2
  392.9 17.8 %shard_map.438 = (f32[576,768]{1,0:T(8,128)}, bf16[2,384,768]{2,1,0:T(8,128)(2,1)}, bf16[2,384,768]{2,1,0:T(8,128)(2,1)}, f32[2,1,576]{2,1,0:T(1,128)}, f32[8,768]{1,0:T(8,128)}) custom-call(s32[1]{0:T(128)} %bitcast.8.refs_0_, f32[576,768]{1,0:T(8,128)} %get-tuple-element.201.refs_1_, f32[576,768]{1,0:T(8,128)} %convolution_add_fusion.refs_1_.refs_2_, ...), custom_call_target="tpu_custom_call" | custom-call | flops 2300000000 | bytes 21022468 | tf_op jit(solution)/shard_map/pallas_call | solution.py:536
  416.7 20.5 %shard_map.439 = (f32[576,768]{1,0:T(8,128)}, bf16[2,384,768]{2,1,0:T(8,128)(2,1)}, bf16[2,384,768]{2,1,0:T(8,128)(2,1)}, f32[2,1,576]{2,1,0:T(1,128)}, f32[8,768]{1,0:T(8,128)}) custom-call(s32[1]{0:T(128)} %bitcast.8.refs_0_, f32[576,768]{1,0:T(8,128)} %get-tuple-element.201.refs_1_, f32[576,768]{1,0:T(8,128)} %convolution_add_fusion.refs_1_.refs_2_, ...), custom_call_target="tpu_custom_call" | custom-call | flops 2300000000 | bytes 22202116 | tf_op jit(solution)/shard_map/pallas_call | solution.py:536
  440.3 3.9 collective-permute-done.69
  444.2 4.1 fusion
  451.3 2.3 convolution_convert_fusion
  470.1 6.0 %collective-permute-done.72 = bf16[256,768]{1,0:T(8,128)(2,1)} collective-permute-done((bf16[256,768]{1,0:T(8,128)(2,1)}, bf16[256,768]{1,0:T(8,128)(2,1)}, u32[]{:S(2)}, u32[]{:S(2)}) %collective-permute-start.72) | collective-permute-done | bytes 393248 | tf_op jit(solution)/shard_map/ppermute | solution.py:558
  476.1 2.5 collective-permute-done.73
  486.9 13.0 %collective-permute-done.75 = bf16[512,768]{1,0:T(8,128)(2,1)} collective-permute-done((bf16[512,768]{1,0:T(8,128)(2,1)}, bf16[512,768]{1,0:T(8,128)(2,1)}, u32[]{:S(2)}, u32[]{:S(2)}) %collective-permute-start.75) | collective-permute-done | bytes 786464 | tf_op jit(solution)/shard_map/ppermute | solution.py:558
  508.0 3.5 multiply_reduce_fusion
  511.5 15.3 %reduce-scatter.6.cloned.1.call-done = bf16[128,768]{1,0:T(8,128)(2,1)} async-done(((bf16[512,768]{1,0:T(8,128)(2,1)}), bf16[128,768]{1,0:T(8,128)(2,1)}) %reduce-scatter.6.cloned.1.call-update) | async-done | bytes 196624 | tf_op jit(solution)/shard_map/reduce_scatter | solution.py:716
  528.8 3.2 multiply_reduce_fusion.2
  538.9 2.7 concatenate.180
  541.7 3.7 collective-permute-done.76.refs_2_
  548.2 4.2 collective-permute-done.77.refs_2_
  561.2 2.1 collective-permute-done.79.refs_2_
  567.6 3.1 collective-permute-done.80.refs_2_
  579.8 2.0 multiply_subtract_fusion.5
  581.8 2.5 multiply_subtract_fusion.3
  589.4 1.9 multiply_subtract_fusion.2
  (698 shorter events, 206.2 us)
Async XLA Ops:
  7.2 51.6 %all-gather.4.cloned.1.call-start = ((), (), s32[]{:S(2)}) async-start(), calls=%async_computation.5 | async-start | bytes 1474560 | tf_op jit(solution)/shard_map/all_gather | solution.py:856
  12.5 67.5 %all-gather.6.cloned.1.call-start = ((), (), s32[]{:S(2)}) async-start(), calls=%async_computation.6 | async-start | bytes 1474560 | tf_op jit(solution)/shard_map/all_gather | solution.py:856
  12.5 38.6 %collective-permute-start = (f32[2804]{0:T(1024)}, f32[2804]{0:T(1024)}, u32[]{:S(2)}, u32[]{:S(2)}) collective-permute-start(f32[2804]{0:T(1024)} %param.40), channel_id=1, source_target_pairs={{0,2},{2,0},{4,6},{6,4},{1,3},{3,1},{5,7},{7,5},{8,10},{10,8},{12,... | collective-permute-start | bytes 33656 | tf_op jit(solution)/shard_map/ppermute | solution.py:558
  15.5 36.3 %collective-permute-start.1 = (f32[2804]{0:T(1024)}, f32[2804]{0:T(1024)}, u32[]{:S(2)}, u32[]{:S(2)}) collective-permute-start(f32[2804]{0:T(1024)} %param.40), channel_id=1, source_target_pairs={{0,4},{2,6},{4,0},{6,2},{1,5},{3,7},{5,1},{7,3},{8,12},{10,14},{12... | collective-permute-start | bytes 33656 | tf_op jit(solution)/shard_map/ppermute | solution.py:558
  17.0 35.5 %collective-permute-start.2 = (f32[2804]{0:T(1024)}, f32[2804]{0:T(1024)}, u32[]{:S(2)}, u32[]{:S(2)}) collective-permute-start(f32[2804]{0:T(1024)} %param.40), channel_id=1, source_target_pairs={{0,6},{2,4},{4,2},{6,0},{1,7},{3,5},{5,3},{7,1},{8,14},{10,12},{12... | collective-permute-start | bytes 33656 | tf_op jit(solution)/shard_map/ppermute | solution.py:558
  18.6 36.7 %collective-permute-start.3 = (bf16[224,256]{1,0:T(8,128)(2,1)}, bf16[224,256]{1,0:T(8,128)(2,1)}, u32[]{:S(2)}, u32[]{:S(2)}) collective-permute-start(bf16[224,256]{1,0:T(8,128)(2,1)} %get-tuple-element.338), channel_id=1, source_target_pairs={{0,2},{2,0},{4,6},{6,4},{1,3},{3,1},{5,7},{7,5},{8,10},{10,8},{12,... | collective-permute-start | bytes 344072 | tf_op jit(solution)/shard_map/ppermute | solution.py:558
  20.6 34.7 %collective-permute-start.4 = (bf16[224,256]{1,0:T(8,128)(2,1)}, bf16[224,256]{1,0:T(8,128)(2,1)}, u32[]{:S(2)}, u32[]{:S(2)}) collective-permute-start(bf16[224,256]{1,0:T(8,128)(2,1)} %get-tuple-element.338), channel_id=1, source_target_pairs={{0,4},{2,6},{4,0},{6,2},{1,5},{3,7},{5,1},{7,3},{8,12},{10,14},{12... | collective-permute-start | bytes 344072 | tf_op jit(solution)/shard_map/ppermute | solution.py:558
  25.0 107.6 %all-gather.8.cloned.1.call-start = ((), (), s32[]{:S(2)}) async-start(), calls=%async_computation.7 | async-start | bytes 2703360 | tf_op jit(solution)/shard_map/all_gather | solution.py:856
  61.5 422.5 %reduce-scatter.14.cloned.1.call-start = ((), (), s32[]{:S(2)}) async-start(), calls=%async_computation.12 | async-start | bytes 491520 | tf_op jit(solution)/shard_map/reduce_scatter | solution.py:716
  87.3 27.9 %collective-permute-start.16 = (bf16[384,1536]{1,0:T(8,128)(2,1)}, bf16[384,1536]{1,0:T(8,128)(2,1)S(1)}, u32[]{:S(2)}, u32[]{:S(2)}) collective-permute-start(bf16[384,1536]{1,0:T(8,128)(2,1)} %all-gather.6.cloned.1.call-done.refs_15_.refs_4_.refs_7_), channel_id=1, source_target_pairs={{0,2},{2,0},{4,6},{6,4},{1,3},{3,1},{5,7},{7,5},{8,10},{10,8},{12,... | collective-permute-start | bytes 3538952 | tf_op jit(solution)/shard_map/ppermute | solution.py:558
  88.4 26.8 %collective-permute-start.17 = (bf16[384,1536]{1,0:T(8,128)(2,1)}, bf16[384,1536]{1,0:T(8,128)(2,1)S(1)}, u32[]{:S(2)}, u32[]{:S(2)}) collective-permute-start(bf16[384,1536]{1,0:T(8,128)(2,1)} %all-gather.6.cloned.1.call-done.refs_15_.refs_4_.refs_7_), channel_id=1, source_target_pairs={{0,4},{2,6},{4,0},{6,2},{1,5},{3,7},{5,1},{7,3},{8,12},{10,14},{12... | collective-permute-start | bytes 3538952 | tf_op jit(solution)/shard_map/ppermute | solution.py:558
  134.3 20.0 %collective-permute-start.28 = (bf16[384,768]{1,0:T(8,128)(2,1)S(1)}, bf16[384,768]{1,0:T(8,128)(2,1)S(1)}, u32[]{:S(2)}, u32[]{:S(2)}) collective-permute-start(bf16[384,768]{1,0:T(8,128)(2,1)S(1)} %slice.983.refs_14_.refs_5_.refs_9_), channel_id=1, source_target_pairs={{0,2},{2,0},{4,6},{6,4},{1,3},{3,1},{5,7},{7,5},{8,10},{10,8},{12,... | collective-permute-start | bytes 1769480 | tf_op jit(solution)/shard_map/ppermute | solution.py:558
  164.4 35.0 %collective-permute-start.37 = (bf16[384,2048]{1,0:T(8,128)(2,1)S(1)}, bf16[384,2048]{1,0:T(8,128)(2,1)S(1)}, u32[]{:S(2)}, u32[]{:S(2)}) collective-permute-start(bf16[384,2048]{1,0:T(8,128)(2,1)S(1)} %slice.984.refs_15_.refs_4_.refs_11_.refs_7_), channel_id=1, source_target_pairs={{0,2},{2,0},{4,6},{6,4},{1,3},{3,1},{5,7},{7,5},{8,10},{10,8},{12,... | collective-permute-start | bytes 4718600 | tf_op jit(solution)/shard_map/ppermute | solution.py:558
  165.1 34.8 %collective-permute-start.38 = (bf16[384,2048]{1,0:T(8,128)(2,1)S(1)}, bf16[384,2048]{1,0:T(8,128)(2,1)}, u32[]{:S(2)}, u32[]{:S(2)}) collective-permute-start(bf16[384,2048]{1,0:T(8,128)(2,1)S(1)} %slice.984.refs_15_.refs_4_.refs_11_.refs_7_), channel_id=1, source_target_pairs={{0,4},{2,6},{4,0},{6,2},{1,5},{3,7},{5,1},{7,3},{8,12},{10,14},{12... | collective-permute-start | bytes 4718600 | tf_op jit(solution)/shard_map/ppermute | solution.py:558
  169.9 53.5 %collective-permute-start.41 = (bf16[384,2048]{1,0:T(8,128)(2,1)S(1)}, bf16[384,2048]{1,0:T(8,128)(2,1)}, u32[]{:S(2)}, u32[]{:S(2)}) collective-permute-start(bf16[384,2048]{1,0:T(8,128)(2,1)S(1)} %slice.984.refs_15_.refs_4_.refs_11_.refs_7_), channel_id=1, source_target_pairs={{0,1},{1,0},{2,3},{3,2},{4,5},{5,4},{6,7},{7,6},{8,9},{9,8},{10,11... | collective-permute-start | bytes 4718600 | tf_op jit(solution)/shard_map/ppermute | solution.py:558
  199.9 23.4 %collective-permute-start.42 = (bf16[384,2048]{1,0:T(8,128)(2,1)S(1)}, bf16[384,2048]{1,0:T(8,128)(2,1)}, u32[]{:S(2)}, u32[]{:S(2)}) collective-permute-start(bf16[384,2048]{1,0:T(8,128)(2,1)S(1)} %collective-permute-done.37.refs_5_.refs_12_.refs_8_), channel_id=1, source_target_pairs={{0,1},{1,0},{2,3},{3,2},{4,5},{5,4},{6,7},{7,6},{8,9},{9,8},{10,11... | collective-permute-start | bytes 4718600 | tf_op jit(solution)/shard_map/ppermute | solution.py:558
  201.2 20.1 %collective-permute-start.39 = (bf16[192,2048]{1,0:T(8,128)(2,1)S(1)}, bf16[192,2048]{1,0:T(8,128)(2,1)}, u32[]{:S(2)}, u32[]{:S(2)}) collective-permute-start(bf16[192,2048]{1,0:T(8,128)(2,1)S(1)} %slice.776), channel_id=1, source_target_pairs={{0,2},{2,0},{4,6},{6,4},{1,3},{3,1},{5,7},{7,5},{8,10},{10,8},{12,... | collective-permute-start | bytes 2359304 | tf_op jit(solution)/shard_map/ppermute | solution.py:558
  202.6 20.7 %collective-permute-start.43 = (bf16[384,2048]{1,0:T(8,128)(2,1)}, bf16[384,2048]{1,0:T(8,128)(2,1)}, u32[]{:S(2)}, u32[]{:S(2)}) collective-permute-start(bf16[384,2048]{1,0:T(8,128)(2,1)} %collective-permute-done.38.refs_6_.refs_13_.refs_9_), channel_id=1, source_target_pairs={{0,1},{1,0},{2,3},{3,2},{4,5},{5,4},{6,7},{7,6},{8,9},{9,8},{10,11... | collective-permute-start | bytes 4718600 | tf_op jit(solution)/shard_map/ppermute | solution.py:558
  202.8 19.8 %collective-permute-start.40 = (bf16[192,2048]{1,0:T(8,128)(2,1)S(1)}, bf16[192,2048]{1,0:T(8,128)(2,1)}, u32[]{:S(2)}, u32[]{:S(2)}) collective-permute-start(bf16[192,2048]{1,0:T(8,128)(2,1)S(1)} %slice.777), channel_id=1, source_target_pairs={{0,4},{2,6},{4,0},{6,2},{1,5},{3,7},{5,1},{7,3},{8,12},{10,14},{12... | collective-permute-start | bytes 2359304 | tf_op jit(solution)/shard_map/ppermute | solution.py:558
  248.9 18.6 %collective-permute-start.46 = (bf16[4,384,512]{2,1,0:T(8,128)(2,1)}, bf16[4,384,512]{2,1,0:T(8,128)(2,1)S(1)}, u32[]{:S(2)}, u32[]{:S(2)}) collective-permute-start(bf16[4,384,512]{2,1,0:T(8,128)(2,1)} %get-tuple-element.163.refs_17_), channel_id=1, source_target_pairs={{0,1},{1,0},{2,3},{3,2},{4,5},{5,4},{6,7},{7,6},{8,9},{9,8},{10,11... | collective-permute-start | bytes 4718600 | tf_op jit(solution)/shard_map/ppermute | solution.py:558
  265.5 24.8 %collective-permute-start.49 = (bf16[2,384,1536]{2,1,0:T(8,128)(2,1)}, bf16[2,384,1536]{2,1,0:T(8,128)(2,1)S(1)}, u32[]{:S(2)}, u32[]{:S(2)}) collective-permute-start(bf16[2,384,1536]{2,1,0:T(8,128)(2,1)} %get-tuple-element.165.refs_18_), channel_id=1, source_target_pairs={{0,1},{1,0},{2,3},{3,2},{4,5},{5,4},{6,7},{7,6},{8,9},{9,8},{10,11... | collective-permute-start | bytes 7077896 | tf_op jit(solution)/shard_map/ppermute | solution.py:558
  268.7 19.2 %collective-permute-start.47 = (bf16[192,512]{1,0:T(8,128)(2,1)S(1)}, bf16[192,512]{1,0:T(8,128)(2,1)S(1)}, u32[]{:S(2)}, u32[]{:S(2)}) collective-permute-start(bf16[192,512]{1,0:T(8,128)(2,1)S(1)} %get-tuple-element.317.refs_19_), channel_id=1, source_target_pairs={{0,2},{2,0},{4,6},{6,4},{1,3},{3,1},{5,7},{7,5},{8,10},{10,8},{12,... | collective-permute-start | bytes 589832 | tf_op jit(solution)/shard_map/ppermute | solution.py:558
  269.9 18.0 %collective-permute-start.48 = (bf16[192,512]{1,0:T(8,128)(2,1)S(1)}, bf16[192,512]{1,0:T(8,128)(2,1)S(1)}, u32[]{:S(2)}, u32[]{:S(2)}) collective-permute-start(bf16[192,512]{1,0:T(8,128)(2,1)S(1)} %get-tuple-element.316.refs_20_), channel_id=1, source_target_pairs={{0,4},{2,6},{4,0},{6,2},{1,5},{3,7},{5,1},{7,3},{8,12},{10,14},{12... | collective-permute-start | bytes 589832 | tf_op jit(solution)/shard_map/ppermute | solution.py:558
  287.0 29.2 %collective-permute-start.54 = (bf16[2,384,1536]{2,1,0:T(8,128)(2,1)}, bf16[2,384,1536]{2,1,0:T(8,128)(2,1)}, u32[]{:S(2)}, u32[]{:S(2)}) collective-permute-start(bf16[2,384,1536]{2,1,0:T(8,128)(2,1)} %get-tuple-element.173.refs_19_), channel_id=1, source_target_pairs={{0,1},{1,0},{2,3},{3,2},{4,5},{5,4},{6,7},{7,6},{8,9},{9,8},{10,11... | collective-permute-start | bytes 7077896 | tf_op jit(solution)/shard_map/ppermute | solution.py:558
  288.0 22.9 %collective-permute-start.51 = (bf16[384,512]{1,0:T(8,128)(2,1)S(1)}, bf16[384,512]{1,0:T(8,128)(2,1)S(1)}, u32[]{:S(2)}, u32[]{:S(2)}) collective-permute-start(bf16[384,512]{1,0:T(8,128)(2,1)S(1)} %pad_maximum_fusion.16.refs_21_), channel_id=1, source_target_pairs={{0,4},{2,6},{4,0},{6,2},{1,5},{3,7},{5,1},{7,3},{8,12},{10,14},{12... | collective-permute-start | bytes 1179656 | tf_op jit(solution)/shard_map/ppermute | solution.py:558
  289.3 21.6 %collective-permute-start.50 = (bf16[384,512]{1,0:T(8,128)(2,1)S(1)}, bf16[384,512]{1,0:T(8,128)(2,1)S(1)}, u32[]{:S(2)}, u32[]{:S(2)}) collective-permute-start(bf16[384,512]{1,0:T(8,128)(2,1)S(1)} %pad_maximum_fusion.15.refs_20_), channel_id=1, source_target_pairs={{0,2},{2,0},{4,6},{6,4},{1,3},{3,1},{5,7},{7,5},{8,10},{10,8},{12,... | collective-permute-start | bytes 1179656 | tf_op jit(solution)/shard_map/ppermute | solution.py:558
  291.1 22.8 %collective-permute-start.52 = (bf16[192,1536]{1,0:T(8,128)(2,1)S(1)}, bf16[192,1536]{1,0:T(8,128)(2,1)}, u32[]{:S(2)}, u32[]{:S(2)}) collective-permute-start(bf16[192,1536]{1,0:T(8,128)(2,1)S(1)} %get-tuple-element.291.refs_22_), channel_id=1, source_target_pairs={{0,2},{2,0},{4,6},{6,4},{1,3},{3,1},{5,7},{7,5},{8,10},{10,8},{12,... | collective-permute-start | bytes 1769480 | tf_op jit(solution)/shard_map/ppermute | solution.py:558
  292.2 21.6 %collective-permute-start.53 = (bf16[192,1536]{1,0:T(8,128)(2,1)S(1)}, bf16[192,1536]{1,0:T(8,128)(2,1)}, u32[]{:S(2)}, u32[]{:S(2)}) collective-permute-start(bf16[192,1536]{1,0:T(8,128)(2,1)S(1)} %get-tuple-element.290.refs_23_), channel_id=1, source_target_pairs={{0,4},{2,6},{4,0},{6,2},{1,5},{3,7},{5,1},{7,3},{8,12},{10,14},{12... | collective-permute-start | bytes 1769480 | tf_op jit(solution)/shard_map/ppermute | solution.py:558
  311.0 31.0 %collective-permute-start.55 = (bf16[2,384,768]{2,1,0:T(8,128)(2,1)}, bf16[2,384,768]{2,1,0:T(8,128)(2,1)}, u32[]{:S(2)}, u32[]{:S(2)}) collective-permute-start(bf16[2,384,768]{2,1,0:T(8,128)(2,1)} %get-tuple-element.179.refs_20_), channel_id=1, source_target_pairs={{0,1},{1,0},{2,3},{3,2},{4,5},{5,4},{6,7},{7,6},{8,9},{9,8},{10,11... | collective-permute-start | bytes 3538952 | tf_op jit(solution)/shard_map/ppermute | solution.py:558
  313.8 172.2 %reduce-scatter.8.cloned.1.call-start = ((), (), s32[]{:S(2)}) async-start(), calls=%async_computation.9 | async-start | bytes 737280 | tf_op jit(solution)/shard_map/reduce_scatter | solution.py:716
  315.2 48.9 %collective-permute-start.56 = (bf16[384,1536]{1,0:T(8,128)(2,1)S(1)}, bf16[384,1536]{1,0:T(8,128)(2,1)}, u32[]{:S(2)}, u32[]{:S(2)}) collective-permute-start(bf16[384,1536]{1,0:T(8,128)(2,1)S(1)} %pad_maximum_fusion.1.refs_22_), channel_id=1, source_target_pairs={{0,2},{2,0},{4,6},{6,4},{1,3},{3,1},{5,7},{7,5},{8,10},{10,8},{12,... | collective-permute-start | bytes 3538952 | tf_op jit(solution)/shard_map/ppermute | solution.py:558
  320.1 44.0 %collective-permute-start.57 = (bf16[384,1536]{1,0:T(8,128)(2,1)S(1)}, bf16[384,1536]{1,0:T(8,128)(2,1)}, u32[]{:S(2)}, u32[]{:S(2)}) collective-permute-start(bf16[384,1536]{1,0:T(8,128)(2,1)S(1)} %pad_maximum_fusion.2.refs_23_), channel_id=1, source_target_pairs={{0,4},{2,6},{4,0},{6,2},{1,5},{3,7},{5,1},{7,3},{8,12},{10,14},{12... | collective-permute-start | bytes 3538952 | tf_op jit(solution)/shard_map/ppermute | solution.py:558
  341.6 21.1 %collective-permute-start.60 = (bf16[2,384,768]{2,1,0:T(8,128)(2,1)}, bf16[2,384,768]{2,1,0:T(8,128)(2,1)}, u32[]{:S(2)}, u32[]{:S(2)}) collective-permute-start(bf16[2,384,768]{2,1,0:T(8,128)(2,1)} %get-tuple-element.190.refs_17_), channel_id=1, source_target_pairs={{0,1},{1,0},{2,3},{3,2},{4,5},{5,4},{6,7},{7,6},{8,9},{9,8},{10,11... | collective-permute-start | bytes 3538952 | tf_op jit(solution)/shard_map/ppermute | solution.py:558
  359.8 28.7 %collective-permute-start.63 = (bf16[2,384,1536]{2,1,0:T(8,128)(2,1)}, bf16[2,384,1536]{2,1,0:T(8,128)(2,1)}, u32[]{:S(2)}, u32[]{:S(2)}) collective-permute-start(bf16[2,384,1536]{2,1,0:T(8,128)(2,1)} %get-tuple-element.194.refs_18_), channel_id=1, source_target_pairs={{0,1},{1,0},{2,3},{3,2},{4,5},{5,4},{6,7},{7,6},{8,9},{9,8},{10,11... | collective-permute-start | bytes 7077896 | tf_op jit(solution)/shard_map/ppermute | solution.py:558
  361.6 23.5 %collective-permute-start.61 = (bf16[384,768]{1,0:T(8,128)(2,1)S(1)}, bf16[384,768]{1,0:T(8,128)(2,1)}, u32[]{:S(2)}, u32[]{:S(2)}) collective-permute-start(bf16[384,768]{1,0:T(8,128)(2,1)S(1)} %pad_maximum_fusion.10.refs_20_), channel_id=1, source_target_pairs={{0,2},{2,0},{4,6},{6,4},{1,3},{3,1},{5,7},{7,5},{8,10},{10,8},{12,... | collective-permute-start | bytes 1769480 | tf_op jit(solution)/shard_map/ppermute | solution.py:558
  364.2 20.9 %collective-permute-start.62 = (bf16[384,768]{1,0:T(8,128)(2,1)S(1)}, bf16[384,768]{1,0:T(8,128)(2,1)S(1)}, u32[]{:S(2)}, u32[]{:S(2)}) collective-permute-start(bf16[384,768]{1,0:T(8,128)(2,1)S(1)} %pad_maximum_fusion.11.refs_21_), channel_id=1, source_target_pairs={{0,4},{2,6},{4,0},{6,2},{1,5},{3,7},{5,1},{7,3},{8,12},{10,14},{12... | collective-permute-start | bytes 1769480 | tf_op jit(solution)/shard_map/ppermute | solution.py:558
  387.7 116.5 %reduce-scatter.12.cloned.1.call-start = ((), (), s32[]{:S(2)}) async-start(), calls=%async_computation.11 | async-start | bytes 1474560 | tf_op jit(solution)/shard_map/reduce_scatter | solution.py:716
  387.9 25.1 %collective-permute-start.66 = (bf16[2,384,1536]{2,1,0:T(8,128)(2,1)}, bf16[2,384,1536]{2,1,0:T(8,128)(2,1)}, u32[]{:S(2)}, u32[]{:S(2)}) collective-permute-start(bf16[2,384,1536]{2,1,0:T(8,128)(2,1)} %get-tuple-element.206.refs_19_), channel_id=1, source_target_pairs={{0,1},{1,0},{2,3},{3,2},{4,5},{5,4},{6,7},{7,6},{8,9},{9,8},{10,11... | collective-permute-start | bytes 7077896 | tf_op jit(solution)/shard_map/ppermute | solution.py:558
  388.3 117.0 %reduce-scatter.10.cloned.1.call-start = ((), (), s32[]{:S(2)}) async-start(), calls=%async_computation.10 | async-start | bytes 1474560 | tf_op jit(solution)/shard_map/reduce_scatter | solution.py:716
  390.8 20.8 %collective-permute-start.64 = (bf16[192,1536]{1,0:T(8,128)(2,1)S(1)}, bf16[192,1536]{1,0:T(8,128)(2,1)S(1)}, u32[]{:S(2)}, u32[]{:S(2)}) collective-permute-start(bf16[192,1536]{1,0:T(8,128)(2,1)S(1)} %get-tuple-element.289.refs_21_), channel_id=1, source_target_pairs={{0,2},{2,0},{4,6},{6,4},{1,3},{3,1},{5,7},{7,5},{8,10},{10,8},{12,... | collective-permute-start | bytes 1769480 | tf_op jit(solution)/shard_map/ppermute | solution.py:558
  391.8 19.8 %collective-permute-start.65 = (bf16[192,1536]{1,0:T(8,128)(2,1)S(1)}, bf16[192,1536]{1,0:T(8,128)(2,1)S(1)}, u32[]{:S(2)}, u32[]{:S(2)}) collective-permute-start(bf16[192,1536]{1,0:T(8,128)(2,1)S(1)} %get-tuple-element.288.refs_22_), channel_id=1, source_target_pairs={{0,4},{2,6},{4,0},{6,2},{1,5},{3,7},{5,1},{7,3},{8,12},{10,14},{12... | collective-permute-start | bytes 1769480 | tf_op jit(solution)/shard_map/ppermute | solution.py:558
  411.4 50.5 %collective-permute-start.71 = (bf16[2,384,768]{2,1,0:T(8,128)(2,1)}, bf16[2,384,768]{2,1,0:T(8,128)(2,1)}, u32[]{:S(2)}, u32[]{:S(2)}) collective-permute-start(bf16[2,384,768]{2,1,0:T(8,128)(2,1)} %get-tuple-element.212.refs_20_), channel_id=1, source_target_pairs={{0,1},{1,0},{2,3},{3,2},{4,5},{5,4},{6,7},{7,6},{8,9},{9,8},{10,11... | collective-permute-start | bytes 3538952 | tf_op jit(solution)/shard_map/ppermute | solution.py:558
  411.8 28.5 %collective-permute-start.68 = (bf16[384,1536]{1,0:T(8,128)(2,1)S(1)}, bf16[384,1536]{1,0:T(8,128)(2,1)}, u32[]{:S(2)}, u32[]{:S(2)}) collective-permute-start(bf16[384,1536]{1,0:T(8,128)(2,1)S(1)} %pad_maximum_fusion.3.refs_21_), channel_id=1, source_target_pairs={{0,2},{2,0},{4,6},{6,4},{1,3},{3,1},{5,7},{7,5},{8,10},{10,8},{12,... | collective-permute-start | bytes 3538952 | tf_op jit(solution)/shard_map/ppermute | solution.py:558
  415.7 28.5 %collective-permute-start.69 = (bf16[384,1536]{1,0:T(8,128)(2,1)S(1)}, bf16[384,1536]{1,0:T(8,128)(2,1)}, u32[]{:S(2)}, u32[]{:S(2)}) collective-permute-start(bf16[384,1536]{1,0:T(8,128)(2,1)S(1)} %pad_maximum_fusion.4.refs_22_), channel_id=1, source_target_pairs={{0,4},{2,6},{4,0},{6,2},{1,5},{3,7},{5,1},{7,3},{8,12},{10,14},{12... | collective-permute-start | bytes 3538952 | tf_op jit(solution)/shard_map/ppermute | solution.py:558
  437.2 24.8 %collective-permute-start.67 = (bf16[2,384,768]{2,1,0:T(8,128)(2,1)}, bf16[2,384,768]{2,1,0:T(8,128)(2,1)}, u32[]{:S(2)}, u32[]{:S(2)}) collective-permute-start(bf16[2,384,768]{2,1,0:T(8,128)(2,1)} %get-tuple-element.218), channel_id=1, source_target_pairs={{0,1},{1,0},{2,3},{3,2},{4,5},{5,4},{6,7},{7,6},{8,9},{9,8},{10,11... | collective-permute-start | bytes 3538952 | tf_op jit(solution)/shard_map/ppermute | solution.py:558
  465.4 61.4 %reduce-scatter.6.cloned.1.call-start = ((), (), s32[]{:S(2)}) async-start(), calls=%async_computation.8 | async-start | bytes 983040 | tf_op jit(solution)/shard_map/reduce_scatter | solution.py:716
  480.6 19.3 %collective-permute-start.75 = (bf16[512,768]{1,0:T(8,128)(2,1)}, bf16[512,768]{1,0:T(8,128)(2,1)}, u32[]{:S(2)}, u32[]{:S(2)}) collective-permute-start(bf16[512,768]{1,0:T(8,128)(2,1)} %fusion.14), channel_id=1, source_target_pairs={{0,4},{2,6},{4,0},{6,2},{1,5},{3,7},{5,1},{7,3},{8,12},{10,14},{12... | collective-permute-start | bytes 2359304 | tf_op jit(solution)/shard_map/ppermute | solution.py:558
  481.7 18.8 %collective-permute-start.74 = (bf16[512,768]{1,0:T(8,128)(2,1)S(1)}, bf16[512,768]{1,0:T(8,128)(2,1)}, u32[]{:S(2)}, u32[]{:S(2)}) collective-permute-start(bf16[512,768]{1,0:T(8,128)(2,1)S(1)} %pad_maximum_fusion.7), channel_id=1, source_target_pairs={{0,2},{2,0},{4,6},{6,4},{1,3},{3,1},{5,7},{7,5},{8,10},{10,8},{12,... | collective-permute-start | bytes 2359304 | tf_op jit(solution)/shard_map/ppermute | solution.py:558
  (175 other events, 1000.0 us)
Sparse Core Ops, SparseCore 0:
  12.6 33.1 all-gather.3
  47.9 29.5 all-gather.5
  79.1 46.3 all-gather.7
  313.9 20.7 reduce-scatter.13
  387.8 21.9 reduce-scatter.7
  412.1 27.6 reduce-scatter.11
  465.6 28.9 reduce-scatter.9
  503.4 23.3 reduce-scatter.5

commit v6 on v5

--- a/solution.py
+++ b/solution.py
@@ -1003,7 +1003,7 @@
                 unit.near = tie(unit.near, weight_sum)
         sending = arrive(2 * layer + 1, middle)
         second, hidden, slope, output = call(
-            functools.partial(mlp_forward_kernel, run, mp, n // 4),
+            functools.partial(mlp_forward_kernel, run, mp, n // 2),
             [((n, D), BF), ((mp, n, fl), BF, "each"), ((mp, n, fl), F32, "each"), ((n, D), F32)],
             [pltpu.VMEM((mp, D, 2 * fl), BF), pltpu.SemaphoreType.DMA((parts,))],
             [place, middle, layer_vecs[layer], ("each", up_bias[layer])]

time: 608 us -> 602 us (level)
  no operation moved by 1% of the time
where the time goes in v6:
time: 602 us; the launch traced here: 595 us
  Pallas kernels  220 us (37%)
  waiting for transfers between devices  117 us (19%)
  other arithmetic  90.9 us (15%)
  local copies, waits for them, and re-layouts  68.2 us (11%)
  starting transfers between devices  65.3 us (11%)
  between operations  24.2 us (4%)
  matrix products  8.93 us (1%)
    pallas_call x18, Pallas kernels, call(): pl.pallas_call(grouped, out_shape=out_shape, in_specs=specs, out_specs=ou...  220 us
    ppermute x83, waiting for transfers between devices, swap(): lax.ppermute(values, axis, [(rank, rank ^ distance) for rank in range(siz...  101 us
    ppermute x83, starting transfers between devices, swap(): lax.ppermute(values, axis, [(rank, rank ^ distance) for rank in range(siz...  64.4 us
    convert_element_type x20, other arithmetic, add_low(): return (left.astype(F32) + right.astype(F32)).astype(BF)  18.6 us
    unnamed x272, local copies, waits for them, and re-layouts  17.5 us
    reduce_scatter x5, waiting for transfers between devices, rows(): self.pieces = lax.psum_scatter(total, 'dp', scatter_dimension=0, tiled=True)  15.3 us
    convert_element_type x4, other arithmetic, summed(): return jnp.concatenate(parts, axis=1).astype(BF).reshape(total.shape)  12.2 us
  transfers between devices with their start and end apart: 91, of which 34 were waited for; matrix products, arithmetic and copies ran while one was open for 20% of the time, Pallas kernels for 33%

profile of v6, /device:TPU:0, one launch (start us, length us, event | category | flops | bytes accessed | tf_op | source)
XLA Modules:
  0.0 594.9 jit_solution(11088461162154093269)
XLA Ops:
  10.7 1.8 concatenate.144
  12.5 3.0 collective-permute-start
  18.6 1.9 collective-permute-start.3
  37.7 1.8 add_multiply_fusion
  57.0 1.8 pad_maximum_fusion.12.refs_10_
  66.9 2.8 convolution_add_fusion.refs_1_.refs_2_
  69.8 7.8 %collective-permute-done.7.refs_6_.refs_10_ = bf16[384,768]{1,0:T(8,128)(2,1)S(1)} collective-permute-done((bf16[384,768]{1,0:T(8,128)(2,1)S(1)}, bf16[384,768]{1,0:T(8,128)(2,1)S(1)}, u32[]{:S(2)}, u32[]{:S(2)}) %collective-permute-start.7) | collective-permute-done | bytes 589856 | tf_op jit(solution)/shard_map/ppermute | solution.py:558
  80.1 6.2 %collective-permute-done.10.refs_9_.refs_13_ = bf16[192,768]{1,0:T(8,128)(2,1)S(1)} collective-permute-done((bf16[192,768]{1,0:T(8,128)(2,1)S(1)}, bf16[192,768]{1,0:T(8,128)(2,1)S(1)}, u32[]{:S(2)}, u32[]{:S(2)}) %collective-permute-start.10) | collective-permute-done | bytes 294944 | tf_op jit(solution)/shard_map/ppermute | solution.py:558
  94.8 20.3 %shard_map.427 = (bf16[576,768]{1,0:T(8,128)(2,1)}, bf16[4,576,576]{2,1,0:T(8,128)(2,1)}, bf16[4,576,192]{2,1,0:T(8,128)(2,1)}, f32[4,576,3]{2,1,0:T(8,128)}, f32[576,768]{1,0:T(8,128)}) custom-call(s32[1]{0:T(128)} %bitcast.8.refs_0_, f32[576,768]{1,0:T(8,128)} %convolution_add_fusion.refs_1_.refs_2_, f32[8,768]{1,0:T(8,128)} %slice_select_fusion.refs_2_.refs_3_, ...), custom_call_target="tpu_custom_call" | custom-call | flops 2300000000 | bytes 13924612 | tf_op jit(solution)/shard_map/pallas_call | solution.py:536
  119.9 2.0 collective-permute-done.20
  123.1 2.8 collective-permute-start.21
  127.3 3.9 collective-permute-start.22
  139.2 13.1 %shard_map.428 = (bf16[576,768]{1,0:T(8,128)(2,1)}, bf16[4,576,768]{2,1,0:T(8,128)(2,1)}, f32[4,576,768]{2,1,0:T(8,128)}, f32[576,768]{1,0:T(8,128)}) custom-call(s32[1]{0:T(128)} %bitcast.8.refs_0_, f32[576,768]{1,0:T(8,128)} %get-tuple-element.140.refs_1_.refs_2_, f32[8,768]{1,0:T(8,128)} %slice_select_fusion.refs_2_.refs_3_, f32[4,1,768]{2,1,0:T(1,128)} %copy.77.refs_3_, ...), custom_call_target="tpu_custom_call" | custom-call | flops 2300000000 | bytes 25104388 | tf_op jit(solution)/shard_map/pallas_call | solution.py:536
  156.3 4.9 collective-permute-done.30.refs_8_.refs_12_
  169.7 20.7 %shard_map.429 = (bf16[576,768]{1,0:T(8,128)(2,1)}, bf16[4,576,576]{2,1,0:T(8,128)(2,1)}, bf16[4,576,192]{2,1,0:T(8,128)(2,1)}, f32[4,576,3]{2,1,0:T(8,128)}, f32[576,768]{1,0:T(8,128)}) custom-call(s32[1]{0:T(128)} %bitcast.8.refs_0_, f32[576,768]{1,0:T(8,128)} %get-tuple-element.148.refs_1_.refs_2_, f32[8,768]{1,0:T(8,128)} %pad.81.refs_2_.refs_3_, ...), custom_call_target="tpu_custom_call" | custom-call | flops 2300000000 | bytes 14317828 | tf_op jit(solution)/shard_map/pallas_call | solution.py:536
  190.4 6.9 %collective-permute-done.37.refs_5_.refs_12_.refs_8_ = bf16[384,2048]{1,0:T(8,128)(2,1)S(1)} collective-permute-done((bf16[384,2048]{1,0:T(8,128)(2,1)S(1)}, bf16[384,2048]{1,0:T(8,128)(2,1)S(1)}, u32[]{:S(2)}, u32[]{:S(2)}) %collective-permute-start.37) | collective-permute-done | bytes 1572896 | tf_op jit(solution)/shard_map/ppermute | solution.py:558
  201.7 17.6 %collective-permute-done.39.refs_7_.refs_14_.refs_10_ = bf16[192,2048]{1,0:T(8,128)(2,1)} collective-permute-done((bf16[192,2048]{1,0:T(8,128)(2,1)S(1)}, bf16[192,2048]{1,0:T(8,128)(2,1)}, u32[]{:S(2)}, u32[]{:S(2)}) %collective-permute-start.39) | collective-permute-done | bytes 786464 | tf_op jit(solution)/shard_map/ppermute | solution.py:558
  223.3 13.1 %shard_map.430 = (bf16[576,768]{1,0:T(8,128)(2,1)}, bf16[4,576,768]{2,1,0:T(8,128)(2,1)}, f32[4,576,768]{2,1,0:T(8,128)}, f32[576,768]{1,0:T(8,128)}) custom-call(s32[1]{0:T(128)} %bitcast.8.refs_0_, f32[576,768]{1,0:T(8,128)} %get-tuple-element.155.refs_1_.refs_2_, f32[8,768]{1,0:T(8,128)} %pad.81.refs_2_.refs_3_, f32[4,1,768]{2,1,0:T(1,128)} %copy.79.refs_3_, ...), custom_call_target="tpu_custom_call" | custom-call | flops 2300000000 | bytes 27660292 | tf_op jit(solution)/shard_map/pallas_call | solution.py:536
  236.5 8.6 %shard_map.431 = (bf16[4,384,512]{2,1,0:T(8,128)(2,1)}, bf16[4,384,512]{2,1,0:T(8,128)(2,1)}, f32[4,1,512]{2,1,0:T(1,128)}, f32[576,768]{1,0:T(8,128)}, f32[8,768]{1,0:T(8,128)}, /*index=5*/f32[8,128]{1,0:T(8,128)}) custom-call(s32[1]{0:T(128)} %bitcast.8.refs_0_, f32[576,768]{1,0:T(8,128)} %get-tuple-element.158.refs_1_, f32[8,768]{1,0:T(8,128)} %pad.82.refs_2_, ...), custom_call_target="tpu_custom_call" | custom-call | flops 2300000000 | bytes 19807496 | tf_op jit(solution)/shard_map/pallas_call | solution.py:536
  247.7 14.1 %shard_map.432 = (f32[576,768]{1,0:T(8,128)}, bf16[2,384,1536]{2,1,0:T(8,128)(2,1)}, bf16[2,384,1536]{2,1,0:T(8,128)(2,1)}, f32[2,1,768]{2,1,0:T(1,128)}, f32[8,768]{1,0:T(8,128)}) custom-call(s32[1]{0:T(128)} %bitcast.8.refs_0_, f32[576,768]{1,0:T(8,128)} %get-tuple-element.159.refs_1_, f32[576,768]{1,0:T(8,128)} %get-tuple-element.155.refs_1_.refs_2_, ...), custom_call_target="tpu_custom_call" | custom-call | flops 2300000000 | bytes 35739652 | tf_op jit(solution)/shard_map/pallas_call | solution.py:536
  267.1 16.2 %shard_map.433 = (f32[576,768]{1,0:T(8,128)}, bf16[2,384,1536]{2,1,0:T(8,128)(2,1)}, bf16[2,384,1536]{2,1,0:T(8,128)(2,1)}, f32[2,1,768]{2,1,0:T(1,128)}, f32[8,768]{1,0:T(8,128)}) custom-call(s32[1]{0:T(128)} %bitcast.8.refs_0_, f32[576,768]{1,0:T(8,128)} %get-tuple-element.159.refs_1_, f32[576,768]{1,0:T(8,128)} %get-tuple-element.155.refs_1_.refs_2_, ...), custom_call_target="tpu_custom_call" | custom-call | flops 2300000000 | bytes 38688772 | tf_op jit(solution)/shard_map/pallas_call | solution.py:536
  289.4 17.8 %shard_map.434 = (f32[576,768]{1,0:T(8,128)}, bf16[2,384,768]{2,1,0:T(8,128)(2,1)}, bf16[2,384,768]{2,1,0:T(8,128)(2,1)}, f32[2,1,576]{2,1,0:T(1,128)}, f32[8,768]{1,0:T(8,128)}) custom-call(s32[1]{0:T(128)} %bitcast.8.refs_0_, f32[576,768]{1,0:T(8,128)} %get-tuple-element.168.refs_1_, f32[576,768]{1,0:T(8,128)} %get-tuple-element.148.refs_1_.refs_2_, ...), custom_call_target="tpu_custom_call" | custom-call | flops 2300000000 | bytes 21219076 | tf_op jit(solution)/shard_map/pallas_call | solution.py:536
  308.0 2.0 fusion.16.refs_21_
  317.6 20.3 %shard_map.435 = (f32[576,768]{1,0:T(8,128)}, bf16[2,384,768]{2,1,0:T(8,128)(2,1)}, bf16[2,384,768]{2,1,0:T(8,128)(2,1)}, f32[2,1,576]{2,1,0:T(1,128)}, f32[8,768]{1,0:T(8,128)}) custom-call(s32[1]{0:T(128)} %bitcast.8.refs_0_, f32[576,768]{1,0:T(8,128)} %get-tuple-element.168.refs_1_, f32[576,768]{1,0:T(8,128)} %get-tuple-element.148.refs_1_.refs_2_, ...), custom_call_target="tpu_custom_call" | custom-call | flops 2300000000 | bytes 22595332 | tf_op jit(solution)/shard_map/pallas_call | solution.py:536
  342.0 14.0 %shard_map.436 = (f32[576,768]{1,0:T(8,128)}, bf16[2,384,1536]{2,1,0:T(8,128)(2,1)}, bf16[2,384,1536]{2,1,0:T(8,128)(2,1)}, f32[2,1,768]{2,1,0:T(1,128)}, f32[8,768]{1,0:T(8,128)}) custom-call(s32[1]{0:T(128)} %bitcast.8.refs_0_, f32[576,768]{1,0:T(8,128)} %get-tuple-element.186.refs_1_, f32[576,768]{1,0:T(8,128)} %get-tuple-element.140.refs_1_.refs_2_, ...), custom_call_target="tpu_custom_call" | custom-call | flops 2300000000 | bytes 32790532 | tf_op jit(solution)/shard_map/pallas_call | solution.py:536
  361.4 3.6 fusion.1.refs_19_
  365.1 16.3 %shard_map.437 = (f32[576,768]{1,0:T(8,128)}, bf16[2,384,1536]{2,1,0:T(8,128)(2,1)}, bf16[2,384,1536]{2,1,0:T(8,128)(2,1)}, f32[2,1,768]{2,1,0:T(1,128)}, f32[8,768]{1,0:T(8,128)}) custom-call(s32[1]{0:T(128)} %bitcast.8.refs_0_, f32[576,768]{1,0:T(8,128)} %get-tuple-element.186.refs_1_, f32[576,768]{1,0:T(8,128)} %get-tuple-element.140.refs_1_.refs_2_, ...), custom_call_target="tpu_custom_call" | custom-call | flops 2300000000 | bytes 37509124 | tf_op jit(solution)/shard_map/pallas_call | solution.py:536
  381.5 2.5 fusion.8.refs_20_
  384.7 2.2 add_convert_fusion.2
  389.1 17.8 %shard_map.438 = (f32[576,768]{1,0:T(8,128)}, bf16[2,384,768]{2,1,0:T(8,128)(2,1)}, bf16[2,384,768]{2,1,0:T(8,128)(2,1)}, f32[2,1,576]{2,1,0:T(1,128)}, f32[8,768]{1,0:T(8,128)}) custom-call(s32[1]{0:T(128)} %bitcast.8.refs_0_, f32[576,768]{1,0:T(8,128)} %get-tuple-element.201.refs_1_, f32[576,768]{1,0:T(8,128)} %convolution_add_fusion.refs_1_.refs_2_, ...), custom_call_target="tpu_custom_call" | custom-call | flops 2300000000 | bytes 21022468 | tf_op jit(solution)/shard_map/pallas_call | solution.py:536
  413.0 20.4 %shard_map.439 = (f32[576,768]{1,0:T(8,128)}, bf16[2,384,768]{2,1,0:T(8,128)(2,1)}, bf16[2,384,768]{2,1,0:T(8,128)(2,1)}, f32[2,1,576]{2,1,0:T(1,128)}, f32[8,768]{1,0:T(8,128)}) custom-call(s32[1]{0:T(128)} %bitcast.8.refs_0_, f32[576,768]{1,0:T(8,128)} %get-tuple-element.201.refs_1_, f32[576,768]{1,0:T(8,128)} %convolution_add_fusion.refs_1_.refs_2_, ...), custom_call_target="tpu_custom_call" | custom-call | flops 2300000000 | bytes 22202116 | tf_op jit(solution)/shard_map/pallas_call | solution.py:536
  436.6 3.9 collective-permute-done.69
  440.5 4.1 fusion
  447.6 2.3 convolution_convert_fusion
  466.3 6.0 %collective-permute-done.72 = bf16[256,768]{1,0:T(8,128)(2,1)} collective-permute-done((bf16[256,768]{1,0:T(8,128)(2,1)}, bf16[256,768]{1,0:T(8,128)(2,1)}, u32[]{:S(2)}, u32[]{:S(2)}) %collective-permute-start.72) | collective-permute-done | bytes 393248 | tf_op jit(solution)/shard_map/ppermute | solution.py:558
  472.4 2.5 collective-permute-done.73
  483.2 13.0 %collective-permute-done.75 = bf16[512,768]{1,0:T(8,128)(2,1)} collective-permute-done((bf16[512,768]{1,0:T(8,128)(2,1)}, bf16[512,768]{1,0:T(8,128)(2,1)}, u32[]{:S(2)}, u32[]{:S(2)}) %collective-permute-start.75) | collective-permute-done | bytes 786464 | tf_op jit(solution)/shard_map/ppermute | solution.py:558
  504.2 3.5 multiply_reduce_fusion
  507.8 15.2 %reduce-scatter.6.cloned.1.call-done = bf16[128,768]{1,0:T(8,128)(2,1)} async-done(((bf16[512,768]{1,0:T(8,128)(2,1)}), bf16[128,768]{1,0:T(8,128)(2,1)}) %reduce-scatter.6.cloned.1.call-update) | async-done | bytes 196624 | tf_op jit(solution)/shard_map/reduce_scatter | solution.py:716
  525.0 3.2 multiply_reduce_fusion.2
  535.2 2.7 concatenate.180
  538.0 3.7 collective-permute-done.76.refs_2_
  544.5 4.2 collective-permute-done.77.refs_2_
  557.5 2.1 collective-permute-done.79.refs_2_
  563.8 3.1 collective-permute-done.80.refs_2_
  576.1 2.0 multiply_subtract_fusion.5
  578.0 2.5 multiply_subtract_fusion.3
  585.6 1.9 multiply_subtract_fusion.2
  (698 shorter events, 206.5 us)
Async XLA Ops:
  7.2 51.6 %all-gather.4.cloned.1.call-start = ((), (), s32[]{:S(2)}) async-start(), calls=%async_computation.5 | async-start | bytes 1474560 | tf_op jit(solution)/shard_map/all_gather | solution.py:856
  12.5 67.7 %all-gather.6.cloned.1.call-start = ((), (), s32[]{:S(2)}) async-start(), calls=%async_computation.6 | async-start | bytes 1474560 | tf_op jit(solution)/shard_map/all_gather | solution.py:856
  12.5 38.6 %collective-permute-start = (f32[2804]{0:T(1024)}, f32[2804]{0:T(1024)}, u32[]{:S(2)}, u32[]{:S(2)}) collective-permute-start(f32[2804]{0:T(1024)} %param.40), channel_id=1, source_target_pairs={{0,2},{2,0},{4,6},{6,4},{1,3},{3,1},{5,7},{7,5},{8,10},{10,8},{12,... | collective-permute-start | bytes 33656 | tf_op jit(solution)/shard_map/ppermute | solution.py:558
  15.5 36.3 %collective-permute-start.1 = (f32[2804]{0:T(1024)}, f32[2804]{0:T(1024)}, u32[]{:S(2)}, u32[]{:S(2)}) collective-permute-start(f32[2804]{0:T(1024)} %param.40), channel_id=1, source_target_pairs={{0,4},{2,6},{4,0},{6,2},{1,5},{3,7},{5,1},{7,3},{8,12},{10,14},{12... | collective-permute-start | bytes 33656 | tf_op jit(solution)/shard_map/ppermute | solution.py:558
  17.0 35.5 %collective-permute-start.2 = (f32[2804]{0:T(1024)}, f32[2804]{0:T(1024)}, u32[]{:S(2)}, u32[]{:S(2)}) collective-permute-start(f32[2804]{0:T(1024)} %param.40), channel_id=1, source_target_pairs={{0,6},{2,4},{4,2},{6,0},{1,7},{3,5},{5,3},{7,1},{8,14},{10,12},{12... | collective-permute-start | bytes 33656 | tf_op jit(solution)/shard_map/ppermute | solution.py:558
  18.6 36.7 %collective-permute-start.3 = (bf16[224,256]{1,0:T(8,128)(2,1)}, bf16[224,256]{1,0:T(8,128)(2,1)}, u32[]{:S(2)}, u32[]{:S(2)}) collective-permute-start(bf16[224,256]{1,0:T(8,128)(2,1)} %get-tuple-element.338), channel_id=1, source_target_pairs={{0,2},{2,0},{4,6},{6,4},{1,3},{3,1},{5,7},{7,5},{8,10},{10,8},{12,... | collective-permute-start | bytes 344072 | tf_op jit(solution)/shard_map/ppermute | solution.py:558
  20.6 34.7 %collective-permute-start.4 = (bf16[224,256]{1,0:T(8,128)(2,1)}, bf16[224,256]{1,0:T(8,128)(2,1)}, u32[]{:S(2)}, u32[]{:S(2)}) collective-permute-start(bf16[224,256]{1,0:T(8,128)(2,1)} %get-tuple-element.338), channel_id=1, source_target_pairs={{0,4},{2,6},{4,0},{6,2},{1,5},{3,7},{5,1},{7,3},{8,12},{10,14},{12... | collective-permute-start | bytes 344072 | tf_op jit(solution)/shard_map/ppermute | solution.py:558
  25.0 107.6 %all-gather.8.cloned.1.call-start = ((), (), s32[]{:S(2)}) async-start(), calls=%async_computation.7 | async-start | bytes 2703360 | tf_op jit(solution)/shard_map/all_gather | solution.py:856
  61.5 418.8 %reduce-scatter.14.cloned.1.call-start = ((), (), s32[]{:S(2)}) async-start(), calls=%async_computation.12 | async-start | bytes 491520 | tf_op jit(solution)/shard_map/reduce_scatter | solution.py:716
  87.5 27.7 %collective-permute-start.16 = (bf16[384,1536]{1,0:T(8,128)(2,1)}, bf16[384,1536]{1,0:T(8,128)(2,1)S(1)}, u32[]{:S(2)}, u32[]{:S(2)}) collective-permute-start(bf16[384,1536]{1,0:T(8,128)(2,1)} %all-gather.6.cloned.1.call-done.refs_15_.refs_4_.refs_7_), channel_id=1, source_target_pairs={{0,2},{2,0},{4,6},{6,4},{1,3},{3,1},{5,7},{7,5},{8,10},{10,8},{12,... | collective-permute-start | bytes 3538952 | tf_op jit(solution)/shard_map/ppermute | solution.py:558
  88.6 26.6 %collective-permute-start.17 = (bf16[384,1536]{1,0:T(8,128)(2,1)}, bf16[384,1536]{1,0:T(8,128)(2,1)S(1)}, u32[]{:S(2)}, u32[]{:S(2)}) collective-permute-start(bf16[384,1536]{1,0:T(8,128)(2,1)} %all-gather.6.cloned.1.call-done.refs_15_.refs_4_.refs_7_), channel_id=1, source_target_pairs={{0,4},{2,6},{4,0},{6,2},{1,5},{3,7},{5,1},{7,3},{8,12},{10,14},{12... | collective-permute-start | bytes 3538952 | tf_op jit(solution)/shard_map/ppermute | solution.py:558
  134.3 18.0 %collective-permute-start.28 = (bf16[384,768]{1,0:T(8,128)(2,1)S(1)}, bf16[384,768]{1,0:T(8,128)(2,1)S(1)}, u32[]{:S(2)}, u32[]{:S(2)}) collective-permute-start(bf16[384,768]{1,0:T(8,128)(2,1)S(1)} %slice.983.refs_14_.refs_5_.refs_9_), channel_id=1, source_target_pairs={{0,2},{2,0},{4,6},{6,4},{1,3},{3,1},{5,7},{7,5},{8,10},{10,8},{12,... | collective-permute-start | bytes 1769480 | tf_op jit(solution)/shard_map/ppermute | solution.py:558
  162.4 35.0 %collective-permute-start.37 = (bf16[384,2048]{1,0:T(8,128)(2,1)S(1)}, bf16[384,2048]{1,0:T(8,128)(2,1)S(1)}, u32[]{:S(2)}, u32[]{:S(2)}) collective-permute-start(bf16[384,2048]{1,0:T(8,128)(2,1)S(1)} %slice.984.refs_15_.refs_4_.refs_11_.refs_7_), channel_id=1, source_target_pairs={{0,2},{2,0},{4,6},{6,4},{1,3},{3,1},{5,7},{7,5},{8,10},{10,8},{12,... | collective-permute-start | bytes 4718600 | tf_op jit(solution)/shard_map/ppermute | solution.py:558
  163.1 34.8 %collective-permute-start.38 = (bf16[384,2048]{1,0:T(8,128)(2,1)S(1)}, bf16[384,2048]{1,0:T(8,128)(2,1)}, u32[]{:S(2)}, u32[]{:S(2)}) collective-permute-start(bf16[384,2048]{1,0:T(8,128)(2,1)S(1)} %slice.984.refs_15_.refs_4_.refs_11_.refs_7_), channel_id=1, source_target_pairs={{0,4},{2,6},{4,0},{6,2},{1,5},{3,7},{5,1},{7,3},{8,12},{10,14},{12... | collective-permute-start | bytes 4718600 | tf_op jit(solution)/shard_map/ppermute | solution.py:558
  167.9 53.5 %collective-permute-start.41 = (bf16[384,2048]{1,0:T(8,128)(2,1)S(1)}, bf16[384,2048]{1,0:T(8,128)(2,1)}, u32[]{:S(2)}, u32[]{:S(2)}) collective-permute-start(bf16[384,2048]{1,0:T(8,128)(2,1)S(1)} %slice.984.refs_15_.refs_4_.refs_11_.refs_7_), channel_id=1, source_target_pairs={{0,1},{1,0},{2,3},{3,2},{4,5},{5,4},{6,7},{7,6},{8,9},{9,8},{10,11... | collective-permute-start | bytes 4718600 | tf_op jit(solution)/shard_map/ppermute | solution.py:558
  197.9 23.4 %collective-permute-start.42 = (bf16[384,2048]{1,0:T(8,128)(2,1)S(1)}, bf16[384,2048]{1,0:T(8,128)(2,1)}, u32[]{:S(2)}, u32[]{:S(2)}) collective-permute-start(bf16[384,2048]{1,0:T(8,128)(2,1)S(1)} %collective-permute-done.37.refs_5_.refs_12_.refs_8_), channel_id=1, source_target_pairs={{0,1},{1,0},{2,3},{3,2},{4,5},{5,4},{6,7},{7,6},{8,9},{9,8},{10,11... | collective-permute-start | bytes 4718600 | tf_op jit(solution)/shard_map/ppermute | solution.py:558
  199.2 20.1 %collective-permute-start.39 = (bf16[192,2048]{1,0:T(8,128)(2,1)S(1)}, bf16[192,2048]{1,0:T(8,128)(2,1)}, u32[]{:S(2)}, u32[]{:S(2)}) collective-permute-start(bf16[192,2048]{1,0:T(8,128)(2,1)S(1)} %slice.776), channel_id=1, source_target_pairs={{0,2},{2,0},{4,6},{6,4},{1,3},{3,1},{5,7},{7,5},{8,10},{10,8},{12,... | collective-permute-start | bytes 2359304 | tf_op jit(solution)/shard_map/ppermute | solution.py:558
  200.6 20.7 %collective-permute-start.43 = (bf16[384,2048]{1,0:T(8,128)(2,1)}, bf16[384,2048]{1,0:T(8,128)(2,1)}, u32[]{:S(2)}, u32[]{:S(2)}) collective-permute-start(bf16[384,2048]{1,0:T(8,128)(2,1)} %collective-permute-done.38.refs_6_.refs_13_.refs_9_), channel_id=1, source_target_pairs={{0,1},{1,0},{2,3},{3,2},{4,5},{5,4},{6,7},{7,6},{8,9},{9,8},{10,11... | collective-permute-start | bytes 4718600 | tf_op jit(solution)/shard_map/ppermute | solution.py:558
  200.8 19.8 %collective-permute-start.40 = (bf16[192,2048]{1,0:T(8,128)(2,1)S(1)}, bf16[192,2048]{1,0:T(8,128)(2,1)}, u32[]{:S(2)}, u32[]{:S(2)}) collective-permute-start(bf16[192,2048]{1,0:T(8,128)(2,1)S(1)} %slice.777), channel_id=1, source_target_pairs={{0,4},{2,6},{4,0},{6,2},{1,5},{3,7},{5,1},{7,3},{8,12},{10,14},{12... | collective-permute-start | bytes 2359304 | tf_op jit(solution)/shard_map/ppermute | solution.py:558
  245.1 18.6 %collective-permute-start.46 = (bf16[4,384,512]{2,1,0:T(8,128)(2,1)}, bf16[4,384,512]{2,1,0:T(8,128)(2,1)S(1)}, u32[]{:S(2)}, u32[]{:S(2)}) collective-permute-start(bf16[4,384,512]{2,1,0:T(8,128)(2,1)} %get-tuple-element.163.refs_17_), channel_id=1, source_target_pairs={{0,1},{1,0},{2,3},{3,2},{4,5},{5,4},{6,7},{7,6},{8,9},{9,8},{10,11... | collective-permute-start | bytes 4718600 | tf_op jit(solution)/shard_map/ppermute | solution.py:558
  261.8 24.8 %collective-permute-start.49 = (bf16[2,384,1536]{2,1,0:T(8,128)(2,1)}, bf16[2,384,1536]{2,1,0:T(8,128)(2,1)S(1)}, u32[]{:S(2)}, u32[]{:S(2)}) collective-permute-start(bf16[2,384,1536]{2,1,0:T(8,128)(2,1)} %get-tuple-element.165.refs_18_), channel_id=1, source_target_pairs={{0,1},{1,0},{2,3},{3,2},{4,5},{5,4},{6,7},{7,6},{8,9},{9,8},{10,11... | collective-permute-start | bytes 7077896 | tf_op jit(solution)/shard_map/ppermute | solution.py:558
  265.0 19.2 %collective-permute-start.47 = (bf16[192,512]{1,0:T(8,128)(2,1)S(1)}, bf16[192,512]{1,0:T(8,128)(2,1)S(1)}, u32[]{:S(2)}, u32[]{:S(2)}) collective-permute-start(bf16[192,512]{1,0:T(8,128)(2,1)S(1)} %get-tuple-element.317.refs_19_), channel_id=1, source_target_pairs={{0,2},{2,0},{4,6},{6,4},{1,3},{3,1},{5,7},{7,5},{8,10},{10,8},{12,... | collective-permute-start | bytes 589832 | tf_op jit(solution)/shard_map/ppermute | solution.py:558
  266.2 18.0 %collective-permute-start.48 = (bf16[192,512]{1,0:T(8,128)(2,1)S(1)}, bf16[192,512]{1,0:T(8,128)(2,1)S(1)}, u32[]{:S(2)}, u32[]{:S(2)}) collective-permute-start(bf16[192,512]{1,0:T(8,128)(2,1)S(1)} %get-tuple-element.316.refs_20_), channel_id=1, source_target_pairs={{0,4},{2,6},{4,0},{6,2},{1,5},{3,7},{5,1},{7,3},{8,12},{10,14},{12... | collective-permute-start | bytes 589832 | tf_op jit(solution)/shard_map/ppermute | solution.py:558
  283.3 29.2 %collective-permute-start.54 = (bf16[2,384,1536]{2,1,0:T(8,128)(2,1)}, bf16[2,384,1536]{2,1,0:T(8,128)(2,1)}, u32[]{:S(2)}, u32[]{:S(2)}) collective-permute-start(bf16[2,384,1536]{2,1,0:T(8,128)(2,1)} %get-tuple-element.173.refs_19_), channel_id=1, source_target_pairs={{0,1},{1,0},{2,3},{3,2},{4,5},{5,4},{6,7},{7,6},{8,9},{9,8},{10,11... | collective-permute-start | bytes 7077896 | tf_op jit(solution)/shard_map/ppermute | solution.py:558
  284.3 22.9 %collective-permute-start.51 = (bf16[384,512]{1,0:T(8,128)(2,1)S(1)}, bf16[384,512]{1,0:T(8,128)(2,1)S(1)}, u32[]{:S(2)}, u32[]{:S(2)}) collective-permute-start(bf16[384,512]{1,0:T(8,128)(2,1)S(1)} %pad_maximum_fusion.16.refs_21_), channel_id=1, source_target_pairs={{0,4},{2,6},{4,0},{6,2},{1,5},{3,7},{5,1},{7,3},{8,12},{10,14},{12... | collective-permute-start | bytes 1179656 | tf_op jit(solution)/shard_map/ppermute | solution.py:558
  285.6 21.6 %collective-permute-start.50 = (bf16[384,512]{1,0:T(8,128)(2,1)S(1)}, bf16[384,512]{1,0:T(8,128)(2,1)S(1)}, u32[]{:S(2)}, u32[]{:S(2)}) collective-permute-start(bf16[384,512]{1,0:T(8,128)(2,1)S(1)} %pad_maximum_fusion.15.refs_20_), channel_id=1, source_target_pairs={{0,2},{2,0},{4,6},{6,4},{1,3},{3,1},{5,7},{7,5},{8,10},{10,8},{12,... | collective-permute-start | bytes 1179656 | tf_op jit(solution)/shard_map/ppermute | solution.py:558
  287.3 22.8 %collective-permute-start.52 = (bf16[192,1536]{1,0:T(8,128)(2,1)S(1)}, bf16[192,1536]{1,0:T(8,128)(2,1)}, u32[]{:S(2)}, u32[]{:S(2)}) collective-permute-start(bf16[192,1536]{1,0:T(8,128)(2,1)S(1)} %get-tuple-element.291.refs_22_), channel_id=1, source_target_pairs={{0,2},{2,0},{4,6},{6,4},{1,3},{3,1},{5,7},{7,5},{8,10},{10,8},{12,... | collective-permute-start | bytes 1769480 | tf_op jit(solution)/shard_map/ppermute | solution.py:558
  288.5 21.6 %collective-permute-start.53 = (bf16[192,1536]{1,0:T(8,128)(2,1)S(1)}, bf16[192,1536]{1,0:T(8,128)(2,1)}, u32[]{:S(2)}, u32[]{:S(2)}) collective-permute-start(bf16[192,1536]{1,0:T(8,128)(2,1)S(1)} %get-tuple-element.290.refs_23_), channel_id=1, source_target_pairs={{0,4},{2,6},{4,0},{6,2},{1,5},{3,7},{5,1},{7,3},{8,12},{10,14},{12... | collective-permute-start | bytes 1769480 | tf_op jit(solution)/shard_map/ppermute | solution.py:558
  307.2 31.0 %collective-permute-start.55 = (bf16[2,384,768]{2,1,0:T(8,128)(2,1)}, bf16[2,384,768]{2,1,0:T(8,128)(2,1)}, u32[]{:S(2)}, u32[]{:S(2)}) collective-permute-start(bf16[2,384,768]{2,1,0:T(8,128)(2,1)} %get-tuple-element.179.refs_20_), channel_id=1, source_target_pairs={{0,1},{1,0},{2,3},{3,2},{4,5},{5,4},{6,7},{7,6},{8,9},{9,8},{10,11... | collective-permute-start | bytes 3538952 | tf_op jit(solution)/shard_map/ppermute | solution.py:558
  310.0 172.2 %reduce-scatter.8.cloned.1.call-start = ((), (), s32[]{:S(2)}) async-start(), calls=%async_computation.9 | async-start | bytes 737280 | tf_op jit(solution)/shard_map/reduce_scatter | solution.py:716
  311.5 48.9 %collective-permute-start.56 = (bf16[384,1536]{1,0:T(8,128)(2,1)S(1)}, bf16[384,1536]{1,0:T(8,128)(2,1)}, u32[]{:S(2)}, u32[]{:S(2)}) collective-permute-start(bf16[384,1536]{1,0:T(8,128)(2,1)S(1)} %pad_maximum_fusion.1.refs_22_), channel_id=1, source_target_pairs={{0,2},{2,0},{4,6},{6,4},{1,3},{3,1},{5,7},{7,5},{8,10},{10,8},{12,... | collective-permute-start | bytes 3538952 | tf_op jit(solution)/shard_map/ppermute | solution.py:558
  316.4 44.0 %collective-permute-start.57 = (bf16[384,1536]{1,0:T(8,128)(2,1)S(1)}, bf16[384,1536]{1,0:T(8,128)(2,1)}, u32[]{:S(2)}, u32[]{:S(2)}) collective-permute-start(bf16[384,1536]{1,0:T(8,128)(2,1)S(1)} %pad_maximum_fusion.2.refs_23_), channel_id=1, source_target_pairs={{0,4},{2,6},{4,0},{6,2},{1,5},{3,7},{5,1},{7,3},{8,12},{10,14},{12... | collective-permute-start | bytes 3538952 | tf_op jit(solution)/shard_map/ppermute | solution.py:558
  337.9 21.1 %collective-permute-start.60 = (bf16[2,384,768]{2,1,0:T(8,128)(2,1)}, bf16[2,384,768]{2,1,0:T(8,128)(2,1)}, u32[]{:S(2)}, u32[]{:S(2)}) collective-permute-start(bf16[2,384,768]{2,1,0:T(8,128)(2,1)} %get-tuple-element.190.refs_17_), channel_id=1, source_target_pairs={{0,1},{1,0},{2,3},{3,2},{4,5},{5,4},{6,7},{7,6},{8,9},{9,8},{10,11... | collective-permute-start | bytes 3538952 | tf_op jit(solution)/shard_map/ppermute | solution.py:558
  356.0 28.7 %collective-permute-start.63 = (bf16[2,384,1536]{2,1,0:T(8,128)(2,1)}, bf16[2,384,1536]{2,1,0:T(8,128)(2,1)}, u32[]{:S(2)}, u32[]{:S(2)}) collective-permute-start(bf16[2,384,1536]{2,1,0:T(8,128)(2,1)} %get-tuple-element.194.refs_18_), channel_id=1, source_target_pairs={{0,1},{1,0},{2,3},{3,2},{4,5},{5,4},{6,7},{7,6},{8,9},{9,8},{10,11... | collective-permute-start | bytes 7077896 | tf_op jit(solution)/shard_map/ppermute | solution.py:558
  357.8 23.5 %collective-permute-start.61 = (bf16[384,768]{1,0:T(8,128)(2,1)S(1)}, bf16[384,768]{1,0:T(8,128)(2,1)}, u32[]{:S(2)}, u32[]{:S(2)}) collective-permute-start(bf16[384,768]{1,0:T(8,128)(2,1)S(1)} %pad_maximum_fusion.10.refs_20_), channel_id=1, source_target_pairs={{0,2},{2,0},{4,6},{6,4},{1,3},{3,1},{5,7},{7,5},{8,10},{10,8},{12,... | collective-permute-start | bytes 1769480 | tf_op jit(solution)/shard_map/ppermute | solution.py:558
  360.5 20.9 %collective-permute-start.62 = (bf16[384,768]{1,0:T(8,128)(2,1)S(1)}, bf16[384,768]{1,0:T(8,128)(2,1)S(1)}, u32[]{:S(2)}, u32[]{:S(2)}) collective-permute-start(bf16[384,768]{1,0:T(8,128)(2,1)S(1)} %pad_maximum_fusion.11.refs_21_), channel_id=1, source_target_pairs={{0,4},{2,6},{4,0},{6,2},{1,5},{3,7},{5,1},{7,3},{8,12},{10,14},{12... | collective-permute-start | bytes 1769480 | tf_op jit(solution)/shard_map/ppermute | solution.py:558
  384.0 116.5 %reduce-scatter.12.cloned.1.call-start = ((), (), s32[]{:S(2)}) async-start(), calls=%async_computation.11 | async-start | bytes 1474560 | tf_op jit(solution)/shard_map/reduce_scatter | solution.py:716
  384.2 25.1 %collective-permute-start.66 = (bf16[2,384,1536]{2,1,0:T(8,128)(2,1)}, bf16[2,384,1536]{2,1,0:T(8,128)(2,1)}, u32[]{:S(2)}, u32[]{:S(2)}) collective-permute-start(bf16[2,384,1536]{2,1,0:T(8,128)(2,1)} %get-tuple-element.206.refs_19_), channel_id=1, source_target_pairs={{0,1},{1,0},{2,3},{3,2},{4,5},{5,4},{6,7},{7,6},{8,9},{9,8},{10,11... | collective-permute-start | bytes 7077896 | tf_op jit(solution)/shard_map/ppermute | solution.py:558
  384.6 117.0 %reduce-scatter.10.cloned.1.call-start = ((), (), s32[]{:S(2)}) async-start(), calls=%async_computation.10 | async-start | bytes 1474560 | tf_op jit(solution)/shard_map/reduce_scatter | solution.py:716
  387.0 20.8 %collective-permute-start.64 = (bf16[192,1536]{1,0:T(8,128)(2,1)S(1)}, bf16[192,1536]{1,0:T(8,128)(2,1)S(1)}, u32[]{:S(2)}, u32[]{:S(2)}) collective-permute-start(bf16[192,1536]{1,0:T(8,128)(2,1)S(1)} %get-tuple-element.289.refs_21_), channel_id=1, source_target_pairs={{0,2},{2,0},{4,6},{6,4},{1,3},{3,1},{5,7},{7,5},{8,10},{10,8},{12,... | collective-permute-start | bytes 1769480 | tf_op jit(solution)/shard_map/ppermute | solution.py:558
  388.0 19.8 %collective-permute-start.65 = (bf16[192,1536]{1,0:T(8,128)(2,1)S(1)}, bf16[192,1536]{1,0:T(8,128)(2,1)S(1)}, u32[]{:S(2)}, u32[]{:S(2)}) collective-permute-start(bf16[192,1536]{1,0:T(8,128)(2,1)S(1)} %get-tuple-element.288.refs_22_), channel_id=1, source_target_pairs={{0,4},{2,6},{4,0},{6,2},{1,5},{3,7},{5,1},{7,3},{8,12},{10,14},{12... | collective-permute-start | bytes 1769480 | tf_op jit(solution)/shard_map/ppermute | solution.py:558
  407.7 50.5 %collective-permute-start.71 = (bf16[2,384,768]{2,1,0:T(8,128)(2,1)}, bf16[2,384,768]{2,1,0:T(8,128)(2,1)}, u32[]{:S(2)}, u32[]{:S(2)}) collective-permute-start(bf16[2,384,768]{2,1,0:T(8,128)(2,1)} %get-tuple-element.212.refs_20_), channel_id=1, source_target_pairs={{0,1},{1,0},{2,3},{3,2},{4,5},{5,4},{6,7},{7,6},{8,9},{9,8},{10,11... | collective-permute-start | bytes 3538952 | tf_op jit(solution)/shard_map/ppermute | solution.py:558
  408.1 28.5 %collective-permute-start.68 = (bf16[384,1536]{1,0:T(8,128)(2,1)S(1)}, bf16[384,1536]{1,0:T(8,128)(2,1)}, u32[]{:S(2)}, u32[]{:S(2)}) collective-permute-start(bf16[384,1536]{1,0:T(8,128)(2,1)S(1)} %pad_maximum_fusion.3.refs_21_), channel_id=1, source_target_pairs={{0,2},{2,0},{4,6},{6,4},{1,3},{3,1},{5,7},{7,5},{8,10},{10,8},{12,... | collective-permute-start | bytes 3538952 | tf_op jit(solution)/shard_map/ppermute | solution.py:558
  411.9 28.5 %collective-permute-start.69 = (bf16[384,1536]{1,0:T(8,128)(2,1)S(1)}, bf16[384,1536]{1,0:T(8,128)(2,1)}, u32[]{:S(2)}, u32[]{:S(2)}) collective-permute-start(bf16[384,1536]{1,0:T(8,128)(2,1)S(1)} %pad_maximum_fusion.4.refs_22_), channel_id=1, source_target_pairs={{0,4},{2,6},{4,0},{6,2},{1,5},{3,7},{5,1},{7,3},{8,12},{10,14},{12... | collective-permute-start | bytes 3538952 | tf_op jit(solution)/shard_map/ppermute | solution.py:558
  433.4 24.8 %collective-permute-start.67 = (bf16[2,384,768]{2,1,0:T(8,128)(2,1)}, bf16[2,384,768]{2,1,0:T(8,128)(2,1)}, u32[]{:S(2)}, u32[]{:S(2)}) collective-permute-start(bf16[2,384,768]{2,1,0:T(8,128)(2,1)} %get-tuple-element.218), channel_id=1, source_target_pairs={{0,1},{1,0},{2,3},{3,2},{4,5},{5,4},{6,7},{7,6},{8,9},{9,8},{10,11... | collective-permute-start | bytes 3538952 | tf_op jit(solution)/shard_map/ppermute | solution.py:558
  461.7 61.3 %reduce-scatter.6.cloned.1.call-start = ((), (), s32[]{:S(2)}) async-start(), calls=%async_computation.8 | async-start | bytes 983040 | tf_op jit(solution)/shard_map/reduce_scatter | solution.py:716
  476.9 19.3 %collective-permute-start.75 = (bf16[512,768]{1,0:T(8,128)(2,1)}, bf16[512,768]{1,0:T(8,128)(2,1)}, u32[]{:S(2)}, u32[]{:S(2)}) collective-permute-start(bf16[512,768]{1,0:T(8,128)(2,1)} %fusion.14), channel_id=1, source_target_pairs={{0,4},{2,6},{4,0},{6,2},{1,5},{3,7},{5,1},{7,3},{8,12},{10,14},{12... | collective-permute-start | bytes 2359304 | tf_op jit(solution)/shard_map/ppermute | solution.py:558
  478.0 18.8 %collective-permute-start.74 = (bf16[512,768]{1,0:T(8,128)(2,1)S(1)}, bf16[512,768]{1,0:T(8,128)(2,1)}, u32[]{:S(2)}, u32[]{:S(2)}) collective-permute-start(bf16[512,768]{1,0:T(8,128)(2,1)S(1)} %pad_maximum_fusion.7), channel_id=1, source_target_pairs={{0,2},{2,0},{4,6},{6,4},{1,3},{3,1},{5,7},{7,5},{8,10},{10,8},{12,... | collective-permute-start | bytes 2359304 | tf_op jit(solution)/shard_map/ppermute | solution.py:558
  (175 other events, 998.4 us)
Sparse Core Ops, SparseCore 0:
  12.6 33.1 all-gather.3
  47.9 29.5 all-gather.5
  79.1 46.3 all-gather.7
  310.2 20.6 reduce-scatter.13
  384.1 21.9 reduce-scatter.7
  408.4 27.5 reduce-scatter.11
  461.8 28.9 reduce-scatter.9
  499.7 23.3 reduce-scatter.5
